TPU v7x, 32 devices: a whole 2x2x4 slice. The times are simulated.
32 devices in a mesh: group: 4 (over y, core), tensor: 8 (over z, x).
Axes of the slice: x: 2, y: 2, z: 4, core: 2. Of those that a mesh axis runs over, the one named last changes fastest.
Arguments:
- resp_query: bfloat16 [256, 4096], P('group', 'tensor'), may hold values from -80 to 80
- resp_key: bfloat16 [256, 4096], P('group', 'tensor'), may hold values from -4 to 4
- resp_value: bfloat16 [256, 4096], P('group', 'tensor'), may hold values from -8 to 8
- prompt_keys: bfloat16 [2048, 4096], P('group', 'tensor'), may hold values from -5 to 5
- prompt_values: bfloat16 [2048, 4096], P('group', 'tensor'), may hold values from -8 to 8
- prompt_of: int32 [8], P('group'), may hold values from 0 to 3
- lengths: int32 [8], P('group'), may hold values from 1 to 32
- residual: bfloat16 [256, 5120], P('group'), may hold values from -4 to 4
- out_weight: bfloat16 [4096, 5120], P('tensor'), may hold values from -0.09375 to 0.09375
- norm_gain: bfloat16 [5120], replicated, may hold values from 0.25 to 1.75
- lm_weight: bfloat16 [5120, 98304], P(None, ('group', 'tensor')), may hold values from -10 to 10
- targets: int32 [256], replicated, may hold values from 0 to 98303
Outputs:
- logprobs: float32 [256], P(('group', 'tensor'))
Inputs may be any that keep to these rules, and one draw needn't show every extreme that they name: prompt_of[r] names the prompt whose keys and values precede response r.
All inputs are finite; a program needn't handle non-finite values.
Results may differ from a plain program's by a relative error of at most 0.0013.
Values may be sent and summed in bfloat16 or wider, within the bound.
No kernel may reach another device: no remote copies, remote signals or barrier semaphores. Data moves between devices by JAX's collectives and lax.ppermute only.
A program may use at most 128 MiB of HBM per device.

v0:
```python
import jax
import jax.numpy as jnp
from jax import lax
from jax.sharding import PartitionSpec as P

HEAD_DIM = 128


NEG = -1e30


def attend(queries, key_rows, value_rows, allowed):
    factor = queries.shape[-1] ** (-0.5)
    scores = (
        jnp.einsum("qhd,khd->hqk", queries, key_rows, preferred_element_type=jnp.float32) * factor
    )
    scores = jnp.where(allowed[None], scores, NEG)
    peak = jnp.max(scores, axis=2)
    weights = jnp.where(allowed[None], jnp.exp(scores - peak[:, :, None]), 0.0)
    totals = jnp.sum(weights, axis=2)
    mixed = jnp.einsum(
        "hqk,khd->hqd", weights, value_rows.astype(jnp.float32), precision=lax.Precision.HIGHEST
    )
    return (peak, totals, mixed)


def combine(former, latter):
    peak = jnp.maximum(former[0], latter[0])
    left_part = jnp.exp(former[0] - peak)
    right_part = jnp.exp(latter[0] - peak)
    return (
        peak,
        former[1] * left_part + latter[1] * right_part,
        former[2] * left_part[..., None] + latter[2] * right_part[..., None],
    )


def normalize(hidden, norm_gain):
    squares = jnp.mean(hidden * hidden, axis=-1, keepdims=True)
    return (hidden * lax.rsqrt(squares + 1e-06) * norm_gain.astype(jnp.float32)).astype(
        jnp.bfloat16
    )


def per_row(row_resp, slot_ids, table):
    return jnp.sum(jnp.where(row_resp[:, None] == slot_ids[None, :], table[None, :], 0), axis=1)


def local(
    resp_query,
    resp_key,
    resp_value,
    prompt_keys,
    prompt_values,
    prompt_of,
    lengths,
    residual,
    out_weight,
    norm_gain,
    lm_weight,
    targets,
):
    head_dim = HEAD_DIM
    row_total = resp_query.shape[0]
    heads_here = resp_query.shape[1] // head_dim
    resp_here = prompt_of.shape[0]
    seq_length = row_total // resp_here
    prompt_length = prompt_keys.shape[0]
    queries = resp_query.reshape(row_total, heads_here, head_dim)
    row_index = jnp.arange(row_total, dtype=jnp.int32)
    row_resp = row_index // seq_length
    row_pos = row_index % seq_length
    slot_ids = jnp.arange(resp_here, dtype=jnp.int32)
    row_prompt = per_row(row_resp, slot_ids, prompt_of)
    row_length = per_row(row_resp, slot_ids, lengths)
    start_state = (
        jnp.full((heads_here, row_total), NEG, jnp.float32),
        jnp.zeros((heads_here, row_total), jnp.float32),
        jnp.zeros((heads_here, row_total, head_dim), jnp.float32),
    )
    key_rows = lax.all_gather(prompt_keys, "group", axis=0, tiled=True)
    value_rows = lax.all_gather(prompt_values, "group", axis=0, tiled=True)
    row_count = key_rows.shape[0]
    key_prompt = jnp.arange(row_count, dtype=jnp.int32) // prompt_length
    allowed = row_prompt[:, None] == key_prompt[None, :]
    found = attend(
        queries,
        key_rows.reshape(row_count, heads_here, head_dim),
        value_rows.reshape(row_count, heads_here, head_dim),
        allowed,
    )
    prefix = combine(start_state, found)
    causal = (
        (row_resp[:, None] == row_resp[None, :])
        & (row_pos[None, :] <= row_pos[:, None])
        & (row_pos[None, :] < row_length[None, :])
    )
    own_stats = attend(
        queries,
        resp_key.reshape(row_total, heads_here, head_dim),
        resp_value.reshape(row_total, heads_here, head_dim),
        causal,
    )
    whole = combine(prefix, own_stats)
    attended = (
        (whole[2] / whole[1][:, :, None])
        .transpose(1, 0, 2)
        .reshape(row_total, heads_here * head_dim)
        .astype(jnp.bfloat16)
    )
    partial_value = jnp.dot(attended, out_weight, preferred_element_type=jnp.float32)
    tensor_index = lax.axis_index("tensor")
    share_rows = row_total // lax.axis_size("tensor")
    voc_here = lm_weight.shape[1]
    flat_index = lax.axis_index(("group", "tensor"))
    vocab_ids = flat_index * voc_here + jnp.arange(voc_here, dtype=jnp.int32)
    summed = lax.psum_scatter(partial_value, "tensor", scatter_dimension=0, tiled=True)
    own_resid = lax.dynamic_slice_in_dim(residual, tensor_index * share_rows, share_rows, 0)
    normed = normalize(own_resid.astype(jnp.float32) + summed, norm_gain)
    piece = lax.all_gather(normed, ("group", "tensor"), axis=0, tiled=True)
    logits = jnp.dot(piece, lm_weight, preferred_element_type=jnp.float32)
    peak_row = jnp.max(logits, axis=1)
    sums_row = jnp.sum(jnp.exp(logits - peak_row[:, None]), axis=1)
    picked = jnp.sum(jnp.where(targets[:, None] == vocab_ids[None, :], logits, 0.0), axis=1)
    terms = jnp.stack([peak_row, sums_row, picked])
    peak_all = lax.pmax(terms[0], ("group", "tensor"))
    totals_all, picked_all = lax.psum(
        (terms[1] * jnp.exp(terms[0] - peak_all), terms[2]), ("group", "tensor")
    )
    logprob_all = picked_all - peak_all - jnp.log(totals_all)
    mine_rows = lax.dynamic_slice_in_dim(logprob_all, flat_index * share_rows, share_rows, 0)
    local_rows = tensor_index * share_rows + jnp.arange(share_rows, dtype=jnp.int32)
    local_len = per_row(local_rows // seq_length, slot_ids, lengths)
    return jnp.where(local_rows % seq_length < local_len, mine_rows, 0.0)


def solution(mesh):
    return jax.shard_map(
        local,
        mesh=mesh,
        in_specs=(
            P("group", "tensor"),
            P("group", "tensor"),
            P("group", "tensor"),
            P("group", "tensor"),
            P("group", "tensor"),
            P("group"),
            P("group"),
            P("group", None),
            P("tensor", None),
            P(),
            P(None, ("group", "tensor")),
            P(),
        ),
        out_specs=P(("group", "tensor")),
        check_vma=False,
    )
```

profile of v0, /device:TPU:0, one launch (start us, length us, event | category | flops | bytes accessed | tf_op | source)
XLA Modules:
  0.0 294.1 jit_solution(9294596529788395)
XLA Ops:
  6.5 0.0 all-gather.4.cloned.1.call-start
  6.6 2.1 copy.28
  8.7 0.0 all-gather.4.cloned.1.call-update
  8.7 0.0 all-gather.6.cloned.1.call-start
  8.8 2.0 copy.31
  10.8 0.0 all-gather.6.cloned.1.call-update
  10.8 0.0 reduce-scatter.2.cloned.1.call-start
  10.9 0.1 select_reduce_fusion.1
  11.0 0.1 and_and_fusion
  11.1 0.2 fusion.49
  11.4 0.1 broadcast_compare_fusion
  11.5 22.7 %all-gather.4.cloned.1.call-done = bf16[2048,512]{0,1:T(8,128)(2,1)} async-done(((bf16[512,512]{0,1:T(8,128)(2,1)}), bf16[2048,512]{0,1:T(8,128)(2,1)}) %all-gather.4.cloned.1.call-update) | async-done | bytes 2097168 | tf_op jit(solution)/shard_map/all_gather | solution.py:81
  34.3 2.3 fusion.48
  36.6 0.5 fusion.1
  37.1 21.3 %all-gather.6.cloned.1.call-done = bf16[2048,512]{0,1:T(8,128)(2,1)} async-done(((bf16[512,512]{0,1:T(8,128)(2,1)}), bf16[2048,512]{0,1:T(8,128)(2,1)}) %all-gather.6.cloned.1.call-update) | async-done | bytes 2097168 | tf_op jit(solution)/shard_map/all_gather | solution.py:82
  58.5 4.0 %fusion.10 = f32[64,4,128]{2,0,1:T(8,128)S(1)} fusion(bf16[2048,4,128]{0,2,1:T(8,128)(2,1)} %bitcast.92, f32[4,64,2048]{2,1,0:T(8,128)S(1)} %get-tuple-element.20, f32[4,64]{1,0:T(4,128)S(1)} %get-tuple-element.19, pred[64,2048]{1,0:T(8,128)(4,1)S(1)} %broadcast_compare_fusion, f32[64,4]{0,1:T(4,128)S(1)} %get-tuple-element.18, ...), kind=kOutput, calls=%fused_computation.16 | convolution fusion | flops 806453248 | bytes 4460544 | tf_op jit(solution)/shard_map/hqk,khd->hqd/dot_general | solution.py:21
  62.5 0.3 fusion.12
  62.8 0.0 copy-start.1
  62.8 4.6 %fusion.17 = f32[64,5120]{1,0:T(8,128)} fusion(bf16[512,5120]{1,0:T(8,128)(2,1)} %param.20, bf16[4,8,8,128]{3,2,1,0:T(8,128)(2,1)S(1)} %fusion.12), kind=kOutput, calls=%fused_computation.28 | convolution fusion | flops 335544320 | bytes 6619136 | tf_op jit(solution)/shard_map/dot_general | solution.py:111
  67.4 0.0 reduce-scatter.2.cloned.1.call-update
  67.4 0.0 all-gather.8.cloned.1.call-start
  67.5 64.4 %reduce-scatter.2.cloned.1.call-done = f32[8,5120]{1,0:T(8,128)} async-done(((f32[64,5120]{1,0:T(8,128)}), f32[8,5120]{1,0:T(8,128)}) %reduce-scatter.2.cloned.1.call-update) | async-done | bytes 163856 | tf_op jit(solution)/shard_map/reduce_scatter | solution.py:117
  131.9 1.1 multiply_reduce_fusion
  133.1 1.7 multiply_convert_fusion
  134.8 0.0 all-gather.8.cloned.1.call-update
  134.8 0.1 fusion.42
  134.9 57.0 %all-gather.8.cloned.1.call-done = bf16[256,5120]{1,0:T(8,128)(2,1)} async-done(((bf16[8,5120]{1,0:T(8,128)(2,1)}), bf16[256,5120]{1,0:T(8,128)(2,1)}) %all-gather.8.cloned.1.call-update) | async-done | bytes 2621456 | tf_op jit(solution)/shard_map/all_gather | solution.py:120
  191.9 14.7 %fusion.50 = (f32[256]{0:T(256)S(1)}, f32[256,3072]{1,0:T(8,128)S(1)}) fusion(bf16[256,5120]{1,0:T(8,128)(2,1)} %all-gather.8.cloned.1.call-done, bf16[5120,3072]{1,0:T(8,128)(2,1)} %param.22), kind=kOutput, calls=%fused_computation.90 | convolution fusion | flops 8053850112 | bytes 37225472 | tf_op jit(solution)/shard_map/dot_general | solution.py:121
  206.6 38.2 %pmax.7 = f32[256]{0:T(256)S(1)} all-reduce(f32[256]{0:T(256)S(1)} %get-tuple-element.23), channel_id=1, replica_groups=mesh['group'=4,'tensor'=8] {'group','tensor'}, use_global_device_ids=true, to_apply=%region_12.13 | all-reduce | flops 256 | bytes 2048 | tf_op jit(solution)/shard_map/pmax | solution.py:126
  244.8 1.0 select_reduce_fusion
  245.9 41.1 %all-reduce = (f32[256]{0:T(256)S(1)}, f32[256]{0:T(256)S(1)}) all-reduce(f32[256]{0:T(256)S(1)} %exponential_multiply_fusion, f32[256]{0:T(256)S(1)} %get-tuple-element.5), channel_id=1, replica_groups=mesh['group'=4,'tensor'=8] {'group','tensor'}, use_global_device_ids=true, to_apply=%region_14.15 | all-reduce | flops 512 | bytes 4096 | tf_op jit(solution)/shard_map/psum | solution.py:127
  287.0 0.6 compare_select_fusion
  (24 shorter events, 0.1 us)
Async XLA Ops:
  6.5 4.6 %copy-start = (bf16[64,512]{1,0:T(8,128)(2,1)S(1)}, bf16[64,512]{1,0:T(8,128)(2,1)}, u32[]{:S(2)}) copy-start(bf16[64,512]{1,0:T(8,128)(2,1)} %param.12) | copy-start | bytes 196612
  6.5 4.4 %copy-start.3 = (s32[2]{0:T(128)S(1)}, s32[2]{0:T(128)}, u32[]{:S(2)}) copy-start(s32[2]{0:T(128)} %param.17) | copy-start | bytes 28
  6.5 4.4 %copy-start.4 = (s32[2]{0:T(128)S(1)}, s32[2]{0:T(128)}, u32[]{:S(2)}) copy-start(s32[2]{0:T(128)} %param.18) | copy-start | bytes 28
  6.5 4.6 %copy-start.5 = (bf16[64,512]{1,0:T(8,128)(2,1)S(1)}, bf16[64,512]{1,0:T(8,128)(2,1)}, u32[]{:S(2)}) copy-start(bf16[64,512]{1,0:T(8,128)(2,1)} %param.13) | copy-start | bytes 196612
  6.5 27.7 %all-gather.4.cloned.1.call-start = ((), (), s32[]{:S(2)}) async-start(), calls=%async_computation.1 | async-start | bytes 2621440 | tf_op jit(solution)/shard_map/all_gather | solution.py:81
  8.7 49.7 %all-gather.6.cloned.1.call-start = ((), (), s32[]{:S(2)}) async-start(), calls=%async_computation.2 | async-start | bytes 2621440 | tf_op jit(solution)/shard_map/all_gather | solution.py:82
  10.8 121.1 %reduce-scatter.2.cloned.1.call-start = ((), (), s32[]{:S(2)}) async-start(), calls=%async_computation.3 | async-start | bytes 1474560 | tf_op jit(solution)/shard_map/reduce_scatter | solution.py:117
  58.5 4.0 %copy-start.6 = (bf16[64,512]{1,0:T(8,128)(2,1)S(1)}, bf16[64,512]{1,0:T(8,128)(2,1)}, u32[]{:S(2)}) copy-start(bf16[64,512]{1,0:T(8,128)(2,1)} %param.14) | copy-start | bytes 196612
  62.8 4.7 %copy-start.1 = (bf16[5120]{0:T(1024)(128)(2,1)S(1)}, bf16[5120]{0:T(1024)(128)(2,1)}, u32[]{:S(2)}) copy-start(bf16[5120]{0:T(1024)(128)(2,1)} %param.21) | copy-start | bytes 30724
  67.4 124.5 %all-gather.8.cloned.1.call-start = ((), (), s32[]{:S(2)}) async-start(), calls=%async_computation.4 | async-start | bytes 2703360 | tf_op jit(solution)/shard_map/all_gather | solution.py:120
  134.9 109.9 %copy-start.2 = (s32[256]{0:T(256)S(1)}, s32[256]{0:T(256)}, u32[]{:S(2)}) copy-start(s32[256]{0:T(256)} %param.23) | copy-start | bytes 3076
Sparse Core Ops, SparseCore 0:
  8.9 25.2 all-gather.3
  35.8 22.5 all-gather.5
  67.5 64.3 reduce-scatter.1
  134.9 56.9 all-gather.7
where the time goes:
time: 295 us; the launch traced here: 294 us
  waiting for transfers between devices  166 us (56%)
  blocking collectives  79.3 us (27%)
  matrix products  26.1 us (9%)
  between operations  13.3 us (5%)
  other arithmetic  5.46 us (2%)
  local copies, waits for them, and re-layouts  4.18 us (1%)
    reduce_scatter x1, waiting for transfers between devices, local(): lax.psum_scatter(partial_value, 'tensor', scatter_dimension=0, tiled=True)  64.4 us
    all_gather x1, waiting for transfers between devices, local(): piece = lax.all_gather(normed, ('group', 'tensor'), axis=0, tiled=True)  57 us
    psum x1, blocking collectives, local(): lax.psum((terms[1] * jnp.exp(terms[0] - peak_all), terms[2]), ('group', '...  41.1 us
    pmax x1, blocking collectives, local(): peak_all = lax.pmax(terms[0], ('group', 'tensor'))  38.2 us
    all_gather x1, waiting for transfers between devices, local(): key_rows = lax.all_gather(prompt_keys, 'group', axis=0, tiled=True)  22.7 us
    all_gather x1, waiting for transfers between devices, local(): value_rows = lax.all_gather(prompt_values, 'group', axis=0, tiled=True)  21.3 us
    dot_general x1, matrix products, local(): logits = jnp.dot(piece, lm_weight, preferred_element_type=jnp.float32)  14.7 us
  transfers between devices with their start and end apart: 4, of which 4 were waited for; matrix products, arithmetic and copies ran while one was open for 2% of the time, Pallas kernels for 0%

commit v1 on v0

v1 whole, which is shorter than its diff:
```python
import functools

import jax
import jax.numpy as jnp
from jax import lax
from jax.experimental import pallas as pl
from jax.experimental.pallas import tpu as pltpu
from jax.sharding import PartitionSpec as P

HEAD_DIM = 128
PLEN = 512
NEG = -1e30
BF16 = jnp.bfloat16
F32 = jnp.float32
VMEM_LIMIT = 56 * 1024 * 1024


def params():
    return pltpu.CompilerParams(vmem_limit_bytes=VMEM_LIMIT)


def vmem():
    return pl.BlockSpec(memory_space=pltpu.VMEM)


def smem():
    return pl.BlockSpec(memory_space=pltpu.SMEM)


def swap(x, axis, distance, size):
    return lax.ppermute(x, axis, [(i, i ^ distance) for i in range(size)])


def head_attend(q, k, v, allowed):
    scores = lax.dot_general(q, k, (((1,), (1,)), ((), ())), preferred_element_type=F32)
    scores = scores * (HEAD_DIM**-0.5)
    if allowed is not None:
        scores = jnp.where(allowed, scores, NEG)
    peak = jnp.max(scores, axis=1, keepdims=True)
    weights = jnp.exp(scores - peak)
    if allowed is not None:
        weights = jnp.where(allowed, weights, 0.0)
    total = jnp.sum(weights, axis=1, keepdims=True)
    high = weights.astype(BF16)
    low = (weights - high.astype(F32)).astype(BF16)
    mixed = jnp.dot(high, v, preferred_element_type=F32) + jnp.dot(
        low, v, preferred_element_type=F32
    )
    return mixed / total, peak + jnp.log(total)


def pack_logs(logs, rows):
    lane = lax.broadcasted_iota(jnp.int32, (rows, 128), 1)
    packed = jnp.zeros((rows, 128), F32)
    for head, log in enumerate(logs):
        first = log.astype(BF16).astype(F32)
        second = (log - first).astype(BF16).astype(F32)
        third = log - first - second
        for part, value in enumerate((first, second, third)):
            packed = jnp.where(lane == 3 * head + part, value, packed)
    return packed.astype(BF16)


def own_kernel(heads, seq, lengths_ref, q_ref, rk_ref, rv_ref, k_ref, v_ref, own_ref, pre_ref):
    rows = q_ref.shape[0]
    row = lax.broadcasted_iota(jnp.int32, (rows, rows), 0)
    col = lax.broadcasted_iota(jnp.int32, (rows, rows), 1)
    live = jnp.zeros((rows, rows), jnp.int32)
    for r in range(rows // seq):
        live = jnp.where(col // seq == r, lengths_ref[r], live)
    allowed = (row // seq == col // seq) & (col <= row) & (col % seq < live)
    logs, pre_logs = [], []
    for h in range(heads):
        part = slice(h * HEAD_DIM, (h + 1) * HEAD_DIM)
        mixed, log = head_attend(q_ref[:, part], rk_ref[:, part], rv_ref[:, part], allowed)
        own_ref[:, part] = mixed
        logs.append(log)
        mixed, log = head_attend(q_ref[:, part], k_ref[:, part], v_ref[:, part], None)
        pre_ref[:, part] = mixed
        pre_logs.append(log)
    lane = lax.broadcasted_iota(jnp.int32, (rows, 128), 1)
    for ref, values in ((own_ref, logs), (pre_ref, pre_logs)):
        packed = jnp.zeros((rows, 128), F32)
        for h in range(heads):
            packed = jnp.where(lane == h, values[h], packed)
        ref[:, heads * HEAD_DIM :] = packed


def prefix_kernel(heads, count, *refs):
    q_refs, (k_ref, v_ref), out_refs = refs[:count], refs[count : count + 2], refs[count + 2 :]
    rows = q_refs[0].shape[0]
    logs = [[] for _ in range(count)]
    for h in range(heads):
        part = slice(h * HEAD_DIM, (h + 1) * HEAD_DIM)
        q = jnp.concatenate([ref[:, part] for ref in q_refs], axis=0)
        mixed, log = head_attend(q, k_ref[:, part], v_ref[:, part], None)
        for i in range(count):
            out_refs[i][:, part] = mixed[i * rows : (i + 1) * rows].astype(BF16)
            logs[i].append(log[i * rows : (i + 1) * rows])
    for i in range(count):
        out_refs[i][:, heads * HEAD_DIM :] = pack_logs(logs[i], rows)


def project_kernel(heads, seq, count, share, plan_ref, *refs):
    own_ref, pre_ref = refs[:2]
    got_refs = refs[2 : 2 + count]
    weight_ref, send_ref, keep_ref, attended_ref, partial_ref = refs[2 + count :]
    rows = own_ref.shape[0]
    blocks = rows // share

    @pl.when(pl.program_id(0) == 0)
    def _():
        row = lax.broadcasted_iota(jnp.int32, (rows, 1), 0)
        wanted = jnp.zeros((rows, 1), jnp.int32)
        for r in range(rows // seq):
            wanted = jnp.where(row // seq == r, plan_ref[1 + count + 1 + r], wanted)
        for h in range(heads):
            part = slice(h * HEAD_DIM, (h + 1) * HEAD_DIM)
            at = heads * HEAD_DIM
            logs = [own_ref[:, at + h : at + h + 1]]
            values = [own_ref[:, part]]
            pre_log = pre_ref[:, at + h : at + h + 1]
            logs.append(jnp.where(wanted == plan_ref[1], pre_log, NEG))
            values.append(pre_ref[:, part])
            for i, ref in enumerate(got_refs):
                three = ref[:, at : at + 128].astype(F32)
                log = (
                    three[:, 3 * h : 3 * h + 1]
                    + three[:, 3 * h + 1 : 3 * h + 2]
                    + three[:, 3 * h + 2 : 3 * h + 3]
                )
                logs.append(jnp.where(wanted == plan_ref[2 + i], log, NEG))
                values.append(ref[:, part].astype(F32))
            peak = functools.reduce(jnp.maximum, logs)
            loads = [jnp.exp(log - peak) for log in logs]
            total = functools.reduce(jnp.add, loads)
            mixed = functools.reduce(jnp.add, [w * v for w, v in zip(loads, values)])
            attended_ref[:, part] = (mixed / total).astype(BF16)

    partial = jnp.dot(attended_ref[...], weight_ref[...], preferred_element_type=F32)
    for b in range(blocks):
        partial_ref[b] = partial[b * share : (b + 1) * share]
    me = plan_ref[0]
    for d in range(blocks):
        block = partial_ref[me ^ d]
        if d % 2:
            send_ref[d // 2] = block.astype(BF16)
        else:
            keep_ref[d // 2] = block


def fold_kernel(keep_ref, got_ref, *out_refs):
    for i, ref in enumerate(out_refs):
        ref[...] = (keep_ref[i] + got_ref[i].astype(F32)).astype(ref.dtype)


def norm_kernel(plan_ref, residual_ref, gain_ref, own_ref, *refs):
    got_refs, out_ref = refs[:-1], refs[-1]
    hidden = own_ref[...]
    for ref in got_refs:
        hidden = hidden + ref[...].astype(F32)
    hidden = hidden + residual_ref[0].astype(F32)
    squares = jnp.mean(hidden * hidden, axis=-1, keepdims=True)
    out_ref[...] = (hidden * lax.rsqrt(squares + 1e-06) * gain_ref[...].astype(F32)).astype(BF16)


def logits_kernel(left_ref, right_ref, target_ref, weight_ref, out_ref, x_ref, peak_ref, sum_ref, pick_ref):
    step = pl.program_id(0)
    half = left_ref.shape[0]
    rows = 2 * half
    width = weight_ref.shape[1]

    @pl.when(step == 0)
    def _():
        x_ref[:half] = left_ref[...]
        x_ref[half:] = right_ref[...]
        peak_ref[...] = jnp.full_like(peak_ref, NEG)
        sum_ref[...] = jnp.zeros_like(sum_ref)
        pick_ref[...] = jnp.zeros_like(pick_ref)

    logits = jnp.dot(x_ref[...], weight_ref[...], preferred_element_type=F32)
    parts = [logits[:, c : c + 128] for c in range(0, width, 128)]
    if width % 128:
        spare = jnp.full((rows, 128 - width % 128), NEG, F32)
        parts[-1] = jnp.concatenate([parts[-1], spare], axis=1)
    lane = lax.broadcasted_iota(jnp.int32, (rows, 128), 1) + step * width
    peak = peak_ref[...]
    higher = functools.reduce(jnp.maximum, parts, peak)
    total = sum_ref[...] * jnp.exp(peak - higher)
    picked = pick_ref[...]
    target = target_ref[...]
    for c, part in enumerate(parts):
        total = total + jnp.exp(part - higher)
        picked = picked + jnp.where(lane + c * 128 == target, part, 0.0)
    peak_ref[...] = higher
    sum_ref[...] = total
    pick_ref[...] = picked

    @pl.when(step == pl.num_programs(0) - 1)
    def _():
        peak = jnp.max(higher, axis=1, keepdims=True)
        sums = jnp.sum(total * jnp.exp(higher - peak), axis=1, keepdims=True)
        pick = jnp.sum(picked, axis=1, keepdims=True)
        place = lax.broadcasted_iota(jnp.int32, (rows, 128), 1)
        three = jnp.where(place == 0, peak, jnp.where(place == 1, sums, pick))
        out_ref[...] = jnp.transpose(three)[:8]


def local(
    group_size,
    tensor_size,
    resp_query,
    resp_key,
    resp_value,
    prompt_keys,
    prompt_values,
    prompt_of,
    lengths,
    residual,
    out_weight,
    norm_gain,
    lm_weight,
    targets,
):
    rows, span = resp_query.shape
    heads = span // HEAD_DIM
    seq = rows // prompt_of.shape[0]
    key_rows = prompt_keys.shape[0]
    assert PLEN % key_rows == 0
    share = rows // tensor_size
    depth = out_weight.shape[1]
    vocab = lm_weight.shape[1]
    group_index = lax.axis_index("group")
    tensor_index = lax.axis_index("tensor")
    i32 = jnp.int32

    distances = list(range(1, group_size))
    queries = [swap(resp_query, "group", d, group_size) for d in distances]
    own, prefix = pl.pallas_call(
        functools.partial(own_kernel, heads, seq),
        out_shape=[jax.ShapeDtypeStruct((rows, span + 128), F32)] * 2,
        in_specs=[smem()] + [vmem()] * 5,
        out_specs=[vmem()] * 2,
        compiler_params=params(),
        name="own_attention",
    )(lengths, resp_query, resp_key, resp_value, prompt_keys, prompt_values)
    answers = pl.pallas_call(
        functools.partial(prefix_kernel, heads, len(distances)),
        out_shape=[jax.ShapeDtypeStruct((rows, span + 128), BF16)] * len(distances),
        in_specs=[vmem()] * (len(distances) + 2),
        out_specs=[vmem()] * len(distances),
        compiler_params=params(),
        name="prefix_attention",
    )(*queries, prompt_keys, prompt_values)
    got = [swap(x, "group", d, group_size) for x, d in zip(answers, distances)]

    holders = (group_index ^ jnp.arange(group_size, dtype=i32)) * key_rows // PLEN
    plan = jnp.concatenate([tensor_index.astype(i32)[None], holders, prompt_of])
    wide = 640 if depth % 640 == 0 else depth
    half_blocks = tensor_size // 2
    send, keep = pl.pallas_call(
        functools.partial(project_kernel, heads, seq, len(distances), share),
        out_shape=[
            jax.ShapeDtypeStruct((half_blocks, share, depth), BF16),
            jax.ShapeDtypeStruct((half_blocks, share, depth), F32),
        ],
        grid=(depth // wide,),
        in_specs=[smem()]
        + [pl.BlockSpec((rows, span + 128), lambda n: (0, 0))] * (2 + len(distances))
        + [pl.BlockSpec((span, wide), lambda n: (0, n))],
        out_specs=[pl.BlockSpec((half_blocks, share, wide), lambda n: (0, 0, n))] * 2,
        scratch_shapes=[pltpu.VMEM((rows, span), BF16), pltpu.VMEM((tensor_size, share, wide), F32)],
        compiler_params=params(),
        name="project",
    )(plan, own, prefix, *got, out_weight)

    got = swap(send, "tensor", 1, tensor_size)
    far = list(range(2, tensor_size, 2))
    folded = pl.pallas_call(
        fold_kernel,
        out_shape=[jax.ShapeDtypeStruct((share, depth), F32)]
        + [jax.ShapeDtypeStruct((share, depth), BF16)] * len(far),
        in_specs=[vmem()] * 2,
        out_specs=[vmem()] * (1 + len(far)),
        compiler_params=params(),
        name="fold",
    )(keep, got)
    got = [swap(x, "tensor", d, tensor_size) for x, d in zip(folded[1:], far)]
    whole = lambda shape: pl.BlockSpec(shape, lambda n, plan: (0,) * len(shape))
    normed = pl.pallas_call(
        norm_kernel,
        out_shape=jax.ShapeDtypeStruct((share, depth), BF16),
        grid_spec=pltpu.PrefetchScalarGridSpec(
            num_scalar_prefetch=1,
            grid=(1,),
            in_specs=[pl.BlockSpec((1, share, depth), lambda n, plan: (plan[0], 0, 0)), whole((1, depth))]
            + [whole((share, depth))] * (1 + len(far)),
            out_specs=whole((share, depth)),
        ),
        compiler_params=params(),
        name="norm",
    )(plan, residual.reshape(tensor_size, share, depth), norm_gain[None], folded[0], *got)

    order = [0] + far
    tokens = jnp.stack([normed] + [swap(normed, "tensor", d, tensor_size) for d in far])
    tokens = jnp.concatenate([tokens, swap(tokens, "tensor", 1, tensor_size)])
    order = order + [d + 1 for d in order]
    above = list(range(2, group_size, 2))
    tokens = jnp.concatenate([tokens] + [swap(tokens, "group", d, group_size) for d in above])
    tokens = tokens.reshape(-1, depth)
    other = swap(tokens, "group", 1, group_size)
    group_order = [0] + above
    group_order = group_order + [d + 1 for d in group_order]
    group_ids = group_index ^ jnp.asarray(group_order, i32)
    tensor_ids = tensor_index ^ jnp.asarray(order, i32)
    block_ids = (group_ids[:, None] * tensor_size + tensor_ids[None, :]).reshape(-1)
    device = group_index * tensor_size + tensor_index
    table = targets.reshape(-1, share)
    wanted = jnp.take(table, block_ids, axis=0).reshape(-1, 1) - device * vocab
    wanted = jnp.where((wanted >= 0) & (wanted < vocab), wanted, -1)

    total_rows = 2 * tokens.shape[0]
    narrow = 256
    stats = pl.pallas_call(
        logits_kernel,
        out_shape=jax.ShapeDtypeStruct((8, total_rows), F32),
        grid=(vocab // narrow,) if vocab % narrow == 0 else (1,),
        in_specs=[
            pl.BlockSpec(tokens.shape, lambda n: (0, 0)),
            pl.BlockSpec(tokens.shape, lambda n: (0, 0)),
            pl.BlockSpec((total_rows, 1), lambda n: (0, 0)),
            pl.BlockSpec((depth, narrow if vocab % narrow == 0 else vocab), lambda n: (0, n)),
        ],
        out_specs=pl.BlockSpec((8, total_rows), lambda n: (0, 0)),
        scratch_shapes=[pltpu.VMEM((total_rows, depth), BF16)]
        + [pltpu.VMEM((total_rows, 128), F32)] * 3,
        compiler_params=params(),
        name="logits",
    )(tokens, other, wanted, lm_weight)

    blocks = stats[:3].reshape(3, -1, share).transpose(1, 0, 2).reshape(-1, 3 * share)
    ids = jnp.arange(group_size * tensor_size, dtype=i32)
    group_step = group_index ^ (ids // tensor_size)
    tensor_step = tensor_index ^ (ids % tensor_size)
    group_place = group_step % 2 * (group_size // 2) + group_step // 2
    tensor_place = tensor_step % 2 * (tensor_size // 2) + tensor_step // 2
    places = group_place * tensor_size + tensor_place
    blocks = jnp.take(blocks, places, axis=0)
    blocks = lax.all_to_all(blocks, ("group", "tensor"), 0, 0, tiled=True)
    peaks, sums, picks = blocks[:, :share], blocks[:, share : 2 * share], blocks[:, 2 * share :]
    peak = jnp.max(peaks, axis=0)
    total = jnp.sum(sums * jnp.exp(peaks - peak[None]), axis=0)
    values = jnp.sum(picks, axis=0) - peak - jnp.log(total)
    local_rows = tensor_index * share + jnp.arange(share, dtype=i32)
    slots = jnp.arange(prompt_of.shape[0], dtype=i32)
    local_len = jnp.sum(
        jnp.where((local_rows // seq)[:, None] == slots[None, :], lengths[None, :], 0), axis=1
    )
    return jnp.where(local_rows % seq < local_len, values, 0.0)


def solution(mesh):
    return jax.shard_map(
        functools.partial(local, mesh.shape["group"], mesh.shape["tensor"]),
        mesh=mesh,
        in_specs=(
            P("group", "tensor"),
            P("group", "tensor"),
            P("group", "tensor"),
            P("group", "tensor"),
            P("group", "tensor"),
            P("group"),
            P("group"),
            P("group", None),
            P("tensor", None),
            P(),
            P(None, ("group", "tensor")),
            P(),
        ),
        out_specs=P(("group", "tensor")),
        check_vma=False,
    )
```

time: 295 us -> 127 us (0.43)
  waiting for transfers between devices: 166 us -> 46.9 us
  blocking collectives: 79.3 us -> 0 us
  Pallas kernels: 0 us -> 39.9 us
  starting transfers between devices: 0.16 us -> 26.8 us
  matrix products: 26.1 us -> 0 us
  between operations: 13.3 us -> 0.22 us
  local copies, waits for them, and re-layouts: 4.18 us -> 8.39 us
    all_gather x3 -> x0, waiting for transfers between devices: 101 us -> none  [the longest x1 57 us: local(): piece = lax.all_gather(normed, ('group', 'tensor'), axis=0, tiled=True)]
    reduce_scatter x1 -> x0, waiting for transfers between devices: 64.4 us -> none  [local(): lax.psum_scatter(partial_value, 'tensor', scatter_dimension=0, tiled=True)]
    psum x1 -> x0, blocking collectives: 41.1 us -> none  [local(): lax.psum((terms[1] * jnp.exp(terms[0] - peak_all), terms[2]), ('group', '...]
    ppermute x0 -> x16, waiting for transfers between devices: none -> 39.9 us  [swap(): return lax.ppermute(x, axis, [(i, i ^ distance) for i in range(size)])]
    pallas_call x0 -> x6, Pallas kernels: none -> 39.9 us  [the longest x1 19.3 us: local(): pl.pallas_call(logits_kernel, out_shape=jax.ShapeDtypeStruct((8, total_ro...]
    pmax x1 -> x0, blocking collectives: 38.2 us -> none  [local(): peak_all = lax.pmax(terms[0], ('group', 'tensor'))]
    dot_general x6 -> x0, matrix products: 26.1 us -> none  [the longest x1 14.7 us: local(): logits = jnp.dot(piece, lm_weight, preferred_element_type=jnp.float32)]
    ppermute x0 -> x16, starting transfers between devices: none -> 19.3 us  [swap(): return lax.ppermute(x, axis, [(i, i ^ distance) for i in range(size)])]
  transfers between devices with their start and end apart: 4 -> 17, of which waited for: 4 -> 13; matrix products, arithmetic and copies ran while one was open for 2% -> 3% of each run, Pallas kernels for 0% -> 3%
where the time goes in v1:
time: 127 us; the launch traced here: 126 us
  waiting for transfers between devices  46.9 us (37%)
  Pallas kernels  39.9 us (31%)
  starting transfers between devices  26.8 us (21%)
  local copies, waits for them, and re-layouts  8.39 us (7%)
  other arithmetic  3.85 us (3%)
    ppermute x16, waiting for transfers between devices, swap(): return lax.ppermute(x, axis, [(i, i ^ distance) for i in range(size)])  39.9 us
    pallas_call x1, Pallas kernels, local(): pl.pallas_call(logits_kernel, out_shape=jax.ShapeDtypeStruct((8, total_ro...  19.3 us
    ppermute x16, starting transfers between devices, swap(): return lax.ppermute(x, axis, [(i, i ^ distance) for i in range(size)])  19.3 us
    pallas_call x1, Pallas kernels, local(): pl.pallas_call(functools.partial(project_kernel, heads, seq, len(distance...  8.36 us
    all_to_all x1, starting transfers between devices, local(): blocks = lax.all_to_all(blocks, ('group', 'tensor'), 0, 0, tiled=True)  7.57 us
    all_to_all x1, waiting for transfers between devices, local(): blocks = lax.all_to_all(blocks, ('group', 'tensor'), 0, 0, tiled=True)  7.02 us
    unnamed x40, local copies, waits for them, and re-layouts  5.25 us
    pallas_call x1, Pallas kernels, local(): pl.pallas_call(functools.partial(own_kernel, heads, seq), out_shape=[jax....  4.13 us
  transfers between devices with their start and end apart: 17, of which 13 were waited for; matrix products, arithmetic and copies ran while one was open for 3% of the time, Pallas kernels for 3%

profile of v1, /device:TPU:0, one launch (start us, length us, event | category | flops | bytes accessed | tf_op | source)
XLA Modules:
  0.0 126.1 jit_solution(8777348644223448471)
XLA Ops:
  0.5 2.6 %collective-permute-start.1 = (bf16[64,512]{1,0:T(8,128)(2,1)}, bf16[64,512]{1,0:T(8,128)(2,1)S(1)}, u32[]{:S(2)}, u32[]{:S(2)}) collective-permute-start(bf16[64,512]{1,0:T(8,128)(2,1)} %q_ref.1), channel_id=1, source_target_pairs={{0,16},{8,24},{16,0},{24,8},{1,17},{9,25},{17,1},{25,9},{2,18},{10... | collective-permute-start | bytes 196616 | tf_op jit(solution)/shard_map/ppermute | solution.py:31
  3.1 4.1 %own_attention.1 = (f32[64,640]{1,0:T(8,128)}, f32[64,640]{1,0:T(8,128)}) custom-call(s32[2]{0:T(128)} %lengths_ref.1, bf16[64,512]{1,0:T(8,128)(2,1)} %q_ref.1, bf16[64,512]{1,0:T(8,128)(2,1)} %rk_ref.1, bf16[64,512]{1,0:T(8,128)(2,1)} %rv_ref.1, bf16[512,512]{1,0:T(8,128)(2,1)} %refs_3_.1, bf16[512,512]{1,0:T(8,128)(2,1)} %refs_4_.1), custom_call_target="tpu_custom_call" | custom-call | tf_op jit(solution)/shard_map/own_attention/pallas_call | solution.py:239
  8.6 3.6 %prefix_attention.1 = (bf16[64,640]{1,0:T(8,128)(2,1)}, bf16[64,640]{1,0:T(8,128)(2,1)}, bf16[64,640]{1,0:T(8,128)(2,1)}) custom-call(bf16[64,512]{1,0:T(8,128)(2,1)} %copy-done.9, bf16[64,512]{1,0:T(8,128)(2,1)} %copy-done.10, bf16[64,512]{1,0:T(8,128)(2,1)} %copy-done.11, bf16[512,512]{1,0:T(8,128)(2,1)} %refs_3_.1, bf16[512,512]{1,0:T(8,128)(2,1)} %refs_4_.1), custom_call_target="tpu_custom_call" | custom-call | tf_op jit(solution)/shard_map/prefix_attention/pallas_call | solution.py:247
  12.3 1.9 %collective-permute-start.4 = (bf16[64,640]{1,0:T(8,128)(2,1)}, bf16[64,640]{1,0:T(8,128)(2,1)S(1)}, u32[]{:S(2)}, u32[]{:S(2)}) collective-permute-start(bf16[64,640]{1,0:T(8,128)(2,1)} %get-tuple-element.19), channel_id=1, source_target_pairs={{0,16},{8,24},{16,0},{24,8},{1,17},{9,25},{17,1},{25,9},{2,18},{10... | collective-permute-start | bytes 245768 | tf_op jit(solution)/shard_map/ppermute | solution.py:31
  14.8 2.5 %collective-permute-done.4.refs_3_ = bf16[64,640]{1,0:T(8,128)(2,1)S(1)} collective-permute-done((bf16[64,640]{1,0:T(8,128)(2,1)}, bf16[64,640]{1,0:T(8,128)(2,1)S(1)}, u32[]{:S(2)}, u32[]{:S(2)}) %collective-permute-start.4) | collective-permute-done | bytes 81952 | tf_op jit(solution)/shard_map/ppermute | solution.py:31
  17.3 1.8 %collective-permute-done.5.refs_4_ = bf16[64,640]{1,0:T(8,128)(2,1)S(1)} collective-permute-done((bf16[64,640]{1,0:T(8,128)(2,1)}, bf16[64,640]{1,0:T(8,128)(2,1)S(1)}, u32[]{:S(2)}, u32[]{:S(2)}) %collective-permute-start.5) | collective-permute-done | bytes 81952 | tf_op jit(solution)/shard_map/ppermute | solution.py:31
  19.7 8.4 %project.1 = (bf16[4,8,5120]{2,1,0:T(8,128)(2,1)}, f32[4,8,5120]{2,1,0:T(8,128)}) custom-call(s32[7]{0:T(128)} %pad_add_fusion.plan_ref, f32[64,640]{1,0:T(8,128)} %get-tuple-element.16.refs_0_, f32[64,640]{1,0:T(8,128)} %get-tuple-element.17.refs_1_, bf16[64,640]{1,0:T(8,128)(2,1)} %copy-done.6, bf16[64,640]{1,0:T(8,128)(2,1)} %copy-done.7, ...), custom_call_target="tpu_custom_call" | custom-call | tf_op jit(solution)/shard_map/project/pallas_call | solution.py:261
  28.1 1.6 %collective-permute-start.6 = (bf16[4,8,5120]{2,1,0:T(8,128)(2,1)}, bf16[4,8,5120]{2,1,0:T(8,128)(2,1)S(1)}, u32[]{:S(2)}, u32[]{:S(2)}) collective-permute-start(bf16[4,8,5120]{2,1,0:T(8,128)(2,1)} %get-tuple-element.22), channel_id=1, source_target_pairs={{0,1},{1,0},{2,3},{3,2},{4,5},{5,4},{6,7},{7,6},{8,9},{9,8},{10,11... | collective-permute-start | bytes 983048 | tf_op jit(solution)/shard_map/ppermute | solution.py:31
  29.6 8.4 %collective-permute-done.6.got_ref = bf16[4,8,5120]{2,1,0:T(8,128)(2,1)S(1)} collective-permute-done((bf16[4,8,5120]{2,1,0:T(8,128)(2,1)}, bf16[4,8,5120]{2,1,0:T(8,128)(2,1)S(1)}, u32[]{:S(2)}, u32[]{:S(2)}) %collective-permute-start.6) | collective-permute-done | bytes 327712 | tf_op jit(solution)/shard_map/ppermute | solution.py:31
  38.0 0.7 copy-done.2
  38.8 1.9 %fold.1 = (f32[8,5120]{1,0:T(8,128)}, bf16[8,5120]{1,0:T(8,128)(2,1)}, bf16[8,5120]{1,0:T(8,128)(2,1)}, bf16[8,5120]{1,0:T(8,128)(2,1)}) custom-call(f32[4,8,5120]{2,1,0:T(8,128)} %get-tuple-element.21.keep_ref, bf16[4,8,5120]{2,1,0:T(8,128)(2,1)} %copy-done.2), custom_call_target="tpu_custom_call" | custom-call | tf_op jit(solution)/shard_map/fold/pallas_call | solution.py:279
  40.7 1.6 %collective-permute-start.7 = (bf16[8,5120]{1,0:T(8,128)(2,1)}, bf16[8,5120]{1,0:T(8,128)(2,1)S(1)}, u32[]{:S(2)}, u32[]{:S(2)}) collective-permute-start(bf16[8,5120]{1,0:T(8,128)(2,1)} %get-tuple-element.24), channel_id=1, source_target_pairs={{0,2},{1,3},{2,0},{3,1},{4,6},{5,7},{6,4},{7,5},{8,10},{9,11},{10,... | collective-permute-start | bytes 245768 | tf_op jit(solution)/shard_map/ppermute | solution.py:31
  42.3 2.6 %collective-permute-start.8 = (bf16[8,5120]{1,0:T(8,128)(2,1)}, bf16[8,5120]{1,0:T(8,128)(2,1)S(1)}, u32[]{:S(2)}, u32[]{:S(2)}) collective-permute-start(bf16[8,5120]{1,0:T(8,128)(2,1)} %get-tuple-element.25), channel_id=1, source_target_pairs={{0,4},{1,5},{2,6},{3,7},{4,0},{5,1},{6,2},{7,3},{8,12},{9,13},{10,... | collective-permute-start | bytes 245768 | tf_op jit(solution)/shard_map/ppermute | solution.py:31
  46.2 4.1 %collective-permute-done.8.refs_1_ = bf16[8,5120]{1,0:T(8,128)(2,1)S(1)} collective-permute-done((bf16[8,5120]{1,0:T(8,128)(2,1)}, bf16[8,5120]{1,0:T(8,128)(2,1)S(1)}, u32[]{:S(2)}, u32[]{:S(2)}) %collective-permute-start.8) | collective-permute-done | bytes 81952 | tf_op jit(solution)/shard_map/ppermute | solution.py:31
  50.3 1.2 collective-permute-done.9.refs_2_
  52.1 2.6 %norm.1 = bf16[8,5120]{1,0:T(8,128)(2,1)} custom-call(s32[7]{0:T(128)} %pad_add_fusion.plan_ref, bf16[8,8,5120]{2,1,0:T(8,128)(2,1)} %bitcast.28, bf16[1,5120]{1,0:T(2,128)(2,1)} %broadcast_in_dim.56.gain_ref, f32[8,5120]{1,0:T(8,128)} %get-tuple-element.23.own_ref, bf16[8,5120]{1,0:T(8,128)(2,1)} %copy-done.3, bf16[8,5120]{1,0:T(8,128)(2,1)} %copy-done.4, ...), custom_call_target="tpu_custom_call" | custom-call | tf_op jit(solution)/shard_map/norm/pallas_call | solution.py:290
  54.7 1.1 collective-permute-start.10
  55.8 1.6 %collective-permute-start.11 = (bf16[8,5120]{1,0:T(8,128)(2,1)}, bf16[8,5120]{1,0:T(8,128)(2,1)S(1)}, u32[]{:S(2)}, u32[]{:S(2)}) collective-permute-start(bf16[8,5120]{1,0:T(8,128)(2,1)} %norm.1), channel_id=1, source_target_pairs={{0,4},{1,5},{2,6},{3,7},{4,0},{5,1},{6,2},{7,3},{8,12},{9,13},{10,... | collective-permute-start | bytes 245768 | tf_op jit(solution)/shard_map/ppermute | solution.py:31
  57.4 1.6 %collective-permute-start.12 = (bf16[8,5120]{1,0:T(8,128)(2,1)}, bf16[8,5120]{1,0:T(8,128)(2,1)S(1)}, u32[]{:S(2)}, u32[]{:S(2)}) collective-permute-start(bf16[8,5120]{1,0:T(8,128)(2,1)} %norm.1), channel_id=1, source_target_pairs={{0,6},{1,7},{2,4},{3,5},{4,2},{5,3},{6,0},{7,1},{8,14},{9,15},{10,... | collective-permute-start | bytes 245768 | tf_op jit(solution)/shard_map/ppermute | solution.py:31
  59.0 0.9 constant_dynamic-update-slice_fusion.4
  60.0 2.8 %collective-permute-done.11 = bf16[8,5120]{1,0:T(8,128)(2,1)S(1)} collective-permute-done((bf16[8,5120]{1,0:T(8,128)(2,1)}, bf16[8,5120]{1,0:T(8,128)(2,1)S(1)}, u32[]{:S(2)}, u32[]{:S(2)}) %collective-permute-start.11) | collective-permute-done | bytes 81952 | tf_op jit(solution)/shard_map/ppermute | solution.py:31
  62.7 1.2 collective-permute-done.12
  64.0 0.9 pad_maximum_fusion
  64.9 1.6 %collective-permute-start.13 = (bf16[4,8,5120]{2,1,0:T(8,128)(2,1)S(1)}, bf16[4,8,5120]{2,1,0:T(8,128)(2,1)S(1)}, u32[]{:S(2)}, u32[]{:S(2)}) collective-permute-start(bf16[4,8,5120]{2,1,0:T(8,128)(2,1)S(1)} %pad_maximum_fusion), channel_id=1, source_target_pairs={{0,1},{1,0},{2,3},{3,2},{4,5},{5,4},{6,7},{7,6},{8,9},{9,8},{10,11... | collective-permute-start | bytes 983048 | tf_op jit(solution)/shard_map/ppermute | solution.py:31
  66.5 5.5 %collective-permute-done.13 = bf16[4,8,5120]{2,1,0:T(8,128)(2,1)S(1)} collective-permute-done((bf16[4,8,5120]{2,1,0:T(8,128)(2,1)S(1)}, bf16[4,8,5120]{2,1,0:T(8,128)(2,1)S(1)}, u32[]{:S(2)}, u32[]{:S(2)}) %collective-permute-start.13) | collective-permute-done | bytes 327712 | tf_op jit(solution)/shard_map/ppermute | solution.py:31
  72.1 2.1 %collective-permute-start.14 = (bf16[8,8,5120]{2,1,0:T(8,128)(2,1)S(1)}, bf16[8,8,5120]{2,1,0:T(8,128)(2,1)S(1)}, u32[]{:S(2)}, u32[]{:S(2)}) collective-permute-start(bf16[8,8,5120]{2,1,0:T(8,128)(2,1)S(1)} %get-tuple-element.29), channel_id=1, source_target_pairs={{0,16},{8,24},{16,0},{24,8},{1,17},{9,25},{17,1},{25,9},{2,18},{10... | collective-permute-start | bytes 1966088 | tf_op jit(solution)/shard_map/ppermute | solution.py:31
  74.4 10.6 %collective-permute-done.14 = bf16[8,8,5120]{2,1,0:T(8,128)(2,1)S(1)} collective-permute-done((bf16[8,8,5120]{2,1,0:T(8,128)(2,1)S(1)}, bf16[8,8,5120]{2,1,0:T(8,128)(2,1)S(1)}, u32[]{:S(2)}, u32[]{:S(2)}) %collective-permute-start.14) | collective-permute-done | bytes 655392 | tf_op jit(solution)/shard_map/ppermute | solution.py:31
  86.9 1.3 %collective-permute-done.15.right_ref = bf16[128,5120]{1,0:T(8,128)(2,1)S(1)} collective-permute-done((bf16[128,5120]{1,0:T(8,128)(2,1)S(1)}, bf16[128,5120]{1,0:T(8,128)(2,1)S(1)}, u32[]{:S(2)}, u32[]{:S(2)}) %collective-permute-start.15) | collective-permute-done | bytes 1310752 | tf_op jit(solution)/shard_map/ppermute | solution.py:31
  88.2 1.1 copy-done.1
  89.3 19.3 %logits.1 = f32[8,256]{1,0:T(8,128)} custom-call(bf16[128,5120]{1,0:T(8,128)(2,1)} %bitcast.26, bf16[128,5120]{1,0:T(8,128)(2,1)} %copy-done.1, s32[256,1]{1,0:T(8,128)} %and_select_fusion.target_ref, bf16[5120,3072]{1,0:T(8,128)(2,1)} %weight_ref.1), custom_call_target="tpu_custom_call" | custom-call | tf_op jit(solution)/shard_map/logits/pallas_call | solution.py:324
  110.8 7.6 %all-to-all-start = ((f32[32,1,24]{2,1,0:T(1,128)}), f32[32,1,24]{2,1,0:T(1,128)S(1)}, u32[]{:S(2)}, u32[]{:S(2)}) async-start(f32[32,1,24]{2,1,0:T(1,128)} %bitcast.12), calls=%async_computation | async-start | bytes 32768 | tf_op jit(solution)/shard_map/all_to_all | solution.py:349
  118.5 7.0 %all-to-all-done = f32[32,1,24]{2,1,0:T(1,128)S(1)} async-done(((f32[32,1,24]{2,1,0:T(1,128)}), f32[32,1,24]{2,1,0:T(1,128)S(1)}, u32[]{:S(2)}, u32[]{:S(2)}) %all-to-all-start) | async-done | bytes 3104 | tf_op jit(solution)/shard_map/all_to_all | solution.py:349
  (81 shorter events, 10.0 us)
Async XLA Ops:
  0.0 14.2 %copy-start.15 = (s32[2]{0:T(128)S(1)}, s32[2]{0:T(128)}, u32[]{:S(2)}) copy-start(s32[2]{0:T(128)} %param.19) | copy-start | bytes 28
  0.0 7.3 %collective-permute-start = (bf16[64,512]{1,0:T(8,128)(2,1)}, bf16[64,512]{1,0:T(8,128)(2,1)S(1)}, u32[]{:S(2)}, u32[]{:S(2)}) collective-permute-start(bf16[64,512]{1,0:T(8,128)(2,1)} %q_ref.1), channel_id=1, source_target_pairs={{0,8},{8,0},{16,24},{24,16},{1,9},{9,1},{17,25},{25,17},{2,10},{10... | collective-permute-start | bytes 196616 | tf_op jit(solution)/shard_map/ppermute | solution.py:31
  0.5 6.8 %collective-permute-start.1 = (bf16[64,512]{1,0:T(8,128)(2,1)}, bf16[64,512]{1,0:T(8,128)(2,1)S(1)}, u32[]{:S(2)}, u32[]{:S(2)}) collective-permute-start(bf16[64,512]{1,0:T(8,128)(2,1)} %q_ref.1), channel_id=1, source_target_pairs={{0,16},{8,24},{16,0},{24,8},{1,17},{9,25},{17,1},{25,9},{2,18},{10... | collective-permute-start | bytes 196616 | tf_op jit(solution)/shard_map/ppermute | solution.py:31
  3.0 4.3 %collective-permute-start.2 = (bf16[64,512]{1,0:T(8,128)(2,1)}, bf16[64,512]{1,0:T(8,128)(2,1)S(1)}, u32[]{:S(2)}, u32[]{:S(2)}) collective-permute-start(bf16[64,512]{1,0:T(8,128)(2,1)} %q_ref.1), channel_id=1, source_target_pairs={{0,24},{8,16},{16,8},{24,0},{1,25},{9,17},{17,9},{25,1},{2,26},{10... | collective-permute-start | bytes 196616 | tf_op jit(solution)/shard_map/ppermute | solution.py:31
  7.3 0.6 copy-start.10
  7.9 0.6 copy-start.11
  12.1 2.7 %collective-permute-start.3 = (bf16[64,640]{1,0:T(8,128)(2,1)}, bf16[64,640]{1,0:T(8,128)(2,1)S(1)}, u32[]{:S(2)}, u32[]{:S(2)}) collective-permute-start(bf16[64,640]{1,0:T(8,128)(2,1)} %get-tuple-element.18), channel_id=1, source_target_pairs={{0,8},{8,0},{16,24},{24,16},{1,9},{9,1},{17,25},{25,17},{2,10},{10... | collective-permute-start | bytes 245768 | tf_op jit(solution)/shard_map/ppermute | solution.py:31
  12.3 5.0 %collective-permute-start.4 = (bf16[64,640]{1,0:T(8,128)(2,1)}, bf16[64,640]{1,0:T(8,128)(2,1)S(1)}, u32[]{:S(2)}, u32[]{:S(2)}) collective-permute-start(bf16[64,640]{1,0:T(8,128)(2,1)} %get-tuple-element.19), channel_id=1, source_target_pairs={{0,16},{8,24},{16,0},{24,8},{1,17},{9,25},{17,1},{25,9},{2,18},{10... | collective-permute-start | bytes 245768 | tf_op jit(solution)/shard_map/ppermute | solution.py:31
  14.2 4.9 %collective-permute-start.5 = (bf16[64,640]{1,0:T(8,128)(2,1)}, bf16[64,640]{1,0:T(8,128)(2,1)S(1)}, u32[]{:S(2)}, u32[]{:S(2)}) collective-permute-start(bf16[64,640]{1,0:T(8,128)(2,1)} %get-tuple-element.20), channel_id=1, source_target_pairs={{0,24},{8,16},{16,8},{24,0},{1,25},{9,17},{17,9},{25,1},{2,26},{10... | collective-permute-start | bytes 245768 | tf_op jit(solution)/shard_map/ppermute | solution.py:31
  14.8 4.3 %copy-start.6 = (bf16[64,640]{1,0:T(8,128)(2,1)}, bf16[64,640]{1,0:T(8,128)(2,1)S(1)}, u32[]{:S(2)}) copy-start(bf16[64,640]{1,0:T(8,128)(2,1)S(1)} %collective-permute-done.3.refs_2_) | copy-start | bytes 245764
  17.3 1.8 %copy-start.7 = (bf16[64,640]{1,0:T(8,128)(2,1)}, bf16[64,640]{1,0:T(8,128)(2,1)S(1)}, u32[]{:S(2)}) copy-start(bf16[64,640]{1,0:T(8,128)(2,1)S(1)} %collective-permute-done.4.refs_3_) | copy-start | bytes 245764
  19.7 25.4 %copy-start.12 = (bf16[5120]{0:T(1024)(128)(2,1)S(1)}, bf16[5120]{0:T(1024)(128)(2,1)}, u32[]{:S(2)}) copy-start(bf16[5120]{0:T(1024)(128)(2,1)} %param.23) | copy-start | bytes 30724
  28.1 9.9 %collective-permute-start.6 = (bf16[4,8,5120]{2,1,0:T(8,128)(2,1)}, bf16[4,8,5120]{2,1,0:T(8,128)(2,1)S(1)}, u32[]{:S(2)}, u32[]{:S(2)}) collective-permute-start(bf16[4,8,5120]{2,1,0:T(8,128)(2,1)} %get-tuple-element.22), channel_id=1, source_target_pairs={{0,1},{1,0},{2,3},{3,2},{4,5},{5,4},{6,7},{7,6},{8,9},{9,8},{10,11... | collective-permute-start | bytes 983048 | tf_op jit(solution)/shard_map/ppermute | solution.py:31
  38.0 0.7 copy-start.2
  40.7 5.5 %collective-permute-start.7 = (bf16[8,5120]{1,0:T(8,128)(2,1)}, bf16[8,5120]{1,0:T(8,128)(2,1)S(1)}, u32[]{:S(2)}, u32[]{:S(2)}) collective-permute-start(bf16[8,5120]{1,0:T(8,128)(2,1)} %get-tuple-element.24), channel_id=1, source_target_pairs={{0,2},{1,3},{2,0},{3,1},{4,6},{5,7},{6,4},{7,5},{8,10},{9,11},{10,... | collective-permute-start | bytes 245768 | tf_op jit(solution)/shard_map/ppermute | solution.py:31
  42.3 8.0 %collective-permute-start.8 = (bf16[8,5120]{1,0:T(8,128)(2,1)}, bf16[8,5120]{1,0:T(8,128)(2,1)S(1)}, u32[]{:S(2)}, u32[]{:S(2)}) collective-permute-start(bf16[8,5120]{1,0:T(8,128)(2,1)} %get-tuple-element.25), channel_id=1, source_target_pairs={{0,4},{1,5},{2,6},{3,7},{4,0},{5,1},{6,2},{7,3},{8,12},{9,13},{10,... | collective-permute-start | bytes 245768 | tf_op jit(solution)/shard_map/ppermute | solution.py:31
  44.9 6.6 %collective-permute-start.9 = (bf16[8,5120]{1,0:T(8,128)(2,1)}, bf16[8,5120]{1,0:T(8,128)(2,1)S(1)}, u32[]{:S(2)}, u32[]{:S(2)}) collective-permute-start(bf16[8,5120]{1,0:T(8,128)(2,1)} %get-tuple-element.26), channel_id=1, source_target_pairs={{0,6},{1,7},{2,4},{3,5},{4,2},{5,3},{6,0},{7,1},{8,14},{9,15},{10,... | collective-permute-start | bytes 245768 | tf_op jit(solution)/shard_map/ppermute | solution.py:31
  46.2 5.3 %copy-start.3 = (bf16[8,5120]{1,0:T(8,128)(2,1)}, bf16[8,5120]{1,0:T(8,128)(2,1)S(1)}, u32[]{:S(2)}) copy-start(bf16[8,5120]{1,0:T(8,128)(2,1)S(1)} %collective-permute-done.7.refs_0_) | copy-start | bytes 245764
  50.3 1.2 copy-start.4
  54.6 19.6 %copy-start.17 = (s32[8]{0:T(128)S(1)}, s32[8]{0:T(128)}, u32[]{:S(2)}) copy-start(s32[8]{0:T(128)} %constant.164.clone) | copy-start | bytes 100
  54.6 19.6 %copy-start.16 = (s32[4]{0:T(128)S(1)}, s32[4]{0:T(128)}, u32[]{:S(2)}) copy-start(s32[4]{0:T(128)} %constant.163.clone) | copy-start | bytes 52
  54.7 5.3 %collective-permute-start.10 = (bf16[8,5120]{1,0:T(8,128)(2,1)}, bf16[8,5120]{1,0:T(8,128)(2,1)S(1)}, u32[]{:S(2)}, u32[]{:S(2)}) collective-permute-start(bf16[8,5120]{1,0:T(8,128)(2,1)} %norm.1), channel_id=1, source_target_pairs={{0,2},{1,3},{2,0},{3,1},{4,6},{5,7},{6,4},{7,5},{8,10},{9,11},{10,... | collective-permute-start | bytes 245768 | tf_op jit(solution)/shard_map/ppermute | solution.py:31
  55.8 7.0 %collective-permute-start.11 = (bf16[8,5120]{1,0:T(8,128)(2,1)}, bf16[8,5120]{1,0:T(8,128)(2,1)S(1)}, u32[]{:S(2)}, u32[]{:S(2)}) collective-permute-start(bf16[8,5120]{1,0:T(8,128)(2,1)} %norm.1), channel_id=1, source_target_pairs={{0,4},{1,5},{2,6},{3,7},{4,0},{5,1},{6,2},{7,3},{8,12},{9,13},{10,... | collective-permute-start | bytes 245768 | tf_op jit(solution)/shard_map/ppermute | solution.py:31
  57.4 6.6 %collective-permute-start.12 = (bf16[8,5120]{1,0:T(8,128)(2,1)}, bf16[8,5120]{1,0:T(8,128)(2,1)S(1)}, u32[]{:S(2)}, u32[]{:S(2)}) collective-permute-start(bf16[8,5120]{1,0:T(8,128)(2,1)} %norm.1), channel_id=1, source_target_pairs={{0,6},{1,7},{2,4},{3,5},{4,2},{5,3},{6,0},{7,1},{8,14},{9,15},{10,... | collective-permute-start | bytes 245768 | tf_op jit(solution)/shard_map/ppermute | solution.py:31
  64.9 7.1 %collective-permute-start.13 = (bf16[4,8,5120]{2,1,0:T(8,128)(2,1)S(1)}, bf16[4,8,5120]{2,1,0:T(8,128)(2,1)S(1)}, u32[]{:S(2)}, u32[]{:S(2)}) collective-permute-start(bf16[4,8,5120]{2,1,0:T(8,128)(2,1)S(1)} %pad_maximum_fusion), channel_id=1, source_target_pairs={{0,1},{1,0},{2,3},{3,2},{4,5},{5,4},{6,7},{7,6},{8,9},{9,8},{10,11... | collective-permute-start | bytes 983048 | tf_op jit(solution)/shard_map/ppermute | solution.py:31
  66.5 18.8 %copy-start.13 = (s32[256]{0:T(256)S(1)}, s32[256]{0:T(256)}, u32[]{:S(2)}) copy-start(s32[256]{0:T(256)} %param.25) | copy-start | bytes 3076
  72.1 12.9 %collective-permute-start.14 = (bf16[8,8,5120]{2,1,0:T(8,128)(2,1)S(1)}, bf16[8,8,5120]{2,1,0:T(8,128)(2,1)S(1)}, u32[]{:S(2)}, u32[]{:S(2)}) collective-permute-start(bf16[8,8,5120]{2,1,0:T(8,128)(2,1)S(1)} %get-tuple-element.29), channel_id=1, source_target_pairs={{0,16},{8,24},{16,0},{24,8},{1,17},{9,25},{17,1},{25,9},{2,18},{10... | collective-permute-start | bytes 1966088 | tf_op jit(solution)/shard_map/ppermute | solution.py:31
  85.1 3.1 %copy-start = (bf16[16,8,5120]{2,1,0:T(8,128)(2,1)}, bf16[16,8,5120]{2,1,0:T(8,128)(2,1)S(1)}, u32[]{:S(2)}) copy-start(bf16[16,8,5120]{2,1,0:T(8,128)(2,1)S(1)} %constant_dynamic-update-slice_fusion.5) | copy-start | bytes 3932164
  85.1 3.1 %collective-permute-start.15 = (bf16[128,5120]{1,0:T(8,128)(2,1)S(1)}, bf16[128,5120]{1,0:T(8,128)(2,1)S(1)}, u32[]{:S(2)}, u32[]{:S(2)}) collective-permute-start(bf16[128,5120]{1,0:T(8,128)(2,1)S(1)} %bitcast.25), channel_id=1, source_target_pairs={{0,8},{8,0},{16,24},{24,16},{1,9},{9,1},{17,25},{25,17},{2,10},{10... | collective-permute-start | bytes 3932168 | tf_op jit(solution)/shard_map/ppermute | solution.py:31
  86.9 31.5 %copy-start.14 = (s32[2]{0:T(128)S(1)}, s32[2]{0:T(128)}, u32[]{:S(2)}) copy-start(s32[2]{0:T(128)} %lengths_ref.1) | copy-start | bytes 28
  88.2 1.1 copy-start.1
  110.8 14.7 %all-to-all-start = ((f32[32,1,24]{2,1,0:T(1,128)}), f32[32,1,24]{2,1,0:T(1,128)S(1)}, u32[]{:S(2)}, u32[]{:S(2)}) async-start(f32[32,1,24]{2,1,0:T(1,128)} %bitcast.12), calls=%async_computation | async-start | bytes 32768 | tf_op jit(solution)/shard_map/all_to_all | solution.py:349
  (3 other events, 1.9 us)

commit v2 on v0

v2 whole, which is shorter than its diff:
```python
import functools

import jax
import jax.numpy as jnp
from jax import lax
from jax.experimental import pallas as pl
from jax.experimental.pallas import tpu as pltpu
from jax.sharding import PartitionSpec as P

HEAD_DIM = 128
PLEN = 512
NEG = -1e30
BF16 = jnp.bfloat16
F32 = jnp.float32
MIB = 1024 * 1024


def params(mib):
    return pltpu.CompilerParams(vmem_limit_bytes=mib * MIB)


def held(x):
    return pltpu.with_memory_space_constraint(x, pltpu.VMEM)


def stored(x):
    return pltpu.with_memory_space_constraint(x, pltpu.HBM)


def anywhere():
    return pl.BlockSpec(memory_space=pl.ANY)


def cost(flops=0, moved=0):
    return pl.CostEstimate(flops=flops, bytes_accessed=moved, transcendentals=0)


def vmem():
    return pl.BlockSpec(memory_space=pltpu.VMEM)


def smem():
    return pl.BlockSpec(memory_space=pltpu.SMEM)


def swap(x, axis, distance, size):
    return lax.ppermute(x, axis, [(i, i ^ distance) for i in range(size)])


def attend(jobs):
    factor = HEAD_DIM**-0.5
    scores = [
        lax.dot_general(q, k, (((1,), (1,)), ((), ())), preferred_element_type=F32)
        for q, k, _, _ in jobs
    ]
    scores = [
        s if job[3] is None else jnp.where(job[3], s, NEG) for s, job in zip(scores, jobs)
    ]
    peaks = [jnp.max(s, axis=1, keepdims=True) for s in scores]
    weights = [jnp.exp((s - peak) * factor) for s, peak in zip(scores, peaks)]
    weights = [
        w if job[3] is None else jnp.where(job[3], w, 0.0) for w, job in zip(weights, jobs)
    ]
    weights = [w.astype(BF16) for w in weights]
    totals = [jnp.sum(w.astype(F32), axis=1, keepdims=True) for w in weights]
    mixed = [
        jnp.dot(w, job[2], preferred_element_type=F32) for w, job in zip(weights, jobs)
    ]
    return [
        (m / total, peak * factor + jnp.log(total))
        for m, total, peak in zip(mixed, totals, peaks)
    ]


def pack_logs(logs, rows):
    lane = lax.broadcasted_iota(jnp.int32, (rows, 128), 1)
    packed = jnp.zeros((rows, 128), F32)
    for head, log in enumerate(logs):
        first = log.astype(BF16).astype(F32)
        second = (log - first).astype(BF16).astype(F32)
        third = log - first - second
        for part, value in enumerate((first, second, third)):
            packed = jnp.where(lane == 3 * head + part, value, packed)
    return packed.astype(BF16)


def own_kernel(heads, seq, lengths_ref, *refs):
    sources, (own_ref, pre_ref), kept, scratch, sems = refs[:6], refs[6:8], refs[8:11], refs[11:14], refs[14]
    places = scratch + kept
    copies = [
        pltpu.make_async_copy(src, dst, sems.at[i]) for i, (src, dst) in enumerate(zip(sources, places))
    ]
    for copy in copies:
        copy.start()
    q_ref, rk_ref, rv_ref, k_ref, v_ref, _ = places
    rows = q_ref.shape[0]
    row = lax.broadcasted_iota(jnp.int32, (rows, rows), 0)
    col = lax.broadcasted_iota(jnp.int32, (rows, rows), 1)
    live = jnp.zeros((rows, rows), jnp.int32)
    for r in range(rows // seq):
        live = jnp.where(col // seq == r, lengths_ref[r], live)
    allowed = (row // seq == col // seq) & (col <= row) & (col % seq < live)
    parts = [slice(h * HEAD_DIM, (h + 1) * HEAD_DIM) for h in range(heads)]
    for copy in copies[:5]:
        copy.wait()
    found = attend(
        [(q_ref[:, p], rk_ref[:, p], rv_ref[:, p], allowed) for p in parts]
        + [(q_ref[:, p], k_ref[:, p], v_ref[:, p], None) for p in parts]
    )
    for h, p in enumerate(parts):
        own_ref[:, p] = found[h][0]
        pre_ref[:, p] = found[heads + h][0]
    logs = [log for _, log in found[:heads]]
    pre_logs = [log for _, log in found[heads:]]
    lane = lax.broadcasted_iota(jnp.int32, (rows, 128), 1)
    for ref, values in ((own_ref, logs), (pre_ref, pre_logs)):
        packed = jnp.zeros((rows, 128), F32)
        for h in range(heads):
            packed = jnp.where(lane == h, values[h], packed)
        ref[:, heads * HEAD_DIM :] = packed
    copies[5].wait()


def prefix_kernel(heads, count, *refs):
    q_refs, (k_ref, v_ref), out_refs = refs[:count], refs[count : count + 2], refs[count + 2 :]
    rows = q_refs[0].shape[0]
    parts = [slice(h * HEAD_DIM, (h + 1) * HEAD_DIM) for h in range(heads)]
    found = attend(
        [
            (jnp.concatenate([ref[:, p] for ref in q_refs], axis=0), k_ref[:, p], v_ref[:, p], None)
            for p in parts
        ]
    )
    for i in range(count):
        rung = slice(i * rows, (i + 1) * rows)
        for h, p in enumerate(parts):
            out_refs[i][:, p] = found[h][0][rung].astype(BF16)
        out_refs[i][:, heads * HEAD_DIM :] = pack_logs([log[rung] for _, log in found], rows)


def project_kernel(heads, seq, share, wide, group_size, key_rows, prompt_ref, *refs):
    count = group_size - 1
    own_ref, pre_ref = refs[:2]
    got_refs = refs[2 : 2 + count]
    weight_ref = refs[2 + count]
    out_refs, (attended_ref, partial_ref) = refs[3 + count : -2], refs[-2:]
    rows = own_ref.shape[0]
    row = lax.broadcasted_iota(jnp.int32, (rows, 1), 0)
    wanted = jnp.zeros((rows, 1), jnp.int32)
    for r in range(rows // seq):
        wanted = jnp.where(row // seq == r, prompt_ref[r], wanted)
    group = lax.axis_index("group")
    holders = [(group ^ d) * key_rows // PLEN for d in range(group_size)]
    for h in range(heads):
        part = slice(h * HEAD_DIM, (h + 1) * HEAD_DIM)
        at = heads * HEAD_DIM
        logs = [own_ref[:, at + h : at + h + 1]]
        values = [own_ref[:, part]]
        pre_log = pre_ref[:, at + h : at + h + 1]
        logs.append(jnp.where(wanted == holders[0], pre_log, NEG))
        values.append(pre_ref[:, part])
        for i, ref in enumerate(got_refs):
            three = ref[:, at : at + 128].astype(F32)
            log = (
                three[:, 3 * h : 3 * h + 1]
                + three[:, 3 * h + 1 : 3 * h + 2]
                + three[:, 3 * h + 2 : 3 * h + 3]
            )
            logs.append(jnp.where(wanted == holders[1 + i], log, NEG))
            values.append(ref[:, part].astype(F32))
        peak = functools.reduce(jnp.maximum, logs)
        loads = [jnp.exp(log - peak) for log in logs]
        total = functools.reduce(jnp.add, loads)
        mixed = functools.reduce(jnp.add, [w * v for w, v in zip(loads, values)])
        attended_ref[:, part] = (mixed / total).astype(BF16)

    me = lax.axis_index("tensor")

    @pl.loop(0, weight_ref.shape[1] // wide)
    def _(n):
        columns = pl.ds(pl.multiple_of(n * wide, 128), wide)
        partial = jnp.dot(attended_ref[...], weight_ref[:, columns], preferred_element_type=F32)
        for b in range(rows // share):
            partial_ref[b] = partial[b * share : (b + 1) * share]
        for d, ref in enumerate(out_refs):
            ref[:, columns] = partial_ref[me ^ d].astype(ref.dtype)


def fetch_kernel(start, count, source_ref, gate_ref, out_ref, sems):
    rows = out_ref.shape[0] // count
    copies = [
        pltpu.make_async_copy(
            source_ref.at[pl.ds(start + i * rows, rows)], out_ref.at[pl.ds(i * rows, rows)], sems.at[i]
        )
        for i in range(count)
    ]
    for copy in copies:
        copy.start()
    for copy in copies:
        copy.wait()


def norm_kernel(residual_ref, gain_ref, *refs):
    terms, out_refs = refs[2:-2], refs[-2:]
    hidden = residual_ref[lax.axis_index("tensor")].astype(F32)
    for ref in terms:
        hidden = hidden + ref[...].astype(F32)
    squares = jnp.mean(hidden * hidden, axis=-1, keepdims=True)
    normed = (hidden * lax.rsqrt(squares + 1e-06) * gain_ref[...].astype(F32)).astype(BF16)
    width = normed.shape[1] // 2
    for i, ref in enumerate(out_refs):
        ref[...] = normed[:, i * width : (i + 1) * width]


def first_kernel(narrow, left_ref, right_ref, weight_ref, out_ref, x_ref):
    half = left_ref.shape[0]
    x_ref[:half] = left_ref[...]
    x_ref[half:] = right_ref[...]

    @pl.loop(0, weight_ref.shape[1] // narrow)
    def _(n):
        columns = pl.ds(n * narrow if narrow % 128 else pl.multiple_of(n * narrow, 128), narrow)
        out_ref[:, columns] = jnp.dot(
            x_ref[...], weight_ref[:, columns], preferred_element_type=F32
        )


def logits_kernel(
    narrow,
    spots,
    tensor_size,
    sum_in_ref,
    left_ref,
    right_ref,
    target_ref,
    weight_ref,
    out_ref,
    x_ref,
    peak_ref,
    sum_ref,
    pick_ref,
    wanted_ref,
    stats_ref,
):
    half = left_ref.shape[0]
    rows = 2 * half
    share = target_ref.shape[1]
    group, tensor = lax.axis_index("group"), lax.axis_index("tensor")
    vocab = weight_ref.shape[1]
    places = [(group ^ g) * tensor_size + (tensor ^ t) for g, t in spots]
    for i, place in enumerate(places):
        wanted_ref[i * share : (i + 1) * share] = target_ref[place]
    wanted = wanted_ref[...] - (group * tensor_size + tensor) * vocab
    wanted_ref[...] = jnp.where((wanted >= 0) & (wanted < vocab), wanted, -1)
    x_ref[:half] = left_ref[...]
    x_ref[half:] = right_ref[...]
    peak_ref[...] = jnp.full_like(peak_ref, NEG)
    sum_ref[...] = jnp.zeros_like(sum_ref)
    pick_ref[...] = jnp.zeros_like(pick_ref)

    @pl.loop(0, weight_ref.shape[1] // narrow)
    def _(n):
        columns = pl.ds(n * narrow if narrow % 128 else pl.multiple_of(n * narrow, 128), narrow)
        logits = sum_in_ref[:, columns] + jnp.dot(
            x_ref[...], weight_ref[:, columns], preferred_element_type=F32
        )
        parts = [logits[:, c : c + 128] for c in range(0, narrow, 128)]
        if narrow % 128:
            spare = jnp.full((rows, 128 - narrow % 128), NEG, F32)
            parts[-1] = jnp.concatenate([parts[-1], spare], axis=1)
        lane = lax.broadcasted_iota(jnp.int32, (rows, 128), 1) + n * narrow
        peak = peak_ref[...]
        higher = functools.reduce(jnp.maximum, parts, peak)
        total = sum_ref[...] * jnp.exp(peak - higher)
        picked = pick_ref[...]
        target = wanted_ref[...]
        for c, part in enumerate(parts):
            total = total + jnp.exp(part - higher)
            picked = picked + jnp.where(lane + c * 128 == target, part, 0.0)
        peak_ref[...] = higher
        sum_ref[...] = total
        pick_ref[...] = picked

    higher = peak_ref[...]
    peak = jnp.max(higher, axis=1, keepdims=True)
    sums = jnp.sum(sum_ref[...] * jnp.exp(higher - peak), axis=1, keepdims=True)
    pick = jnp.sum(pick_ref[...], axis=1, keepdims=True)
    place = lax.broadcasted_iota(jnp.int32, (rows, 128), 1)
    three = jnp.where(place == 0, peak, jnp.where(place == 1, sums, pick))
    for i, place in enumerate(places):
        stats_ref[place] = three[i * share : (i + 1) * share]
    out_ref[...] = jnp.transpose(stats_ref[...].reshape(rows, 128))[:8]


def local(
    group_size,
    tensor_size,
    resp_query,
    resp_key,
    resp_value,
    prompt_keys,
    prompt_values,
    prompt_of,
    lengths,
    residual,
    out_weight,
    norm_gain,
    lm_weight,
    targets,
):
    rows, span = resp_query.shape
    heads = span // HEAD_DIM
    seq = rows // prompt_of.shape[0]
    key_rows = prompt_keys.shape[0]
    assert PLEN % key_rows == 0
    share = rows // tensor_size
    depth = out_weight.shape[1]
    vocab = lm_weight.shape[1]
    tensor_index = lax.axis_index("tensor")
    i32 = jnp.int32

    distances = list(range(1, group_size))
    queries = [swap(resp_query, "group", d, group_size) for d in distances]
    inputs = (resp_query, resp_key, resp_value, prompt_keys, prompt_values, out_weight)
    own, prefix, keys, values, weight = pl.pallas_call(
        functools.partial(own_kernel, heads, seq),
        out_shape=[jax.ShapeDtypeStruct((rows, span + 128), F32)] * 2
        + [pltpu.VMEM(x.shape, x.dtype) for x in inputs[3:]],
        in_specs=[smem()] + [anywhere()] * 6,
        out_specs=[vmem()] * 5,
        scratch_shapes=[pltpu.VMEM(x.shape, x.dtype) for x in inputs[:3]]
        + [pltpu.SemaphoreType.DMA((6,))],
        compiler_params=params(6),
        cost_estimate=cost(moved=14 * MIB),
        name="own_attention",
    )(lengths, *map(stored, inputs))
    keys, values, weight = held(keys), held(values), held(weight)
    answers = pl.pallas_call(
        functools.partial(prefix_kernel, heads, len(distances)),
        out_shape=[jax.ShapeDtypeStruct((rows, span + 128), BF16)] * len(distances),
        in_specs=[vmem()] * (len(distances) + 2),
        out_specs=[vmem()] * len(distances),
        compiler_params=params(8),
        name="prefix_attention",
    )(*map(held, queries), keys, values)
    got = [swap(x, "group", d, group_size) for x, d in zip(answers, distances)]

    wide = 640 if depth % 640 == 0 else depth
    shares = pl.pallas_call(
        functools.partial(project_kernel, heads, seq, share, wide, group_size, key_rows),
        out_shape=[
            jax.ShapeDtypeStruct((share, depth), BF16 if d else F32) for d in range(tensor_size)
        ],
        in_specs=[smem()] + [vmem()] * (3 + len(distances)),
        out_specs=[vmem()] * tensor_size,
        scratch_shapes=[
            pltpu.VMEM((rows, span), BF16),
            pltpu.VMEM((tensor_size, share, wide), F32),
        ],
        compiler_params=params(6),
        name="project",
    )(prompt_of, *map(held, (own, prefix, *got)), weight)

    weights = []
    for i in range(2):
        weights.append(
            pl.pallas_call(
                functools.partial(fetch_kernel, i * (depth // 2), 4),
                out_shape=pltpu.VMEM((depth // 2, vocab), BF16),
                in_specs=[anywhere()] * 2,
                out_specs=vmem(),
                scratch_shapes=[pltpu.SemaphoreType.DMA((4,))],
                compiler_params=params(1),
                cost_estimate=cost(moved=depth // 2 * vocab * 2),
                name="fetch",
            )(stored(lm_weight), shares[1])
        )

    got = [swap(x, "tensor", d, tensor_size) for d, x in enumerate(shares) if d]
    normed = pl.pallas_call(
        norm_kernel,
        out_shape=[jax.ShapeDtypeStruct((share, depth // 2), BF16)] * 2,
        in_specs=[vmem()] * 2 + [anywhere()] * 2 + [vmem()] * tensor_size,
        out_specs=[vmem()] * 2,
        compiler_params=params(4),
        name="norm",
    )(
        *map(held, (residual.reshape(tensor_size, share, depth), norm_gain[None], *weights)),
        *map(held, (shares[0], *got)),
    )

    far = list(range(2, tensor_size, 2))
    above = list(range(2, group_size, 2))
    order = [0] + far
    here = [(g, x) for g in [0] + above for x in (0, 1)]
    mesh_ids = [(g, t) for g in range(group_size) for t in range(tensor_size)]
    routes = {
        (g, x): [(a * tensor_size + b, (a ^ g) * tensor_size + (b ^ x)) for a, b in mesh_ids]
        for g, x in here
    }
    halves = []
    for part in normed:
        tokens = jnp.stack([part] + [swap(part, "tensor", d, tensor_size) for d in far])
        pieces = [
            lax.ppermute(tokens, ("group", "tensor"), routes[place]) if any(place) else tokens
            for place in here
        ]
        tokens = jnp.concatenate(pieces).reshape(-1, depth // 2)
        halves.append((tokens, swap(tokens, "group", 1, group_size)))
    spots = [(g + c, t + x) for c in (0, 1) for g, x in here for t in order]
    total_rows = 2 * tokens.shape[0]
    narrow = 512 if vocab % 512 == 0 else vocab
    limit = 10 if total_rows <= 256 else 24
    work = 2 * total_rows * (depth // 2) * vocab
    first = pl.pallas_call(
        functools.partial(first_kernel, narrow),
        out_shape=pltpu.VMEM((total_rows, vocab), F32),
        in_specs=[vmem()] * 3,
        out_specs=vmem(),
        scratch_shapes=[pltpu.VMEM((total_rows, depth // 2), BF16)],
        compiler_params=params(limit),
        cost_estimate=cost(flops=work),
        name="logits_first",
    )(*map(held, (*halves[0], weights[0])))
    stats = pl.pallas_call(
        functools.partial(logits_kernel, narrow, spots, tensor_size),
        out_shape=jax.ShapeDtypeStruct((8, total_rows), F32),
        in_specs=[vmem()] * 5,
        out_specs=vmem(),
        scratch_shapes=[pltpu.VMEM((total_rows, depth // 2), BF16)]
        + [pltpu.VMEM((total_rows, 128), F32)] * 3
        + [pltpu.VMEM((total_rows, 1), i32), pltpu.VMEM((len(spots), share, 128), F32)],
        compiler_params=params(limit),
        cost_estimate=cost(flops=work),
        name="logits",
    )(*map(held, (first, *halves[1])), targets.reshape(-1, share, 1), held(weights[1]))

    blocks = stats[:3].reshape(3, -1, share).transpose(1, 0, 2).reshape(-1, 3 * share)
    blocks = lax.all_to_all(blocks, ("group", "tensor"), 0, 0, tiled=True)
    peaks, sums, picks = blocks[:, :share], blocks[:, share : 2 * share], blocks[:, 2 * share :]
    peak = jnp.max(peaks, axis=0)
    total = jnp.sum(sums * jnp.exp(peaks - peak[None]), axis=0)
    values = jnp.sum(picks, axis=0) - peak - jnp.log(total)
    local_rows = tensor_index * share + jnp.arange(share, dtype=i32)
    slots = jnp.arange(prompt_of.shape[0], dtype=i32)
    local_len = jnp.sum(
        jnp.where((local_rows // seq)[:, None] == slots[None, :], lengths[None, :], 0), axis=1
    )
    return jnp.where(local_rows % seq < local_len, values, 0.0)


def solution(mesh):
    return jax.shard_map(
        functools.partial(local, mesh.shape["group"], mesh.shape["tensor"]),
        mesh=mesh,
        in_specs=(
            P("group", "tensor"),
            P("group", "tensor"),
            P("group", "tensor"),
            P("group", "tensor"),
            P("group", "tensor"),
            P("group"),
            P("group"),
            P("group", None),
            P("tensor", None),
            P(),
            P(None, ("group", "tensor")),
            P(),
        ),
        out_specs=P(("group", "tensor")),
        check_vma=False,
    )
```

time: 295 us -> 108 us (0.37)
  waiting for transfers between devices: 166 us -> 20 us
  blocking collectives: 79.3 us -> 0 us
  Pallas kernels: 0 us -> 36.6 us
  starting transfers between devices: 0.16 us -> 36.1 us
  matrix products: 26.1 us -> 0 us
  between operations: 13.3 us -> 0.39 us
  local copies, waits for them, and re-layouts: 4.18 us -> 14 us
  other arithmetic: 5.46 us -> 0.79 us
    all_gather x3 -> x0, waiting for transfers between devices: 101 us -> none  [the longest x1 57 us: local(): piece = lax.all_gather(normed, ('group', 'tensor'), axis=0, tiled=True)]
    reduce_scatter x1 -> x0, waiting for transfers between devices: 64.4 us -> none  [local(): lax.psum_scatter(partial_value, 'tensor', scatter_dimension=0, tiled=True)]
    psum x1 -> x0, blocking collectives: 41.1 us -> none  [local(): lax.psum((terms[1] * jnp.exp(terms[0] - peak_all), terms[2]), ('group', '...]
    pmax x1 -> x0, blocking collectives: 38.2 us -> none  [local(): peak_all = lax.pmax(terms[0], ('group', 'tensor'))]
    pallas_call x0 -> x8, Pallas kernels: none -> 36.6 us  [the longest x2 16.9 us: local(): pl.pallas_call(functools.partial(fetch_kernel, i * (depth // 2), 4), out_...]
    ppermute x0 -> x27, starting transfers between devices: none -> 32.9 us  [the longest x21 25.3 us: swap(): return lax.ppermute(x, axis, [(i, i ^ distance) for i in range(size)])]
    dot_general x6 -> x0, matrix products: 26.1 us -> none  [the longest x1 14.7 us: local(): logits = jnp.dot(piece, lm_weight, preferred_element_type=jnp.float32)]
    ppermute x0 -> x27, waiting for transfers between devices: none -> 13 us  [the longest x21 6.75 us: swap(): return lax.ppermute(x, axis, [(i, i ^ distance) for i in range(size)])]
  transfers between devices with their start and end apart: 4 -> 28, of which waited for: 4 -> 9; matrix products, arithmetic and copies ran while one was open for 2% -> 1% of each run, Pallas kernels for 0% -> 24%
where the time goes in v2:
time: 108 us
  Pallas kernels  36.6 us (34%)
  starting transfers between devices  36.1 us (33%)
  waiting for transfers between devices  20 us (19%)
  local copies, waits for them, and re-layouts  14 us (13%)
    ppermute x21, starting transfers between devices, swap(): return lax.ppermute(x, axis, [(i, i ^ distance) for i in range(size)])  25.3 us
    pallas_call x2, Pallas kernels, local(): pl.pallas_call(functools.partial(fetch_kernel, i * (depth // 2), 4), out_...  16.9 us
    unnamed x29, local copies, waits for them, and re-layouts  12.2 us
    ppermute x6, starting transfers between devices, local(): lax.ppermute(tokens, ('group', 'tensor'), routes[place])  7.56 us
    all_to_all x1, waiting for transfers between devices, local(): blocks = lax.all_to_all(blocks, ('group', 'tensor'), 0, 0, tiled=True)  7.01 us
    ppermute x21, waiting for transfers between devices, swap(): return lax.ppermute(x, axis, [(i, i ^ distance) for i in range(size)])  6.75 us
    ppermute x6, waiting for transfers between devices, local(): lax.ppermute(tokens, ('group', 'tensor'), routes[place])  6.26 us
    pallas_call x1, Pallas kernels, local(): pl.pallas_call(functools.partial(logits_kernel, narrow, spots, tensor_siz...  6.23 us
  transfers between devices with their start and end apart: 28, of which 9 were waited for; matrix products, arithmetic and copies ran while one was open for 1% of the time, Pallas kernels for 24%

profile of v2, /device:TPU:0, one launch (start us, length us, event | category | flops | bytes accessed | tf_op | source)
XLA Modules:
  0.0 107.9 jit_solution(3757433706445046341)
XLA Ops:
  0.5 2.5 %collective-permute-start.1 = (bf16[64,512]{1,0:T(8,128)(2,1)}, bf16[64,512]{1,0:T(8,128)(2,1)S(1)}, u32[]{:S(2)}, u32[]{:S(2)}) collective-permute-start(bf16[64,512]{1,0:T(8,128)(2,1)} %refs_0_.1), channel_id=1, source_target_pairs={{0,16},{8,24},{16,0},{24,8},{1,17},{9,25},{17,1},{25,9},{2,18},{10... | collective-permute-start | bytes 196616 | tf_op jit(solution)/shard_map/ppermute | solution.py:47
  3.8 3.5 %own_attention.1 = (f32[64,640]{1,0:T(8,128)S(1)}, f32[64,640]{1,0:T(8,128)S(1)}, bf16[512,512]{1,0:T(8,128)(2,1)S(1)}, bf16[512,512]{1,0:T(8,128)(2,1)S(1)}, bf16[512,5120]{1,0:T(8,128)(2,1)S(1)}) custom-call(s32[2]{0:T(128)S(1)} %copy-done.6, bf16[64,512]{1,0:T(8,128)(2,1)} %refs_0_.1, bf16[64,512]{1,0:T(8,128)(2,1)} %refs_1_.1, bf16[64,512]{1,0:T(8,128)(2,1)} %refs_2_.1, ...), custom_call_target="tpu_custom_call" | custom-call | bytes 14680064 | tf_op jit(solution)/shard_map/own_attention/pallas_call | solution.py:325
  7.3 0.9 prefix_attention.1
  8.3 1.9 %collective-permute-start.4 = (bf16[64,640]{1,0:T(8,128)(2,1)S(1)}, bf16[64,640]{1,0:T(8,128)(2,1)S(1)}, u32[]{:S(2)}, u32[]{:S(2)}) collective-permute-start(bf16[64,640]{1,0:T(8,128)(2,1)S(1)} %get-tuple-element.28), channel_id=1, source_target_pairs={{0,16},{8,24},{16,0},{24,8},{1,17},{9,25},{17,1},{25,9},{2,18},{10... | collective-permute-start | bytes 245768 | tf_op jit(solution)/shard_map/ppermute | solution.py:47
  10.3 2.9 %collective-permute-done.4.refs_3_ = bf16[64,640]{1,0:T(8,128)(2,1)S(1)} collective-permute-done((bf16[64,640]{1,0:T(8,128)(2,1)S(1)}, bf16[64,640]{1,0:T(8,128)(2,1)S(1)}, u32[]{:S(2)}, u32[]{:S(2)}) %collective-permute-start.4) | collective-permute-done | bytes 81952 | tf_op jit(solution)/shard_map/ppermute | solution.py:47
  13.1 1.7 %collective-permute-done.5.refs_4_ = bf16[64,640]{1,0:T(8,128)(2,1)S(1)} collective-permute-done((bf16[64,640]{1,0:T(8,128)(2,1)S(1)}, bf16[64,640]{1,0:T(8,128)(2,1)S(1)}, u32[]{:S(2)}, u32[]{:S(2)}) %collective-permute-start.5) | collective-permute-done | bytes 81952 | tf_op jit(solution)/shard_map/ppermute | solution.py:47
  15.5 3.8 %project.1 = (f32[8,5120]{1,0:T(8,128)S(1)}, bf16[8,5120]{1,0:T(8,128)(2,1)S(1)}, bf16[8,5120]{1,0:T(8,128)(2,1)S(1)}, bf16[8,5120]{1,0:T(8,128)(2,1)S(1)}, bf16...) custom-call(s32[2]{0:T(128)S(1)} %copy-done.5, ...), custom_call_target="tpu_custom_call" | custom-call | tf_op jit(solution)/shard_map/project/pallas_call | solution.py:349
  19.3 1.7 %collective-permute-start.6 = (bf16[8,5120]{1,0:T(8,128)(2,1)S(1)}, bf16[8,5120]{1,0:T(8,128)(2,1)S(1)}, u32[]{:S(2)}, u32[]{:S(2)}) collective-permute-start(bf16[8,5120]{1,0:T(8,128)(2,1)S(1)} %get-tuple-element.31.gate_ref), channel_id=1, source_target_pairs={{0,1},{1,0},{2,3},{3,2},{4,5},{5,4},{6,7},{7,6},{8,9},{9,8},{10,11... | collective-permute-start | bytes 245768 | tf_op jit(solution)/shard_map/ppermute | solution.py:47
  21.0 1.6 %collective-permute-start.7 = (bf16[8,5120]{1,0:T(8,128)(2,1)S(1)}, bf16[8,5120]{1,0:T(8,128)(2,1)S(1)}, u32[]{:S(2)}, u32[]{:S(2)}) collective-permute-start(bf16[8,5120]{1,0:T(8,128)(2,1)S(1)} %get-tuple-element.33), channel_id=1, source_target_pairs={{0,2},{1,3},{2,0},{3,1},{4,6},{5,7},{6,4},{7,5},{8,10},{9,11},{10,... | collective-permute-start | bytes 245768 | tf_op jit(solution)/shard_map/ppermute | solution.py:47
  22.8 2.7 %collective-permute-start.9 = (bf16[8,5120]{1,0:T(8,128)(2,1)S(1)}, bf16[8,5120]{1,0:T(8,128)(2,1)S(1)}, u32[]{:S(2)}, u32[]{:S(2)}) collective-permute-start(bf16[8,5120]{1,0:T(8,128)(2,1)S(1)} %get-tuple-element.35), channel_id=1, source_target_pairs={{0,4},{1,5},{2,6},{3,7},{4,0},{5,1},{6,2},{7,3},{8,12},{9,13},{10,... | collective-permute-start | bytes 245768 | tf_op jit(solution)/shard_map/ppermute | solution.py:47
  25.6 1.3 %collective-permute-start.10 = (bf16[8,5120]{1,0:T(8,128)(2,1)S(1)}, bf16[8,5120]{1,0:T(8,128)(2,1)S(1)}, u32[]{:S(2)}, u32[]{:S(2)}) collective-permute-start(bf16[8,5120]{1,0:T(8,128)(2,1)S(1)} %get-tuple-element.36), channel_id=1, source_target_pairs={{0,5},{1,4},{2,7},{3,6},{4,1},{5,0},{6,3},{7,2},{8,13},{9,12},{10,... | collective-permute-start | bytes 245768 | tf_op jit(solution)/shard_map/ppermute | solution.py:47
  26.8 3.7 %collective-permute-start.11 = (bf16[8,5120]{1,0:T(8,128)(2,1)S(1)}, bf16[8,5120]{1,0:T(8,128)(2,1)S(1)}, u32[]{:S(2)}, u32[]{:S(2)}) collective-permute-start(bf16[8,5120]{1,0:T(8,128)(2,1)S(1)} %get-tuple-element.37), channel_id=1, source_target_pairs={{0,6},{1,7},{2,4},{3,5},{4,2},{5,3},{6,0},{7,1},{8,14},{9,15},{10,... | collective-permute-start | bytes 245768 | tf_op jit(solution)/shard_map/ppermute | solution.py:47
  30.5 0.7 broadcast_in_dim.25.gain_ref
  31.2 5.6 %fetch.2.refs_0_.weight_ref = bf16[2560,3072]{1,0:T(8,128)(2,1)S(1)} custom-call(bf16[5120,3072]{1,0:T(8,128)(2,1)} %source_ref.3, bf16[8,5120]{1,0:T(8,128)(2,1)S(1)} %get-tuple-element.31.gate_ref), custom_call_target="tpu_custom_call" | custom-call | bytes 15728640 | tf_op jit(solution)/shard_map/fetch/pallas_call | solution.py:367
  36.8 11.3 %fetch.3.refs_1_.weight_ref = bf16[2560,3072]{1,0:T(8,128)(2,1)S(1)} custom-call(bf16[5120,3072]{1,0:T(8,128)(2,1)} %source_ref.3, bf16[8,5120]{1,0:T(8,128)(2,1)S(1)} %get-tuple-element.31.gate_ref), custom_call_target="tpu_custom_call" | custom-call | bytes 15728640 | tf_op jit(solution)/shard_map/fetch/pallas_call | solution.py:367
  48.4 5.2 %copy-done = bf16[2560,3072]{1,0:T(8,128)(2,1)} copy-done((bf16[2560,3072]{1,0:T(8,128)(2,1)}, bf16[2560,3072]{1,0:T(8,128)(2,1)S(1)}, u32[]{:S(2)}) %copy-start) | copy-done | bytes 15728664
  53.6 4.3 %collective-permute-start.14 = (bf16[8,2560]{1,0:T(8,128)(2,1)S(1)}, bf16[8,2560]{1,0:T(8,128)(2,1)S(1)}, u32[]{:S(2)}, u32[]{:S(2)}) collective-permute-start(bf16[8,2560]{1,0:T(8,128)(2,1)S(1)} %get-tuple-element.39), channel_id=1, source_target_pairs={{0,4},{1,5},{2,6},{3,7},{4,0},{5,1},{6,2},{7,3},{8,12},{9,13},{10,... | collective-permute-start | bytes 122888 | tf_op jit(solution)/shard_map/ppermute | solution.py:47
  58.5 3.8 %collective-permute-start.21 = (bf16[8,2560]{1,0:T(8,128)(2,1)S(1)}, bf16[8,2560]{1,0:T(8,128)(2,1)S(1)}, u32[]{:S(2)}, u32[]{:S(2)}) collective-permute-start(bf16[8,2560]{1,0:T(8,128)(2,1)S(1)} %get-tuple-element.40), channel_id=1, source_target_pairs={{0,4},{1,5},{2,6},{3,7},{4,0},{5,1},{6,2},{7,3},{8,12},{9,13},{10,... | collective-permute-start | bytes 122888 | tf_op jit(solution)/shard_map/ppermute | solution.py:47
  62.4 1.6 %collective-permute-done.15 = bf16[8,2560]{1,0:T(8,128)(2,1)S(1)} collective-permute-done((bf16[8,2560]{1,0:T(8,128)(2,1)S(1)}, bf16[8,2560]{1,0:T(8,128)(2,1)S(1)}, u32[]{:S(2)}, u32[]{:S(2)}) %collective-permute-start.15) | collective-permute-done | bytes 40992 | tf_op jit(solution)/shard_map/ppermute | solution.py:47
  64.0 1.6 %collective-permute-start.16 = (bf16[4,8,2560]{2,1,0:T(8,128)(2,1)S(1)}, bf16[4,8,2560]{2,1,0:T(8,128)(2,1)S(1)}, u32[]{:S(2)}, u32[]{:S(2)}) collective-permute-start(bf16[4,8,2560]{2,1,0:T(8,128)(2,1)S(1)} %pad_maximum_fusion), channel_id=1, source_target_pairs={{0,1},{1,0},{2,3},{3,2},{4,5},{5,4},{6,7},{7,6},{8,9},{9,8},{10,11... | collective-permute-start | bytes 491528 | tf_op jit(solution)/shard_map/ppermute | solution.py:405
  66.2 1.3 %collective-permute-start.18 = (bf16[4,8,2560]{2,1,0:T(8,128)(2,1)S(1)}, bf16[4,8,2560]{2,1,0:T(8,128)(2,1)S(1)}, u32[]{:S(2)}, u32[]{:S(2)}) collective-permute-start(bf16[4,8,2560]{2,1,0:T(8,128)(2,1)S(1)} %pad_maximum_fusion), channel_id=1, source_target_pairs={{0,17},{1,16},{2,19},{3,18},{4,21},{5,20},{6,23},{7,22},{8,25},{9,... | collective-permute-start | bytes 491528 | tf_op jit(solution)/shard_map/ppermute | solution.py:405
  68.1 1.6 %collective-permute-start.23 = (bf16[4,8,2560]{2,1,0:T(8,128)(2,1)S(1)}, bf16[4,8,2560]{2,1,0:T(8,128)(2,1)S(1)}, u32[]{:S(2)}, u32[]{:S(2)}) collective-permute-start(bf16[4,8,2560]{2,1,0:T(8,128)(2,1)S(1)} %pad_maximum_fusion.1), channel_id=1, source_target_pairs={{0,1},{1,0},{2,3},{3,2},{4,5},{5,4},{6,7},{7,6},{8,9},{9,8},{10,11... | collective-permute-start | bytes 491528 | tf_op jit(solution)/shard_map/ppermute | solution.py:405
  69.7 0.9 collective-permute-start.24
  71.2 1.5 %collective-permute-start.25 = (bf16[4,8,2560]{2,1,0:T(8,128)(2,1)S(1)}, bf16[4,8,2560]{2,1,0:T(8,128)(2,1)S(1)}, u32[]{:S(2)}, u32[]{:S(2)}) collective-permute-start(bf16[4,8,2560]{2,1,0:T(8,128)(2,1)S(1)} %pad_maximum_fusion.1), channel_id=1, source_target_pairs={{0,17},{1,16},{2,19},{3,18},{4,21},{5,20},{6,23},{7,22},{8,25},{9,... | collective-permute-start | bytes 491528 | tf_op jit(solution)/shard_map/ppermute | solution.py:405
  72.7 2.4 %collective-permute-done.17 = bf16[4,8,2560]{2,1,0:T(8,128)(2,1)S(1)} collective-permute-done((bf16[4,8,2560]{2,1,0:T(8,128)(2,1)S(1)}, bf16[4,8,2560]{2,1,0:T(8,128)(2,1)S(1)}, u32[]{:S(2)}, u32[]{:S(2)}) %collective-permute-start.17) | collective-permute-done | bytes 163872 | tf_op jit(solution)/shard_map/ppermute | solution.py:405
  75.2 0.9 collective-permute-done.23
  76.2 2.4 %collective-permute-done.24 = bf16[4,8,2560]{2,1,0:T(8,128)(2,1)S(1)} collective-permute-done((bf16[4,8,2560]{2,1,0:T(8,128)(2,1)S(1)}, bf16[4,8,2560]{2,1,0:T(8,128)(2,1)S(1)}, u32[]{:S(2)}, u32[]{:S(2)}) %collective-permute-start.24) | collective-permute-done | bytes 163872 | tf_op jit(solution)/shard_map/ppermute | solution.py:405
  79.0 5.6 %copy-done.3 = bf16[2560,3072]{1,0:T(8,128)(2,1)S(1)} copy-done((bf16[2560,3072]{1,0:T(8,128)(2,1)S(1)}, bf16[2560,3072]{1,0:T(8,128)(2,1)}, u32[]{:S(2)}) %copy-start.3) | copy-done | bytes 15728664
  84.6 5.1 %logits_first.1.sum_in_ref = f32[256,3072]{1,0:T(8,128)S(1)} custom-call(bf16[128,2560]{1,0:T(8,128)(2,1)S(1)} %bitcast.25, bf16[128,2560]{1,0:T(8,128)(2,1)S(1)} %collective-permute-done.19.right_ref, bf16[2560,3072]{1,0:T(8,128)(2,1)S(1)} %copy-done.3), custom_call_target="tpu_custom_call" | custom-call | flops 4026531840 | tf_op jit(solution)/shard_map/logits_first/pallas_call | solution.py:415
  89.8 6.2 %logits.1 = f32[8,256]{1,0:T(8,128)S(1)} custom-call(f32[256,3072]{1,0:T(8,128)S(1)} %logits_first.1.sum_in_ref, bf16[128,2560]{1,0:T(8,128)(2,1)S(1)} %bitcast.23, bf16[128,2560]{1,0:T(8,128)(2,1)S(1)} %collective-permute-done.26.right_ref, s32[32,8,1]{2,1,0:T(8,128)S(1)} %reshape.45.target_ref, bf16[2560,3072]{1,0:T(8,128)(2,1)S(1)} %copy-done.1), custom_call_target="tpu_custom_call" | custom-call | flops 4026531840 | tf_op jit(solution)/shard_map/logits/pallas_call | solution.py:425
  96.9 3.2 %all-to-all-start = ((f32[32,1,24]{2,1,0:T(1,128)}), f32[32,1,24]{2,1,0:T(1,128)S(1)}, u32[]{:S(2)}, u32[]{:S(2)}) async-start(f32[32,1,24]{2,1,0:T(1,128)} %copy.20), calls=%async_computation | async-start | bytes 32768 | tf_op jit(solution)/shard_map/all_to_all | solution.py:439
  100.2 7.0 %all-to-all-done = f32[32,1,24]{2,1,0:T(1,128)S(1)} async-done(((f32[32,1,24]{2,1,0:T(1,128)}), f32[32,1,24]{2,1,0:T(1,128)S(1)}, u32[]{:S(2)}, u32[]{:S(2)}) %all-to-all-start) | async-done | bytes 3104 | tf_op jit(solution)/shard_map/all_to_all | solution.py:439
  (76 shorter events, 7.1 us)
Async XLA Ops:
  0.0 7.3 %collective-permute-start = (bf16[64,512]{1,0:T(8,128)(2,1)}, bf16[64,512]{1,0:T(8,128)(2,1)S(1)}, u32[]{:S(2)}, u32[]{:S(2)}) collective-permute-start(bf16[64,512]{1,0:T(8,128)(2,1)} %refs_0_.1), channel_id=1, source_target_pairs={{0,8},{8,0},{16,24},{24,16},{1,9},{9,1},{17,25},{25,17},{2,10},{10... | collective-permute-start | bytes 196616 | tf_op jit(solution)/shard_map/ppermute | solution.py:47
  0.5 6.8 %collective-permute-start.1 = (bf16[64,512]{1,0:T(8,128)(2,1)}, bf16[64,512]{1,0:T(8,128)(2,1)S(1)}, u32[]{:S(2)}, u32[]{:S(2)}) collective-permute-start(bf16[64,512]{1,0:T(8,128)(2,1)} %refs_0_.1), channel_id=1, source_target_pairs={{0,16},{8,24},{16,0},{24,8},{1,17},{9,25},{17,1},{25,9},{2,18},{10... | collective-permute-start | bytes 196616 | tf_op jit(solution)/shard_map/ppermute | solution.py:47
  3.0 4.3 %collective-permute-start.2 = (bf16[64,512]{1,0:T(8,128)(2,1)}, bf16[64,512]{1,0:T(8,128)(2,1)S(1)}, u32[]{:S(2)}, u32[]{:S(2)}) collective-permute-start(bf16[64,512]{1,0:T(8,128)(2,1)} %refs_0_.1), channel_id=1, source_target_pairs={{0,24},{8,16},{16,8},{24,0},{1,25},{9,17},{17,9},{25,1},{2,26},{10... | collective-permute-start | bytes 196616 | tf_op jit(solution)/shard_map/ppermute | solution.py:47
  8.2 2.1 %collective-permute-start.3 = (bf16[64,640]{1,0:T(8,128)(2,1)S(1)}, bf16[64,640]{1,0:T(8,128)(2,1)S(1)}, u32[]{:S(2)}, u32[]{:S(2)}) collective-permute-start(bf16[64,640]{1,0:T(8,128)(2,1)S(1)} %get-tuple-element.27), channel_id=1, source_target_pairs={{0,8},{8,0},{16,24},{24,16},{1,9},{9,1},{17,25},{25,17},{2,10},{10... | collective-permute-start | bytes 245768 | tf_op jit(solution)/shard_map/ppermute | solution.py:47
  8.3 4.8 %collective-permute-start.4 = (bf16[64,640]{1,0:T(8,128)(2,1)S(1)}, bf16[64,640]{1,0:T(8,128)(2,1)S(1)}, u32[]{:S(2)}, u32[]{:S(2)}) collective-permute-start(bf16[64,640]{1,0:T(8,128)(2,1)S(1)} %get-tuple-element.28), channel_id=1, source_target_pairs={{0,16},{8,24},{16,0},{24,8},{1,17},{9,25},{17,1},{25,9},{2,18},{10... | collective-permute-start | bytes 245768 | tf_op jit(solution)/shard_map/ppermute | solution.py:47
  10.2 4.6 %collective-permute-start.5 = (bf16[64,640]{1,0:T(8,128)(2,1)S(1)}, bf16[64,640]{1,0:T(8,128)(2,1)S(1)}, u32[]{:S(2)}, u32[]{:S(2)}) collective-permute-start(bf16[64,640]{1,0:T(8,128)(2,1)S(1)} %get-tuple-element.29), channel_id=1, source_target_pairs={{0,24},{8,16},{16,8},{24,0},{1,25},{9,17},{17,9},{25,1},{2,26},{10... | collective-permute-start | bytes 245768 | tf_op jit(solution)/shard_map/ppermute | solution.py:47
  19.3 7.5 %collective-permute-start.6 = (bf16[8,5120]{1,0:T(8,128)(2,1)S(1)}, bf16[8,5120]{1,0:T(8,128)(2,1)S(1)}, u32[]{:S(2)}, u32[]{:S(2)}) collective-permute-start(bf16[8,5120]{1,0:T(8,128)(2,1)S(1)} %get-tuple-element.31.gate_ref), channel_id=1, source_target_pairs={{0,1},{1,0},{2,3},{3,2},{4,5},{5,4},{6,7},{7,6},{8,9},{9,8},{10,11... | collective-permute-start | bytes 245768 | tf_op jit(solution)/shard_map/ppermute | solution.py:47
  21.0 9.5 %collective-permute-start.7 = (bf16[8,5120]{1,0:T(8,128)(2,1)S(1)}, bf16[8,5120]{1,0:T(8,128)(2,1)S(1)}, u32[]{:S(2)}, u32[]{:S(2)}) collective-permute-start(bf16[8,5120]{1,0:T(8,128)(2,1)S(1)} %get-tuple-element.33), channel_id=1, source_target_pairs={{0,2},{1,3},{2,0},{3,1},{4,6},{5,7},{6,4},{7,5},{8,10},{9,11},{10,... | collective-permute-start | bytes 245768 | tf_op jit(solution)/shard_map/ppermute | solution.py:47
  22.6 25.6 %collective-permute-start.8 = (bf16[8,5120]{1,0:T(8,128)(2,1)S(1)}, bf16[8,5120]{1,0:T(8,128)(2,1)S(1)}, u32[]{:S(2)}, u32[]{:S(2)}) collective-permute-start(bf16[8,5120]{1,0:T(8,128)(2,1)S(1)} %get-tuple-element.34), channel_id=1, source_target_pairs={{0,3},{1,2},{2,1},{3,0},{4,7},{5,6},{6,5},{7,4},{8,11},{9,10},{10,... | collective-permute-start | bytes 245768 | tf_op jit(solution)/shard_map/ppermute | solution.py:47
  22.8 25.3 %collective-permute-start.9 = (bf16[8,5120]{1,0:T(8,128)(2,1)S(1)}, bf16[8,5120]{1,0:T(8,128)(2,1)S(1)}, u32[]{:S(2)}, u32[]{:S(2)}) collective-permute-start(bf16[8,5120]{1,0:T(8,128)(2,1)S(1)} %get-tuple-element.35), channel_id=1, source_target_pairs={{0,4},{1,5},{2,6},{3,7},{4,0},{5,1},{6,2},{7,3},{8,12},{9,13},{10,... | collective-permute-start | bytes 245768 | tf_op jit(solution)/shard_map/ppermute | solution.py:47
  25.6 22.6 %collective-permute-start.10 = (bf16[8,5120]{1,0:T(8,128)(2,1)S(1)}, bf16[8,5120]{1,0:T(8,128)(2,1)S(1)}, u32[]{:S(2)}, u32[]{:S(2)}) collective-permute-start(bf16[8,5120]{1,0:T(8,128)(2,1)S(1)} %get-tuple-element.36), channel_id=1, source_target_pairs={{0,5},{1,4},{2,7},{3,6},{4,1},{5,0},{6,3},{7,2},{8,13},{9,12},{10,... | collective-permute-start | bytes 245768 | tf_op jit(solution)/shard_map/ppermute | solution.py:47
  26.8 21.3 %collective-permute-start.11 = (bf16[8,5120]{1,0:T(8,128)(2,1)S(1)}, bf16[8,5120]{1,0:T(8,128)(2,1)S(1)}, u32[]{:S(2)}, u32[]{:S(2)}) collective-permute-start(bf16[8,5120]{1,0:T(8,128)(2,1)S(1)} %get-tuple-element.37), channel_id=1, source_target_pairs={{0,6},{1,7},{2,4},{3,5},{4,2},{5,3},{6,0},{7,1},{8,14},{9,15},{10,... | collective-permute-start | bytes 245768 | tf_op jit(solution)/shard_map/ppermute | solution.py:47
  30.5 17.7 %collective-permute-start.12 = (bf16[8,5120]{1,0:T(8,128)(2,1)S(1)}, bf16[8,5120]{1,0:T(8,128)(2,1)S(1)}, u32[]{:S(2)}, u32[]{:S(2)}) collective-permute-start(bf16[8,5120]{1,0:T(8,128)(2,1)S(1)} %get-tuple-element.38), channel_id=1, source_target_pairs={{0,7},{1,6},{2,5},{3,4},{4,3},{5,2},{6,1},{7,0},{8,15},{9,14},{10,... | collective-permute-start | bytes 245768 | tf_op jit(solution)/shard_map/ppermute | solution.py:47
  36.8 11.4 %copy-start.2 = (bf16[2560,3072]{1,0:T(8,128)(2,1)}, bf16[2560,3072]{1,0:T(8,128)(2,1)S(1)}, u32[]{:S(2)}) copy-start(bf16[2560,3072]{1,0:T(8,128)(2,1)S(1)} %fetch.2.refs_0_.weight_ref) | copy-start | bytes 47185924
  36.8 11.4 %copy-start.4 = (bf16[64,5120]{1,0:T(8,128)(2,1)S(1)}, bf16[64,5120]{1,0:T(8,128)(2,1)}, u32[]{:S(2)}) copy-start(bf16[64,5120]{1,0:T(8,128)(2,1)} %param.19) | copy-start | bytes 1966084
  48.2 30.6 %copy-start.8 = (s32[256]{0:T(256)S(1)}, s32[256]{0:T(256)}, u32[]{:S(2)}) copy-start(s32[256]{0:T(256)} %param.23) | copy-start | bytes 3076
  53.6 8.7 %collective-permute-start.13 = (bf16[8,2560]{1,0:T(8,128)(2,1)S(1)}, bf16[8,2560]{1,0:T(8,128)(2,1)S(1)}, u32[]{:S(2)}, u32[]{:S(2)}) collective-permute-start(bf16[8,2560]{1,0:T(8,128)(2,1)S(1)} %get-tuple-element.39), channel_id=1, source_target_pairs={{0,2},{1,3},{2,0},{3,1},{4,6},{5,7},{6,4},{7,5},{8,10},{9,11},{10,... | collective-permute-start | bytes 122888 | tf_op jit(solution)/shard_map/ppermute | solution.py:47
  53.6 8.8 %collective-permute-start.14 = (bf16[8,2560]{1,0:T(8,128)(2,1)S(1)}, bf16[8,2560]{1,0:T(8,128)(2,1)S(1)}, u32[]{:S(2)}, u32[]{:S(2)}) collective-permute-start(bf16[8,2560]{1,0:T(8,128)(2,1)S(1)} %get-tuple-element.39), channel_id=1, source_target_pairs={{0,4},{1,5},{2,6},{3,7},{4,0},{5,1},{6,2},{7,3},{8,12},{9,13},{10,... | collective-permute-start | bytes 122888 | tf_op jit(solution)/shard_map/ppermute | solution.py:47
  57.9 6.1 %collective-permute-start.15 = (bf16[8,2560]{1,0:T(8,128)(2,1)S(1)}, bf16[8,2560]{1,0:T(8,128)(2,1)S(1)}, u32[]{:S(2)}, u32[]{:S(2)}) collective-permute-start(bf16[8,2560]{1,0:T(8,128)(2,1)S(1)} %get-tuple-element.39), channel_id=1, source_target_pairs={{0,6},{1,7},{2,4},{3,5},{4,2},{5,3},{6,0},{7,1},{8,14},{9,15},{10,... | collective-permute-start | bytes 122888 | tf_op jit(solution)/shard_map/ppermute | solution.py:47
  58.0 8.2 %collective-permute-start.20 = (bf16[8,2560]{1,0:T(8,128)(2,1)S(1)}, bf16[8,2560]{1,0:T(8,128)(2,1)S(1)}, u32[]{:S(2)}, u32[]{:S(2)}) collective-permute-start(bf16[8,2560]{1,0:T(8,128)(2,1)S(1)} %get-tuple-element.40), channel_id=1, source_target_pairs={{0,2},{1,3},{2,0},{3,1},{4,6},{5,7},{6,4},{7,5},{8,10},{9,11},{10,... | collective-permute-start | bytes 122888 | tf_op jit(solution)/shard_map/ppermute | solution.py:47
  58.5 9.1 %collective-permute-start.21 = (bf16[8,2560]{1,0:T(8,128)(2,1)S(1)}, bf16[8,2560]{1,0:T(8,128)(2,1)S(1)}, u32[]{:S(2)}, u32[]{:S(2)}) collective-permute-start(bf16[8,2560]{1,0:T(8,128)(2,1)S(1)} %get-tuple-element.40), channel_id=1, source_target_pairs={{0,4},{1,5},{2,6},{3,7},{4,0},{5,1},{6,2},{7,3},{8,12},{9,13},{10,... | collective-permute-start | bytes 122888 | tf_op jit(solution)/shard_map/ppermute | solution.py:47
  62.3 5.8 %collective-permute-start.22 = (bf16[8,2560]{1,0:T(8,128)(2,1)S(1)}, bf16[8,2560]{1,0:T(8,128)(2,1)S(1)}, u32[]{:S(2)}, u32[]{:S(2)}) collective-permute-start(bf16[8,2560]{1,0:T(8,128)(2,1)S(1)} %get-tuple-element.40), channel_id=1, source_target_pairs={{0,6},{1,7},{2,4},{3,5},{4,2},{5,3},{6,0},{7,1},{8,14},{9,15},{10,... | collective-permute-start | bytes 122888 | tf_op jit(solution)/shard_map/ppermute | solution.py:47
  64.0 7.2 %collective-permute-start.16 = (bf16[4,8,2560]{2,1,0:T(8,128)(2,1)S(1)}, bf16[4,8,2560]{2,1,0:T(8,128)(2,1)S(1)}, u32[]{:S(2)}, u32[]{:S(2)}) collective-permute-start(bf16[4,8,2560]{2,1,0:T(8,128)(2,1)S(1)} %pad_maximum_fusion), channel_id=1, source_target_pairs={{0,1},{1,0},{2,3},{3,2},{4,5},{5,4},{6,7},{7,6},{8,9},{9,8},{10,11... | collective-permute-start | bytes 491528 | tf_op jit(solution)/shard_map/ppermute | solution.py:405
  65.6 9.5 %collective-permute-start.17 = (bf16[4,8,2560]{2,1,0:T(8,128)(2,1)S(1)}, bf16[4,8,2560]{2,1,0:T(8,128)(2,1)S(1)}, u32[]{:S(2)}, u32[]{:S(2)}) collective-permute-start(bf16[4,8,2560]{2,1,0:T(8,128)(2,1)S(1)} %pad_maximum_fusion), channel_id=1, source_target_pairs={{0,16},{1,17},{2,18},{3,19},{4,20},{5,21},{6,22},{7,23},{8,24},{9,... | collective-permute-start | bytes 491528 | tf_op jit(solution)/shard_map/ppermute | solution.py:405
  66.2 8.9 %collective-permute-start.18 = (bf16[4,8,2560]{2,1,0:T(8,128)(2,1)S(1)}, bf16[4,8,2560]{2,1,0:T(8,128)(2,1)S(1)}, u32[]{:S(2)}, u32[]{:S(2)}) collective-permute-start(bf16[4,8,2560]{2,1,0:T(8,128)(2,1)S(1)} %pad_maximum_fusion), channel_id=1, source_target_pairs={{0,17},{1,16},{2,19},{3,18},{4,21},{5,20},{6,23},{7,22},{8,25},{9,... | collective-permute-start | bytes 491528 | tf_op jit(solution)/shard_map/ppermute | solution.py:405
  68.1 8.0 %collective-permute-start.23 = (bf16[4,8,2560]{2,1,0:T(8,128)(2,1)S(1)}, bf16[4,8,2560]{2,1,0:T(8,128)(2,1)S(1)}, u32[]{:S(2)}, u32[]{:S(2)}) collective-permute-start(bf16[4,8,2560]{2,1,0:T(8,128)(2,1)S(1)} %pad_maximum_fusion.1), channel_id=1, source_target_pairs={{0,1},{1,0},{2,3},{3,2},{4,5},{5,4},{6,7},{7,6},{8,9},{9,8},{10,11... | collective-permute-start | bytes 491528 | tf_op jit(solution)/shard_map/ppermute | solution.py:405
  69.7 8.9 %collective-permute-start.24 = (bf16[4,8,2560]{2,1,0:T(8,128)(2,1)S(1)}, bf16[4,8,2560]{2,1,0:T(8,128)(2,1)S(1)}, u32[]{:S(2)}, u32[]{:S(2)}) collective-permute-start(bf16[4,8,2560]{2,1,0:T(8,128)(2,1)S(1)} %pad_maximum_fusion.1), channel_id=1, source_target_pairs={{0,16},{1,17},{2,18},{3,19},{4,20},{5,21},{6,22},{7,23},{8,24},{9,... | collective-permute-start | bytes 491528 | tf_op jit(solution)/shard_map/ppermute | solution.py:405
  71.2 7.4 %collective-permute-start.25 = (bf16[4,8,2560]{2,1,0:T(8,128)(2,1)S(1)}, bf16[4,8,2560]{2,1,0:T(8,128)(2,1)S(1)}, u32[]{:S(2)}, u32[]{:S(2)}) collective-permute-start(bf16[4,8,2560]{2,1,0:T(8,128)(2,1)S(1)} %pad_maximum_fusion.1), channel_id=1, source_target_pairs={{0,17},{1,16},{2,19},{3,18},{4,21},{5,20},{6,23},{7,22},{8,25},{9,... | collective-permute-start | bytes 491528 | tf_op jit(solution)/shard_map/ppermute | solution.py:405
  75.2 3.8 %collective-permute-start.19 = (bf16[128,2560]{1,0:T(8,128)(2,1)S(1)}, bf16[128,2560]{1,0:T(8,128)(2,1)S(1)}, u32[]{:S(2)}, u32[]{:S(2)}) collective-permute-start(bf16[128,2560]{1,0:T(8,128)(2,1)S(1)} %bitcast.24), channel_id=1, source_target_pairs={{0,8},{8,0},{16,24},{24,16},{1,9},{9,1},{17,25},{25,17},{2,10},{10... | collective-permute-start | bytes 1966088 | tf_op jit(solution)/shard_map/ppermute | solution.py:47
  78.7 11.1 %collective-permute-start.26 = (bf16[128,2560]{1,0:T(8,128)(2,1)S(1)}, bf16[128,2560]{1,0:T(8,128)(2,1)S(1)}, u32[]{:S(2)}, u32[]{:S(2)}) collective-permute-start(bf16[128,2560]{1,0:T(8,128)(2,1)S(1)} %bitcast.22), channel_id=1, source_target_pairs={{0,8},{8,0},{16,24},{24,16},{1,9},{9,1},{17,25},{25,17},{2,10},{10... | collective-permute-start | bytes 1966088 | tf_op jit(solution)/shard_map/ppermute | solution.py:47
  84.6 15.5 %copy-start.7 = (s32[2]{0:T(128)S(1)}, s32[2]{0:T(128)}, u32[]{:S(2)}) copy-start(s32[2]{0:T(128)} %lengths_ref.1) | copy-start | bytes 28
  96.9 10.3 %all-to-all-start = ((f32[32,1,24]{2,1,0:T(1,128)}), f32[32,1,24]{2,1,0:T(1,128)S(1)}, u32[]{:S(2)}, u32[]{:S(2)}) async-start(f32[32,1,24]{2,1,0:T(1,128)} %copy.20), calls=%async_computation | async-start | bytes 32768 | tf_op jit(solution)/shard_map/all_to_all | solution.py:439
  (5 other events, 23.3 us)

commit v3 on v2

--- a/solution.py
+++ b/solution.py
@@ -84,15 +84,20 @@
     return packed.astype(BF16)
 
 
-def own_kernel(heads, seq, lengths_ref, *refs):
-    sources, (own_ref, pre_ref), kept, scratch, sems = refs[:6], refs[6:8], refs[8:11], refs[11:14], refs[14]
-    places = scratch + kept
+def load_kernel(count, *refs):
+    sems = refs[2 * count]
     copies = [
-        pltpu.make_async_copy(src, dst, sems.at[i]) for i, (src, dst) in enumerate(zip(sources, places))
+        pltpu.make_async_copy(refs[i], refs[count + i], sems.at[i]) for i in range(count)
     ]
     for copy in copies:
         copy.start()
-    q_ref, rk_ref, rv_ref, k_ref, v_ref, _ = places
+    for copy in copies:
+        copy.wait()
+
+
+def own_kernel(
+    heads, seq, lengths_ref, q_ref, rk_ref, rv_ref, k_ref, v_ref, gate_ref, early_ref, own_ref, pre_ref
+):
     rows = q_ref.shape[0]
     row = lax.broadcasted_iota(jnp.int32, (rows, rows), 0)
     col = lax.broadcasted_iota(jnp.int32, (rows, rows), 1)
@@ -101,8 +106,6 @@
         live = jnp.where(col // seq == r, lengths_ref[r], live)
     allowed = (row // seq == col // seq) & (col <= row) & (col % seq < live)
     parts = [slice(h * HEAD_DIM, (h + 1) * HEAD_DIM) for h in range(heads)]
-    for copy in copies[:5]:
-        copy.wait()
     found = attend(
         [(q_ref[:, p], rk_ref[:, p], rv_ref[:, p], allowed) for p in parts]
         + [(q_ref[:, p], k_ref[:, p], v_ref[:, p], None) for p in parts]
@@ -110,15 +113,12 @@
     for h, p in enumerate(parts):
         own_ref[:, p] = found[h][0]
         pre_ref[:, p] = found[heads + h][0]
-    logs = [log for _, log in found[:heads]]
-    pre_logs = [log for _, log in found[heads:]]
     lane = lax.broadcasted_iota(jnp.int32, (rows, 128), 1)
-    for ref, values in ((own_ref, logs), (pre_ref, pre_logs)):
+    for ref, values in ((own_ref, found[:heads]), (pre_ref, found[heads:])):
         packed = jnp.zeros((rows, 128), F32)
         for h in range(heads):
-            packed = jnp.where(lane == h, values[h], packed)
+            packed = jnp.where(lane == h, values[h][1], packed)
         ref[:, heads * HEAD_DIM :] = packed
-    copies[5].wait()
 
 
 def prefix_kernel(heads, count, *refs):
@@ -138,7 +138,7 @@
         out_refs[i][:, heads * HEAD_DIM :] = pack_logs([log[rung] for _, log in found], rows)
 
 
-def project_kernel(heads, seq, share, wide, group_size, key_rows, prompt_ref, *refs):
+def project_kernel(heads, seq, share, wide, group_size, key_rows, gate_ref, prompt_ref, *refs):
     count = group_size - 1
     own_ref, pre_ref = refs[:2]
     got_refs = refs[2 : 2 + count]
@@ -200,19 +200,36 @@
         copy.wait()
 
 
-def norm_kernel(residual_ref, gain_ref, *refs):
-    terms, out_refs = refs[2:-2], refs[-2:]
+def column_kernel(count, *refs):
+    terms, out_refs = refs[:count], refs[-2:]
+    width = out_refs[0].shape[2]
+    for i, ref in enumerate(terms):
+        for half, out_ref in enumerate(out_refs):
+            out_ref[i] = ref[:, half * width : (half + 1) * width]
+
+
+def norm_kernel(first_gate_ref, second_gate_ref, residual_ref, gain_ref, *refs):
+    terms, out_ref = refs[:-1], refs[-1]
     hidden = residual_ref[lax.axis_index("tensor")].astype(F32)
     for ref in terms:
         hidden = hidden + ref[...].astype(F32)
     squares = jnp.mean(hidden * hidden, axis=-1, keepdims=True)
     normed = (hidden * lax.rsqrt(squares + 1e-06) * gain_ref[...].astype(F32)).astype(BF16)
-    width = normed.shape[1] // 2
-    for i, ref in enumerate(out_refs):
-        ref[...] = normed[:, i * width : (i + 1) * width]
-
-
-def first_kernel(narrow, left_ref, right_ref, weight_ref, out_ref, x_ref):
+    out_ref[...] = normed
+
+
+def quarter_dots(x_ref, weight_refs, columns):
+    depth = weight_refs[0].shape[0]
+    return functools.reduce(
+        jnp.add,
+        [
+            jnp.dot(x_ref[:, i * depth : (i + 1) * depth], ref[:, columns], preferred_element_type=F32)
+            for i, ref in enumerate(weight_refs)
+        ],
+    )
+
+
+def first_kernel(narrow, left_ref, right_ref, weight_ref, next_ref, out_ref, x_ref):
     half = left_ref.shape[0]
     x_ref[:half] = left_ref[...]
     x_ref[half:] = right_ref[...]
@@ -220,9 +237,7 @@
     @pl.loop(0, weight_ref.shape[1] // narrow)
     def _(n):
         columns = pl.ds(n * narrow if narrow % 128 else pl.multiple_of(n * narrow, 128), narrow)
-        out_ref[:, columns] = jnp.dot(
-            x_ref[...], weight_ref[:, columns], preferred_element_type=F32
-        )
+        out_ref[:, columns] = quarter_dots(x_ref, (weight_ref, next_ref), columns)
 
 
 def logits_kernel(
@@ -234,13 +249,13 @@
     right_ref,
     target_ref,
     weight_ref,
+    next_ref,
     out_ref,
     x_ref,
     peak_ref,
     sum_ref,
     pick_ref,
     wanted_ref,
-    stats_ref,
 ):
     half = left_ref.shape[0]
     rows = 2 * half
@@ -261,9 +276,7 @@
     @pl.loop(0, weight_ref.shape[1] // narrow)
     def _(n):
         columns = pl.ds(n * narrow if narrow % 128 else pl.multiple_of(n * narrow, 128), narrow)
-        logits = sum_in_ref[:, columns] + jnp.dot(
-            x_ref[...], weight_ref[:, columns], preferred_element_type=F32
-        )
+        logits = sum_in_ref[:, columns] + quarter_dots(x_ref, (weight_ref, next_ref), columns)
         parts = [logits[:, c : c + 128] for c in range(0, narrow, 128)]
         if narrow % 128:
             spare = jnp.full((rows, 128 - narrow % 128), NEG, F32)
@@ -285,11 +298,27 @@
     peak = jnp.max(higher, axis=1, keepdims=True)
     sums = jnp.sum(sum_ref[...] * jnp.exp(higher - peak), axis=1, keepdims=True)
     pick = jnp.sum(pick_ref[...], axis=1, keepdims=True)
-    place = lax.broadcasted_iota(jnp.int32, (rows, 128), 1)
-    three = jnp.where(place == 0, peak, jnp.where(place == 1, sums, pick))
+    row = lax.broadcasted_iota(jnp.int32, (rows, 128), 0)
+    lane = lax.broadcasted_iota(jnp.int32, (rows, 128), 1)
+    three = jnp.where(lane // share == 0, peak, jnp.where(lane // share == 1, sums, pick))
+    three = jnp.where((row - lane) % share == 0, three, 0.0)
     for i, place in enumerate(places):
-        stats_ref[place] = three[i * share : (i + 1) * share]
-    out_ref[...] = jnp.transpose(stats_ref[...].reshape(rows, 128))[:8]
+        out_ref[place] = jnp.sum(three[i * share : (i + 1) * share], axis=0, keepdims=True)
+
+
+def final_kernel(seq, share, lengths_ref, stats_ref, out_ref):
+    stats = stats_ref[...].reshape(stats_ref.shape[0], 128)
+    count = lengths_ref.shape[0]
+    peak = jnp.max(stats, axis=0, keepdims=True)
+    sums = pltpu.roll(stats, 128 - share, 1)
+    picks = pltpu.roll(stats, 128 - 2 * share, 1)
+    total = jnp.sum(sums * jnp.exp(stats - peak), axis=0, keepdims=True)
+    values = jnp.sum(picks, axis=0, keepdims=True) - peak - jnp.log(total)
+    token = lax.broadcasted_iota(jnp.int32, (1, 128), 1) + lax.axis_index("tensor") * share
+    live = jnp.zeros((1, 128), jnp.int32)
+    for r in range(count):
+        live = jnp.where(token // seq == r, lengths_ref[r], live)
+    out_ref[...] = jnp.where(token % seq < live, values, 0.0)
 
 
 def local(
@@ -316,25 +345,23 @@
     share = rows // tensor_size
     depth = out_weight.shape[1]
     vocab = lm_weight.shape[1]
-    tensor_index = lax.axis_index("tensor")
     i32 = jnp.int32
 
     distances = list(range(1, group_size))
     queries = [swap(resp_query, "group", d, group_size) for d in distances]
+    wanted = targets.reshape(-1, share, 1)
     inputs = (resp_query, resp_key, resp_value, prompt_keys, prompt_values, out_weight)
-    own, prefix, keys, values, weight = pl.pallas_call(
-        functools.partial(own_kernel, heads, seq),
-        out_shape=[jax.ShapeDtypeStruct((rows, span + 128), F32)] * 2
-        + [pltpu.VMEM(x.shape, x.dtype) for x in inputs[3:]],
-        in_specs=[smem()] + [anywhere()] * 6,
-        out_specs=[vmem()] * 5,
-        scratch_shapes=[pltpu.VMEM(x.shape, x.dtype) for x in inputs[:3]]
-        + [pltpu.SemaphoreType.DMA((6,))],
-        compiler_params=params(6),
-        cost_estimate=cost(moved=14 * MIB),
-        name="own_attention",
-    )(lengths, *map(stored, inputs))
-    keys, values, weight = held(keys), held(values), held(weight)
+    loaded = pl.pallas_call(
+        functools.partial(load_kernel, len(inputs)),
+        out_shape=[pltpu.VMEM(x.shape, x.dtype) for x in inputs],
+        in_specs=[anywhere()] * len(inputs),
+        out_specs=[vmem()] * len(inputs),
+        scratch_shapes=[pltpu.SemaphoreType.DMA((len(inputs),))],
+        compiler_params=params(1),
+        cost_estimate=cost(moved=7 * MIB),
+        name="load",
+    )(*map(stored, inputs))
+    query, own_keys, own_values, keys, values, weight = map(held, loaded)
     answers = pl.pallas_call(
         functools.partial(prefix_kernel, heads, len(distances)),
         out_shape=[jax.ShapeDtypeStruct((rows, span + 128), BF16)] * len(distances),
@@ -344,6 +371,31 @@
         name="prefix_attention",
     )(*map(held, queries), keys, values)
     got = [swap(x, "group", d, group_size) for x, d in zip(answers, distances)]
+    own, prefix = pl.pallas_call(
+        functools.partial(own_kernel, heads, seq),
+        out_shape=[jax.ShapeDtypeStruct((rows, span + 128), F32)] * 2,
+        in_specs=[smem()] + [vmem()] * 5 + [anywhere()] * 2,
+        out_specs=[vmem()] * 2,
+        compiler_params=params(6),
+        cost_estimate=cost(moved=8 * MIB),
+        name="own_attention",
+    )(stored(lengths), query, own_keys, own_values, keys, values, answers[0], wanted)
+
+    def fetch(quarter, gate):
+        return held(
+            pl.pallas_call(
+                functools.partial(fetch_kernel, quarter * (depth // 4), 4),
+                out_shape=pltpu.VMEM((depth // 4, vocab), BF16),
+                in_specs=[anywhere()] * 2,
+                out_specs=vmem(),
+                scratch_shapes=[pltpu.SemaphoreType.DMA((4,))],
+                compiler_params=params(1),
+                cost_estimate=cost(moved=depth // 4 * vocab * 2),
+                name="fetch",
+            )(stored(lm_weight), gate)
+        )
+
+    quarters = [fetch(0, answers[0])]
 
     wide = 640 if depth % 640 == 0 else depth
     shares = pl.pallas_call(
@@ -351,7 +403,7 @@
         out_shape=[
             jax.ShapeDtypeStruct((share, depth), BF16 if d else F32) for d in range(tensor_size)
         ],
-        in_specs=[smem()] + [vmem()] * (3 + len(distances)),
+        in_specs=[anywhere(), smem()] + [vmem()] * (3 + len(distances)),
         out_specs=[vmem()] * tensor_size,
         scratch_shapes=[
             pltpu.VMEM((rows, span), BF16),
@@ -359,33 +411,20 @@
         ],
         compiler_params=params(6),
         name="project",
-    )(prompt_of, *map(held, (own, prefix, *got)), weight)
-
-    weights = []
-    for i in range(2):
-        weights.append(
-            pl.pallas_call(
-                functools.partial(fetch_kernel, i * (depth // 2), 4),
-                out_shape=pltpu.VMEM((depth // 2, vocab), BF16),
-                in_specs=[anywhere()] * 2,
-                out_specs=vmem(),
-                scratch_shapes=[pltpu.SemaphoreType.DMA((4,))],
-                compiler_params=params(1),
-                cost_estimate=cost(moved=depth // 2 * vocab * 2),
-                name="fetch",
-            )(stored(lm_weight), shares[1])
-        )
+    )(quarters[0], stored(prompt_of), *map(held, (own, prefix, *got)), weight)
+    quarters += [fetch(1, shares[1]), fetch(2, shares[1])]
 
     got = [swap(x, "tensor", d, tensor_size) for d, x in enumerate(shares) if d]
     normed = pl.pallas_call(
         norm_kernel,
-        out_shape=[jax.ShapeDtypeStruct((share, depth // 2), BF16)] * 2,
-        in_specs=[vmem()] * 2 + [anywhere()] * 2 + [vmem()] * tensor_size,
-        out_specs=[vmem()] * 2,
+        out_shape=jax.ShapeDtypeStruct((share, depth), BF16),
+        in_specs=[anywhere()] * 2 + [vmem()] * (2 + tensor_size),
+        out_specs=vmem(),
         compiler_params=params(4),
         name="norm",
     )(
-        *map(held, (residual.reshape(tensor_size, share, depth), norm_gain[None], *weights)),
+        *quarters[1:],
+        *map(held, (residual.reshape(tensor_size, share, depth), norm_gain[None])),
         *map(held, (shares[0], *got)),
     )
 
@@ -398,9 +437,18 @@
         (g, x): [(a * tensor_size + b, (a ^ g) * tensor_size + (b ^ x)) for a, b in mesh_ids]
         for g, x in here
     }
+    column = [normed] + [swap(normed, "tensor", d, tensor_size) for d in far]
+    quarters.append(fetch(3, normed))
+    columns = pl.pallas_call(
+        functools.partial(column_kernel, len(column)),
+        out_shape=[jax.ShapeDtypeStruct((len(column), share, depth // 2), BF16)] * 2,
+        in_specs=[vmem()] * len(column) + [anywhere()],
+        out_specs=[vmem()] * 2,
+        compiler_params=params(2),
+        name="column",
+    )(*map(held, column), quarters[3])
     halves = []
-    for part in normed:
-        tokens = jnp.stack([part] + [swap(part, "tensor", d, tensor_size) for d in far])
+    for tokens in columns:
         pieces = [
             lax.ppermute(tokens, ("group", "tensor"), routes[place]) if any(place) else tokens
             for place in here
@@ -409,44 +457,42 @@
         halves.append((tokens, swap(tokens, "group", 1, group_size)))
     spots = [(g + c, t + x) for c in (0, 1) for g, x in here for t in order]
     total_rows = 2 * tokens.shape[0]
-    narrow = 512 if vocab % 512 == 0 else vocab
+    narrow = 1024 if vocab % 1024 == 0 else vocab
     limit = 10 if total_rows <= 256 else 24
     work = 2 * total_rows * (depth // 2) * vocab
     first = pl.pallas_call(
         functools.partial(first_kernel, narrow),
         out_shape=pltpu.VMEM((total_rows, vocab), F32),
-        in_specs=[vmem()] * 3,
+        in_specs=[vmem()] * 4,
         out_specs=vmem(),
         scratch_shapes=[pltpu.VMEM((total_rows, depth // 2), BF16)],
         compiler_params=params(limit),
         cost_estimate=cost(flops=work),
         name="logits_first",
-    )(*map(held, (*halves[0], weights[0])))
+    )(*map(held, (*halves[0], *quarters[:2])))
     stats = pl.pallas_call(
         functools.partial(logits_kernel, narrow, spots, tensor_size),
-        out_shape=jax.ShapeDtypeStruct((8, total_rows), F32),
-        in_specs=[vmem()] * 5,
+        out_shape=jax.ShapeDtypeStruct((len(spots), 1, 128), F32),
+        in_specs=[vmem()] * 6,
         out_specs=vmem(),
         scratch_shapes=[pltpu.VMEM((total_rows, depth // 2), BF16)]
         + [pltpu.VMEM((total_rows, 128), F32)] * 3
-        + [pltpu.VMEM((total_rows, 1), i32), pltpu.VMEM((len(spots), share, 128), F32)],
+        + [pltpu.VMEM((total_rows, 1), i32)],
         compiler_params=params(limit),
         cost_estimate=cost(flops=work),
         name="logits",
-    )(*map(held, (first, *halves[1])), targets.reshape(-1, share, 1), held(weights[1]))
-
-    blocks = stats[:3].reshape(3, -1, share).transpose(1, 0, 2).reshape(-1, 3 * share)
-    blocks = lax.all_to_all(blocks, ("group", "tensor"), 0, 0, tiled=True)
-    peaks, sums, picks = blocks[:, :share], blocks[:, share : 2 * share], blocks[:, 2 * share :]
-    peak = jnp.max(peaks, axis=0)
-    total = jnp.sum(sums * jnp.exp(peaks - peak[None]), axis=0)
-    values = jnp.sum(picks, axis=0) - peak - jnp.log(total)
-    local_rows = tensor_index * share + jnp.arange(share, dtype=i32)
-    slots = jnp.arange(prompt_of.shape[0], dtype=i32)
-    local_len = jnp.sum(
-        jnp.where((local_rows // seq)[:, None] == slots[None, :], lengths[None, :], 0), axis=1
-    )
-    return jnp.where(local_rows % seq < local_len, values, 0.0)
+    )(*map(held, (first, *halves[1])), wanted, *map(held, quarters[2:]))
+
+    stats = lax.all_to_all(stats, ("group", "tensor"), 0, 0, tiled=True)
+    values = pl.pallas_call(
+        functools.partial(final_kernel, seq, share),
+        out_shape=jax.ShapeDtypeStruct((1, 128), F32),
+        in_specs=[smem(), vmem()],
+        out_specs=vmem(),
+        compiler_params=params(4),
+        name="final",
+    )(stored(lengths), stats)
+    return values[0, :share]
 
 
 def solution(mesh):

time: 108 us -> 93.7 us (0.87)
  blocking collectives: 0 us -> 11.8 us
  local copies, waits for them, and re-layouts: 14 us -> 3.76 us
  waiting for transfers between devices: 20 us -> 13.5 us
  starting transfers between devices: 36.1 us -> 30 us
  Pallas kernels: 36.6 us -> 34 us
    all_to_all x0 -> x1, blocking collectives: none -> 11.8 us  [local(): stats = lax.all_to_all(stats, ('group', 'tensor'), 0, 0, tiled=True)]
    unnamed x29 -> x10, local copies, waits for them, and re-layouts: 12.2 us -> 2.35 us
    all_to_all x1 -> x0, waiting for transfers between devices: 7.01 us -> none  [local(): blocks = lax.all_to_all(blocks, ('group', 'tensor'), 0, 0, tiled=True)]
    all_to_all x1 -> x0, starting transfers between devices: 3.18 us -> none  [local(): blocks = lax.all_to_all(blocks, ('group', 'tensor'), 0, 0, tiled=True)]
    ppermute x6, waiting for transfers between devices: 6.26 us -> 9.37 us  [local(): lax.ppermute(tokens, ('group', 'tensor'), routes[place])]
    ppermute x21 -> x18, waiting for transfers between devices: 6.75 us -> 4.1 us  [swap(): return lax.ppermute(x, axis, [(i, i ^ distance) for i in range(size)])]
    ppermute x21 -> x18, starting transfers between devices: 25.3 us -> 23.2 us  [swap(): return lax.ppermute(x, axis, [(i, i ^ distance) for i in range(size)])]
    pallas_call x1, Pallas kernels: 3.51 us -> 1.4 us  [local(): pl.pallas_call(functools.partial(own_kernel, heads, seq), out_shape=[jax....]
  transfers between devices with their start and end apart: 28 -> 24, of which waited for: 9 -> 7; matrix products, arithmetic and copies ran while one was open for 1% -> 1% of each run, Pallas kernels for 24% -> 24%
where the time goes in v3:
time: 93.7 us; the launch traced here: 93.5 us
  Pallas kernels  34 us (36%)
  starting transfers between devices  30 us (32%)
  waiting for transfers between devices  13.5 us (14%)
  blocking collectives  11.8 us (13%)
  local copies, waits for them, and re-layouts  3.76 us (4%)
    ppermute x18, starting transfers between devices, swap(): return lax.ppermute(x, axis, [(i, i ^ distance) for i in range(size)])  23.2 us
    pallas_call x4, Pallas kernels, fetch(): pl.pallas_call(functools.partial(fetch_kernel, quarter * (depth // 4), 4)...  13.6 us
    all_to_all x1, blocking collectives, local(): stats = lax.all_to_all(stats, ('group', 'tensor'), 0, 0, tiled=True)  11.8 us
    ppermute x6, waiting for transfers between devices, local(): lax.ppermute(tokens, ('group', 'tensor'), routes[place])  9.37 us
    ppermute x6, starting transfers between devices, local(): lax.ppermute(tokens, ('group', 'tensor'), routes[place])  6.83 us
    pallas_call x1, Pallas kernels, local(): pl.pallas_call(functools.partial(logits_kernel, narrow, spots, tensor_siz...  5.61 us
    pallas_call x1, Pallas kernels, local(): pl.pallas_call(functools.partial(first_kernel, narrow), out_shape=pltpu.V...  4.64 us
    ppermute x18, waiting for transfers between devices, swap(): return lax.ppermute(x, axis, [(i, i ^ distance) for i in range(size)])  4.1 us
  transfers between devices with their start and end apart: 24, of which 7 were waited for; matrix products, arithmetic and copies ran while one was open for 1% of the time, Pallas kernels for 24%

profile of v3, /device:TPU:0, one launch (start us, length us, event | category | flops | bytes accessed | tf_op | source)
XLA Modules:
  0.0 93.5 jit_solution(13502457345488867067)
XLA Ops:
  0.5 2.5 %collective-permute-start.1 = (bf16[64,512]{1,0:T(8,128)(2,1)}, bf16[64,512]{1,0:T(8,128)(2,1)S(1)}, u32[]{:S(2)}, u32[]{:S(2)}) collective-permute-start(bf16[64,512]{1,0:T(8,128)(2,1)} %refs_0_.1), channel_id=1, source_target_pairs={{0,16},{8,24},{16,0},{24,8},{1,17},{9,25},{17,1},{25,9},{2,18},{10... | collective-permute-start | bytes 196616 | tf_op jit(solution)/shard_map/ppermute | solution.py:47
  3.1 3.0 %load.1 = (bf16[64,512]{1,0:T(8,128)(2,1)S(1)}, bf16[64,512]{1,0:T(8,128)(2,1)S(1)}, bf16[64,512]{1,0:T(8,128)(2,1)S(1)}, bf16[512,512]{1,0:T(8,128)(2,1)S(1)}, ...) custom-call(bf16[64,512]{1,0:T(8,128)(2,1)} %refs_0_.1, bf16[64,512]{1,0:T(8,128)(2,1)} %refs_1_.1, ...), custom_call_target="tpu_custom_call" | custom-call | bytes 7340032 | tf_op jit(solution)/shard_map/load/pallas_call | solution.py:354
  6.1 2.3 %copy-done = bf16[512,5120]{1,0:T(8,128)(2,1)} copy-done((bf16[512,5120]{1,0:T(8,128)(2,1)}, bf16[512,5120]{1,0:T(8,128)(2,1)S(1)}, u32[]{:S(2)}) %copy-start) | copy-done | bytes 5242904
  9.5 1.9 %collective-permute-start.4 = (bf16[64,640]{1,0:T(8,128)(2,1)S(1)}, bf16[64,640]{1,0:T(8,128)(2,1)S(1)}, u32[]{:S(2)}, u32[]{:S(2)}) collective-permute-start(bf16[64,640]{1,0:T(8,128)(2,1)S(1)} %get-tuple-element.34), channel_id=1, source_target_pairs={{0,16},{8,24},{16,0},{24,8},{1,17},{9,25},{17,1},{25,9},{2,18},{10... | collective-permute-start | bytes 245768 | tf_op jit(solution)/shard_map/ppermute | solution.py:47
  11.4 0.9 reshape.16.early_ref.target_ref
  12.3 3.5 %fetch.4.gate_ref.weight_ref = bf16[1280,3072]{1,0:T(8,128)(2,1)S(1)} custom-call(bf16[5120,3072]{1,0:T(8,128)(2,1)} %source_ref.7, bf16[64,640]{1,0:T(8,128)(2,1)S(1)} %get-tuple-element.28.gate_ref), custom_call_target="tpu_custom_call" | custom-call | bytes 7864320 | tf_op jit(solution)/shard_map/fetch/pallas_call | solution.py:386
  15.8 1.4 %own_attention.1 = (f32[64,640]{1,0:T(8,128)S(1)}, f32[64,640]{1,0:T(8,128)S(1)}) custom-call(s32[2]{0:T(128)} %lengths_ref.3, bf16[64,512]{1,0:T(8,128)(2,1)S(1)} %get-tuple-element.29.q_ref, bf16[64,512]{1,0:T(8,128)(2,1)S(1)} %get-tuple-element.30.rk_ref, bf16[64,512]{1,0:T(8,128)(2,1)S(1)} %get-tuple-element.31.rv_ref, ...), custom_call_target="tpu_custom_call" | custom-call | bytes 8388608 | tf_op jit(solution)/shard_map/own_attention/pallas_call | solution.py:374
  17.3 3.9 %project.1 = (f32[8,5120]{1,0:T(8,128)S(1)}, bf16[8,5120]{1,0:T(8,128)(2,1)S(1)}, bf16[8,5120]{1,0:T(8,128)(2,1)S(1)}, bf16[8,5120]{1,0:T(8,128)(2,1)S(1)}, bf16...) custom-call(bf16[1280,3072]{1,0:T(8,128)(2,1)S(1)} %fetch.4.gate_ref, ...), custom_call_target="tpu_custom_call" | custom-call | tf_op jit(solution)/shard_map/project/pallas_call | solution.py:401
  21.2 1.6 %collective-permute-start.6 = (bf16[8,5120]{1,0:T(8,128)(2,1)S(1)}, bf16[8,5120]{1,0:T(8,128)(2,1)S(1)}, u32[]{:S(2)}, u32[]{:S(2)}) collective-permute-start(bf16[8,5120]{1,0:T(8,128)(2,1)S(1)} %get-tuple-element.37.gate_ref), channel_id=1, source_target_pairs={{0,1},{1,0},{2,3},{3,2},{4,5},{5,4},{6,7},{7,6},{8,9},{9,8},{10,11... | collective-permute-start | bytes 245768 | tf_op jit(solution)/shard_map/ppermute | solution.py:47
  22.8 1.6 %collective-permute-start.7 = (bf16[8,5120]{1,0:T(8,128)(2,1)S(1)}, bf16[8,5120]{1,0:T(8,128)(2,1)S(1)}, u32[]{:S(2)}, u32[]{:S(2)}) collective-permute-start(bf16[8,5120]{1,0:T(8,128)(2,1)S(1)} %get-tuple-element.39), channel_id=1, source_target_pairs={{0,2},{1,3},{2,0},{3,1},{4,6},{5,7},{6,4},{7,5},{8,10},{9,11},{10,... | collective-permute-start | bytes 245768 | tf_op jit(solution)/shard_map/ppermute | solution.py:47
  24.7 2.6 %collective-permute-start.9 = (bf16[8,5120]{1,0:T(8,128)(2,1)S(1)}, bf16[8,5120]{1,0:T(8,128)(2,1)S(1)}, u32[]{:S(2)}, u32[]{:S(2)}) collective-permute-start(bf16[8,5120]{1,0:T(8,128)(2,1)S(1)} %get-tuple-element.41), channel_id=1, source_target_pairs={{0,4},{1,5},{2,6},{3,7},{4,0},{5,1},{6,2},{7,3},{8,12},{9,13},{10,... | collective-permute-start | bytes 245768 | tf_op jit(solution)/shard_map/ppermute | solution.py:47
  27.4 1.3 %collective-permute-start.10 = (bf16[8,5120]{1,0:T(8,128)(2,1)S(1)}, bf16[8,5120]{1,0:T(8,128)(2,1)S(1)}, u32[]{:S(2)}, u32[]{:S(2)}) collective-permute-start(bf16[8,5120]{1,0:T(8,128)(2,1)S(1)} %get-tuple-element.42), channel_id=1, source_target_pairs={{0,5},{1,4},{2,7},{3,6},{4,1},{5,0},{6,3},{7,2},{8,13},{9,12},{10,... | collective-permute-start | bytes 245768 | tf_op jit(solution)/shard_map/ppermute | solution.py:47
  28.6 3.6 %collective-permute-start.11 = (bf16[8,5120]{1,0:T(8,128)(2,1)S(1)}, bf16[8,5120]{1,0:T(8,128)(2,1)S(1)}, u32[]{:S(2)}, u32[]{:S(2)}) collective-permute-start(bf16[8,5120]{1,0:T(8,128)(2,1)S(1)} %get-tuple-element.43), channel_id=1, source_target_pairs={{0,6},{1,7},{2,4},{3,5},{4,2},{5,3},{6,0},{7,1},{8,14},{9,15},{10,... | collective-permute-start | bytes 245768 | tf_op jit(solution)/shard_map/ppermute | solution.py:47
  32.4 3.3 %fetch.5.first_gate_ref.next_ref = bf16[1280,3072]{1,0:T(8,128)(2,1)S(1)} custom-call(bf16[5120,3072]{1,0:T(8,128)(2,1)} %source_ref.7, bf16[8,5120]{1,0:T(8,128)(2,1)S(1)} %get-tuple-element.37.gate_ref), custom_call_target="tpu_custom_call" | custom-call | bytes 7864320 | tf_op jit(solution)/shard_map/fetch/pallas_call | solution.py:386
  35.8 3.4 %fetch.6.second_gate_ref.weight_ref = bf16[1280,3072]{1,0:T(8,128)(2,1)S(1)} custom-call(bf16[5120,3072]{1,0:T(8,128)(2,1)} %source_ref.7, bf16[8,5120]{1,0:T(8,128)(2,1)S(1)} %get-tuple-element.37.gate_ref), custom_call_target="tpu_custom_call" | custom-call | bytes 7864320 | tf_op jit(solution)/shard_map/fetch/pallas_call | solution.py:386
  39.2 1.3 %collective-permute-done.10.refs_5_ = bf16[8,5120]{1,0:T(8,128)(2,1)S(1)} collective-permute-done((bf16[8,5120]{1,0:T(8,128)(2,1)S(1)}, bf16[8,5120]{1,0:T(8,128)(2,1)S(1)}, u32[]{:S(2)}, u32[]{:S(2)}) %collective-permute-start.10) | collective-permute-done | bytes 81952 | tf_op jit(solution)/shard_map/ppermute | solution.py:47
  40.8 3.4 %collective-permute-start.13 = (bf16[8,5120]{1,0:T(8,128)(2,1)S(1)}, bf16[8,5120]{1,0:T(8,128)(2,1)S(1)}, u32[]{:S(2)}, u32[]{:S(2)}) collective-permute-start(bf16[8,5120]{1,0:T(8,128)(2,1)S(1)} %norm.1.gate_ref.refs_0_), channel_id=1, source_target_pairs={{0,2},{1,3},{2,0},{3,1},{4,6},{5,7},{6,4},{7,5},{8,10},{9,11},{10,... | collective-permute-start | bytes 245768 | tf_op jit(solution)/shard_map/ppermute | solution.py:47
  44.2 1.8 %collective-permute-start.14 = (bf16[8,5120]{1,0:T(8,128)(2,1)S(1)}, bf16[8,5120]{1,0:T(8,128)(2,1)S(1)}, u32[]{:S(2)}, u32[]{:S(2)}) collective-permute-start(bf16[8,5120]{1,0:T(8,128)(2,1)S(1)} %norm.1.gate_ref.refs_0_), channel_id=1, source_target_pairs={{0,4},{1,5},{2,6},{3,7},{4,0},{5,1},{6,2},{7,3},{8,12},{9,13},{10,... | collective-permute-start | bytes 245768 | tf_op jit(solution)/shard_map/ppermute | solution.py:47
  46.0 1.4 %collective-permute-start.15 = (bf16[8,5120]{1,0:T(8,128)(2,1)S(1)}, bf16[8,5120]{1,0:T(8,128)(2,1)S(1)}, u32[]{:S(2)}, u32[]{:S(2)}) collective-permute-start(bf16[8,5120]{1,0:T(8,128)(2,1)S(1)} %norm.1.gate_ref.refs_0_), channel_id=1, source_target_pairs={{0,6},{1,7},{2,4},{3,5},{4,2},{5,3},{6,0},{7,1},{8,14},{9,15},{10,... | collective-permute-start | bytes 245768 | tf_op jit(solution)/shard_map/ppermute | solution.py:47
  47.4 3.3 %fetch.7.refs_4_.next_ref = bf16[1280,3072]{1,0:T(8,128)(2,1)S(1)} custom-call(bf16[5120,3072]{1,0:T(8,128)(2,1)} %source_ref.7, bf16[8,5120]{1,0:T(8,128)(2,1)S(1)} %norm.1.gate_ref.refs_0_), custom_call_target="tpu_custom_call" | custom-call | bytes 7864320 | tf_op jit(solution)/shard_map/fetch/pallas_call | solution.py:386
  50.8 2.7 %collective-permute-done.14.refs_2_ = bf16[8,5120]{1,0:T(8,128)(2,1)S(1)} collective-permute-done((bf16[8,5120]{1,0:T(8,128)(2,1)S(1)}, bf16[8,5120]{1,0:T(8,128)(2,1)S(1)}, u32[]{:S(2)}, u32[]{:S(2)}) %collective-permute-start.14) | collective-permute-done | bytes 81952 | tf_op jit(solution)/shard_map/ppermute | solution.py:47
  53.5 2.0 %collective-permute-start.18 = (bf16[4,8,2560]{2,1,0:T(8,128)(2,1)S(1)}, bf16[4,8,2560]{2,1,0:T(8,128)(2,1)S(1)}, u32[]{:S(2)}, u32[]{:S(2)}) collective-permute-start(bf16[4,8,2560]{2,1,0:T(8,128)(2,1)S(1)} %get-tuple-element.45), channel_id=1, source_target_pairs={{0,17},{1,16},{2,19},{3,18},{4,21},{5,20},{6,23},{7,22},{8,25},{9,... | collective-permute-start | bytes 491528 | tf_op jit(solution)/shard_map/ppermute | solution.py:453
  56.0 1.1 %collective-permute-start.16 = (bf16[4,8,2560]{2,1,0:T(8,128)(2,1)S(1)}, bf16[4,8,2560]{2,1,0:T(8,128)(2,1)S(1)}, u32[]{:S(2)}, u32[]{:S(2)}) collective-permute-start(bf16[4,8,2560]{2,1,0:T(8,128)(2,1)S(1)} %get-tuple-element.45), channel_id=1, source_target_pairs={{0,1},{1,0},{2,3},{3,2},{4,5},{5,4},{6,7},{7,6},{8,9},{9,8},{10,11... | collective-permute-start | bytes 491528 | tf_op jit(solution)/shard_map/ppermute | solution.py:453
  57.1 1.9 %collective-permute-start.22 = (bf16[4,8,2560]{2,1,0:T(8,128)(2,1)S(1)}, bf16[4,8,2560]{2,1,0:T(8,128)(2,1)S(1)}, u32[]{:S(2)}, u32[]{:S(2)}) collective-permute-start(bf16[4,8,2560]{2,1,0:T(8,128)(2,1)S(1)} %get-tuple-element.46), channel_id=1, source_target_pairs={{0,17},{1,16},{2,19},{3,18},{4,21},{5,20},{6,23},{7,22},{8,25},{9,... | collective-permute-start | bytes 491528 | tf_op jit(solution)/shard_map/ppermute | solution.py:453
  59.5 2.2 %collective-permute-done.18 = bf16[4,8,2560]{2,1,0:T(8,128)(2,1)S(1)} collective-permute-done((bf16[4,8,2560]{2,1,0:T(8,128)(2,1)S(1)}, bf16[4,8,2560]{2,1,0:T(8,128)(2,1)S(1)}, u32[]{:S(2)}, u32[]{:S(2)}) %collective-permute-start.18) | collective-permute-done | bytes 163872 | tf_op jit(solution)/shard_map/ppermute | solution.py:453
  61.7 0.9 collective-permute-start.20
  62.6 3.0 %collective-permute-done.17 = bf16[4,8,2560]{2,1,0:T(8,128)(2,1)S(1)} collective-permute-done((bf16[4,8,2560]{2,1,0:T(8,128)(2,1)S(1)}, bf16[4,8,2560]{2,1,0:T(8,128)(2,1)S(1)}, u32[]{:S(2)}, u32[]{:S(2)}) %collective-permute-start.17) | collective-permute-done | bytes 163872 | tf_op jit(solution)/shard_map/ppermute | solution.py:453
  65.8 2.4 %collective-permute-done.22 = bf16[4,8,2560]{2,1,0:T(8,128)(2,1)S(1)} collective-permute-done((bf16[4,8,2560]{2,1,0:T(8,128)(2,1)S(1)}, bf16[4,8,2560]{2,1,0:T(8,128)(2,1)S(1)}, u32[]{:S(2)}, u32[]{:S(2)}) %collective-permute-start.22) | collective-permute-done | bytes 163872 | tf_op jit(solution)/shard_map/ppermute | solution.py:453
  68.9 1.0 %collective-permute-done.20 = bf16[4,8,2560]{2,1,0:T(8,128)(2,1)S(1)} collective-permute-done((bf16[4,8,2560]{2,1,0:T(8,128)(2,1)S(1)}, bf16[4,8,2560]{2,1,0:T(8,128)(2,1)S(1)}, u32[]{:S(2)}, u32[]{:S(2)}) %collective-permute-start.20) | collective-permute-done | bytes 163872 | tf_op jit(solution)/shard_map/ppermute | solution.py:453
  70.1 4.6 %logits_first.1.sum_in_ref = f32[256,3072]{1,0:T(8,128)S(1)} custom-call(bf16[128,2560]{1,0:T(8,128)(2,1)S(1)} %maximum_bitcast_fusion.left_ref, bf16[128,2560]{1,0:T(8,128)(2,1)S(1)} %collective-permute-done.19.right_ref, bf16[1280,3072]{1,0:T(8,128)(2,1)S(1)} %fetch.4.gate_ref.weight_ref, bf16[1280,3072]{1,0:T(8,128)(2,1)S(1)} %fetch.5.first_gate_ref.next_ref), custom_call_target="tpu_custom_call" | custom-call | flops 4026531840 | tf_op jit(solution)/shard_map/logits_first/pallas_call | solution.py:463
  74.7 5.6 %logits.1 = f32[32,1,128]{2,1,0:T(1,128)S(1)} custom-call(f32[256,3072]{1,0:T(8,128)S(1)} %logits_first.1.sum_in_ref, bf16[128,2560]{1,0:T(8,128)(2,1)S(1)} %maximum_bitcast_fusion.1.left_ref, bf16[128,2560]{1,0:T(8,128)(2,1)S(1)} %collective-permute-done.23.right_ref, s32[32,8,1]{2,1,0:T(8,128)S(1)} %reshape.16.early_ref.target_ref, ...), custom_call_target="tpu_custom_call" | custom-call | flops 4026531840 | tf_op jit(solution)/shard_map/logits/pallas_call | solution.py:473
  80.4 11.8 %all_to_all.5.stats_ref = f32[32,1,128]{2,1,0:T(1,128)S(1)} all-to-all(f32[32,1,128]{2,1,0:T(1,128)S(1)} %logits.1), channel_id=1, replica_groups=mesh['group'=4,'tensor'=8] {'group','tensor'}, dimensions={0} | all-to-all | bytes 32768 | tf_op jit(solution)/shard_map/all_to_all | solution.py:486
  (46 shorter events, 5.7 us)
Async XLA Ops:
  0.0 8.4 %collective-permute-start = (bf16[64,512]{1,0:T(8,128)(2,1)}, bf16[64,512]{1,0:T(8,128)(2,1)S(1)}, u32[]{:S(2)}, u32[]{:S(2)}) collective-permute-start(bf16[64,512]{1,0:T(8,128)(2,1)} %refs_0_.1), channel_id=1, source_target_pairs={{0,8},{8,0},{16,24},{24,16},{1,9},{9,1},{17,25},{25,17},{2,10},{10... | collective-permute-start | bytes 196616 | tf_op jit(solution)/shard_map/ppermute | solution.py:47
  0.5 8.0 %collective-permute-start.1 = (bf16[64,512]{1,0:T(8,128)(2,1)}, bf16[64,512]{1,0:T(8,128)(2,1)S(1)}, u32[]{:S(2)}, u32[]{:S(2)}) collective-permute-start(bf16[64,512]{1,0:T(8,128)(2,1)} %refs_0_.1), channel_id=1, source_target_pairs={{0,16},{8,24},{16,0},{24,8},{1,17},{9,25},{17,1},{25,9},{2,18},{10... | collective-permute-start | bytes 196616 | tf_op jit(solution)/shard_map/ppermute | solution.py:47
  3.0 5.5 %collective-permute-start.2 = (bf16[64,512]{1,0:T(8,128)(2,1)}, bf16[64,512]{1,0:T(8,128)(2,1)S(1)}, u32[]{:S(2)}, u32[]{:S(2)}) collective-permute-start(bf16[64,512]{1,0:T(8,128)(2,1)} %refs_0_.1), channel_id=1, source_target_pairs={{0,24},{8,16},{16,8},{24,0},{1,25},{9,17},{17,9},{25,1},{2,26},{10... | collective-permute-start | bytes 196616 | tf_op jit(solution)/shard_map/ppermute | solution.py:47
  6.1 2.3 %copy-start = (bf16[512,5120]{1,0:T(8,128)(2,1)}, bf16[512,5120]{1,0:T(8,128)(2,1)S(1)}, u32[]{:S(2)}) copy-start(bf16[512,5120]{1,0:T(8,128)(2,1)S(1)} %get-tuple-element.36.refs_5_) | copy-start | bytes 15728644
  8.4 8.8 %slice-start = ((s8[5242880]{0:T(1024)(128)(4,1)}), s8[1048576]{0:T(1024)(128)(4,1)S(1)}, s32[]{:S(2)}) async-start(s8[5242880]{0:T(1024)(128)(4,1)} %bitcast.7), calls=%async_computation.1 | async-start | bytes 2097152
  9.3 7.9 %collective-permute-start.3 = (bf16[64,640]{1,0:T(8,128)(2,1)S(1)}, bf16[64,640]{1,0:T(8,128)(2,1)S(1)}, u32[]{:S(2)}, u32[]{:S(2)}) collective-permute-start(bf16[64,640]{1,0:T(8,128)(2,1)S(1)} %get-tuple-element.28.gate_ref), channel_id=1, source_target_pairs={{0,8},{8,0},{16,24},{24,16},{1,9},{9,1},{17,25},{25,17},{2,10},{10... | collective-permute-start | bytes 245768 | tf_op jit(solution)/shard_map/ppermute | solution.py:47
  9.5 7.7 %collective-permute-start.4 = (bf16[64,640]{1,0:T(8,128)(2,1)S(1)}, bf16[64,640]{1,0:T(8,128)(2,1)S(1)}, u32[]{:S(2)}, u32[]{:S(2)}) collective-permute-start(bf16[64,640]{1,0:T(8,128)(2,1)S(1)} %get-tuple-element.34), channel_id=1, source_target_pairs={{0,16},{8,24},{16,0},{24,8},{1,17},{9,25},{17,1},{25,9},{2,18},{10... | collective-permute-start | bytes 245768 | tf_op jit(solution)/shard_map/ppermute | solution.py:47
  11.4 5.8 %collective-permute-start.5 = (bf16[64,640]{1,0:T(8,128)(2,1)S(1)}, bf16[64,640]{1,0:T(8,128)(2,1)S(1)}, u32[]{:S(2)}, u32[]{:S(2)}) collective-permute-start(bf16[64,640]{1,0:T(8,128)(2,1)S(1)} %get-tuple-element.35), channel_id=1, source_target_pairs={{0,24},{8,16},{16,8},{24,0},{1,25},{9,17},{17,9},{25,1},{2,26},{10... | collective-permute-start | bytes 245768 | tf_op jit(solution)/shard_map/ppermute | solution.py:47
  12.3 5.0 %slice-start.1 = ((s8[5242880]{0:T(1024)(128)(4,1)}), s8[4194304]{0:T(1024)(128)(4,1)S(1)}, s32[]{:S(2)}) async-start(s8[5242880]{0:T(1024)(128)(4,1)} %bitcast.7), calls=%async_computation.2 | async-start | bytes 8388608
  15.8 16.6 %copy-start.2 = (bf16[5120]{0:T(1024)(128)(2,1)S(1)}, bf16[5120]{0:T(1024)(128)(2,1)}, u32[]{:S(2)}) copy-start(bf16[5120]{0:T(1024)(128)(2,1)} %param.21) | copy-start | bytes 30724
  21.2 7.5 %collective-permute-start.6 = (bf16[8,5120]{1,0:T(8,128)(2,1)S(1)}, bf16[8,5120]{1,0:T(8,128)(2,1)S(1)}, u32[]{:S(2)}, u32[]{:S(2)}) collective-permute-start(bf16[8,5120]{1,0:T(8,128)(2,1)S(1)} %get-tuple-element.37.gate_ref), channel_id=1, source_target_pairs={{0,1},{1,0},{2,3},{3,2},{4,5},{5,4},{6,7},{7,6},{8,9},{9,8},{10,11... | collective-permute-start | bytes 245768 | tf_op jit(solution)/shard_map/ppermute | solution.py:47
  22.8 9.5 %collective-permute-start.7 = (bf16[8,5120]{1,0:T(8,128)(2,1)S(1)}, bf16[8,5120]{1,0:T(8,128)(2,1)S(1)}, u32[]{:S(2)}, u32[]{:S(2)}) collective-permute-start(bf16[8,5120]{1,0:T(8,128)(2,1)S(1)} %get-tuple-element.39), channel_id=1, source_target_pairs={{0,2},{1,3},{2,0},{3,1},{4,6},{5,7},{6,4},{7,5},{8,10},{9,11},{10,... | collective-permute-start | bytes 245768 | tf_op jit(solution)/shard_map/ppermute | solution.py:47
  24.4 14.8 %collective-permute-start.8 = (bf16[8,5120]{1,0:T(8,128)(2,1)S(1)}, bf16[8,5120]{1,0:T(8,128)(2,1)S(1)}, u32[]{:S(2)}, u32[]{:S(2)}) collective-permute-start(bf16[8,5120]{1,0:T(8,128)(2,1)S(1)} %get-tuple-element.40), channel_id=1, source_target_pairs={{0,3},{1,2},{2,1},{3,0},{4,7},{5,6},{6,5},{7,4},{8,11},{9,10},{10,... | collective-permute-start | bytes 245768 | tf_op jit(solution)/shard_map/ppermute | solution.py:47
  24.7 14.5 %collective-permute-start.9 = (bf16[8,5120]{1,0:T(8,128)(2,1)S(1)}, bf16[8,5120]{1,0:T(8,128)(2,1)S(1)}, u32[]{:S(2)}, u32[]{:S(2)}) collective-permute-start(bf16[8,5120]{1,0:T(8,128)(2,1)S(1)} %get-tuple-element.41), channel_id=1, source_target_pairs={{0,4},{1,5},{2,6},{3,7},{4,0},{5,1},{6,2},{7,3},{8,12},{9,13},{10,... | collective-permute-start | bytes 245768 | tf_op jit(solution)/shard_map/ppermute | solution.py:47
  27.4 13.2 %collective-permute-start.10 = (bf16[8,5120]{1,0:T(8,128)(2,1)S(1)}, bf16[8,5120]{1,0:T(8,128)(2,1)S(1)}, u32[]{:S(2)}, u32[]{:S(2)}) collective-permute-start(bf16[8,5120]{1,0:T(8,128)(2,1)S(1)} %get-tuple-element.42), channel_id=1, source_target_pairs={{0,5},{1,4},{2,7},{3,6},{4,1},{5,0},{6,3},{7,2},{8,13},{9,12},{10,... | collective-permute-start | bytes 245768 | tf_op jit(solution)/shard_map/ppermute | solution.py:47
  28.6 11.9 %collective-permute-start.11 = (bf16[8,5120]{1,0:T(8,128)(2,1)S(1)}, bf16[8,5120]{1,0:T(8,128)(2,1)S(1)}, u32[]{:S(2)}, u32[]{:S(2)}) collective-permute-start(bf16[8,5120]{1,0:T(8,128)(2,1)S(1)} %get-tuple-element.43), channel_id=1, source_target_pairs={{0,6},{1,7},{2,4},{3,5},{4,2},{5,3},{6,0},{7,1},{8,14},{9,15},{10,... | collective-permute-start | bytes 245768 | tf_op jit(solution)/shard_map/ppermute | solution.py:47
  32.3 8.2 %collective-permute-start.12 = (bf16[8,5120]{1,0:T(8,128)(2,1)S(1)}, bf16[8,5120]{1,0:T(8,128)(2,1)S(1)}, u32[]{:S(2)}, u32[]{:S(2)}) collective-permute-start(bf16[8,5120]{1,0:T(8,128)(2,1)S(1)} %get-tuple-element.44), channel_id=1, source_target_pairs={{0,7},{1,6},{2,5},{3,4},{4,3},{5,2},{6,1},{7,0},{8,15},{9,14},{10,... | collective-permute-start | bytes 245768 | tf_op jit(solution)/shard_map/ppermute | solution.py:47
  35.7 4.8 %copy-start.1 = (bf16[64,5120]{1,0:T(8,128)(2,1)S(1)}, bf16[64,5120]{1,0:T(8,128)(2,1)}, u32[]{:S(2)}) copy-start(bf16[64,5120]{1,0:T(8,128)(2,1)} %param.19) | copy-start | bytes 1966084
  40.8 10.0 %collective-permute-start.13 = (bf16[8,5120]{1,0:T(8,128)(2,1)S(1)}, bf16[8,5120]{1,0:T(8,128)(2,1)S(1)}, u32[]{:S(2)}, u32[]{:S(2)}) collective-permute-start(bf16[8,5120]{1,0:T(8,128)(2,1)S(1)} %norm.1.gate_ref.refs_0_), channel_id=1, source_target_pairs={{0,2},{1,3},{2,0},{3,1},{4,6},{5,7},{6,4},{7,5},{8,10},{9,11},{10,... | collective-permute-start | bytes 245768 | tf_op jit(solution)/shard_map/ppermute | solution.py:47
  44.2 9.3 %collective-permute-start.14 = (bf16[8,5120]{1,0:T(8,128)(2,1)S(1)}, bf16[8,5120]{1,0:T(8,128)(2,1)S(1)}, u32[]{:S(2)}, u32[]{:S(2)}) collective-permute-start(bf16[8,5120]{1,0:T(8,128)(2,1)S(1)} %norm.1.gate_ref.refs_0_), channel_id=1, source_target_pairs={{0,4},{1,5},{2,6},{3,7},{4,0},{5,1},{6,2},{7,3},{8,12},{9,13},{10,... | collective-permute-start | bytes 245768 | tf_op jit(solution)/shard_map/ppermute | solution.py:47
  46.0 7.5 %collective-permute-start.15 = (bf16[8,5120]{1,0:T(8,128)(2,1)S(1)}, bf16[8,5120]{1,0:T(8,128)(2,1)S(1)}, u32[]{:S(2)}, u32[]{:S(2)}) collective-permute-start(bf16[8,5120]{1,0:T(8,128)(2,1)S(1)} %norm.1.gate_ref.refs_0_), channel_id=1, source_target_pairs={{0,6},{1,7},{2,4},{3,5},{4,2},{5,3},{6,0},{7,1},{8,14},{9,15},{10,... | collective-permute-start | bytes 245768 | tf_op jit(solution)/shard_map/ppermute | solution.py:47
  53.5 8.2 %collective-permute-start.18 = (bf16[4,8,2560]{2,1,0:T(8,128)(2,1)S(1)}, bf16[4,8,2560]{2,1,0:T(8,128)(2,1)S(1)}, u32[]{:S(2)}, u32[]{:S(2)}) collective-permute-start(bf16[4,8,2560]{2,1,0:T(8,128)(2,1)S(1)} %get-tuple-element.45), channel_id=1, source_target_pairs={{0,17},{1,16},{2,19},{3,18},{4,21},{5,20},{6,23},{7,22},{8,25},{9,... | collective-permute-start | bytes 491528 | tf_op jit(solution)/shard_map/ppermute | solution.py:453
  55.5 10.2 %collective-permute-start.17 = (bf16[4,8,2560]{2,1,0:T(8,128)(2,1)S(1)}, bf16[4,8,2560]{2,1,0:T(8,128)(2,1)S(1)}, u32[]{:S(2)}, u32[]{:S(2)}) collective-permute-start(bf16[4,8,2560]{2,1,0:T(8,128)(2,1)S(1)} %get-tuple-element.45), channel_id=1, source_target_pairs={{0,16},{1,17},{2,18},{3,19},{4,20},{5,21},{6,22},{7,23},{8,24},{9,... | collective-permute-start | bytes 491528 | tf_op jit(solution)/shard_map/ppermute | solution.py:453
  56.0 9.7 %collective-permute-start.16 = (bf16[4,8,2560]{2,1,0:T(8,128)(2,1)S(1)}, bf16[4,8,2560]{2,1,0:T(8,128)(2,1)S(1)}, u32[]{:S(2)}, u32[]{:S(2)}) collective-permute-start(bf16[4,8,2560]{2,1,0:T(8,128)(2,1)S(1)} %get-tuple-element.45), channel_id=1, source_target_pairs={{0,1},{1,0},{2,3},{3,2},{4,5},{5,4},{6,7},{7,6},{8,9},{9,8},{10,11... | collective-permute-start | bytes 491528 | tf_op jit(solution)/shard_map/ppermute | solution.py:453
  57.1 11.1 %collective-permute-start.22 = (bf16[4,8,2560]{2,1,0:T(8,128)(2,1)S(1)}, bf16[4,8,2560]{2,1,0:T(8,128)(2,1)S(1)}, u32[]{:S(2)}, u32[]{:S(2)}) collective-permute-start(bf16[4,8,2560]{2,1,0:T(8,128)(2,1)S(1)} %get-tuple-element.46), channel_id=1, source_target_pairs={{0,17},{1,16},{2,19},{3,18},{4,21},{5,20},{6,23},{7,22},{8,25},{9,... | collective-permute-start | bytes 491528 | tf_op jit(solution)/shard_map/ppermute | solution.py:453
  59.0 9.9 %collective-permute-start.21 = (bf16[4,8,2560]{2,1,0:T(8,128)(2,1)S(1)}, bf16[4,8,2560]{2,1,0:T(8,128)(2,1)S(1)}, u32[]{:S(2)}, u32[]{:S(2)}) collective-permute-start(bf16[4,8,2560]{2,1,0:T(8,128)(2,1)S(1)} %get-tuple-element.46), channel_id=1, source_target_pairs={{0,16},{1,17},{2,18},{3,19},{4,20},{5,21},{6,22},{7,23},{8,24},{9,... | collective-permute-start | bytes 491528 | tf_op jit(solution)/shard_map/ppermute | solution.py:453
  61.7 8.2 %collective-permute-start.20 = (bf16[4,8,2560]{2,1,0:T(8,128)(2,1)S(1)}, bf16[4,8,2560]{2,1,0:T(8,128)(2,1)S(1)}, u32[]{:S(2)}, u32[]{:S(2)}) collective-permute-start(bf16[4,8,2560]{2,1,0:T(8,128)(2,1)S(1)} %get-tuple-element.46), channel_id=1, source_target_pairs={{0,1},{1,0},{2,3},{3,2},{4,5},{5,4},{6,7},{7,6},{8,9},{9,8},{10,11... | collective-permute-start | bytes 491528 | tf_op jit(solution)/shard_map/ppermute | solution.py:453
  65.7 4.3 %collective-permute-start.19 = (bf16[128,2560]{1,0:T(8,128)(2,1)S(1)}, bf16[128,2560]{1,0:T(8,128)(2,1)S(1)}, u32[]{:S(2)}, u32[]{:S(2)}) collective-permute-start(bf16[128,2560]{1,0:T(8,128)(2,1)S(1)} %maximum_bitcast_fusion.left_ref), channel_id=1, source_target_pairs={{0,8},{8,0},{16,24},{24,16},{1,9},{9,1},{17,25},{25,17},{2,10},{10... | collective-permute-start | bytes 1966088 | tf_op jit(solution)/shard_map/ppermute | solution.py:47
  70.0 4.7 %collective-permute-start.23 = (bf16[128,2560]{1,0:T(8,128)(2,1)S(1)}, bf16[128,2560]{1,0:T(8,128)(2,1)S(1)}, u32[]{:S(2)}, u32[]{:S(2)}) collective-permute-start(bf16[128,2560]{1,0:T(8,128)(2,1)S(1)} %maximum_bitcast_fusion.1.left_ref), channel_id=1, source_target_pairs={{0,8},{8,0},{16,24},{24,16},{1,9},{9,1},{17,25},{25,17},{2,10},{10... | collective-permute-start | bytes 1966088 | tf_op jit(solution)/shard_map/ppermute | solution.py:47

commit v4 on v3

--- a/solution.py
+++ b/solution.py
@@ -84,7 +84,7 @@
     return packed.astype(BF16)
 
 
-def load_kernel(count, *refs):
+def load_kernel(count, gate_ref, *refs):
     sems = refs[2 * count]
     copies = [
         pltpu.make_async_copy(refs[i], refs[count + i], sems.at[i]) for i in range(count)
@@ -96,7 +96,7 @@
 
 
 def own_kernel(
-    heads, seq, lengths_ref, q_ref, rk_ref, rv_ref, k_ref, v_ref, gate_ref, early_ref, own_ref, pre_ref
+    heads, seq, lengths_ref, prompt_ref, q_ref, rk_ref, rv_ref, k_ref, v_ref, gate_ref, own_ref
 ):
     rows = q_ref.shape[0]
     row = lax.broadcasted_iota(jnp.int32, (rows, rows), 0)
@@ -110,15 +110,25 @@
         [(q_ref[:, p], rk_ref[:, p], rv_ref[:, p], allowed) for p in parts]
         + [(q_ref[:, p], k_ref[:, p], v_ref[:, p], None) for p in parts]
     )
+    here = wanted_prompts(seq, rows, prompt_ref) == lax.axis_index("group") * k_ref.shape[0] // PLEN
+    lane = lax.broadcasted_iota(jnp.int32, (rows, 128), 1)
+    packed = jnp.zeros((rows, 128), F32)
     for h, p in enumerate(parts):
-        own_ref[:, p] = found[h][0]
-        pre_ref[:, p] = found[heads + h][0]
-    lane = lax.broadcasted_iota(jnp.int32, (rows, 128), 1)
-    for ref, values in ((own_ref, found[:heads]), (pre_ref, found[heads:])):
-        packed = jnp.zeros((rows, 128), F32)
-        for h in range(heads):
-            packed = jnp.where(lane == h, values[h][1], packed)
-        ref[:, heads * HEAD_DIM :] = packed
+        (first, log), (second, other) = found[h], found[heads + h]
+        other = jnp.where(here, other, NEG)
+        peak = jnp.maximum(log, other)
+        left, right = jnp.exp(log - peak), jnp.exp(other - peak)
+        own_ref[:, p] = (first * left + second * right) / (left + right)
+        packed = jnp.where(lane == h, peak + jnp.log(left + right), packed)
+    own_ref[:, heads * HEAD_DIM :] = packed
+
+
+def wanted_prompts(seq, rows, prompt_ref):
+    row = lax.broadcasted_iota(jnp.int32, (rows, 1), 0)
+    wanted = jnp.zeros((rows, 1), jnp.int32)
+    for r in range(rows // seq):
+        wanted = jnp.where(row // seq == r, prompt_ref[r], wanted)
+    return wanted
 
 
 def prefix_kernel(heads, count, *refs):
@@ -138,35 +148,26 @@
         out_refs[i][:, heads * HEAD_DIM :] = pack_logs([log[rung] for _, log in found], rows)
 
 
-def project_kernel(heads, seq, share, wide, group_size, key_rows, gate_ref, prompt_ref, *refs):
-    count = group_size - 1
-    own_ref, pre_ref = refs[:2]
-    got_refs = refs[2 : 2 + count]
-    weight_ref = refs[2 + count]
-    out_refs, (attended_ref, partial_ref) = refs[3 + count : -2], refs[-2:]
+def project_kernel(heads, seq, share, wide, group_size, key_rows, prompt_ref, own_ref, *refs):
+    got_refs, weight_ref = refs[: group_size - 1], refs[group_size - 1]
+    out_refs, (attended_ref, partial_ref) = refs[group_size:-2], refs[-2:]
     rows = own_ref.shape[0]
-    row = lax.broadcasted_iota(jnp.int32, (rows, 1), 0)
-    wanted = jnp.zeros((rows, 1), jnp.int32)
-    for r in range(rows // seq):
-        wanted = jnp.where(row // seq == r, prompt_ref[r], wanted)
+    wanted = wanted_prompts(seq, rows, prompt_ref)
     group = lax.axis_index("group")
-    holders = [(group ^ d) * key_rows // PLEN for d in range(group_size)]
+    holders = [(group ^ d) * key_rows // PLEN for d in range(1, group_size)]
     for h in range(heads):
         part = slice(h * HEAD_DIM, (h + 1) * HEAD_DIM)
         at = heads * HEAD_DIM
         logs = [own_ref[:, at + h : at + h + 1]]
         values = [own_ref[:, part]]
-        pre_log = pre_ref[:, at + h : at + h + 1]
-        logs.append(jnp.where(wanted == holders[0], pre_log, NEG))
-        values.append(pre_ref[:, part])
-        for i, ref in enumerate(got_refs):
+        for holder, ref in zip(holders, got_refs):
             three = ref[:, at : at + 128].astype(F32)
             log = (
                 three[:, 3 * h : 3 * h + 1]
                 + three[:, 3 * h + 1 : 3 * h + 2]
                 + three[:, 3 * h + 2 : 3 * h + 3]
             )
-            logs.append(jnp.where(wanted == holders[1 + i], log, NEG))
+            logs.append(jnp.where(wanted == holder, log, NEG))
             values.append(ref[:, part].astype(F32))
         peak = functools.reduce(jnp.maximum, logs)
         loads = [jnp.exp(log - peak) for log in logs]
@@ -208,8 +209,8 @@
             out_ref[i] = ref[:, half * width : (half + 1) * width]
 
 
-def norm_kernel(first_gate_ref, second_gate_ref, residual_ref, gain_ref, *refs):
-    terms, out_ref = refs[:-1], refs[-1]
+def norm_kernel(residual_ref, gain_ref, *refs):
+    terms, out_ref = refs[3:-1], refs[-1]
     hidden = residual_ref[lax.axis_index("tensor")].astype(F32)
     for ref in terms:
         hidden = hidden + ref[...].astype(F32)
@@ -318,7 +319,7 @@
     live = jnp.zeros((1, 128), jnp.int32)
     for r in range(count):
         live = jnp.where(token // seq == r, lengths_ref[r], live)
-    out_ref[...] = jnp.where(token % seq < live, values, 0.0)
+    out_ref[...] = jnp.where(token % seq < live, values, 0.0)[0, :share]
 
 
 def local(
@@ -350,18 +351,18 @@
     distances = list(range(1, group_size))
     queries = [swap(resp_query, "group", d, group_size) for d in distances]
     wanted = targets.reshape(-1, share, 1)
-    inputs = (resp_query, resp_key, resp_value, prompt_keys, prompt_values, out_weight)
+    inputs = (resp_query, resp_key, resp_value, prompt_keys, prompt_values)
     loaded = pl.pallas_call(
         functools.partial(load_kernel, len(inputs)),
         out_shape=[pltpu.VMEM(x.shape, x.dtype) for x in inputs],
-        in_specs=[anywhere()] * len(inputs),
+        in_specs=[anywhere()] * (1 + len(inputs)),
         out_specs=[vmem()] * len(inputs),
         scratch_shapes=[pltpu.SemaphoreType.DMA((len(inputs),))],
         compiler_params=params(1),
-        cost_estimate=cost(moved=7 * MIB),
+        cost_estimate=cost(moved=2 * MIB),
         name="load",
-    )(*map(stored, inputs))
-    query, own_keys, own_values, keys, values, weight = map(held, loaded)
+    )(wanted, *map(stored, inputs))
+    query, own_keys, own_values, keys, values = map(held, loaded)
     answers = pl.pallas_call(
         functools.partial(prefix_kernel, heads, len(distances)),
         out_shape=[jax.ShapeDtypeStruct((rows, span + 128), BF16)] * len(distances),
@@ -371,39 +372,39 @@
         name="prefix_attention",
     )(*map(held, queries), keys, values)
     got = [swap(x, "group", d, group_size) for x, d in zip(answers, distances)]
-    own, prefix = pl.pallas_call(
+    own = pl.pallas_call(
         functools.partial(own_kernel, heads, seq),
-        out_shape=[jax.ShapeDtypeStruct((rows, span + 128), F32)] * 2,
-        in_specs=[smem()] + [vmem()] * 5 + [anywhere()] * 2,
-        out_specs=[vmem()] * 2,
+        out_shape=jax.ShapeDtypeStruct((rows, span + 128), F32),
+        in_specs=[smem()] * 2 + [vmem()] * 5 + [anywhere()],
+        out_specs=vmem(),
         compiler_params=params(6),
         cost_estimate=cost(moved=8 * MIB),
         name="own_attention",
-    )(stored(lengths), query, own_keys, own_values, keys, values, answers[0], wanted)
-
-    def fetch(quarter, gate):
+    )(stored(lengths), stored(prompt_of), query, own_keys, own_values, keys, values, answers[0])
+
+    def fetch(source, start, count, gate):
         return held(
             pl.pallas_call(
-                functools.partial(fetch_kernel, quarter * (depth // 4), 4),
-                out_shape=pltpu.VMEM((depth // 4, vocab), BF16),
+                functools.partial(fetch_kernel, start, 4),
+                out_shape=pltpu.VMEM((count, source.shape[1]), BF16),
                 in_specs=[anywhere()] * 2,
                 out_specs=vmem(),
                 scratch_shapes=[pltpu.SemaphoreType.DMA((4,))],
                 compiler_params=params(1),
-                cost_estimate=cost(moved=depth // 4 * vocab * 2),
+                cost_estimate=cost(moved=count * source.shape[1] * 2),
                 name="fetch",
-            )(stored(lm_weight), gate)
+            )(stored(source), gate)
         )
 
-    quarters = [fetch(0, answers[0])]
-
-    wide = 640 if depth % 640 == 0 else depth
+    weight = fetch(out_weight, 0, span, answers[0])
+
+    wide = 1024 if depth % 1024 == 0 else depth
     shares = pl.pallas_call(
         functools.partial(project_kernel, heads, seq, share, wide, group_size, key_rows),
         out_shape=[
             jax.ShapeDtypeStruct((share, depth), BF16 if d else F32) for d in range(tensor_size)
         ],
-        in_specs=[anywhere(), smem()] + [vmem()] * (3 + len(distances)),
+        in_specs=[smem()] + [vmem()] * (2 + len(distances)),
         out_specs=[vmem()] * tensor_size,
         scratch_shapes=[
             pltpu.VMEM((rows, span), BF16),
@@ -411,20 +412,21 @@
         ],
         compiler_params=params(6),
         name="project",
-    )(quarters[0], stored(prompt_of), *map(held, (own, prefix, *got)), weight)
-    quarters += [fetch(1, shares[1]), fetch(2, shares[1])]
-
-    got = [swap(x, "tensor", d, tensor_size) for d, x in enumerate(shares) if d]
+    )(stored(prompt_of), *map(held, (own, *got)), weight)
+    quarter = depth // 4
+    quarters = [fetch(lm_weight, i * quarter, quarter, shares[1]) for i in range(3)]
+
+    got = [swap(shares[d], "tensor", d, tensor_size) for d in range(tensor_size - 1, 0, -1)]
     normed = pl.pallas_call(
         norm_kernel,
         out_shape=jax.ShapeDtypeStruct((share, depth), BF16),
-        in_specs=[anywhere()] * 2 + [vmem()] * (2 + tensor_size),
+        in_specs=[vmem()] * 2 + [anywhere()] * 3 + [vmem()] * tensor_size,
         out_specs=vmem(),
         compiler_params=params(4),
         name="norm",
     )(
-        *quarters[1:],
         *map(held, (residual.reshape(tensor_size, share, depth), norm_gain[None])),
+        *quarters,
         *map(held, (shares[0], *got)),
     )
 
@@ -432,13 +434,9 @@
     above = list(range(2, group_size, 2))
     order = [0] + far
     here = [(g, x) for g in [0] + above for x in (0, 1)]
-    mesh_ids = [(g, t) for g in range(group_size) for t in range(tensor_size)]
-    routes = {
-        (g, x): [(a * tensor_size + b, (a ^ g) * tensor_size + (b ^ x)) for a, b in mesh_ids]
-        for g, x in here
-    }
-    column = [normed] + [swap(normed, "tensor", d, tensor_size) for d in far]
-    quarters.append(fetch(3, normed))
+    column = [swap(normed, "tensor", d, tensor_size) for d in far[::-1]]
+    column = [normed] + column[::-1]
+    quarters.append(fetch(lm_weight, 3 * quarter, quarter, normed))
     columns = pl.pallas_call(
         functools.partial(column_kernel, len(column)),
         out_shape=[jax.ShapeDtypeStruct((len(column), share, depth // 2), BF16)] * 2,
@@ -447,17 +445,20 @@
         compiler_params=params(2),
         name="column",
     )(*map(held, column), quarters[3])
+    left, right = columns
+    left = jnp.concatenate([left, swap(left, "tensor", 1, tensor_size)])
+    right = [right] + [swap(right, "group", d, group_size) for d in above]
+    left = [left] + [swap(left, "group", d, group_size) for d in above]
+    across = swap(jnp.concatenate(right), "tensor", 1, tensor_size)
+    across = jnp.split(across, len(right))
+    right = [x for pair in zip(right, across) for x in pair]
     halves = []
-    for tokens in columns:
-        pieces = [
-            lax.ppermute(tokens, ("group", "tensor"), routes[place]) if any(place) else tokens
-            for place in here
-        ]
+    for pieces in (left, right):
         tokens = jnp.concatenate(pieces).reshape(-1, depth // 2)
         halves.append((tokens, swap(tokens, "group", 1, group_size)))
     spots = [(g + c, t + x) for c in (0, 1) for g, x in here for t in order]
     total_rows = 2 * tokens.shape[0]
-    narrow = 1024 if vocab % 1024 == 0 else vocab
+    narrow = 1536 if vocab % 1536 == 0 else vocab
     limit = 10 if total_rows <= 256 else 24
     work = 2 * total_rows * (depth // 2) * vocab
     first = pl.pallas_call(
@@ -484,15 +485,14 @@
     )(*map(held, (first, *halves[1])), wanted, *map(held, quarters[2:]))
 
     stats = lax.all_to_all(stats, ("group", "tensor"), 0, 0, tiled=True)
-    values = pl.pallas_call(
+    return pl.pallas_call(
         functools.partial(final_kernel, seq, share),
-        out_shape=jax.ShapeDtypeStruct((1, 128), F32),
+        out_shape=jax.ShapeDtypeStruct((share,), F32),
         in_specs=[smem(), vmem()],
         out_specs=vmem(),
         compiler_params=params(4),
         name="final",
     )(stored(lengths), stats)
-    return values[0, :share]
 
 
 def solution(mesh):

time: 93.7 us -> 92.8 us (level)
  local copies, waits for them, and re-layouts: 3.76 us -> 0.92 us
  waiting for transfers between devices: 13.5 us -> 14.6 us
    ppermute x18 -> x22, waiting for transfers between devices: 4.1 us -> 14.6 us  [swap(): return lax.ppermute(x, axis, [(i, i ^ distance) for i in range(size)])]
    ppermute x6 -> x0, waiting for transfers between devices: 9.37 us -> none  [local(): lax.ppermute(tokens, ('group', 'tensor'), routes[place])]
    ppermute x6 -> x0, starting transfers between devices: 6.83 us -> none  [local(): lax.ppermute(tokens, ('group', 'tensor'), routes[place])]
    ppermute x18 -> x22, starting transfers between devices: 23.2 us -> 30 us  [swap(): return lax.ppermute(x, axis, [(i, i ^ distance) for i in range(size)])]
    unnamed x10 -> x4, local copies, waits for them, and re-layouts: 2.35 us -> 0.01 us
    pallas_call x5 -> x6, Pallas kernels: 15 us -> 17.3 us  [the longest x5 16 us: fetch(): pl.pallas_call(functools.partial(fetch_kernel, start, 4), out_shape=pltpu...]
    pallas_call x1, Pallas kernels: 2.97 us -> 1.36 us  [local(): pl.pallas_call(functools.partial(load_kernel, len(inputs)), out_shape=[pl...]
  transfers between devices with their start and end apart: 24 -> 22, of which waited for: 7 -> 9; matrix products, arithmetic and copies ran while one was open for 1% -> 1% of each run, Pallas kernels for 24% -> 25%
where the time goes in v4:
time: 92.8 us; the launch traced here: 92.6 us
  Pallas kernels  34.3 us (37%)
  starting transfers between devices  30 us (32%)
  waiting for transfers between devices  14.6 us (16%)
  blocking collectives  12.3 us (13%)
    ppermute x22, starting transfers between devices, swap(): return lax.ppermute(x, axis, [(i, i ^ distance) for i in range(size)])  30 us
    pallas_call x5, Pallas kernels, fetch(): pl.pallas_call(functools.partial(fetch_kernel, start, 4), out_shape=pltpu...  16 us
    ppermute x22, waiting for transfers between devices, swap(): return lax.ppermute(x, axis, [(i, i ^ distance) for i in range(size)])  14.6 us
    all_to_all x1, blocking collectives, local(): stats = lax.all_to_all(stats, ('group', 'tensor'), 0, 0, tiled=True)  12.3 us
    pallas_call x1, Pallas kernels, local(): pl.pallas_call(functools.partial(logits_kernel, narrow, spots, tensor_siz...  5.43 us
    pallas_call x1, Pallas kernels, local(): pl.pallas_call(functools.partial(first_kernel, narrow), out_shape=pltpu.V...  4.47 us
    pallas_call x1, Pallas kernels, local(): pl.pallas_call(functools.partial(project_kernel, heads, seq, share, wide,...  3.33 us
  transfers between devices with their start and end apart: 22, of which 9 were waited for; matrix products, arithmetic and copies ran while one was open for 1% of the time, Pallas kernels for 25%

profile of v4, /device:TPU:0, one launch (start us, length us, event | category | flops | bytes accessed | tf_op | source)
XLA Modules:
  0.0 92.6 jit_solution(1466670283222569721)
XLA Ops:
  0.5 2.5 %collective-permute-start.1 = (bf16[64,512]{1,0:T(8,128)(2,1)}, bf16[64,512]{1,0:T(8,128)(2,1)S(1)}, u32[]{:S(2)}, u32[]{:S(2)}) collective-permute-start(bf16[64,512]{1,0:T(8,128)(2,1)} %refs_0_.1), channel_id=1, source_target_pairs={{0,16},{8,24},{16,0},{24,8},{1,17},{9,25},{17,1},{25,9},{2,18},{10... | collective-permute-start | bytes 196616 | tf_op jit(solution)/shard_map/ppermute | solution.py:47
  3.1 0.9 reshape.16.gate_ref.target_ref
  4.0 1.4 %load.1 = (bf16[64,512]{1,0:T(8,128)(2,1)S(1)}, bf16[64,512]{1,0:T(8,128)(2,1)S(1)}, bf16[64,512]{1,0:T(8,128)(2,1)S(1)}, bf16[512,512]{1,0:T(8,128)(2,1)S(1)}, bf16[512,512]{1,0:T(8,128)(2,1)S(1)}) custom-call(s32[32,8,1]{2,1,0:T(8,128)S(1)} %reshape.16.gate_ref.target_ref, bf16[64,512]{1,0:T(8,128)(2,1)} %refs_0_.1, bf16[64,512]{1,0:T(8,128)(2,1)} %refs_1_.1, ...), custom_call_target="tpu_custom_call" | custom-call | bytes 2097152 | tf_op jit(solution)/shard_map/load/pallas_call | solution.py:355
  5.9 1.3 %collective-permute-done.2.refs_2_ = bf16[64,512]{1,0:T(8,128)(2,1)S(1)} collective-permute-done((bf16[64,512]{1,0:T(8,128)(2,1)}, bf16[64,512]{1,0:T(8,128)(2,1)S(1)}, u32[]{:S(2)}, u32[]{:S(2)}) %collective-permute-start.2) | collective-permute-done | bytes 65568 | tf_op jit(solution)/shard_map/ppermute | solution.py:47
  7.3 0.8 prefix_attention.1
  8.3 1.5 %collective-permute-start.4 = (bf16[64,640]{1,0:T(8,128)(2,1)S(1)}, bf16[64,640]{1,0:T(8,128)(2,1)S(1)}, u32[]{:S(2)}, u32[]{:S(2)}) collective-permute-start(bf16[64,640]{1,0:T(8,128)(2,1)S(1)} %get-tuple-element.29), channel_id=1, source_target_pairs={{0,16},{8,24},{16,0},{24,8},{1,17},{9,25},{17,1},{25,9},{2,18},{10... | collective-permute-start | bytes 245768 | tf_op jit(solution)/shard_map/ppermute | solution.py:47
  10.0 2.5 %fetch.5.refs_3_ = bf16[512,5120]{1,0:T(8,128)(2,1)S(1)} custom-call(bf16[512,5120]{1,0:T(8,128)(2,1)} %source_ref.5, bf16[64,640]{1,0:T(8,128)(2,1)S(1)} %get-tuple-element.28.gate_ref), custom_call_target="tpu_custom_call" | custom-call | bytes 5242880 | tf_op jit(solution)/shard_map/fetch/pallas_call | solution.py:387
  12.6 1.3 %own_attention.1.own_ref = f32[64,640]{1,0:T(8,128)S(1)} custom-call(s32[2]{0:T(128)} %lengths_ref.3, s32[2]{0:T(128)} %prompt_ref.3, bf16[64,512]{1,0:T(8,128)(2,1)S(1)} %get-tuple-element.23.q_ref, bf16[64,512]{1,0:T(8,128)(2,1)S(1)} %get-tuple-element.24.rk_ref, bf16[64,512]{1,0:T(8,128)(2,1)S(1)} %get-tuple-element.25.rv_ref, ...), custom_call_target="tpu_custom_call" | custom-call | bytes 8388608 | tf_op jit(solution)/shard_map/own_attention/pallas_call | solution.py:375
  14.6 3.3 %project.1 = (f32[8,5120]{1,0:T(8,128)S(1)}, bf16[8,5120]{1,0:T(8,128)(2,1)S(1)}, bf16[8,5120]{1,0:T(8,128)(2,1)S(1)}, bf16[8,5120]{1,0:T(8,128)(2,1)S(1)}, bf16...) custom-call(s32[2]{0:T(128)} %prompt_ref.3, ...), custom_call_target="tpu_custom_call" | custom-call | tf_op jit(solution)/shard_map/project/pallas_call | solution.py:402
  17.9 4.6 %collective-permute-start.6 = (bf16[8,5120]{1,0:T(8,128)(2,1)S(1)}, bf16[8,5120]{1,0:T(8,128)(2,1)S(1)}, u32[]{:S(2)}, u32[]{:S(2)}) collective-permute-start(bf16[8,5120]{1,0:T(8,128)(2,1)S(1)} %get-tuple-element.33), channel_id=1, source_target_pairs={{0,7},{1,6},{2,5},{3,4},{4,3},{5,2},{6,1},{7,0},{8,15},{9,14},{10,... | collective-permute-start | bytes 245768 | tf_op jit(solution)/shard_map/ppermute | solution.py:47
  23.5 2.1 %collective-permute-start.9 = (bf16[8,5120]{1,0:T(8,128)(2,1)S(1)}, bf16[8,5120]{1,0:T(8,128)(2,1)S(1)}, u32[]{:S(2)}, u32[]{:S(2)}) collective-permute-start(bf16[8,5120]{1,0:T(8,128)(2,1)S(1)} %get-tuple-element.36), channel_id=1, source_target_pairs={{0,4},{1,5},{2,6},{3,7},{4,0},{5,1},{6,2},{7,3},{8,12},{9,13},{10,... | collective-permute-start | bytes 245768 | tf_op jit(solution)/shard_map/ppermute | solution.py:47
  25.6 2.2 %collective-permute-start.10 = (bf16[8,5120]{1,0:T(8,128)(2,1)S(1)}, bf16[8,5120]{1,0:T(8,128)(2,1)S(1)}, u32[]{:S(2)}, u32[]{:S(2)}) collective-permute-start(bf16[8,5120]{1,0:T(8,128)(2,1)S(1)} %get-tuple-element.37), channel_id=1, source_target_pairs={{0,3},{1,2},{2,1},{3,0},{4,7},{5,6},{6,5},{7,4},{8,11},{9,10},{10,... | collective-permute-start | bytes 245768 | tf_op jit(solution)/shard_map/ppermute | solution.py:47
  27.8 4.0 %collective-permute-start.11 = (bf16[8,5120]{1,0:T(8,128)(2,1)S(1)}, bf16[8,5120]{1,0:T(8,128)(2,1)S(1)}, u32[]{:S(2)}, u32[]{:S(2)}) collective-permute-start(bf16[8,5120]{1,0:T(8,128)(2,1)S(1)} %get-tuple-element.38), channel_id=1, source_target_pairs={{0,2},{1,3},{2,0},{3,1},{4,6},{5,7},{6,4},{7,5},{8,10},{9,11},{10,... | collective-permute-start | bytes 245768 | tf_op jit(solution)/shard_map/ppermute | solution.py:47
  31.8 1.6 %collective-permute-start.12 = (bf16[8,5120]{1,0:T(8,128)(2,1)S(1)}, bf16[8,5120]{1,0:T(8,128)(2,1)S(1)}, u32[]{:S(2)}, u32[]{:S(2)}) collective-permute-start(bf16[8,5120]{1,0:T(8,128)(2,1)S(1)} %get-tuple-element.31.gate_ref), channel_id=1, source_target_pairs={{0,1},{1,0},{2,3},{3,2},{4,5},{5,4},{6,7},{7,6},{8,9},{9,8},{10,11... | collective-permute-start | bytes 245768 | tf_op jit(solution)/shard_map/ppermute | solution.py:47
  33.4 3.3 %fetch.6.refs_0_.weight_ref = bf16[1280,3072]{1,0:T(8,128)(2,1)S(1)} custom-call(bf16[5120,3072]{1,0:T(8,128)(2,1)} %source_ref.9, bf16[8,5120]{1,0:T(8,128)(2,1)S(1)} %get-tuple-element.31.gate_ref), custom_call_target="tpu_custom_call" | custom-call | bytes 7864320 | tf_op jit(solution)/shard_map/fetch/pallas_call | solution.py:387
  36.7 3.3 %fetch.7.refs_1_.next_ref = bf16[1280,3072]{1,0:T(8,128)(2,1)S(1)} custom-call(bf16[5120,3072]{1,0:T(8,128)(2,1)} %source_ref.9, bf16[8,5120]{1,0:T(8,128)(2,1)S(1)} %get-tuple-element.31.gate_ref), custom_call_target="tpu_custom_call" | custom-call | bytes 7864320 | tf_op jit(solution)/shard_map/fetch/pallas_call | solution.py:387
  40.1 3.4 %fetch.8.refs_2_.weight_ref = bf16[1280,3072]{1,0:T(8,128)(2,1)S(1)} custom-call(bf16[5120,3072]{1,0:T(8,128)(2,1)} %source_ref.9, bf16[8,5120]{1,0:T(8,128)(2,1)S(1)} %get-tuple-element.31.gate_ref), custom_call_target="tpu_custom_call" | custom-call | bytes 7864320 | tf_op jit(solution)/shard_map/fetch/pallas_call | solution.py:387
  43.8 1.7 %collective-permute-start.13 = (bf16[8,5120]{1,0:T(8,128)(2,1)S(1)}, bf16[8,5120]{1,0:T(8,128)(2,1)S(1)}, u32[]{:S(2)}, u32[]{:S(2)}) collective-permute-start(bf16[8,5120]{1,0:T(8,128)(2,1)S(1)} %norm.1.gate_ref.refs_0_), channel_id=1, source_target_pairs={{0,2},{1,3},{2,0},{3,1},{4,6},{5,7},{6,4},{7,5},{8,10},{9,11},{10,... | collective-permute-start | bytes 245768 | tf_op jit(solution)/shard_map/ppermute | solution.py:47
  45.5 2.1 %collective-permute-start.14 = (bf16[8,5120]{1,0:T(8,128)(2,1)S(1)}, bf16[8,5120]{1,0:T(8,128)(2,1)S(1)}, u32[]{:S(2)}, u32[]{:S(2)}) collective-permute-start(bf16[8,5120]{1,0:T(8,128)(2,1)S(1)} %norm.1.gate_ref.refs_0_), channel_id=1, source_target_pairs={{0,4},{1,5},{2,6},{3,7},{4,0},{5,1},{6,2},{7,3},{8,12},{9,13},{10,... | collective-permute-start | bytes 245768 | tf_op jit(solution)/shard_map/ppermute | solution.py:47
  48.3 3.3 %fetch.9.refs_4_.next_ref = bf16[1280,3072]{1,0:T(8,128)(2,1)S(1)} custom-call(bf16[5120,3072]{1,0:T(8,128)(2,1)} %source_ref.9, bf16[8,5120]{1,0:T(8,128)(2,1)S(1)} %norm.1.gate_ref.refs_0_), custom_call_target="tpu_custom_call" | custom-call | bytes 7864320 | tf_op jit(solution)/shard_map/fetch/pallas_call | solution.py:387
  51.9 1.9 %collective-permute-done.15.refs_3_ = bf16[8,5120]{1,0:T(8,128)(2,1)S(1)} collective-permute-done((bf16[8,5120]{1,0:T(8,128)(2,1)S(1)}, bf16[8,5120]{1,0:T(8,128)(2,1)S(1)}, u32[]{:S(2)}, u32[]{:S(2)}) %collective-permute-start.15) | collective-permute-done | bytes 81952 | tf_op jit(solution)/shard_map/ppermute | solution.py:47
  54.6 1.7 %collective-permute-start.19 = (bf16[4,8,2560]{2,1,0:T(8,128)(2,1)S(1)}, bf16[4,8,2560]{2,1,0:T(8,128)(2,1)S(1)}, u32[]{:S(2)}, u32[]{:S(2)}) collective-permute-start(bf16[4,8,2560]{2,1,0:T(8,128)(2,1)S(1)} %get-tuple-element.40), channel_id=1, source_target_pairs={{0,16},{8,24},{16,0},{24,8},{1,17},{9,25},{17,1},{25,9},{2,18},{10... | collective-permute-start | bytes 491528 | tf_op jit(solution)/shard_map/ppermute | solution.py:47
  56.3 3.0 %collective-permute-done.16 = bf16[4,8,2560]{2,1,0:T(8,128)(2,1)S(1)} collective-permute-done((bf16[4,8,2560]{2,1,0:T(8,128)(2,1)S(1)}, bf16[4,8,2560]{2,1,0:T(8,128)(2,1)S(1)}, u32[]{:S(2)}, u32[]{:S(2)}) %collective-permute-start.16) | collective-permute-done | bytes 163872 | tf_op jit(solution)/shard_map/ppermute | solution.py:47
  59.4 1.1 %collective-permute-start.17 = (bf16[8,8,2560]{2,1,0:T(8,128)(2,1)S(1)}, bf16[8,8,2560]{2,1,0:T(8,128)(2,1)S(1)}, u32[]{:S(2)}, u32[]{:S(2)}) collective-permute-start(bf16[8,8,2560]{2,1,0:T(8,128)(2,1)S(1)} %pad_maximum_fusion), channel_id=1, source_target_pairs={{0,16},{8,24},{16,0},{24,8},{1,17},{9,25},{17,1},{25,9},{2,18},{10... | collective-permute-start | bytes 983048 | tf_op jit(solution)/shard_map/ppermute | solution.py:47
  60.4 1.2 %collective-permute-done.19 = bf16[4,8,2560]{2,1,0:T(8,128)(2,1)S(1)} collective-permute-done((bf16[4,8,2560]{2,1,0:T(8,128)(2,1)S(1)}, bf16[4,8,2560]{2,1,0:T(8,128)(2,1)S(1)}, u32[]{:S(2)}, u32[]{:S(2)}) %collective-permute-start.19) | collective-permute-done | bytes 163872 | tf_op jit(solution)/shard_map/ppermute | solution.py:47
  61.7 1.4 %collective-permute-start.20 = (bf16[8,8,2560]{2,1,0:T(8,128)(2,1)S(1)}, bf16[8,8,2560]{2,1,0:T(8,128)(2,1)S(1)}, u32[]{:S(2)}, u32[]{:S(2)}) collective-permute-start(bf16[8,8,2560]{2,1,0:T(8,128)(2,1)S(1)} %pad_maximum_fusion.1), channel_id=1, source_target_pairs={{0,1},{1,0},{2,3},{3,2},{4,5},{5,4},{6,7},{7,6},{8,9},{9,8},{10,11... | collective-permute-start | bytes 983048 | tf_op jit(solution)/shard_map/ppermute | solution.py:47
  63.0 3.5 %collective-permute-done.17 = bf16[8,8,2560]{2,1,0:T(8,128)(2,1)S(1)} collective-permute-done((bf16[8,8,2560]{2,1,0:T(8,128)(2,1)S(1)}, bf16[8,8,2560]{2,1,0:T(8,128)(2,1)S(1)}, u32[]{:S(2)}, u32[]{:S(2)}) %collective-permute-start.17) | collective-permute-done | bytes 327712 | tf_op jit(solution)/shard_map/ppermute | solution.py:47
  66.7 2.1 %collective-permute-done.20 = bf16[8,8,2560]{2,1,0:T(8,128)(2,1)S(1)} collective-permute-done((bf16[8,8,2560]{2,1,0:T(8,128)(2,1)S(1)}, bf16[8,8,2560]{2,1,0:T(8,128)(2,1)S(1)}, u32[]{:S(2)}, u32[]{:S(2)}) %collective-permute-start.20) | collective-permute-done | bytes 327712 | tf_op jit(solution)/shard_map/ppermute | solution.py:47
  69.0 4.5 %logits_first.1.sum_in_ref = f32[256,3072]{1,0:T(8,128)S(1)} custom-call(bf16[128,2560]{1,0:T(8,128)(2,1)S(1)} %maximum_bitcast_fusion.left_ref, bf16[128,2560]{1,0:T(8,128)(2,1)S(1)} %collective-permute-done.18.right_ref, bf16[1280,3072]{1,0:T(8,128)(2,1)S(1)} %fetch.6.refs_0_.weight_ref, bf16[1280,3072]{1,0:T(8,128)(2,1)S(1)} %fetch.7.refs_1_.next_ref), custom_call_target="tpu_custom_call" | custom-call | flops 4026531840 | tf_op jit(solution)/shard_map/logits_first/pallas_call | solution.py:464
  73.5 5.4 %logits.1 = f32[32,1,128]{2,1,0:T(1,128)S(1)} custom-call(f32[256,3072]{1,0:T(8,128)S(1)} %logits_first.1.sum_in_ref, bf16[128,2560]{1,0:T(8,128)(2,1)S(1)} %maximum_bitcast_fusion.1.left_ref, bf16[128,2560]{1,0:T(8,128)(2,1)S(1)} %collective-permute-done.21.right_ref, s32[32,8,1]{2,1,0:T(8,128)S(1)} %reshape.16.gate_ref.target_ref, ...), custom_call_target="tpu_custom_call" | custom-call | flops 4026531840 | tf_op jit(solution)/shard_map/logits/pallas_call | solution.py:474
  78.9 12.3 %all_to_all.5.stats_ref = f32[32,1,128]{2,1,0:T(1,128)S(1)} all-to-all(f32[32,1,128]{2,1,0:T(1,128)S(1)} %logits.1), channel_id=1, replica_groups=mesh['group'=4,'tensor'=8] {'group','tensor'}, dimensions={0} | all-to-all | bytes 32768 | tf_op jit(solution)/shard_map/all_to_all | solution.py:487
  91.3 1.3 %final.1 = f32[8]{0:T(128)} custom-call(s32[2]{0:T(128)} %lengths_ref.3, f32[32,1,128]{2,1,0:T(1,128)S(1)} %all_to_all.5.stats_ref), custom_call_target="tpu_custom_call" | custom-call | tf_op jit(solution)/shard_map/final/pallas_call | solution.py:488
  (38 shorter events, 5.6 us)
Async XLA Ops:
  0.0 5.4 %collective-permute-start = (bf16[64,512]{1,0:T(8,128)(2,1)}, bf16[64,512]{1,0:T(8,128)(2,1)S(1)}, u32[]{:S(2)}, u32[]{:S(2)}) collective-permute-start(bf16[64,512]{1,0:T(8,128)(2,1)} %refs_0_.1), channel_id=1, source_target_pairs={{0,8},{8,0},{16,24},{24,16},{1,9},{9,1},{17,25},{25,17},{2,10},{10... | collective-permute-start | bytes 196616 | tf_op jit(solution)/shard_map/ppermute | solution.py:47
  0.5 5.5 %collective-permute-start.1 = (bf16[64,512]{1,0:T(8,128)(2,1)}, bf16[64,512]{1,0:T(8,128)(2,1)S(1)}, u32[]{:S(2)}, u32[]{:S(2)}) collective-permute-start(bf16[64,512]{1,0:T(8,128)(2,1)} %refs_0_.1), channel_id=1, source_target_pairs={{0,16},{8,24},{16,0},{24,8},{1,17},{9,25},{17,1},{25,9},{2,18},{10... | collective-permute-start | bytes 196616 | tf_op jit(solution)/shard_map/ppermute | solution.py:47
  3.0 4.3 %collective-permute-start.2 = (bf16[64,512]{1,0:T(8,128)(2,1)}, bf16[64,512]{1,0:T(8,128)(2,1)S(1)}, u32[]{:S(2)}, u32[]{:S(2)}) collective-permute-start(bf16[64,512]{1,0:T(8,128)(2,1)} %refs_0_.1), channel_id=1, source_target_pairs={{0,24},{8,16},{16,8},{24,0},{1,25},{9,17},{17,9},{25,1},{2,26},{10... | collective-permute-start | bytes 196616 | tf_op jit(solution)/shard_map/ppermute | solution.py:47
  8.1 5.8 %collective-permute-start.3 = (bf16[64,640]{1,0:T(8,128)(2,1)S(1)}, bf16[64,640]{1,0:T(8,128)(2,1)S(1)}, u32[]{:S(2)}, u32[]{:S(2)}) collective-permute-start(bf16[64,640]{1,0:T(8,128)(2,1)S(1)} %get-tuple-element.28.gate_ref), channel_id=1, source_target_pairs={{0,8},{8,0},{16,24},{24,16},{1,9},{9,1},{17,25},{25,17},{2,10},{10... | collective-permute-start | bytes 245768 | tf_op jit(solution)/shard_map/ppermute | solution.py:47
  8.3 5.6 %collective-permute-start.4 = (bf16[64,640]{1,0:T(8,128)(2,1)S(1)}, bf16[64,640]{1,0:T(8,128)(2,1)S(1)}, u32[]{:S(2)}, u32[]{:S(2)}) collective-permute-start(bf16[64,640]{1,0:T(8,128)(2,1)S(1)} %get-tuple-element.29), channel_id=1, source_target_pairs={{0,16},{8,24},{16,0},{24,8},{1,17},{9,25},{17,1},{25,9},{2,18},{10... | collective-permute-start | bytes 245768 | tf_op jit(solution)/shard_map/ppermute | solution.py:47
  9.8 23.5 %copy-start.1 = (bf16[5120]{0:T(1024)(128)(2,1)S(1)}, bf16[5120]{0:T(1024)(128)(2,1)}, u32[]{:S(2)}) copy-start(bf16[5120]{0:T(1024)(128)(2,1)} %param.21) | copy-start | bytes 30724
  9.8 4.7 %collective-permute-start.5 = (bf16[64,640]{1,0:T(8,128)(2,1)S(1)}, bf16[64,640]{1,0:T(8,128)(2,1)S(1)}, u32[]{:S(2)}, u32[]{:S(2)}) collective-permute-start(bf16[64,640]{1,0:T(8,128)(2,1)S(1)} %get-tuple-element.30), channel_id=1, source_target_pairs={{0,24},{8,16},{16,8},{24,0},{1,25},{9,17},{17,9},{25,1},{2,26},{10... | collective-permute-start | bytes 245768 | tf_op jit(solution)/shard_map/ppermute | solution.py:47
  17.9 9.9 %collective-permute-start.6 = (bf16[8,5120]{1,0:T(8,128)(2,1)S(1)}, bf16[8,5120]{1,0:T(8,128)(2,1)S(1)}, u32[]{:S(2)}, u32[]{:S(2)}) collective-permute-start(bf16[8,5120]{1,0:T(8,128)(2,1)S(1)} %get-tuple-element.33), channel_id=1, source_target_pairs={{0,7},{1,6},{2,5},{3,4},{4,3},{5,2},{6,1},{7,0},{8,15},{9,14},{10,... | collective-permute-start | bytes 245768 | tf_op jit(solution)/shard_map/ppermute | solution.py:47
  22.5 9.3 %collective-permute-start.7 = (bf16[8,5120]{1,0:T(8,128)(2,1)S(1)}, bf16[8,5120]{1,0:T(8,128)(2,1)S(1)}, u32[]{:S(2)}, u32[]{:S(2)}) collective-permute-start(bf16[8,5120]{1,0:T(8,128)(2,1)S(1)} %get-tuple-element.34), channel_id=1, source_target_pairs={{0,6},{1,7},{2,4},{3,5},{4,2},{5,3},{6,0},{7,1},{8,14},{9,15},{10,... | collective-permute-start | bytes 245768 | tf_op jit(solution)/shard_map/ppermute | solution.py:47
  22.7 20.8 %collective-permute-start.8 = (bf16[8,5120]{1,0:T(8,128)(2,1)S(1)}, bf16[8,5120]{1,0:T(8,128)(2,1)S(1)}, u32[]{:S(2)}, u32[]{:S(2)}) collective-permute-start(bf16[8,5120]{1,0:T(8,128)(2,1)S(1)} %get-tuple-element.35), channel_id=1, source_target_pairs={{0,5},{1,4},{2,7},{3,6},{4,1},{5,0},{6,3},{7,2},{8,13},{9,12},{10,... | collective-permute-start | bytes 245768 | tf_op jit(solution)/shard_map/ppermute | solution.py:47
  23.5 20.1 %collective-permute-start.9 = (bf16[8,5120]{1,0:T(8,128)(2,1)S(1)}, bf16[8,5120]{1,0:T(8,128)(2,1)S(1)}, u32[]{:S(2)}, u32[]{:S(2)}) collective-permute-start(bf16[8,5120]{1,0:T(8,128)(2,1)S(1)} %get-tuple-element.36), channel_id=1, source_target_pairs={{0,4},{1,5},{2,6},{3,7},{4,0},{5,1},{6,2},{7,3},{8,12},{9,13},{10,... | collective-permute-start | bytes 245768 | tf_op jit(solution)/shard_map/ppermute | solution.py:47
  25.6 17.9 %collective-permute-start.10 = (bf16[8,5120]{1,0:T(8,128)(2,1)S(1)}, bf16[8,5120]{1,0:T(8,128)(2,1)S(1)}, u32[]{:S(2)}, u32[]{:S(2)}) collective-permute-start(bf16[8,5120]{1,0:T(8,128)(2,1)S(1)} %get-tuple-element.37), channel_id=1, source_target_pairs={{0,3},{1,2},{2,1},{3,0},{4,7},{5,6},{6,5},{7,4},{8,11},{9,10},{10,... | collective-permute-start | bytes 245768 | tf_op jit(solution)/shard_map/ppermute | solution.py:47
  27.8 15.7 %collective-permute-start.11 = (bf16[8,5120]{1,0:T(8,128)(2,1)S(1)}, bf16[8,5120]{1,0:T(8,128)(2,1)S(1)}, u32[]{:S(2)}, u32[]{:S(2)}) collective-permute-start(bf16[8,5120]{1,0:T(8,128)(2,1)S(1)} %get-tuple-element.38), channel_id=1, source_target_pairs={{0,2},{1,3},{2,0},{3,1},{4,6},{5,7},{6,4},{7,5},{8,10},{9,11},{10,... | collective-permute-start | bytes 245768 | tf_op jit(solution)/shard_map/ppermute | solution.py:47
  31.8 11.8 %collective-permute-start.12 = (bf16[8,5120]{1,0:T(8,128)(2,1)S(1)}, bf16[8,5120]{1,0:T(8,128)(2,1)S(1)}, u32[]{:S(2)}, u32[]{:S(2)}) collective-permute-start(bf16[8,5120]{1,0:T(8,128)(2,1)S(1)} %get-tuple-element.31.gate_ref), channel_id=1, source_target_pairs={{0,1},{1,0},{2,3},{3,2},{4,5},{5,4},{6,7},{7,6},{8,9},{9,8},{10,11... | collective-permute-start | bytes 245768 | tf_op jit(solution)/shard_map/ppermute | solution.py:47
  40.1 3.5 %copy-start = (bf16[64,5120]{1,0:T(8,128)(2,1)S(1)}, bf16[64,5120]{1,0:T(8,128)(2,1)}, u32[]{:S(2)}) copy-start(bf16[64,5120]{1,0:T(8,128)(2,1)} %param.19) | copy-start | bytes 1966084
  43.8 7.8 %collective-permute-start.13 = (bf16[8,5120]{1,0:T(8,128)(2,1)S(1)}, bf16[8,5120]{1,0:T(8,128)(2,1)S(1)}, u32[]{:S(2)}, u32[]{:S(2)}) collective-permute-start(bf16[8,5120]{1,0:T(8,128)(2,1)S(1)} %norm.1.gate_ref.refs_0_), channel_id=1, source_target_pairs={{0,2},{1,3},{2,0},{3,1},{4,6},{5,7},{6,4},{7,5},{8,10},{9,11},{10,... | collective-permute-start | bytes 245768 | tf_op jit(solution)/shard_map/ppermute | solution.py:47
  45.5 6.4 %collective-permute-start.14 = (bf16[8,5120]{1,0:T(8,128)(2,1)S(1)}, bf16[8,5120]{1,0:T(8,128)(2,1)S(1)}, u32[]{:S(2)}, u32[]{:S(2)}) collective-permute-start(bf16[8,5120]{1,0:T(8,128)(2,1)S(1)} %norm.1.gate_ref.refs_0_), channel_id=1, source_target_pairs={{0,4},{1,5},{2,6},{3,7},{4,0},{5,1},{6,2},{7,3},{8,12},{9,13},{10,... | collective-permute-start | bytes 245768 | tf_op jit(solution)/shard_map/ppermute | solution.py:47
  47.6 6.2 %collective-permute-start.15 = (bf16[8,5120]{1,0:T(8,128)(2,1)S(1)}, bf16[8,5120]{1,0:T(8,128)(2,1)S(1)}, u32[]{:S(2)}, u32[]{:S(2)}) collective-permute-start(bf16[8,5120]{1,0:T(8,128)(2,1)S(1)} %norm.1.gate_ref.refs_0_), channel_id=1, source_target_pairs={{0,6},{1,7},{2,4},{3,5},{4,2},{5,3},{6,0},{7,1},{8,14},{9,15},{10,... | collective-permute-start | bytes 245768 | tf_op jit(solution)/shard_map/ppermute | solution.py:47
  53.9 5.5 %collective-permute-start.16 = (bf16[4,8,2560]{2,1,0:T(8,128)(2,1)S(1)}, bf16[4,8,2560]{2,1,0:T(8,128)(2,1)S(1)}, u32[]{:S(2)}, u32[]{:S(2)}) collective-permute-start(bf16[4,8,2560]{2,1,0:T(8,128)(2,1)S(1)} %get-tuple-element.39), channel_id=1, source_target_pairs={{0,1},{1,0},{2,3},{3,2},{4,5},{5,4},{6,7},{7,6},{8,9},{9,8},{10,11... | collective-permute-start | bytes 491528 | tf_op jit(solution)/shard_map/ppermute | solution.py:47
  54.6 7.0 %collective-permute-start.19 = (bf16[4,8,2560]{2,1,0:T(8,128)(2,1)S(1)}, bf16[4,8,2560]{2,1,0:T(8,128)(2,1)S(1)}, u32[]{:S(2)}, u32[]{:S(2)}) collective-permute-start(bf16[4,8,2560]{2,1,0:T(8,128)(2,1)S(1)} %get-tuple-element.40), channel_id=1, source_target_pairs={{0,16},{8,24},{16,0},{24,8},{1,17},{9,25},{17,1},{25,9},{2,18},{10... | collective-permute-start | bytes 491528 | tf_op jit(solution)/shard_map/ppermute | solution.py:47
  59.4 7.1 %collective-permute-start.17 = (bf16[8,8,2560]{2,1,0:T(8,128)(2,1)S(1)}, bf16[8,8,2560]{2,1,0:T(8,128)(2,1)S(1)}, u32[]{:S(2)}, u32[]{:S(2)}) collective-permute-start(bf16[8,8,2560]{2,1,0:T(8,128)(2,1)S(1)} %pad_maximum_fusion), channel_id=1, source_target_pairs={{0,16},{8,24},{16,0},{24,8},{1,17},{9,25},{17,1},{25,9},{2,18},{10... | collective-permute-start | bytes 983048 | tf_op jit(solution)/shard_map/ppermute | solution.py:47
  61.7 7.1 %collective-permute-start.20 = (bf16[8,8,2560]{2,1,0:T(8,128)(2,1)S(1)}, bf16[8,8,2560]{2,1,0:T(8,128)(2,1)S(1)}, u32[]{:S(2)}, u32[]{:S(2)}) collective-permute-start(bf16[8,8,2560]{2,1,0:T(8,128)(2,1)S(1)} %pad_maximum_fusion.1), channel_id=1, source_target_pairs={{0,1},{1,0},{2,3},{3,2},{4,5},{5,4},{6,7},{7,6},{8,9},{9,8},{10,11... | collective-permute-start | bytes 983048 | tf_op jit(solution)/shard_map/ppermute | solution.py:47
  66.6 2.4 %collective-permute-start.18 = (bf16[128,2560]{1,0:T(8,128)(2,1)S(1)}, bf16[128,2560]{1,0:T(8,128)(2,1)S(1)}, u32[]{:S(2)}, u32[]{:S(2)}) collective-permute-start(bf16[128,2560]{1,0:T(8,128)(2,1)S(1)} %maximum_bitcast_fusion.left_ref), channel_id=1, source_target_pairs={{0,8},{8,0},{16,24},{24,16},{1,9},{9,1},{17,25},{25,17},{2,10},{10... | collective-permute-start | bytes 1966088 | tf_op jit(solution)/shard_map/ppermute | solution.py:47
  68.9 4.6 %collective-permute-start.21 = (bf16[128,2560]{1,0:T(8,128)(2,1)S(1)}, bf16[128,2560]{1,0:T(8,128)(2,1)S(1)}, u32[]{:S(2)}, u32[]{:S(2)}) collective-permute-start(bf16[128,2560]{1,0:T(8,128)(2,1)S(1)} %maximum_bitcast_fusion.1.left_ref), channel_id=1, source_target_pairs={{0,8},{8,0},{16,24},{24,16},{1,9},{9,1},{17,25},{25,17},{2,10},{10... | collective-permute-start | bytes 1966088 | tf_op jit(solution)/shard_map/ppermute | solution.py:47

commit v5 on v4

--- a/solution.py
+++ b/solution.py
@@ -95,9 +95,36 @@
         copy.wait()
 
 
+def carried(source_ref, start, out_ref, sems):
+    count = sems.shape[0]
+    rows = out_ref.shape[0] // count
+    return [
+        pltpu.make_async_copy(
+            source_ref.at[pl.ds(start + i * rows, rows)], out_ref.at[pl.ds(i * rows, rows)], sems.at[i]
+        )
+        for i in range(count)
+    ]
+
+
 def own_kernel(
-    heads, seq, lengths_ref, prompt_ref, q_ref, rk_ref, rv_ref, k_ref, v_ref, gate_ref, own_ref
+    heads,
+    seq,
+    lengths_ref,
+    prompt_ref,
+    q_ref,
+    rk_ref,
+    rv_ref,
+    k_ref,
+    v_ref,
+    source_ref,
+    gate_ref,
+    own_ref,
+    weight_ref,
+    sems,
 ):
+    copies = carried(source_ref, 0, weight_ref, sems)
+    for copy in copies:
+        copy.start()
     rows = q_ref.shape[0]
     row = lax.broadcasted_iota(jnp.int32, (rows, rows), 0)
     col = lax.broadcasted_iota(jnp.int32, (rows, rows), 1)
@@ -121,6 +148,8 @@
         own_ref[:, p] = (first * left + second * right) / (left + right)
         packed = jnp.where(lane == h, peak + jnp.log(left + right), packed)
     own_ref[:, heads * HEAD_DIM :] = packed
+    for copy in copies:
+        copy.wait()
 
 
 def wanted_prompts(seq, rows, prompt_ref):
@@ -149,8 +178,12 @@
 
 
 def project_kernel(heads, seq, share, wide, group_size, key_rows, prompt_ref, own_ref, *refs):
-    got_refs, weight_ref = refs[: group_size - 1], refs[group_size - 1]
-    out_refs, (attended_ref, partial_ref) = refs[group_size:-2], refs[-2:]
+    got_refs, refs = refs[: group_size - 1], refs[group_size - 1 :]
+    weight_ref, source_ref, send_left_ref, keep_left_ref, keep_right_ref = refs[:5]
+    send_right_refs, (quarter_ref, attended_ref, partial_ref, sems) = refs[5:-4], refs[-4:]
+    copies = carried(source_ref, 0, quarter_ref, sems)
+    for copy in copies:
+        copy.start()
     rows = own_ref.shape[0]
     wanted = wanted_prompts(seq, rows, prompt_ref)
     group = lax.axis_index("group")
@@ -176,25 +209,53 @@
         attended_ref[:, part] = (mixed / total).astype(BF16)
 
     me = lax.axis_index("tensor")
-
-    @pl.loop(0, weight_ref.shape[1] // wide)
+    blocks = rows // share
+    half = send_left_ref.shape[2]
+
+    def multiply(columns):
+        partial = jnp.dot(attended_ref[...], weight_ref[:, columns], preferred_element_type=F32)
+        for b in range(blocks):
+            partial_ref[b] = partial[b * share : (b + 1) * share]
+
+    @pl.loop(0, half // wide)
     def _(n):
         columns = pl.ds(pl.multiple_of(n * wide, 128), wide)
-        partial = jnp.dot(attended_ref[...], weight_ref[:, columns], preferred_element_type=F32)
-        for b in range(rows // share):
-            partial_ref[b] = partial[b * share : (b + 1) * share]
-        for d, ref in enumerate(out_refs):
-            ref[:, columns] = partial_ref[me ^ d].astype(ref.dtype)
-
-
-def fetch_kernel(start, count, source_ref, gate_ref, out_ref, sems):
-    rows = out_ref.shape[0] // count
-    copies = [
-        pltpu.make_async_copy(
-            source_ref.at[pl.ds(start + i * rows, rows)], out_ref.at[pl.ds(i * rows, rows)], sems.at[i]
-        )
-        for i in range(count)
-    ]
+        multiply(columns)
+        for d in range(0, blocks, 2):
+            keep_left_ref[d // 2, :, columns] = partial_ref[me ^ d]
+            send_left_ref[d // 2, :, columns] = partial_ref[me ^ (d + 1)].astype(BF16)
+
+    @pl.loop(0, half // wide)
+    def _(n):
+        columns = pl.ds(pl.multiple_of(n * wide, 128), wide)
+        multiply(pl.ds(pl.multiple_of(half + n * wide, 128), wide))
+        for d in range(blocks):
+            block = partial_ref[me ^ d]
+            if d < 2:
+                keep_right_ref[d, :, columns] = block
+            else:
+                send_right_refs[d // 2 - 1][d % 2, :, columns] = block.astype(BF16)
+
+    for copy in copies:
+        copy.wait()
+
+
+def fold_left_kernel(gate_ref, keep_ref, got_ref, *out_refs):
+    for i, ref in enumerate(out_refs):
+        ref[...] = (keep_ref[i] + got_ref[i].astype(F32)).astype(ref.dtype)
+
+
+def fold_right_kernel(gate_ref, keep_ref, *refs):
+    got_refs, out_refs = refs[:-2], refs[-2:]
+    for i, ref in enumerate(out_refs):
+        total = keep_ref[i]
+        for got_ref in got_refs:
+            total = total + got_ref[i].astype(F32)
+        ref[...] = total.astype(ref.dtype)
+
+
+def fetch_kernel(start, source_ref, gate_ref, out_ref, sems):
+    copies = carried(source_ref, start, out_ref, sems)
     for copy in copies:
         copy.start()
     for copy in copies:
@@ -209,14 +270,21 @@
             out_ref[i] = ref[:, half * width : (half + 1) * width]
 
 
-def norm_kernel(residual_ref, gain_ref, *refs):
-    terms, out_ref = refs[3:-1], refs[-1]
-    hidden = residual_ref[lax.axis_index("tensor")].astype(F32)
-    for ref in terms:
-        hidden = hidden + ref[...].astype(F32)
-    squares = jnp.mean(hidden * hidden, axis=-1, keepdims=True)
-    normed = (hidden * lax.rsqrt(squares + 1e-06) * gain_ref[...].astype(F32)).astype(BF16)
-    out_ref[...] = normed
+def norm_kernel(far_count, residual_ref, gain_ref, *refs):
+    left_refs, right_refs, out_ref = refs[: 1 + far_count], refs[1 + far_count : -1], refs[-1]
+    residual = residual_ref[lax.axis_index("tensor")].astype(F32)
+    width = residual.shape[1] // 2
+    halves = []
+    for i, terms in enumerate((left_refs, right_refs)):
+        hidden = residual[:, i * width : (i + 1) * width]
+        for ref in terms:
+            hidden = hidden + ref[...].astype(F32)
+        halves.append(hidden)
+    squares = sum(jnp.sum(hidden * hidden, axis=-1, keepdims=True) for hidden in halves)
+    scale = lax.rsqrt(squares / residual.shape[1] + 1e-06)
+    for i, hidden in enumerate(halves):
+        columns = slice(i * width, (i + 1) * width)
+        out_ref[:, columns] = (hidden * scale * gain_ref[:, columns].astype(F32)).astype(BF16)
 
 
 def quarter_dots(x_ref, weight_refs, columns):
@@ -230,7 +298,12 @@
     )
 
 
-def first_kernel(narrow, left_ref, right_ref, weight_ref, next_ref, out_ref, x_ref):
+def first_kernel(
+    narrow, left_ref, right_ref, weight_ref, next_ref, source_ref, out_ref, last_ref, x_ref, sems
+):
+    copies = carried(source_ref, source_ref.shape[0] - last_ref.shape[0], last_ref, sems)
+    for copy in copies:
+        copy.start()
     half = left_ref.shape[0]
     x_ref[:half] = left_ref[...]
     x_ref[half:] = right_ref[...]
@@ -239,6 +312,9 @@
     def _(n):
         columns = pl.ds(n * narrow if narrow % 128 else pl.multiple_of(n * narrow, 128), narrow)
         out_ref[:, columns] = quarter_dots(x_ref, (weight_ref, next_ref), columns)
+
+    for copy in copies:
+        copy.wait()
 
 
 def logits_kernel(
@@ -372,20 +448,34 @@
         name="prefix_attention",
     )(*map(held, queries), keys, values)
     got = [swap(x, "group", d, group_size) for x, d in zip(answers, distances)]
-    own = pl.pallas_call(
+    own, weight = pl.pallas_call(
         functools.partial(own_kernel, heads, seq),
-        out_shape=jax.ShapeDtypeStruct((rows, span + 128), F32),
-        in_specs=[smem()] * 2 + [vmem()] * 5 + [anywhere()],
-        out_specs=vmem(),
+        out_shape=[
+            jax.ShapeDtypeStruct((rows, span + 128), F32),
+            pltpu.VMEM(out_weight.shape, BF16),
+        ],
+        in_specs=[smem()] * 2 + [vmem()] * 5 + [anywhere()] * 2,
+        out_specs=[vmem()] * 2,
+        scratch_shapes=[pltpu.SemaphoreType.DMA((4,))],
         compiler_params=params(6),
         cost_estimate=cost(moved=8 * MIB),
         name="own_attention",
-    )(stored(lengths), stored(prompt_of), query, own_keys, own_values, keys, values, answers[0])
+    )(
+        stored(lengths),
+        stored(prompt_of),
+        query,
+        own_keys,
+        own_values,
+        keys,
+        values,
+        stored(out_weight),
+        answers[0],
+    )
 
     def fetch(source, start, count, gate):
         return held(
             pl.pallas_call(
-                functools.partial(fetch_kernel, start, 4),
+                functools.partial(fetch_kernel, start),
                 out_shape=pltpu.VMEM((count, source.shape[1]), BF16),
                 in_specs=[anywhere()] * 2,
                 out_specs=vmem(),
@@ -396,55 +486,83 @@
             )(stored(source), gate)
         )
 
-    weight = fetch(out_weight, 0, span, answers[0])
-
-    wide = 1024 if depth % 1024 == 0 else depth
-    shares = pl.pallas_call(
+    half = depth // 2
+    quarter = depth // 4
+    wide = 1280 if half % 1280 == 0 else half
+    pairs = tensor_size // 2
+    send_left, keep_left, keep_right, *rest = pl.pallas_call(
         functools.partial(project_kernel, heads, seq, share, wide, group_size, key_rows),
         out_shape=[
-            jax.ShapeDtypeStruct((share, depth), BF16 if d else F32) for d in range(tensor_size)
-        ],
-        in_specs=[smem()] + [vmem()] * (2 + len(distances)),
-        out_specs=[vmem()] * tensor_size,
+            jax.ShapeDtypeStruct((pairs, share, half), BF16),
+            jax.ShapeDtypeStruct((pairs, share, half), F32),
+            jax.ShapeDtypeStruct((2, share, half), F32),
+        ]
+        + [jax.ShapeDtypeStruct((2, share, half), BF16)] * (pairs - 1)
+        + [pltpu.VMEM((quarter, vocab), BF16)],
+        in_specs=[smem()] + [vmem()] * (2 + len(distances)) + [anywhere()],
+        out_specs=[vmem()] * (3 + pairs),
         scratch_shapes=[
             pltpu.VMEM((rows, span), BF16),
             pltpu.VMEM((tensor_size, share, wide), F32),
+            pltpu.SemaphoreType.DMA((4,)),
         ],
         compiler_params=params(6),
+        cost_estimate=cost(moved=quarter * vocab * 2),
         name="project",
-    )(stored(prompt_of), *map(held, (own, *got)), weight)
-    quarter = depth // 4
-    quarters = [fetch(lm_weight, i * quarter, quarter, shares[1]) for i in range(3)]
-
-    got = [swap(shares[d], "tensor", d, tensor_size) for d in range(tensor_size - 1, 0, -1)]
+    )(stored(prompt_of), *map(held, (own, *got)), held(weight), stored(lm_weight))
+    quarters = [held(rest.pop()), fetch(lm_weight, quarter, quarter, send_left)]
+
+    far = list(range(2, tensor_size, 2))
+    got_left = swap(send_left, "tensor", 1, tensor_size)
+    got_right = [swap(x, "tensor", d, tensor_size) for x, d in zip(rest[::-1], far[::-1])]
+    left = pl.pallas_call(
+        fold_left_kernel,
+        out_shape=[jax.ShapeDtypeStruct((share, half), F32)]
+        + [jax.ShapeDtypeStruct((share, half), BF16)] * len(far),
+        in_specs=[anywhere()] + [vmem()] * 2,
+        out_specs=[vmem()] * (1 + len(far)),
+        compiler_params=params(2),
+        name="fold_left",
+    )(quarters[1], held(keep_left), held(got_left))
+    got_left = [swap(x, "tensor", d, tensor_size) for x, d in zip(left[:0:-1], far[::-1])]
+    right = pl.pallas_call(
+        fold_right_kernel,
+        out_shape=[
+            jax.ShapeDtypeStruct((share, half), F32),
+            jax.ShapeDtypeStruct((share, half), BF16),
+        ],
+        in_specs=[anywhere()] + [vmem()] * (1 + len(far)),
+        out_specs=[vmem()] * 2,
+        compiler_params=params(2),
+        name="fold_right",
+    )(left[1], *map(held, (keep_right, *got_right)))
+    got_right = swap(right[1], "tensor", 1, tensor_size)
     normed = pl.pallas_call(
-        norm_kernel,
+        functools.partial(norm_kernel, len(far)),
         out_shape=jax.ShapeDtypeStruct((share, depth), BF16),
-        in_specs=[vmem()] * 2 + [anywhere()] * 3 + [vmem()] * tensor_size,
+        in_specs=[vmem()] * (5 + len(far)),
         out_specs=vmem(),
         compiler_params=params(4),
         name="norm",
     )(
         *map(held, (residual.reshape(tensor_size, share, depth), norm_gain[None])),
-        *quarters,
-        *map(held, (shares[0], *got)),
+        *map(held, (left[0], *got_left, right[0], got_right)),
     )
 
-    far = list(range(2, tensor_size, 2))
     above = list(range(2, group_size, 2))
     order = [0] + far
     here = [(g, x) for g in [0] + above for x in (0, 1)]
     column = [swap(normed, "tensor", d, tensor_size) for d in far[::-1]]
     column = [normed] + column[::-1]
-    quarters.append(fetch(lm_weight, 3 * quarter, quarter, normed))
+    quarters.append(fetch(lm_weight, 2 * quarter, quarter, normed))
     columns = pl.pallas_call(
         functools.partial(column_kernel, len(column)),
-        out_shape=[jax.ShapeDtypeStruct((len(column), share, depth // 2), BF16)] * 2,
+        out_shape=[jax.ShapeDtypeStruct((len(column), share, half), BF16)] * 2,
         in_specs=[vmem()] * len(column) + [anywhere()],
         out_specs=[vmem()] * 2,
         compiler_params=params(2),
         name="column",
-    )(*map(held, column), quarters[3])
+    )(*map(held, column), quarters[2])
     left, right = columns
     left = jnp.concatenate([left, swap(left, "tensor", 1, tensor_size)])
     right = [right] + [swap(right, "group", d, group_size) for d in above]
@@ -454,35 +572,38 @@
     right = [x for pair in zip(right, across) for x in pair]
     halves = []
     for pieces in (left, right):
-        tokens = jnp.concatenate(pieces).reshape(-1, depth // 2)
+        tokens = jnp.concatenate(pieces).reshape(-1, half)
         halves.append((tokens, swap(tokens, "group", 1, group_size)))
     spots = [(g + c, t + x) for c in (0, 1) for g, x in here for t in order]
     total_rows = 2 * tokens.shape[0]
     narrow = 1536 if vocab % 1536 == 0 else vocab
     limit = 10 if total_rows <= 256 else 24
-    work = 2 * total_rows * (depth // 2) * vocab
-    first = pl.pallas_call(
+    work = 2 * total_rows * (half) * vocab
+    first, last = pl.pallas_call(
         functools.partial(first_kernel, narrow),
-        out_shape=pltpu.VMEM((total_rows, vocab), F32),
-        in_specs=[vmem()] * 4,
-        out_specs=vmem(),
-        scratch_shapes=[pltpu.VMEM((total_rows, depth // 2), BF16)],
+        out_shape=[pltpu.VMEM((total_rows, vocab), F32), pltpu.VMEM((quarter, vocab), BF16)],
+        in_specs=[vmem()] * 4 + [anywhere()],
+        out_specs=[vmem()] * 2,
+        scratch_shapes=[
+            pltpu.VMEM((total_rows, half), BF16),
+            pltpu.SemaphoreType.DMA((4,)),
+        ],
         compiler_params=params(limit),
         cost_estimate=cost(flops=work),
         name="logits_first",
-    )(*map(held, (*halves[0], *quarters[:2])))
+    )(*map(held, (*halves[0], *quarters[:2])), stored(lm_weight))
     stats = pl.pallas_call(
         functools.partial(logits_kernel, narrow, spots, tensor_size),
         out_shape=jax.ShapeDtypeStruct((len(spots), 1, 128), F32),
         in_specs=[vmem()] * 6,
         out_specs=vmem(),
-        scratch_shapes=[pltpu.VMEM((total_rows, depth // 2), BF16)]
+        scratch_shapes=[pltpu.VMEM((total_rows, half), BF16)]
         + [pltpu.VMEM((total_rows, 128), F32)] * 3
         + [pltpu.VMEM((total_rows, 1), i32)],
         compiler_params=params(limit),
         cost_estimate=cost(flops=work),
         name="logits",
-    )(*map(held, (first, *halves[1])), wanted, *map(held, quarters[2:]))
+    )(*map(held, (first, *halves[1])), wanted, held(quarters[2]), held(last))
 
     stats = lax.all_to_all(stats, ("group", "tensor"), 0, 0, tiled=True)
     return pl.pallas_call(

time: 92.8 us -> 83.9 us (0.904)
  Pallas kernels: 34.3 us -> 28 us
  waiting for transfers between devices: 14.6 us -> 19.5 us
  starting transfers between devices: 30 us -> 25.4 us
  blocking collectives: 12.3 us -> 9.46 us
    pallas_call x8 -> x7, Pallas kernels: 22 us -> 14.8 us  [the longest x2 6.69 us: fetch(): pl.pallas_call(functools.partial(fetch_kernel, start), out_shape=pltpu.VM...]
    ppermute x22 -> x23, waiting for transfers between devices: 14.6 us -> 19.5 us  [swap(): return lax.ppermute(x, axis, [(i, i ^ distance) for i in range(size)])]
    ppermute x22 -> x23, starting transfers between devices: 30 us -> 25.4 us  [swap(): return lax.ppermute(x, axis, [(i, i ^ distance) for i in range(size)])]
    all_to_all x1, blocking collectives: 12.3 us -> 9.46 us  [local(): stats = lax.all_to_all(stats, ('group', 'tensor'), 0, 0, tiled=True)]
    pallas_call x1, Pallas kernels: 3.33 us -> 4.27 us  [local(): pl.pallas_call(functools.partial(project_kernel, heads, seq, share, wide,...]
  transfers between devices with their start and end apart: 22 -> 23, of which waited for: 9 -> 11; matrix products, arithmetic and copies ran while one was open for 1% -> 1% of each run, Pallas kernels for 25% -> 19%
where the time goes in v5:
time: 83.9 us; the launch traced here: 83.7 us
  Pallas kernels  28 us (33%)
  starting transfers between devices  25.4 us (30%)
  waiting for transfers between devices  19.5 us (23%)
  blocking collectives  9.46 us (11%)
  local copies, waits for them, and re-layouts  0.93 us (1%)
    ppermute x23, starting transfers between devices, swap(): return lax.ppermute(x, axis, [(i, i ^ distance) for i in range(size)])  25.4 us
    ppermute x23, waiting for transfers between devices, swap(): return lax.ppermute(x, axis, [(i, i ^ distance) for i in range(size)])  19.5 us
    all_to_all x1, blocking collectives, local(): stats = lax.all_to_all(stats, ('group', 'tensor'), 0, 0, tiled=True)  9.46 us
    pallas_call x2, Pallas kernels, fetch(): pl.pallas_call(functools.partial(fetch_kernel, start), out_shape=pltpu.VM...  6.69 us
    pallas_call x1, Pallas kernels, local(): pl.pallas_call(functools.partial(logits_kernel, narrow, spots, tensor_siz...  5.43 us
    pallas_call x1, Pallas kernels, local(): pl.pallas_call(functools.partial(first_kernel, narrow), out_shape=[pltpu....  4.52 us
    pallas_call x1, Pallas kernels, local(): pl.pallas_call(functools.partial(project_kernel, heads, seq, share, wide,...  4.27 us
    pallas_call x1, Pallas kernels, local(): pl.pallas_call(functools.partial(own_kernel, heads, seq), out_shape=[jax....  3.37 us
  transfers between devices with their start and end apart: 23, of which 11 were waited for; matrix products, arithmetic and copies ran while one was open for 1% of the time, Pallas kernels for 19%

profile of v5, /device:TPU:0, one launch (start us, length us, event | category | flops | bytes accessed | tf_op | source)
XLA Modules:
  0.0 83.7 jit_solution(15290848679344499986)
XLA Ops:
  0.5 2.5 %collective-permute-start.1 = (bf16[64,512]{1,0:T(8,128)(2,1)}, bf16[64,512]{1,0:T(8,128)(2,1)S(1)}, u32[]{:S(2)}, u32[]{:S(2)}) collective-permute-start(bf16[64,512]{1,0:T(8,128)(2,1)} %refs_0_.1), channel_id=1, source_target_pairs={{0,16},{8,24},{16,0},{24,8},{1,17},{9,25},{17,1},{25,9},{2,18},{10... | collective-permute-start | bytes 196616 | tf_op jit(solution)/shard_map/ppermute | solution.py:47
  3.1 0.9 %reshape.16.gate_ref.target_ref = s32[32,8,1]{2,1,0:T(8,128)S(1)} reshape(s32[256]{0:T(256)} %param.23) | data formatting | bytes 2048 | tf_op jit(solution)/shard_map/reshape | solution.py:429
  4.0 1.4 %load.1 = (bf16[64,512]{1,0:T(8,128)(2,1)S(1)}, bf16[64,512]{1,0:T(8,128)(2,1)S(1)}, bf16[64,512]{1,0:T(8,128)(2,1)S(1)}, bf16[512,512]{1,0:T(8,128)(2,1)S(1)}, bf16[512,512]{1,0:T(8,128)(2,1)S(1)}) custom-call(s32[32,8,1]{2,1,0:T(8,128)S(1)} %reshape.16.gate_ref.target_ref, bf16[64,512]{1,0:T(8,128)(2,1)} %refs_0_.1, bf16[64,512]{1,0:T(8,128)(2,1)} %refs_1_.1, ...), custom_call_target="tpu_custom_call" | custom-call | bytes 2097152 | tf_op jit(solution)/shard_map/load/pallas_call | solution.py:431
  5.9 1.3 %collective-permute-done.2.refs_2_ = bf16[64,512]{1,0:T(8,128)(2,1)S(1)} collective-permute-done((bf16[64,512]{1,0:T(8,128)(2,1)}, bf16[64,512]{1,0:T(8,128)(2,1)S(1)}, u32[]{:S(2)}, u32[]{:S(2)}) %collective-permute-start.2) | collective-permute-done | bytes 65568 | tf_op jit(solution)/shard_map/ppermute | solution.py:47
  7.3 0.8 %prefix_attention.1 = (bf16[64,640]{1,0:T(8,128)(2,1)S(1)}, bf16[64,640]{1,0:T(8,128)(2,1)S(1)}, bf16[64,640]{1,0:T(8,128)(2,1)S(1)}) custom-call(bf16[64,512]{1,0:T(8,128)(2,1)S(1)} %collective-permute-done.refs_0_, bf16[64,512]{1,0:T(8,128)(2,1)S(1)} %collective-permute-done.1.refs_1_, bf16[64,512]{1,0:T(8,128)(2,1)S(1)} %collective-permute-done.2.refs_2_, ...), custom_call_target="tpu_custom_call" | custom-call | tf_op jit(solution)/shard_map/prefix_attention/pallas_call | solution.py:442
  8.3 1.5 %collective-permute-start.4 = (bf16[64,640]{1,0:T(8,128)(2,1)S(1)}, bf16[64,640]{1,0:T(8,128)(2,1)S(1)}, u32[]{:S(2)}, u32[]{:S(2)}) collective-permute-start(bf16[64,640]{1,0:T(8,128)(2,1)S(1)} %get-tuple-element.39), channel_id=1, source_target_pairs={{0,16},{8,24},{16,0},{24,8},{1,17},{9,25},{17,1},{25,9},{2,18},{10... | collective-permute-start | bytes 245768 | tf_op jit(solution)/shard_map/ppermute | solution.py:47
  10.0 3.4 %own_attention.1 = (f32[64,640]{1,0:T(8,128)S(1)}, bf16[512,5120]{1,0:T(8,128)(2,1)S(1)}) custom-call(s32[2]{0:T(128)} %lengths_ref.3, s32[2]{0:T(128)} %prompt_ref.3, bf16[64,512]{1,0:T(8,128)(2,1)S(1)} %get-tuple-element.32.q_ref, bf16[64,512]{1,0:T(8,128)(2,1)S(1)} %get-tuple-element.33.rk_ref, bf16[64,512]{1,0:T(8,128)(2,1)S(1)} %get-tuple-element.34.rv_ref, ...), custom_call_target="tpu_custom_call" | custom-call | bytes 8388608 | tf_op jit(solution)/shard_map/own_attention/pallas_call | solution.py:451
  13.4 1.1 %collective-permute-done.5.refs_2_ = bf16[64,640]{1,0:T(8,128)(2,1)S(1)} collective-permute-done((bf16[64,640]{1,0:T(8,128)(2,1)S(1)}, bf16[64,640]{1,0:T(8,128)(2,1)S(1)}, u32[]{:S(2)}, u32[]{:S(2)}) %collective-permute-start.5) | collective-permute-done | bytes 81952 | tf_op jit(solution)/shard_map/ppermute | solution.py:47
  14.6 4.3 %project.1 = (bf16[4,8,2560]{2,1,0:T(8,128)(2,1)S(1)}, f32[4,8,2560]{2,1,0:T(8,128)S(1)}, f32[2,8,2560]{2,1,0:T(8,128)S(1)}, bf16[2,8,2560]{2,1,0:T(8,128)(2,1)S...) custom-call(s32[2]{0:T(128)} %prompt_ref.3, ...), custom_call_target="tpu_custom_call" | custom-call | bytes 7864320 | tf_op jit(solution)/shard_map/project/pallas_call | solution.py:493
  18.8 1.6 %collective-permute-start.6 = (bf16[4,8,2560]{2,1,0:T(8,128)(2,1)S(1)}, bf16[4,8,2560]{2,1,0:T(8,128)(2,1)S(1)}, u32[]{:S(2)}, u32[]{:S(2)}) collective-permute-start(bf16[4,8,2560]{2,1,0:T(8,128)(2,1)S(1)} %get-tuple-element.42.gate_ref), channel_id=1, source_target_pairs={{0,1},{1,0},{2,3},{3,2},{4,5},{5,4},{6,7},{7,6},{8,9},{9,8},{10,11... | collective-permute-start | bytes 491528 | tf_op jit(solution)/shard_map/ppermute | solution.py:47
  20.4 3.6 %collective-permute-start.10 = (bf16[2,8,2560]{2,1,0:T(8,128)(2,1)S(1)}, bf16[2,8,2560]{2,1,0:T(8,128)(2,1)S(1)}, u32[]{:S(2)}, u32[]{:S(2)}) collective-permute-start(bf16[2,8,2560]{2,1,0:T(8,128)(2,1)S(1)} %get-tuple-element.49), channel_id=1, source_target_pairs={{0,6},{1,7},{2,4},{3,5},{4,2},{5,3},{6,0},{7,1},{8,14},{9,15},{10,... | collective-permute-start | bytes 245768 | tf_op jit(solution)/shard_map/ppermute | solution.py:47
  24.0 0.8 collective-permute-start.12
  24.8 3.3 %fetch.2.gate_ref.next_ref = bf16[1280,3072]{1,0:T(8,128)(2,1)S(1)} custom-call(bf16[5120,3072]{1,0:T(8,128)(2,1)} %source_ref.7, bf16[4,8,2560]{2,1,0:T(8,128)(2,1)S(1)} %get-tuple-element.42.gate_ref), custom_call_target="tpu_custom_call" | custom-call | bytes 7864320 | tf_op jit(solution)/shard_map/fetch/pallas_call | solution.py:477
  28.2 3.7 %collective-permute-start.7 = (bf16[8,2560]{1,0:T(8,128)(2,1)S(1)}, bf16[8,2560]{1,0:T(8,128)(2,1)S(1)}, u32[]{:S(2)}, u32[]{:S(2)}) collective-permute-start(bf16[8,2560]{1,0:T(8,128)(2,1)S(1)} %get-tuple-element.45), channel_id=1, source_target_pairs={{0,6},{1,7},{2,4},{3,5},{4,2},{5,3},{6,0},{7,1},{8,14},{9,15},{10,... | collective-permute-start | bytes 122888 | tf_op jit(solution)/shard_map/ppermute | solution.py:47
  31.9 0.8 collective-permute-start.9
  33.4 0.7 collective-permute-done.7.refs_1_
  34.1 2.7 %collective-permute-done.8.refs_2_ = bf16[8,2560]{1,0:T(8,128)(2,1)S(1)} collective-permute-done((bf16[8,2560]{1,0:T(8,128)(2,1)S(1)}, bf16[8,2560]{1,0:T(8,128)(2,1)S(1)}, u32[]{:S(2)}, u32[]{:S(2)}) %collective-permute-start.8) | collective-permute-done | bytes 40992 | tf_op jit(solution)/shard_map/ppermute | solution.py:47
  37.0 1.3 %collective-permute-start.14 = (bf16[8,5120]{1,0:T(8,128)(2,1)S(1)}, bf16[8,5120]{1,0:T(8,128)(2,1)S(1)}, u32[]{:S(2)}, u32[]{:S(2)}) collective-permute-start(bf16[8,5120]{1,0:T(8,128)(2,1)S(1)} %norm.1.gate_ref.refs_0_), channel_id=1, source_target_pairs={{0,2},{1,3},{2,0},{3,1},{4,6},{5,7},{6,4},{7,5},{8,10},{9,11},{10,... | collective-permute-start | bytes 245768 | tf_op jit(solution)/shard_map/ppermute | solution.py:47
  38.3 2.9 %collective-permute-start.15 = (bf16[8,5120]{1,0:T(8,128)(2,1)S(1)}, bf16[8,5120]{1,0:T(8,128)(2,1)S(1)}, u32[]{:S(2)}, u32[]{:S(2)}) collective-permute-start(bf16[8,5120]{1,0:T(8,128)(2,1)S(1)} %norm.1.gate_ref.refs_0_), channel_id=1, source_target_pairs={{0,4},{1,5},{2,6},{3,7},{4,0},{5,1},{6,2},{7,3},{8,12},{9,13},{10,... | collective-permute-start | bytes 245768 | tf_op jit(solution)/shard_map/ppermute | solution.py:47
  41.4 3.3 %fetch.3.refs_4_.weight_ref = bf16[1280,3072]{1,0:T(8,128)(2,1)S(1)} custom-call(bf16[5120,3072]{1,0:T(8,128)(2,1)} %source_ref.7, bf16[8,5120]{1,0:T(8,128)(2,1)S(1)} %norm.1.gate_ref.refs_0_), custom_call_target="tpu_custom_call" | custom-call | bytes 7864320 | tf_op jit(solution)/shard_map/fetch/pallas_call | solution.py:477
  45.2 2.3 %collective-permute-done.16.refs_3_ = bf16[8,5120]{1,0:T(8,128)(2,1)S(1)} collective-permute-done((bf16[8,5120]{1,0:T(8,128)(2,1)S(1)}, bf16[8,5120]{1,0:T(8,128)(2,1)S(1)}, u32[]{:S(2)}, u32[]{:S(2)}) %collective-permute-start.16) | collective-permute-done | bytes 81952 | tf_op jit(solution)/shard_map/ppermute | solution.py:47
  47.5 0.6 collective-permute-start.17
  48.1 1.0 %collective-permute-start.20 = (bf16[4,8,2560]{2,1,0:T(8,128)(2,1)S(1)}, bf16[4,8,2560]{2,1,0:T(8,128)(2,1)S(1)}, u32[]{:S(2)}, u32[]{:S(2)}) collective-permute-start(bf16[4,8,2560]{2,1,0:T(8,128)(2,1)S(1)} %get-tuple-element.57), channel_id=1, source_target_pairs={{0,16},{8,24},{16,0},{24,8},{1,17},{9,25},{17,1},{25,9},{2,18},{10... | collective-permute-start | bytes 491528 | tf_op jit(solution)/shard_map/ppermute | solution.py:47
  49.1 4.5 %collective-permute-done.17 = bf16[4,8,2560]{2,1,0:T(8,128)(2,1)S(1)} collective-permute-done((bf16[4,8,2560]{2,1,0:T(8,128)(2,1)S(1)}, bf16[4,8,2560]{2,1,0:T(8,128)(2,1)S(1)}, u32[]{:S(2)}, u32[]{:S(2)}) %collective-permute-start.17) | collective-permute-done | bytes 163872 | tf_op jit(solution)/shard_map/ppermute | solution.py:47
  53.6 1.5 %collective-permute-start.18 = (bf16[8,8,2560]{2,1,0:T(8,128)(2,1)S(1)}, bf16[8,8,2560]{2,1,0:T(8,128)(2,1)S(1)}, u32[]{:S(2)}, u32[]{:S(2)}) collective-permute-start(bf16[8,8,2560]{2,1,0:T(8,128)(2,1)S(1)} %pad_maximum_fusion), channel_id=1, source_target_pairs={{0,16},{8,24},{16,0},{24,8},{1,17},{9,25},{17,1},{25,9},{2,18},{10... | collective-permute-start | bytes 983048 | tf_op jit(solution)/shard_map/ppermute | solution.py:47
  55.2 1.6 %collective-permute-start.21 = (bf16[8,8,2560]{2,1,0:T(8,128)(2,1)S(1)}, bf16[8,8,2560]{2,1,0:T(8,128)(2,1)S(1)}, u32[]{:S(2)}, u32[]{:S(2)}) collective-permute-start(bf16[8,8,2560]{2,1,0:T(8,128)(2,1)S(1)} %pad_maximum_fusion.1), channel_id=1, source_target_pairs={{0,1},{1,0},{2,3},{3,2},{4,5},{5,4},{6,7},{7,6},{8,9},{9,8},{10,11... | collective-permute-start | bytes 983048 | tf_op jit(solution)/shard_map/ppermute | solution.py:47
  56.8 4.0 %collective-permute-done.18 = bf16[8,8,2560]{2,1,0:T(8,128)(2,1)S(1)} collective-permute-done((bf16[8,8,2560]{2,1,0:T(8,128)(2,1)S(1)}, bf16[8,8,2560]{2,1,0:T(8,128)(2,1)S(1)}, u32[]{:S(2)}, u32[]{:S(2)}) %collective-permute-start.18) | collective-permute-done | bytes 327712 | tf_op jit(solution)/shard_map/ppermute | solution.py:47
  60.9 1.4 %collective-permute-done.21 = bf16[8,8,2560]{2,1,0:T(8,128)(2,1)S(1)} collective-permute-done((bf16[8,8,2560]{2,1,0:T(8,128)(2,1)S(1)}, bf16[8,8,2560]{2,1,0:T(8,128)(2,1)S(1)}, u32[]{:S(2)}, u32[]{:S(2)}) %collective-permute-start.21) | collective-permute-done | bytes 327712 | tf_op jit(solution)/shard_map/ppermute | solution.py:47
  63.0 4.5 %logits_first.1 = (f32[256,3072]{1,0:T(8,128)S(1)}, bf16[1280,3072]{1,0:T(8,128)(2,1)S(1)}) custom-call(bf16[128,2560]{1,0:T(8,128)(2,1)S(1)} %maximum_bitcast_fusion.left_ref, bf16[128,2560]{1,0:T(8,128)(2,1)S(1)} %collective-permute-done.19.right_ref, bf16[1280,3072]{1,0:T(8,128)(2,1)S(1)} %get-tuple-element.55.weight_ref, ...), custom_call_target="tpu_custom_call" | custom-call | flops 4026531840 | tf_op jit(solution)/shard_map/logits_first/pallas_call | solution.py:582
  67.6 5.4 %logits.1 = f32[32,1,128]{2,1,0:T(1,128)S(1)} custom-call(f32[256,3072]{1,0:T(8,128)S(1)} %get-tuple-element.56.sum_in_ref, bf16[128,2560]{1,0:T(8,128)(2,1)S(1)} %maximum_bitcast_fusion.1.left_ref, bf16[128,2560]{1,0:T(8,128)(2,1)S(1)} %collective-permute-done.22.right_ref, s32[32,8,1]{2,1,0:T(8,128)S(1)} %reshape.16.gate_ref.target_ref, ...), custom_call_target="tpu_custom_call" | custom-call | flops 4026531840 | tf_op jit(solution)/shard_map/logits/pallas_call | solution.py:595
  73.0 9.5 %all_to_all.5.stats_ref = f32[32,1,128]{2,1,0:T(1,128)S(1)} all-to-all(f32[32,1,128]{2,1,0:T(1,128)S(1)} %logits.1), channel_id=1, replica_groups=mesh['group'=4,'tensor'=8] {'group','tensor'}, dimensions={0} | all-to-all | bytes 32768 | tf_op jit(solution)/shard_map/all_to_all | solution.py:608
  82.4 1.3 %final.1 = f32[8]{0:T(128)} custom-call(s32[2]{0:T(128)} %lengths_ref.3, f32[32,1,128]{2,1,0:T(1,128)S(1)} %all_to_all.5.stats_ref), custom_call_target="tpu_custom_call" | custom-call | tf_op jit(solution)/shard_map/final/pallas_call | solution.py:609
  (39 shorter events, 4.0 us)
Async XLA Ops:
  0.0 5.4 %collective-permute-start = (bf16[64,512]{1,0:T(8,128)(2,1)}, bf16[64,512]{1,0:T(8,128)(2,1)S(1)}, u32[]{:S(2)}, u32[]{:S(2)}) collective-permute-start(bf16[64,512]{1,0:T(8,128)(2,1)} %refs_0_.1), channel_id=1, source_target_pairs={{0,8},{8,0},{16,24},{24,16},{1,9},{9,1},{17,25},{25,17},{2,10},{10... | collective-permute-start | bytes 196616 | tf_op jit(solution)/shard_map/ppermute | solution.py:47
  0.5 5.5 %collective-permute-start.1 = (bf16[64,512]{1,0:T(8,128)(2,1)}, bf16[64,512]{1,0:T(8,128)(2,1)S(1)}, u32[]{:S(2)}, u32[]{:S(2)}) collective-permute-start(bf16[64,512]{1,0:T(8,128)(2,1)} %refs_0_.1), channel_id=1, source_target_pairs={{0,16},{8,24},{16,0},{24,8},{1,17},{9,25},{17,1},{25,9},{2,18},{10... | collective-permute-start | bytes 196616 | tf_op jit(solution)/shard_map/ppermute | solution.py:47
  3.0 4.3 %collective-permute-start.2 = (bf16[64,512]{1,0:T(8,128)(2,1)}, bf16[64,512]{1,0:T(8,128)(2,1)S(1)}, u32[]{:S(2)}, u32[]{:S(2)}) collective-permute-start(bf16[64,512]{1,0:T(8,128)(2,1)} %refs_0_.1), channel_id=1, source_target_pairs={{0,24},{8,16},{16,8},{24,0},{1,25},{9,17},{17,9},{25,1},{2,26},{10... | collective-permute-start | bytes 196616 | tf_op jit(solution)/shard_map/ppermute | solution.py:47
  8.1 5.3 %collective-permute-start.3 = (bf16[64,640]{1,0:T(8,128)(2,1)S(1)}, bf16[64,640]{1,0:T(8,128)(2,1)S(1)}, u32[]{:S(2)}, u32[]{:S(2)}) collective-permute-start(bf16[64,640]{1,0:T(8,128)(2,1)S(1)} %get-tuple-element.37.gate_ref), channel_id=1, source_target_pairs={{0,8},{8,0},{16,24},{24,16},{1,9},{9,1},{17,25},{25,17},{2,10},{10... | collective-permute-start | bytes 245768 | tf_op jit(solution)/shard_map/ppermute | solution.py:47
  8.3 5.1 %collective-permute-start.4 = (bf16[64,640]{1,0:T(8,128)(2,1)S(1)}, bf16[64,640]{1,0:T(8,128)(2,1)S(1)}, u32[]{:S(2)}, u32[]{:S(2)}) collective-permute-start(bf16[64,640]{1,0:T(8,128)(2,1)S(1)} %get-tuple-element.39), channel_id=1, source_target_pairs={{0,16},{8,24},{16,0},{24,8},{1,17},{9,25},{17,1},{25,9},{2,18},{10... | collective-permute-start | bytes 245768 | tf_op jit(solution)/shard_map/ppermute | solution.py:47
  9.8 4.7 %collective-permute-start.5 = (bf16[64,640]{1,0:T(8,128)(2,1)S(1)}, bf16[64,640]{1,0:T(8,128)(2,1)S(1)}, u32[]{:S(2)}, u32[]{:S(2)}) collective-permute-start(bf16[64,640]{1,0:T(8,128)(2,1)S(1)} %get-tuple-element.40), channel_id=1, source_target_pairs={{0,24},{8,16},{16,8},{24,0},{1,25},{9,17},{17,9},{25,1},{2,26},{10... | collective-permute-start | bytes 245768 | tf_op jit(solution)/shard_map/ppermute | solution.py:47
  18.8 9.3 %collective-permute-start.6 = (bf16[4,8,2560]{2,1,0:T(8,128)(2,1)S(1)}, bf16[4,8,2560]{2,1,0:T(8,128)(2,1)S(1)}, u32[]{:S(2)}, u32[]{:S(2)}) collective-permute-start(bf16[4,8,2560]{2,1,0:T(8,128)(2,1)S(1)} %get-tuple-element.42.gate_ref), channel_id=1, source_target_pairs={{0,1},{1,0},{2,3},{3,2},{4,5},{5,4},{6,7},{7,6},{8,9},{9,8},{10,11... | collective-permute-start | bytes 491528 | tf_op jit(solution)/shard_map/ppermute | solution.py:47
  20.4 11.5 %collective-permute-start.10 = (bf16[2,8,2560]{2,1,0:T(8,128)(2,1)S(1)}, bf16[2,8,2560]{2,1,0:T(8,128)(2,1)S(1)}, u32[]{:S(2)}, u32[]{:S(2)}) collective-permute-start(bf16[2,8,2560]{2,1,0:T(8,128)(2,1)S(1)} %get-tuple-element.49), channel_id=1, source_target_pairs={{0,6},{1,7},{2,4},{3,5},{4,2},{5,3},{6,0},{7,1},{8,14},{9,15},{10,... | collective-permute-start | bytes 245768 | tf_op jit(solution)/shard_map/ppermute | solution.py:47
  24.0 8.7 %collective-permute-start.11 = (bf16[2,8,2560]{2,1,0:T(8,128)(2,1)S(1)}, bf16[2,8,2560]{2,1,0:T(8,128)(2,1)S(1)}, u32[]{:S(2)}, u32[]{:S(2)}) collective-permute-start(bf16[2,8,2560]{2,1,0:T(8,128)(2,1)S(1)} %get-tuple-element.50), channel_id=1, source_target_pairs={{0,4},{1,5},{2,6},{3,7},{4,0},{5,1},{6,2},{7,3},{8,12},{9,13},{10,... | collective-permute-start | bytes 245768 | tf_op jit(solution)/shard_map/ppermute | solution.py:47
  24.0 8.7 %collective-permute-start.12 = (bf16[2,8,2560]{2,1,0:T(8,128)(2,1)S(1)}, bf16[2,8,2560]{2,1,0:T(8,128)(2,1)S(1)}, u32[]{:S(2)}, u32[]{:S(2)}) collective-permute-start(bf16[2,8,2560]{2,1,0:T(8,128)(2,1)S(1)} %get-tuple-element.51), channel_id=1, source_target_pairs={{0,2},{1,3},{2,0},{3,1},{4,6},{5,7},{6,4},{7,5},{8,10},{9,11},{10,... | collective-permute-start | bytes 245768 | tf_op jit(solution)/shard_map/ppermute | solution.py:47
  28.1 5.2 %copy-start.1 = (bf16[5120]{0:T(1024)(128)(2,1)S(1)}, bf16[5120]{0:T(1024)(128)(2,1)}, u32[]{:S(2)}) copy-start(bf16[5120]{0:T(1024)(128)(2,1)} %param.21) | copy-start | bytes 30724
  28.2 8.7 %copy-start = (bf16[64,5120]{1,0:T(8,128)(2,1)S(1)}, bf16[64,5120]{1,0:T(8,128)(2,1)}, u32[]{:S(2)}) copy-start(bf16[64,5120]{1,0:T(8,128)(2,1)} %param.19) | copy-start | bytes 1966084
  28.2 5.9 %collective-permute-start.7 = (bf16[8,2560]{1,0:T(8,128)(2,1)S(1)}, bf16[8,2560]{1,0:T(8,128)(2,1)S(1)}, u32[]{:S(2)}, u32[]{:S(2)}) collective-permute-start(bf16[8,2560]{1,0:T(8,128)(2,1)S(1)} %get-tuple-element.45), channel_id=1, source_target_pairs={{0,6},{1,7},{2,4},{3,5},{4,2},{5,3},{6,0},{7,1},{8,14},{9,15},{10,... | collective-permute-start | bytes 122888 | tf_op jit(solution)/shard_map/ppermute | solution.py:47
  31.9 4.9 %collective-permute-start.8 = (bf16[8,2560]{1,0:T(8,128)(2,1)S(1)}, bf16[8,2560]{1,0:T(8,128)(2,1)S(1)}, u32[]{:S(2)}, u32[]{:S(2)}) collective-permute-start(bf16[8,2560]{1,0:T(8,128)(2,1)S(1)} %get-tuple-element.46), channel_id=1, source_target_pairs={{0,4},{1,5},{2,6},{3,7},{4,0},{5,1},{6,2},{7,3},{8,12},{9,13},{10,... | collective-permute-start | bytes 122888 | tf_op jit(solution)/shard_map/ppermute | solution.py:47
  31.9 4.9 %collective-permute-start.9 = (bf16[8,2560]{1,0:T(8,128)(2,1)S(1)}, bf16[8,2560]{1,0:T(8,128)(2,1)S(1)}, u32[]{:S(2)}, u32[]{:S(2)}) collective-permute-start(bf16[8,2560]{1,0:T(8,128)(2,1)S(1)} %get-tuple-element.47.gate_ref), channel_id=1, source_target_pairs={{0,2},{1,3},{2,0},{3,1},{4,6},{5,7},{6,4},{7,5},{8,10},{9,11},{10,... | collective-permute-start | bytes 122888 | tf_op jit(solution)/shard_map/ppermute | solution.py:47
  32.7 4.1 %collective-permute-start.13 = (bf16[8,2560]{1,0:T(8,128)(2,1)S(1)}, bf16[8,2560]{1,0:T(8,128)(2,1)S(1)}, u32[]{:S(2)}, u32[]{:S(2)}) collective-permute-start(bf16[8,2560]{1,0:T(8,128)(2,1)S(1)} %get-tuple-element.53), channel_id=1, source_target_pairs={{0,1},{1,0},{2,3},{3,2},{4,5},{5,4},{6,7},{7,6},{8,9},{9,8},{10,11... | collective-permute-start | bytes 122888 | tf_op jit(solution)/shard_map/ppermute | solution.py:47
  37.0 7.8 %collective-permute-start.14 = (bf16[8,5120]{1,0:T(8,128)(2,1)S(1)}, bf16[8,5120]{1,0:T(8,128)(2,1)S(1)}, u32[]{:S(2)}, u32[]{:S(2)}) collective-permute-start(bf16[8,5120]{1,0:T(8,128)(2,1)S(1)} %norm.1.gate_ref.refs_0_), channel_id=1, source_target_pairs={{0,2},{1,3},{2,0},{3,1},{4,6},{5,7},{6,4},{7,5},{8,10},{9,11},{10,... | collective-permute-start | bytes 245768 | tf_op jit(solution)/shard_map/ppermute | solution.py:47
  38.3 6.9 %collective-permute-start.15 = (bf16[8,5120]{1,0:T(8,128)(2,1)S(1)}, bf16[8,5120]{1,0:T(8,128)(2,1)S(1)}, u32[]{:S(2)}, u32[]{:S(2)}) collective-permute-start(bf16[8,5120]{1,0:T(8,128)(2,1)S(1)} %norm.1.gate_ref.refs_0_), channel_id=1, source_target_pairs={{0,4},{1,5},{2,6},{3,7},{4,0},{5,1},{6,2},{7,3},{8,12},{9,13},{10,... | collective-permute-start | bytes 245768 | tf_op jit(solution)/shard_map/ppermute | solution.py:47
  41.2 6.2 %collective-permute-start.16 = (bf16[8,5120]{1,0:T(8,128)(2,1)S(1)}, bf16[8,5120]{1,0:T(8,128)(2,1)S(1)}, u32[]{:S(2)}, u32[]{:S(2)}) collective-permute-start(bf16[8,5120]{1,0:T(8,128)(2,1)S(1)} %norm.1.gate_ref.refs_0_), channel_id=1, source_target_pairs={{0,6},{1,7},{2,4},{3,5},{4,2},{5,3},{6,0},{7,1},{8,14},{9,15},{10,... | collective-permute-start | bytes 245768 | tf_op jit(solution)/shard_map/ppermute | solution.py:47
  47.5 6.2 %collective-permute-start.17 = (bf16[4,8,2560]{2,1,0:T(8,128)(2,1)S(1)}, bf16[4,8,2560]{2,1,0:T(8,128)(2,1)S(1)}, u32[]{:S(2)}, u32[]{:S(2)}) collective-permute-start(bf16[4,8,2560]{2,1,0:T(8,128)(2,1)S(1)} %get-tuple-element.54), channel_id=1, source_target_pairs={{0,1},{1,0},{2,3},{3,2},{4,5},{5,4},{6,7},{7,6},{8,9},{9,8},{10,11... | collective-permute-start | bytes 491528 | tf_op jit(solution)/shard_map/ppermute | solution.py:47
  48.1 7.1 %collective-permute-start.20 = (bf16[4,8,2560]{2,1,0:T(8,128)(2,1)S(1)}, bf16[4,8,2560]{2,1,0:T(8,128)(2,1)S(1)}, u32[]{:S(2)}, u32[]{:S(2)}) collective-permute-start(bf16[4,8,2560]{2,1,0:T(8,128)(2,1)S(1)} %get-tuple-element.57), channel_id=1, source_target_pairs={{0,16},{8,24},{16,0},{24,8},{1,17},{9,25},{17,1},{25,9},{2,18},{10... | collective-permute-start | bytes 491528 | tf_op jit(solution)/shard_map/ppermute | solution.py:47
  53.6 7.1 %collective-permute-start.18 = (bf16[8,8,2560]{2,1,0:T(8,128)(2,1)S(1)}, bf16[8,8,2560]{2,1,0:T(8,128)(2,1)S(1)}, u32[]{:S(2)}, u32[]{:S(2)}) collective-permute-start(bf16[8,8,2560]{2,1,0:T(8,128)(2,1)S(1)} %pad_maximum_fusion), channel_id=1, source_target_pairs={{0,16},{8,24},{16,0},{24,8},{1,17},{9,25},{17,1},{25,9},{2,18},{10... | collective-permute-start | bytes 983048 | tf_op jit(solution)/shard_map/ppermute | solution.py:47
  55.2 7.1 %collective-permute-start.21 = (bf16[8,8,2560]{2,1,0:T(8,128)(2,1)S(1)}, bf16[8,8,2560]{2,1,0:T(8,128)(2,1)S(1)}, u32[]{:S(2)}, u32[]{:S(2)}) collective-permute-start(bf16[8,8,2560]{2,1,0:T(8,128)(2,1)S(1)} %pad_maximum_fusion.1), channel_id=1, source_target_pairs={{0,1},{1,0},{2,3},{3,2},{4,5},{5,4},{6,7},{7,6},{8,9},{9,8},{10,11... | collective-permute-start | bytes 983048 | tf_op jit(solution)/shard_map/ppermute | solution.py:47
  60.9 2.2 %collective-permute-start.19 = (bf16[128,2560]{1,0:T(8,128)(2,1)S(1)}, bf16[128,2560]{1,0:T(8,128)(2,1)S(1)}, u32[]{:S(2)}, u32[]{:S(2)}) collective-permute-start(bf16[128,2560]{1,0:T(8,128)(2,1)S(1)} %maximum_bitcast_fusion.left_ref), channel_id=1, source_target_pairs={{0,8},{8,0},{16,24},{24,16},{1,9},{9,1},{17,25},{25,17},{2,10},{10... | collective-permute-start | bytes 1966088 | tf_op jit(solution)/shard_map/ppermute | solution.py:47
  62.4 5.1 %collective-permute-start.22 = (bf16[128,2560]{1,0:T(8,128)(2,1)S(1)}, bf16[128,2560]{1,0:T(8,128)(2,1)S(1)}, u32[]{:S(2)}, u32[]{:S(2)}) collective-permute-start(bf16[128,2560]{1,0:T(8,128)(2,1)S(1)} %maximum_bitcast_fusion.1.left_ref), channel_id=1, source_target_pairs={{0,8},{8,0},{16,24},{24,16},{1,9},{9,1},{17,25},{25,17},{2,10},{10... | collective-permute-start | bytes 1966088 | tf_op jit(solution)/shard_map/ppermute | solution.py:47

commit v6 on v5

--- a/solution.py
+++ b/solution.py
@@ -109,6 +109,7 @@
 def own_kernel(
     heads,
     seq,
+    share,
     lengths_ref,
     prompt_ref,
     q_ref,
@@ -119,6 +120,7 @@
     source_ref,
     gate_ref,
     own_ref,
+    live_ref,
     weight_ref,
     sems,
 ):
@@ -148,6 +150,11 @@
         own_ref[:, p] = (first * left + second * right) / (left + right)
         packed = jnp.where(lane == h, peak + jnp.log(left + right), packed)
     own_ref[:, heads * HEAD_DIM :] = packed
+    token = lax.broadcasted_iota(jnp.int32, live_ref.shape, 1) + lax.axis_index("tensor") * share
+    length = jnp.zeros(live_ref.shape, jnp.int32)
+    for r in range(rows // seq):
+        length = jnp.where(token // seq == r, lengths_ref[r], length)
+    live_ref[...] = jnp.where(token % seq < length, 1.0, 0.0)
     for copy in copies:
         copy.wait()
 
@@ -179,15 +186,12 @@
 
 def project_kernel(heads, seq, share, wide, group_size, key_rows, prompt_ref, own_ref, *refs):
     got_refs, refs = refs[: group_size - 1], refs[group_size - 1 :]
-    weight_ref, source_ref, send_left_ref, keep_left_ref, keep_right_ref = refs[:5]
-    send_right_refs, (quarter_ref, attended_ref, partial_ref, sems) = refs[5:-4], refs[-4:]
-    copies = carried(source_ref, 0, quarter_ref, sems)
-    for copy in copies:
-        copy.start()
+    weight_ref, send_left_ref, keep_left_ref, keep_right_ref = refs[:4]
+    send_right_refs, (attended_ref, partial_ref) = refs[4:-2], refs[-2:]
     rows = own_ref.shape[0]
     wanted = wanted_prompts(seq, rows, prompt_ref)
     group = lax.axis_index("group")
-    holders = [(group ^ d) * key_rows // PLEN for d in range(1, group_size)]
+    holders = [(group ^ d) * key_rows // PLEN for d in range(group_size - 1, 0, -1)]
     for h in range(heads):
         part = slice(h * HEAD_DIM, (h + 1) * HEAD_DIM)
         at = heads * HEAD_DIM
@@ -236,11 +240,8 @@
             else:
                 send_right_refs[d // 2 - 1][d % 2, :, columns] = block.astype(BF16)
 
-    for copy in copies:
-        copy.wait()
-
-
-def fold_left_kernel(gate_ref, keep_ref, got_ref, *out_refs):
+
+def fold_left_kernel(keep_ref, got_ref, *out_refs):
     for i, ref in enumerate(out_refs):
         ref[...] = (keep_ref[i] + got_ref[i].astype(F32)).astype(ref.dtype)
 
@@ -285,6 +286,14 @@
     for i, hidden in enumerate(halves):
         columns = slice(i * width, (i + 1) * width)
         out_ref[:, columns] = (hidden * scale * gain_ref[:, columns].astype(F32)).astype(BF16)
+
+
+def join_kernel(count, *refs):
+    out_ref = refs[-1]
+    start = 0
+    for ref in refs[:count]:
+        out_ref[start : start + ref.shape[0]] = ref[...]
+        start += ref.shape[0]
 
 
 def quarter_dots(x_ref, weight_refs, columns):
@@ -383,19 +392,14 @@
         out_ref[place] = jnp.sum(three[i * share : (i + 1) * share], axis=0, keepdims=True)
 
 
-def final_kernel(seq, share, lengths_ref, stats_ref, out_ref):
+def final_kernel(share, live_ref, stats_ref, out_ref):
     stats = stats_ref[...].reshape(stats_ref.shape[0], 128)
-    count = lengths_ref.shape[0]
     peak = jnp.max(stats, axis=0, keepdims=True)
     sums = pltpu.roll(stats, 128 - share, 1)
     picks = pltpu.roll(stats, 128 - 2 * share, 1)
     total = jnp.sum(sums * jnp.exp(stats - peak), axis=0, keepdims=True)
     values = jnp.sum(picks, axis=0, keepdims=True) - peak - jnp.log(total)
-    token = lax.broadcasted_iota(jnp.int32, (1, 128), 1) + lax.axis_index("tensor") * share
-    live = jnp.zeros((1, 128), jnp.int32)
-    for r in range(count):
-        live = jnp.where(token // seq == r, lengths_ref[r], live)
-    out_ref[...] = jnp.where(token % seq < live, values, 0.0)[0, :share]
+    out_ref[...] = jnp.where(live_ref[:1] > 0.0, values, 0.0)[0, :share]
 
 
 def local(
@@ -424,7 +428,7 @@
     vocab = lm_weight.shape[1]
     i32 = jnp.int32
 
-    distances = list(range(1, group_size))
+    distances = list(range(group_size - 1, 0, -1))
     queries = [swap(resp_query, "group", d, group_size) for d in distances]
     wanted = targets.reshape(-1, share, 1)
     inputs = (resp_query, resp_key, resp_value, prompt_keys, prompt_values)
@@ -448,14 +452,15 @@
         name="prefix_attention",
     )(*map(held, queries), keys, values)
     got = [swap(x, "group", d, group_size) for x, d in zip(answers, distances)]
-    own, weight = pl.pallas_call(
-        functools.partial(own_kernel, heads, seq),
+    own, live, weight = pl.pallas_call(
+        functools.partial(own_kernel, heads, seq, share),
         out_shape=[
             jax.ShapeDtypeStruct((rows, span + 128), F32),
+            jax.ShapeDtypeStruct((8, 128), F32),
             pltpu.VMEM(out_weight.shape, BF16),
         ],
         in_specs=[smem()] * 2 + [vmem()] * 5 + [anywhere()] * 2,
-        out_specs=[vmem()] * 2,
+        out_specs=[vmem()] * 3,
         scratch_shapes=[pltpu.SemaphoreType.DMA((4,))],
         compiler_params=params(6),
         cost_estimate=cost(moved=8 * MIB),
@@ -497,20 +502,16 @@
             jax.ShapeDtypeStruct((pairs, share, half), F32),
             jax.ShapeDtypeStruct((2, share, half), F32),
         ]
-        + [jax.ShapeDtypeStruct((2, share, half), BF16)] * (pairs - 1)
-        + [pltpu.VMEM((quarter, vocab), BF16)],
-        in_specs=[smem()] + [vmem()] * (2 + len(distances)) + [anywhere()],
-        out_specs=[vmem()] * (3 + pairs),
+        + [jax.ShapeDtypeStruct((2, share, half), BF16)] * (pairs - 1),
+        in_specs=[smem()] + [vmem()] * (2 + len(distances)),
+        out_specs=[vmem()] * (2 + pairs),
         scratch_shapes=[
             pltpu.VMEM((rows, span), BF16),
             pltpu.VMEM((tensor_size, share, wide), F32),
-            pltpu.SemaphoreType.DMA((4,)),
         ],
         compiler_params=params(6),
-        cost_estimate=cost(moved=quarter * vocab * 2),
         name="project",
-    )(stored(prompt_of), *map(held, (own, *got)), held(weight), stored(lm_weight))
-    quarters = [held(rest.pop()), fetch(lm_weight, quarter, quarter, send_left)]
+    )(stored(prompt_of), *map(held, (own, *got)), held(weight))
 
     far = list(range(2, tensor_size, 2))
     got_left = swap(send_left, "tensor", 1, tensor_size)
@@ -519,11 +520,11 @@
         fold_left_kernel,
         out_shape=[jax.ShapeDtypeStruct((share, half), F32)]
         + [jax.ShapeDtypeStruct((share, half), BF16)] * len(far),
-        in_specs=[anywhere()] + [vmem()] * 2,
+        in_specs=[vmem()] * 2,
         out_specs=[vmem()] * (1 + len(far)),
         compiler_params=params(2),
         name="fold_left",
-    )(quarters[1], held(keep_left), held(got_left))
+    )(held(keep_left), held(got_left))
     got_left = [swap(x, "tensor", d, tensor_size) for x, d in zip(left[:0:-1], far[::-1])]
     right = pl.pallas_call(
         fold_right_kernel,
@@ -554,7 +555,7 @@
     here = [(g, x) for g in [0] + above for x in (0, 1)]
     column = [swap(normed, "tensor", d, tensor_size) for d in far[::-1]]
     column = [normed] + column[::-1]
-    quarters.append(fetch(lm_weight, 2 * quarter, quarter, normed))
+    third = fetch(lm_weight, 2 * quarter, quarter, normed)
     columns = pl.pallas_call(
         functools.partial(column_kernel, len(column)),
         out_shape=[jax.ShapeDtypeStruct((len(column), share, half), BF16)] * 2,
@@ -562,21 +563,36 @@
         out_specs=[vmem()] * 2,
         compiler_params=params(2),
         name="column",
-    )(*map(held, column), quarters[2])
+    )(*map(held, column), third)
+
+    def join(pieces, gate):
+        blocks = sum(x.shape[0] for x in pieces)
+        return pl.pallas_call(
+            functools.partial(join_kernel, len(pieces)),
+            out_shape=jax.ShapeDtypeStruct((blocks, share, half), BF16),
+            in_specs=[vmem()] * len(pieces) + [anywhere()],
+            out_specs=vmem(),
+            compiler_params=params(2),
+            name="join",
+        )(*map(held, pieces), gate)
+
     left, right = columns
-    left = jnp.concatenate([left, swap(left, "tensor", 1, tensor_size)])
+    got_left = swap(left, "tensor", 1, tensor_size)
+    first_quarter = fetch(lm_weight, 0, quarter, left)
     right = [right] + [swap(right, "group", d, group_size) for d in above]
-    left = [left] + [swap(left, "group", d, group_size) for d in above]
+    left = join([left, got_left], first_quarter)
+    got_left = [swap(left, "group", d, group_size) for d in above]
+    second_quarter = fetch(lm_weight, quarter, quarter, left)
     across = swap(jnp.concatenate(right), "tensor", 1, tensor_size)
     across = jnp.split(across, len(right))
     right = [x for pair in zip(right, across) for x in pair]
     halves = []
-    for pieces in (left, right):
-        tokens = jnp.concatenate(pieces).reshape(-1, half)
+    for tokens in (join([left] + got_left, second_quarter), jnp.concatenate(right)):
+        tokens = tokens.reshape(-1, half)
         halves.append((tokens, swap(tokens, "group", 1, group_size)))
     spots = [(g + c, t + x) for c in (0, 1) for g, x in here for t in order]
     total_rows = 2 * tokens.shape[0]
-    narrow = 1536 if vocab % 1536 == 0 else vocab
+    narrow = 3072 if vocab % 3072 == 0 else vocab
     limit = 10 if total_rows <= 256 else 24
     work = 2 * total_rows * (half) * vocab
     first, last = pl.pallas_call(
@@ -591,7 +607,7 @@
         compiler_params=params(limit),
         cost_estimate=cost(flops=work),
         name="logits_first",
-    )(*map(held, (*halves[0], *quarters[:2])), stored(lm_weight))
+    )(*map(held, (*halves[0], first_quarter, second_quarter)), stored(lm_weight))
     stats = pl.pallas_call(
         functools.partial(logits_kernel, narrow, spots, tensor_size),
         out_shape=jax.ShapeDtypeStruct((len(spots), 1, 128), F32),
@@ -603,17 +619,17 @@
         compiler_params=params(limit),
         cost_estimate=cost(flops=work),
         name="logits",
-    )(*map(held, (first, *halves[1])), wanted, held(quarters[2]), held(last))
+    )(*map(held, (first, *halves[1])), wanted, held(third), held(last))
 
     stats = lax.all_to_all(stats, ("group", "tensor"), 0, 0, tiled=True)
     return pl.pallas_call(
-        functools.partial(final_kernel, seq, share),
+        functools.partial(final_kernel, share),
         out_shape=jax.ShapeDtypeStruct((share,), F32),
-        in_specs=[smem(), vmem()],
+        in_specs=[vmem()] * 2,
         out_specs=vmem(),
         compiler_params=params(4),
         name="final",
-    )(stored(lengths), stats)
+    )(held(live), held(stats))
 
 
 def solution(mesh):

time: 83.9 us -> 84.4 us (level)
  Pallas kernels: 28 us -> 31.8 us
  waiting for transfers between devices: 19.5 us -> 16.9 us
    pallas_call x2 -> x3, Pallas kernels: 6.69 us -> 10 us  [fetch(): pl.pallas_call(functools.partial(fetch_kernel, start), out_shape=pltpu.VM...]
    ppermute x23, waiting for transfers between devices: 19.5 us -> 16.9 us  [swap(): return lax.ppermute(x, axis, [(i, i ^ distance) for i in range(size)])]
    pallas_call x1, Pallas kernels: 4.52 us -> 6.77 us  [local(): pl.pallas_call(functools.partial(first_kernel, narrow), out_shape=[pltpu....]
    pallas_call x1, Pallas kernels: 4.27 us -> 3.27 us  [local(): pl.pallas_call(functools.partial(project_kernel, heads, seq, share, wide,...]
    pallas_call x2 -> x4, Pallas kernels: 4.65 us -> 4.22 us  [the longest x1 3.54 us: local(): pl.pallas_call(functools.partial(own_kernel, heads, seq, share), out_shap...]
  transfers between devices with their start and end apart: 23 -> 23, of which waited for: 11 -> 10; matrix products, arithmetic and copies ran while one was open for 1% -> 1% of each run, Pallas kernels for 19% -> 26%
where the time goes in v6:
time: 84.4 us; the launch traced here: 84.2 us
  Pallas kernels  31.8 us (38%)
  starting transfers between devices  25.4 us (30%)
  waiting for transfers between devices  16.9 us (20%)
  blocking collectives  8.84 us (10%)
  local copies, waits for them, and re-layouts  0.93 us (1%)
    ppermute x23, starting transfers between devices, swap(): return lax.ppermute(x, axis, [(i, i ^ distance) for i in range(size)])  25.4 us
    ppermute x23, waiting for transfers between devices, swap(): return lax.ppermute(x, axis, [(i, i ^ distance) for i in range(size)])  16.9 us
    pallas_call x3, Pallas kernels, fetch(): pl.pallas_call(functools.partial(fetch_kernel, start), out_shape=pltpu.VM...  10 us
    all_to_all x1, blocking collectives, local(): stats = lax.all_to_all(stats, ('group', 'tensor'), 0, 0, tiled=True)  8.84 us
    pallas_call x1, Pallas kernels, local(): pl.pallas_call(functools.partial(first_kernel, narrow), out_shape=[pltpu....  6.77 us
    pallas_call x1, Pallas kernels, local(): pl.pallas_call(functools.partial(logits_kernel, narrow, spots, tensor_siz...  5.01 us
    pallas_call x1, Pallas kernels, local(): pl.pallas_call(functools.partial(own_kernel, heads, seq, share), out_shap...  3.54 us
    pallas_call x1, Pallas kernels, local(): pl.pallas_call(functools.partial(project_kernel, heads, seq, share, wide,...  3.27 us
  transfers between devices with their start and end apart: 23, of which 10 were waited for; matrix products, arithmetic and copies ran while one was open for 1% of the time, Pallas kernels for 26%

profile of v6, /device:TPU:0, one launch (start us, length us, event | category | flops | bytes accessed | tf_op | source)
XLA Modules:
  0.0 84.2 jit_solution(9463357454439522097)
XLA Ops:
  0.0 2.4 %collective-permute-start = (bf16[64,512]{1,0:T(8,128)(2,1)}, bf16[64,512]{1,0:T(8,128)(2,1)S(1)}, u32[]{:S(2)}, u32[]{:S(2)}) collective-permute-start(bf16[64,512]{1,0:T(8,128)(2,1)} %refs_0_.1), channel_id=1, source_target_pairs={{0,24},{8,16},{16,8},{24,0},{1,25},{9,17},{17,9},{25,1},{2,26},{10... | collective-permute-start | bytes 196616 | tf_op jit(solution)/shard_map/ppermute | solution.py:47
  3.1 0.9 %reshape.16.gate_ref.target_ref = s32[32,8,1]{2,1,0:T(8,128)S(1)} reshape(s32[256]{0:T(256)} %param.23) | data formatting | bytes 2048 | tf_op jit(solution)/shard_map/reshape | solution.py:433
  4.0 1.4 %load.1 = (bf16[64,512]{1,0:T(8,128)(2,1)S(1)}, bf16[64,512]{1,0:T(8,128)(2,1)S(1)}, bf16[64,512]{1,0:T(8,128)(2,1)S(1)}, bf16[512,512]{1,0:T(8,128)(2,1)S(1)}, bf16[512,512]{1,0:T(8,128)(2,1)S(1)}) custom-call(s32[32,8,1]{2,1,0:T(8,128)S(1)} %reshape.16.gate_ref.target_ref, bf16[64,512]{1,0:T(8,128)(2,1)} %refs_0_.1, bf16[64,512]{1,0:T(8,128)(2,1)} %refs_1_.1, ...), custom_call_target="tpu_custom_call" | custom-call | bytes 2097152 | tf_op jit(solution)/shard_map/load/pallas_call | solution.py:435
  5.4 1.9 %collective-permute-done.1.refs_1_ = bf16[64,512]{1,0:T(8,128)(2,1)S(1)} collective-permute-done((bf16[64,512]{1,0:T(8,128)(2,1)}, bf16[64,512]{1,0:T(8,128)(2,1)S(1)}, u32[]{:S(2)}, u32[]{:S(2)}) %collective-permute-start.1) | collective-permute-done | bytes 65568 | tf_op jit(solution)/shard_map/ppermute | solution.py:47
  7.3 0.8 %prefix_attention.1 = (bf16[64,640]{1,0:T(8,128)(2,1)S(1)}, bf16[64,640]{1,0:T(8,128)(2,1)S(1)}, bf16[64,640]{1,0:T(8,128)(2,1)S(1)}) custom-call(bf16[64,512]{1,0:T(8,128)(2,1)S(1)} %collective-permute-done.refs_0_, bf16[64,512]{1,0:T(8,128)(2,1)S(1)} %collective-permute-done.1.refs_1_, bf16[64,512]{1,0:T(8,128)(2,1)S(1)} %collective-permute-done.2.refs_2_, ...), custom_call_target="tpu_custom_call" | custom-call | tf_op jit(solution)/shard_map/prefix_attention/pallas_call | solution.py:446
  8.2 1.5 %collective-permute-start.3 = (bf16[64,640]{1,0:T(8,128)(2,1)S(1)}, bf16[64,640]{1,0:T(8,128)(2,1)S(1)}, u32[]{:S(2)}, u32[]{:S(2)}) collective-permute-start(bf16[64,640]{1,0:T(8,128)(2,1)S(1)} %get-tuple-element.37.gate_ref), channel_id=1, source_target_pairs={{0,24},{8,16},{16,8},{24,0},{1,25},{9,17},{17,9},{25,1},{2,26},{10... | collective-permute-start | bytes 245768 | tf_op jit(solution)/shard_map/ppermute | solution.py:47
  10.1 3.5 %own_attention.1 = (f32[64,640]{1,0:T(8,128)S(1)}, f32[8,128]{1,0:T(8,128)S(1)}, bf16[512,5120]{1,0:T(8,128)(2,1)S(1)}) custom-call(s32[2]{0:T(128)} %lengths_ref.1, s32[2]{0:T(128)} %prompt_ref.3, bf16[64,512]{1,0:T(8,128)(2,1)S(1)} %get-tuple-element.32.q_ref, bf16[64,512]{1,0:T(8,128)(2,1)S(1)} %get-tuple-element.33.rk_ref, ...), custom_call_target="tpu_custom_call" | custom-call | bytes 8388608 | tf_op jit(solution)/shard_map/own_attention/pallas_call | solution.py:455
  13.6 1.1 %collective-permute-done.4.refs_1_ = bf16[64,640]{1,0:T(8,128)(2,1)S(1)} collective-permute-done((bf16[64,640]{1,0:T(8,128)(2,1)S(1)}, bf16[64,640]{1,0:T(8,128)(2,1)S(1)}, u32[]{:S(2)}, u32[]{:S(2)}) %collective-permute-start.4) | collective-permute-done | bytes 81952 | tf_op jit(solution)/shard_map/ppermute | solution.py:47
  14.7 3.3 %project.1 = (bf16[4,8,2560]{2,1,0:T(8,128)(2,1)S(1)}, f32[4,8,2560]{2,1,0:T(8,128)S(1)}, f32[2,8,2560]{2,1,0:T(8,128)S(1)}, bf16[2,8,2560]{2,1,0:T(8,128)(2,1)S...) custom-call(s32[2]{0:T(128)} %prompt_ref.3, f32[64,640]{1,0:T(8,128)S(1)} %get-tuple-element.39.own_ref, ...), custom_call_target="tpu_custom_call" | custom-call | tf_op jit(solution)/shard_map/project/pallas_call | solution.py:498
  18.0 1.7 %collective-permute-start.6 = (bf16[4,8,2560]{2,1,0:T(8,128)(2,1)S(1)}, bf16[4,8,2560]{2,1,0:T(8,128)(2,1)S(1)}, u32[]{:S(2)}, u32[]{:S(2)}) collective-permute-start(bf16[4,8,2560]{2,1,0:T(8,128)(2,1)S(1)} %get-tuple-element.44), channel_id=1, source_target_pairs={{0,1},{1,0},{2,3},{3,2},{4,5},{5,4},{6,7},{7,6},{8,9},{9,8},{10,11... | collective-permute-start | bytes 491528 | tf_op jit(solution)/shard_map/ppermute | solution.py:47
  19.7 3.6 %collective-permute-start.10 = (bf16[2,8,2560]{2,1,0:T(8,128)(2,1)S(1)}, bf16[2,8,2560]{2,1,0:T(8,128)(2,1)S(1)}, u32[]{:S(2)}, u32[]{:S(2)}) collective-permute-start(bf16[2,8,2560]{2,1,0:T(8,128)(2,1)S(1)} %get-tuple-element.50), channel_id=1, source_target_pairs={{0,6},{1,7},{2,4},{3,5},{4,2},{5,3},{6,0},{7,1},{8,14},{9,15},{10,... | collective-permute-start | bytes 245768 | tf_op jit(solution)/shard_map/ppermute | solution.py:47
  23.3 0.8 collective-permute-start.12
  24.2 3.9 %collective-permute-start.7 = (bf16[8,2560]{1,0:T(8,128)(2,1)S(1)}, bf16[8,2560]{1,0:T(8,128)(2,1)S(1)}, u32[]{:S(2)}, u32[]{:S(2)}) collective-permute-start(bf16[8,2560]{1,0:T(8,128)(2,1)S(1)} %get-tuple-element.46), channel_id=1, source_target_pairs={{0,6},{1,7},{2,4},{3,5},{4,2},{5,3},{6,0},{7,1},{8,14},{9,15},{10,... | collective-permute-start | bytes 122888 | tf_op jit(solution)/shard_map/ppermute | solution.py:47
  28.1 1.8 %collective-permute-start.9 = (bf16[8,2560]{1,0:T(8,128)(2,1)S(1)}, bf16[8,2560]{1,0:T(8,128)(2,1)S(1)}, u32[]{:S(2)}, u32[]{:S(2)}) collective-permute-start(bf16[8,2560]{1,0:T(8,128)(2,1)S(1)} %get-tuple-element.48.gate_ref), channel_id=1, source_target_pairs={{0,2},{1,3},{2,0},{3,1},{4,6},{5,7},{6,4},{7,5},{8,10},{9,11},{10,... | collective-permute-start | bytes 122888 | tf_op jit(solution)/shard_map/ppermute | solution.py:47
  29.9 2.5 %collective-permute-done.11.refs_1_ = bf16[2,8,2560]{2,1,0:T(8,128)(2,1)S(1)} collective-permute-done((bf16[2,8,2560]{2,1,0:T(8,128)(2,1)S(1)}, bf16[2,8,2560]{2,1,0:T(8,128)(2,1)S(1)}, u32[]{:S(2)}, u32[]{:S(2)}) %collective-permute-start.11) | collective-permute-done | bytes 81952 | tf_op jit(solution)/shard_map/ppermute | solution.py:47
  32.8 0.8 collective-permute-done.8.refs_2_
  33.6 2.9 %collective-permute-done.13.refs_5_ = bf16[8,2560]{1,0:T(8,128)(2,1)S(1)} collective-permute-done((bf16[8,2560]{1,0:T(8,128)(2,1)S(1)}, bf16[8,2560]{1,0:T(8,128)(2,1)S(1)}, u32[]{:S(2)}, u32[]{:S(2)}) %collective-permute-start.13) | collective-permute-done | bytes 40992 | tf_op jit(solution)/shard_map/ppermute | solution.py:47
  36.9 3.3 %collective-permute-start.15 = (bf16[8,5120]{1,0:T(8,128)(2,1)S(1)}, bf16[8,5120]{1,0:T(8,128)(2,1)S(1)}, u32[]{:S(2)}, u32[]{:S(2)}) collective-permute-start(bf16[8,5120]{1,0:T(8,128)(2,1)S(1)} %norm.1.gate_ref.refs_0_), channel_id=1, source_target_pairs={{0,4},{1,5},{2,6},{3,7},{4,0},{5,1},{6,2},{7,3},{8,12},{9,13},{10,... | collective-permute-start | bytes 245768 | tf_op jit(solution)/shard_map/ppermute | solution.py:47
  40.3 0.9 %collective-permute-start.16 = (bf16[8,5120]{1,0:T(8,128)(2,1)S(1)}, bf16[8,5120]{1,0:T(8,128)(2,1)S(1)}, u32[]{:S(2)}, u32[]{:S(2)}) collective-permute-start(bf16[8,5120]{1,0:T(8,128)(2,1)S(1)} %norm.1.gate_ref.refs_0_), channel_id=1, source_target_pairs={{0,6},{1,7},{2,4},{3,5},{4,2},{5,3},{6,0},{7,1},{8,14},{9,15},{10,... | collective-permute-start | bytes 245768 | tf_op jit(solution)/shard_map/ppermute | solution.py:47
  41.1 3.3 %fetch.3.refs_4_.weight_ref = bf16[1280,3072]{1,0:T(8,128)(2,1)S(1)} custom-call(bf16[5120,3072]{1,0:T(8,128)(2,1)} %source_ref.9, bf16[8,5120]{1,0:T(8,128)(2,1)S(1)} %norm.1.gate_ref.refs_0_), custom_call_target="tpu_custom_call" | custom-call | bytes 7864320 | tf_op jit(solution)/shard_map/fetch/pallas_call | solution.py:482
  44.5 2.0 %collective-permute-done.16.refs_3_ = bf16[8,5120]{1,0:T(8,128)(2,1)S(1)} collective-permute-done((bf16[8,5120]{1,0:T(8,128)(2,1)S(1)}, bf16[8,5120]{1,0:T(8,128)(2,1)S(1)}, u32[]{:S(2)}, u32[]{:S(2)}) %collective-permute-start.16) | collective-permute-done | bytes 81952 | tf_op jit(solution)/shard_map/ppermute | solution.py:47
  46.6 1.5 %collective-permute-start.20 = (bf16[4,8,2560]{2,1,0:T(8,128)(2,1)S(1)}, bf16[4,8,2560]{2,1,0:T(8,128)(2,1)S(1)}, u32[]{:S(2)}, u32[]{:S(2)}) collective-permute-start(bf16[4,8,2560]{2,1,0:T(8,128)(2,1)S(1)} %get-tuple-element.57), channel_id=1, source_target_pairs={{0,16},{8,24},{16,0},{24,8},{1,17},{9,25},{17,1},{25,9},{2,18},{10... | collective-permute-start | bytes 491528 | tf_op jit(solution)/shard_map/ppermute | solution.py:47
  48.1 3.3 %fetch.4.refs_2_.weight_ref = bf16[1280,3072]{1,0:T(8,128)(2,1)S(1)} custom-call(bf16[5120,3072]{1,0:T(8,128)(2,1)} %source_ref.9, bf16[4,8,2560]{2,1,0:T(8,128)(2,1)S(1)} %get-tuple-element.55.gate_ref.refs_0_), custom_call_target="tpu_custom_call" | custom-call | bytes 7864320 | tf_op jit(solution)/shard_map/fetch/pallas_call | solution.py:482
  51.5 2.1 %collective-permute-done.17.refs_1_ = bf16[4,8,2560]{2,1,0:T(8,128)(2,1)S(1)} collective-permute-done((bf16[4,8,2560]{2,1,0:T(8,128)(2,1)S(1)}, bf16[4,8,2560]{2,1,0:T(8,128)(2,1)S(1)}, u32[]{:S(2)}, u32[]{:S(2)}) %collective-permute-start.17) | collective-permute-done | bytes 163872 | tf_op jit(solution)/shard_map/ppermute | solution.py:47
  53.6 1.6 %collective-permute-start.18 = (bf16[8,8,2560]{2,1,0:T(8,128)(2,1)S(1)}, bf16[8,8,2560]{2,1,0:T(8,128)(2,1)S(1)}, u32[]{:S(2)}, u32[]{:S(2)}) collective-permute-start(bf16[8,8,2560]{2,1,0:T(8,128)(2,1)S(1)} %join.2.gate_ref.refs_0_), channel_id=1, source_target_pairs={{0,16},{8,24},{16,0},{24,8},{1,17},{9,25},{17,1},{25,9},{2,18},{10... | collective-permute-start | bytes 983048 | tf_op jit(solution)/shard_map/ppermute | solution.py:47
  55.6 3.3 %fetch.5.refs_2_.next_ref = bf16[1280,3072]{1,0:T(8,128)(2,1)S(1)} custom-call(bf16[5120,3072]{1,0:T(8,128)(2,1)} %source_ref.9, bf16[8,8,2560]{2,1,0:T(8,128)(2,1)S(1)} %join.2.gate_ref.refs_0_), custom_call_target="tpu_custom_call" | custom-call | bytes 7864320 | tf_op jit(solution)/shard_map/fetch/pallas_call | solution.py:482
  59.0 1.8 %collective-permute-done.18.refs_1_ = bf16[8,8,2560]{2,1,0:T(8,128)(2,1)S(1)} collective-permute-done((bf16[8,8,2560]{2,1,0:T(8,128)(2,1)S(1)}, bf16[8,8,2560]{2,1,0:T(8,128)(2,1)S(1)}, u32[]{:S(2)}, u32[]{:S(2)}) %collective-permute-start.18) | collective-permute-done | bytes 327712 | tf_op jit(solution)/shard_map/ppermute | solution.py:47
  60.9 1.5 %collective-permute-done.21 = bf16[8,8,2560]{2,1,0:T(8,128)(2,1)S(1)} collective-permute-done((bf16[8,8,2560]{2,1,0:T(8,128)(2,1)S(1)}, bf16[8,8,2560]{2,1,0:T(8,128)(2,1)S(1)}, u32[]{:S(2)}, u32[]{:S(2)}) %collective-permute-start.21) | collective-permute-done | bytes 327712 | tf_op jit(solution)/shard_map/ppermute | solution.py:47
  63.0 6.8 %logits_first.1 = (f32[256,3072]{1,0:T(8,128)S(1)}, bf16[1280,3072]{1,0:T(8,128)(2,1)S(1)}) custom-call(bf16[128,2560]{1,0:T(8,128)(2,1)S(1)} %bitcast.5, bf16[128,2560]{1,0:T(8,128)(2,1)S(1)} %collective-permute-done.19.right_ref, bf16[1280,3072]{1,0:T(8,128)(2,1)S(1)} %fetch.4.refs_2_.weight_ref, bf16[1280,3072]{1,0:T(8,128)(2,1)S(1)} %fetch.5.refs_2_.next_ref, ...), custom_call_target="tpu_custom_call" | custom-call | flops 4026531840 | tf_op jit(solution)/shard_map/logits_first/pallas_call | solution.py:598
  69.8 5.0 %logits.1 = f32[32,1,128]{2,1,0:T(1,128)S(1)} custom-call(f32[256,3072]{1,0:T(8,128)S(1)} %get-tuple-element.56.sum_in_ref, bf16[128,2560]{1,0:T(8,128)(2,1)S(1)} %maximum_bitcast_fusion.left_ref, bf16[128,2560]{1,0:T(8,128)(2,1)S(1)} %collective-permute-done.22.right_ref, s32[32,8,1]{2,1,0:T(8,128)S(1)} %reshape.16.gate_ref.target_ref, ...), custom_call_target="tpu_custom_call" | custom-call | flops 4026531840 | tf_op jit(solution)/shard_map/logits/pallas_call | solution.py:611
  74.8 8.8 %all_to_all.5.stats_ref = f32[32,1,128]{2,1,0:T(1,128)S(1)} all-to-all(f32[32,1,128]{2,1,0:T(1,128)S(1)} %logits.1), channel_id=1, replica_groups=mesh['group'=4,'tensor'=8] {'group','tensor'}, dimensions={0} | all-to-all | bytes 32768 | tf_op jit(solution)/shard_map/all_to_all | solution.py:624
  83.6 0.6 final.1
  (40 shorter events, 3.2 us)
Async XLA Ops:
  0.0 5.4 %collective-permute-start = (bf16[64,512]{1,0:T(8,128)(2,1)}, bf16[64,512]{1,0:T(8,128)(2,1)S(1)}, u32[]{:S(2)}, u32[]{:S(2)}) collective-permute-start(bf16[64,512]{1,0:T(8,128)(2,1)} %refs_0_.1), channel_id=1, source_target_pairs={{0,24},{8,16},{16,8},{24,0},{1,25},{9,17},{17,9},{25,1},{2,26},{10... | collective-permute-start | bytes 196616 | tf_op jit(solution)/shard_map/ppermute | solution.py:47
  2.4 4.9 %collective-permute-start.1 = (bf16[64,512]{1,0:T(8,128)(2,1)}, bf16[64,512]{1,0:T(8,128)(2,1)S(1)}, u32[]{:S(2)}, u32[]{:S(2)}) collective-permute-start(bf16[64,512]{1,0:T(8,128)(2,1)} %refs_0_.1), channel_id=1, source_target_pairs={{0,16},{8,24},{16,0},{24,8},{1,17},{9,25},{17,1},{25,9},{2,18},{10... | collective-permute-start | bytes 196616 | tf_op jit(solution)/shard_map/ppermute | solution.py:47
  3.0 4.3 %collective-permute-start.2 = (bf16[64,512]{1,0:T(8,128)(2,1)}, bf16[64,512]{1,0:T(8,128)(2,1)S(1)}, u32[]{:S(2)}, u32[]{:S(2)}) collective-permute-start(bf16[64,512]{1,0:T(8,128)(2,1)} %refs_0_.1), channel_id=1, source_target_pairs={{0,8},{8,0},{16,24},{24,16},{1,9},{9,1},{17,25},{25,17},{2,10},{10... | collective-permute-start | bytes 196616 | tf_op jit(solution)/shard_map/ppermute | solution.py:47
  4.0 28.8 %copy-start.1 = (bf16[5120]{0:T(1024)(128)(2,1)S(1)}, bf16[5120]{0:T(1024)(128)(2,1)}, u32[]{:S(2)}) copy-start(bf16[5120]{0:T(1024)(128)(2,1)} %param.21) | copy-start | bytes 30724
  4.0 32.5 %copy-start = (bf16[64,5120]{1,0:T(8,128)(2,1)S(1)}, bf16[64,5120]{1,0:T(8,128)(2,1)}, u32[]{:S(2)}) copy-start(bf16[64,5120]{1,0:T(8,128)(2,1)} %param.19) | copy-start | bytes 1966084
  8.2 5.5 %collective-permute-start.3 = (bf16[64,640]{1,0:T(8,128)(2,1)S(1)}, bf16[64,640]{1,0:T(8,128)(2,1)S(1)}, u32[]{:S(2)}, u32[]{:S(2)}) collective-permute-start(bf16[64,640]{1,0:T(8,128)(2,1)S(1)} %get-tuple-element.37.gate_ref), channel_id=1, source_target_pairs={{0,24},{8,16},{16,8},{24,0},{1,25},{9,17},{17,9},{25,1},{2,26},{10... | collective-permute-start | bytes 245768 | tf_op jit(solution)/shard_map/ppermute | solution.py:47
  9.6 5.1 %collective-permute-start.4 = (bf16[64,640]{1,0:T(8,128)(2,1)S(1)}, bf16[64,640]{1,0:T(8,128)(2,1)S(1)}, u32[]{:S(2)}, u32[]{:S(2)}) collective-permute-start(bf16[64,640]{1,0:T(8,128)(2,1)S(1)} %get-tuple-element.40), channel_id=1, source_target_pairs={{0,16},{8,24},{16,0},{24,8},{1,17},{9,25},{17,1},{25,9},{2,18},{10... | collective-permute-start | bytes 245768 | tf_op jit(solution)/shard_map/ppermute | solution.py:47
  10.0 4.7 %collective-permute-start.5 = (bf16[64,640]{1,0:T(8,128)(2,1)S(1)}, bf16[64,640]{1,0:T(8,128)(2,1)S(1)}, u32[]{:S(2)}, u32[]{:S(2)}) collective-permute-start(bf16[64,640]{1,0:T(8,128)(2,1)S(1)} %get-tuple-element.41), channel_id=1, source_target_pairs={{0,8},{8,0},{16,24},{24,16},{1,9},{9,1},{17,25},{25,17},{2,10},{10... | collective-permute-start | bytes 245768 | tf_op jit(solution)/shard_map/ppermute | solution.py:47
  18.0 6.1 %collective-permute-start.6 = (bf16[4,8,2560]{2,1,0:T(8,128)(2,1)S(1)}, bf16[4,8,2560]{2,1,0:T(8,128)(2,1)S(1)}, u32[]{:S(2)}, u32[]{:S(2)}) collective-permute-start(bf16[4,8,2560]{2,1,0:T(8,128)(2,1)S(1)} %get-tuple-element.44), channel_id=1, source_target_pairs={{0,1},{1,0},{2,3},{3,2},{4,5},{5,4},{6,7},{7,6},{8,9},{9,8},{10,11... | collective-permute-start | bytes 491528 | tf_op jit(solution)/shard_map/ppermute | solution.py:47
  19.7 8.3 %collective-permute-start.10 = (bf16[2,8,2560]{2,1,0:T(8,128)(2,1)S(1)}, bf16[2,8,2560]{2,1,0:T(8,128)(2,1)S(1)}, u32[]{:S(2)}, u32[]{:S(2)}) collective-permute-start(bf16[2,8,2560]{2,1,0:T(8,128)(2,1)S(1)} %get-tuple-element.50), channel_id=1, source_target_pairs={{0,6},{1,7},{2,4},{3,5},{4,2},{5,3},{6,0},{7,1},{8,14},{9,15},{10,... | collective-permute-start | bytes 245768 | tf_op jit(solution)/shard_map/ppermute | solution.py:47
  23.3 9.0 %collective-permute-start.11 = (bf16[2,8,2560]{2,1,0:T(8,128)(2,1)S(1)}, bf16[2,8,2560]{2,1,0:T(8,128)(2,1)S(1)}, u32[]{:S(2)}, u32[]{:S(2)}) collective-permute-start(bf16[2,8,2560]{2,1,0:T(8,128)(2,1)S(1)} %get-tuple-element.51), channel_id=1, source_target_pairs={{0,4},{1,5},{2,6},{3,7},{4,0},{5,1},{6,2},{7,3},{8,12},{9,13},{10,... | collective-permute-start | bytes 245768 | tf_op jit(solution)/shard_map/ppermute | solution.py:47
  23.3 9.0 %collective-permute-start.12 = (bf16[2,8,2560]{2,1,0:T(8,128)(2,1)S(1)}, bf16[2,8,2560]{2,1,0:T(8,128)(2,1)S(1)}, u32[]{:S(2)}, u32[]{:S(2)}) collective-permute-start(bf16[2,8,2560]{2,1,0:T(8,128)(2,1)S(1)} %get-tuple-element.52), channel_id=1, source_target_pairs={{0,2},{1,3},{2,0},{3,1},{4,6},{5,7},{6,4},{7,5},{8,10},{9,11},{10,... | collective-permute-start | bytes 245768 | tf_op jit(solution)/shard_map/ppermute | solution.py:47
  24.2 8.7 %collective-permute-start.7 = (bf16[8,2560]{1,0:T(8,128)(2,1)S(1)}, bf16[8,2560]{1,0:T(8,128)(2,1)S(1)}, u32[]{:S(2)}, u32[]{:S(2)}) collective-permute-start(bf16[8,2560]{1,0:T(8,128)(2,1)S(1)} %get-tuple-element.46), channel_id=1, source_target_pairs={{0,6},{1,7},{2,4},{3,5},{4,2},{5,3},{6,0},{7,1},{8,14},{9,15},{10,... | collective-permute-start | bytes 122888 | tf_op jit(solution)/shard_map/ppermute | solution.py:47
  28.1 5.5 %collective-permute-start.8 = (bf16[8,2560]{1,0:T(8,128)(2,1)S(1)}, bf16[8,2560]{1,0:T(8,128)(2,1)S(1)}, u32[]{:S(2)}, u32[]{:S(2)}) collective-permute-start(bf16[8,2560]{1,0:T(8,128)(2,1)S(1)} %get-tuple-element.47), channel_id=1, source_target_pairs={{0,4},{1,5},{2,6},{3,7},{4,0},{5,1},{6,2},{7,3},{8,12},{9,13},{10,... | collective-permute-start | bytes 122888 | tf_op jit(solution)/shard_map/ppermute | solution.py:47
  28.1 5.5 %collective-permute-start.9 = (bf16[8,2560]{1,0:T(8,128)(2,1)S(1)}, bf16[8,2560]{1,0:T(8,128)(2,1)S(1)}, u32[]{:S(2)}, u32[]{:S(2)}) collective-permute-start(bf16[8,2560]{1,0:T(8,128)(2,1)S(1)} %get-tuple-element.48.gate_ref), channel_id=1, source_target_pairs={{0,2},{1,3},{2,0},{3,1},{4,6},{5,7},{6,4},{7,5},{8,10},{9,11},{10,... | collective-permute-start | bytes 122888 | tf_op jit(solution)/shard_map/ppermute | solution.py:47
  32.4 4.1 %collective-permute-start.13 = (bf16[8,2560]{1,0:T(8,128)(2,1)S(1)}, bf16[8,2560]{1,0:T(8,128)(2,1)S(1)}, u32[]{:S(2)}, u32[]{:S(2)}) collective-permute-start(bf16[8,2560]{1,0:T(8,128)(2,1)S(1)} %get-tuple-element.54), channel_id=1, source_target_pairs={{0,1},{1,0},{2,3},{3,2},{4,5},{5,4},{6,7},{7,6},{8,9},{9,8},{10,11... | collective-permute-start | bytes 122888 | tf_op jit(solution)/shard_map/ppermute | solution.py:47
  36.7 7.8 %collective-permute-start.14 = (bf16[8,5120]{1,0:T(8,128)(2,1)S(1)}, bf16[8,5120]{1,0:T(8,128)(2,1)S(1)}, u32[]{:S(2)}, u32[]{:S(2)}) collective-permute-start(bf16[8,5120]{1,0:T(8,128)(2,1)S(1)} %norm.1.gate_ref.refs_0_), channel_id=1, source_target_pairs={{0,2},{1,3},{2,0},{3,1},{4,6},{5,7},{6,4},{7,5},{8,10},{9,11},{10,... | collective-permute-start | bytes 245768 | tf_op jit(solution)/shard_map/ppermute | solution.py:47
  36.9 7.6 %collective-permute-start.15 = (bf16[8,5120]{1,0:T(8,128)(2,1)S(1)}, bf16[8,5120]{1,0:T(8,128)(2,1)S(1)}, u32[]{:S(2)}, u32[]{:S(2)}) collective-permute-start(bf16[8,5120]{1,0:T(8,128)(2,1)S(1)} %norm.1.gate_ref.refs_0_), channel_id=1, source_target_pairs={{0,4},{1,5},{2,6},{3,7},{4,0},{5,1},{6,2},{7,3},{8,12},{9,13},{10,... | collective-permute-start | bytes 245768 | tf_op jit(solution)/shard_map/ppermute | solution.py:47
  40.3 6.2 %collective-permute-start.16 = (bf16[8,5120]{1,0:T(8,128)(2,1)S(1)}, bf16[8,5120]{1,0:T(8,128)(2,1)S(1)}, u32[]{:S(2)}, u32[]{:S(2)}) collective-permute-start(bf16[8,5120]{1,0:T(8,128)(2,1)S(1)} %norm.1.gate_ref.refs_0_), channel_id=1, source_target_pairs={{0,6},{1,7},{2,4},{3,5},{4,2},{5,3},{6,0},{7,1},{8,14},{9,15},{10,... | collective-permute-start | bytes 245768 | tf_op jit(solution)/shard_map/ppermute | solution.py:47
  46.5 7.1 %collective-permute-start.17 = (bf16[4,8,2560]{2,1,0:T(8,128)(2,1)S(1)}, bf16[4,8,2560]{2,1,0:T(8,128)(2,1)S(1)}, u32[]{:S(2)}, u32[]{:S(2)}) collective-permute-start(bf16[4,8,2560]{2,1,0:T(8,128)(2,1)S(1)} %get-tuple-element.55.gate_ref.refs_0_), channel_id=1, source_target_pairs={{0,1},{1,0},{2,3},{3,2},{4,5},{5,4},{6,7},{7,6},{8,9},{9,8},{10,11... | collective-permute-start | bytes 491528 | tf_op jit(solution)/shard_map/ppermute | solution.py:47
  46.6 8.6 %collective-permute-start.20 = (bf16[4,8,2560]{2,1,0:T(8,128)(2,1)S(1)}, bf16[4,8,2560]{2,1,0:T(8,128)(2,1)S(1)}, u32[]{:S(2)}, u32[]{:S(2)}) collective-permute-start(bf16[4,8,2560]{2,1,0:T(8,128)(2,1)S(1)} %get-tuple-element.57), channel_id=1, source_target_pairs={{0,16},{8,24},{16,0},{24,8},{1,17},{9,25},{17,1},{25,9},{2,18},{10... | collective-permute-start | bytes 491528 | tf_op jit(solution)/shard_map/ppermute | solution.py:47
  53.6 7.1 %collective-permute-start.18 = (bf16[8,8,2560]{2,1,0:T(8,128)(2,1)S(1)}, bf16[8,8,2560]{2,1,0:T(8,128)(2,1)S(1)}, u32[]{:S(2)}, u32[]{:S(2)}) collective-permute-start(bf16[8,8,2560]{2,1,0:T(8,128)(2,1)S(1)} %join.2.gate_ref.refs_0_), channel_id=1, source_target_pairs={{0,16},{8,24},{16,0},{24,8},{1,17},{9,25},{17,1},{25,9},{2,18},{10... | collective-permute-start | bytes 983048 | tf_op jit(solution)/shard_map/ppermute | solution.py:47
  55.3 7.1 %collective-permute-start.21 = (bf16[8,8,2560]{2,1,0:T(8,128)(2,1)S(1)}, bf16[8,8,2560]{2,1,0:T(8,128)(2,1)S(1)}, u32[]{:S(2)}, u32[]{:S(2)}) collective-permute-start(bf16[8,8,2560]{2,1,0:T(8,128)(2,1)S(1)} %pad_maximum_fusion), channel_id=1, source_target_pairs={{0,1},{1,0},{2,3},{3,2},{4,5},{5,4},{6,7},{7,6},{8,9},{9,8},{10,11... | collective-permute-start | bytes 983048 | tf_op jit(solution)/shard_map/ppermute | solution.py:47
  60.8 2.2 %collective-permute-start.19 = (bf16[128,2560]{1,0:T(8,128)(2,1)S(1)}, bf16[128,2560]{1,0:T(8,128)(2,1)S(1)}, u32[]{:S(2)}, u32[]{:S(2)}) collective-permute-start(bf16[128,2560]{1,0:T(8,128)(2,1)S(1)} %bitcast.4), channel_id=1, source_target_pairs={{0,8},{8,0},{16,24},{24,16},{1,9},{9,1},{17,25},{25,17},{2,10},{10... | collective-permute-start | bytes 1966088 | tf_op jit(solution)/shard_map/ppermute | solution.py:47
  62.5 7.2 %collective-permute-start.22 = (bf16[128,2560]{1,0:T(8,128)(2,1)S(1)}, bf16[128,2560]{1,0:T(8,128)(2,1)S(1)}, u32[]{:S(2)}, u32[]{:S(2)}) collective-permute-start(bf16[128,2560]{1,0:T(8,128)(2,1)S(1)} %maximum_bitcast_fusion.left_ref), channel_id=1, source_target_pairs={{0,8},{8,0},{16,24},{24,16},{1,9},{9,1},{17,25},{25,17},{2,10},{10... | collective-permute-start | bytes 1966088 | tf_op jit(solution)/shard_map/ppermute | solution.py:47

commit v7 on v6

--- a/solution.py
+++ b/solution.py
@@ -82,6 +82,11 @@
         for part, value in enumerate((first, second, third)):
             packed = jnp.where(lane == 3 * head + part, value, packed)
     return packed.astype(BF16)
+
+
+def pass_kernel(count, *refs):
+    for ref, out_ref in zip(refs, refs[-count:]):
+        out_ref[...] = ref[...]
 
 
 def load_kernel(count, gate_ref, *refs):
@@ -117,16 +122,10 @@
     rv_ref,
     k_ref,
     v_ref,
-    source_ref,
     gate_ref,
     own_ref,
     live_ref,
-    weight_ref,
-    sems,
 ):
-    copies = carried(source_ref, 0, weight_ref, sems)
-    for copy in copies:
-        copy.start()
     rows = q_ref.shape[0]
     row = lax.broadcasted_iota(jnp.int32, (rows, rows), 0)
     col = lax.broadcasted_iota(jnp.int32, (rows, rows), 1)
@@ -155,8 +154,6 @@
     for r in range(rows // seq):
         length = jnp.where(token // seq == r, lengths_ref[r], length)
     live_ref[...] = jnp.where(token % seq < length, 1.0, 0.0)
-    for copy in copies:
-        copy.wait()
 
 
 def wanted_prompts(seq, rows, prompt_ref):
@@ -170,6 +167,7 @@
 def prefix_kernel(heads, count, *refs):
     q_refs, (k_ref, v_ref), out_refs = refs[:count], refs[count : count + 2], refs[count + 2 :]
     rows = q_refs[0].shape[0]
+    places = [(ref, i) for ref in out_refs for i in range(ref.shape[0])]
     parts = [slice(h * HEAD_DIM, (h + 1) * HEAD_DIM) for h in range(heads)]
     found = attend(
         [
@@ -177,65 +175,93 @@
             for p in parts
         ]
     )
-    for i in range(count):
+    for i, (out_ref, place) in enumerate(places):
         rung = slice(i * rows, (i + 1) * rows)
         for h, p in enumerate(parts):
-            out_refs[i][:, p] = found[h][0][rung].astype(BF16)
-        out_refs[i][:, heads * HEAD_DIM :] = pack_logs([log[rung] for _, log in found], rows)
-
-
-def project_kernel(heads, seq, share, wide, group_size, key_rows, prompt_ref, own_ref, *refs):
-    got_refs, refs = refs[: group_size - 1], refs[group_size - 1 :]
-    weight_ref, send_left_ref, keep_left_ref, keep_right_ref = refs[:4]
-    send_right_refs, (attended_ref, partial_ref) = refs[4:-2], refs[-2:]
+            out_ref[place, :, p] = found[h][0][rung].astype(BF16)
+        out_ref[place, :, heads * HEAD_DIM :] = pack_logs([log[rung] for _, log in found], rows)
+
+
+def unpack_log(three, h):
+    three = three.astype(F32)
+    return three[:, 3 * h : 3 * h + 1] + three[:, 3 * h + 1 : 3 * h + 2] + three[:, 3 * h + 2 : 3 * h + 3]
+
+
+def blend(logs, values):
+    peak = functools.reduce(jnp.maximum, logs)
+    loads = [jnp.exp(log - peak) for log in logs]
+    total = functools.reduce(jnp.add, loads)
+    mixed = functools.reduce(jnp.add, [w * v for w, v in zip(loads, values)])
+    return mixed / total, peak + jnp.log(total)
+
+
+def merge_kernel(heads, seq, key_rows, count, *refs):
+    prompt_refs, (stay_ref, cross_ref), out_refs = refs[:count], refs[count : count + 2], refs[count + 2 :]
+    rows = stay_ref.shape[1]
+    group = lax.axis_index("group")
+    at = heads * HEAD_DIM
+    for i, (prompt_ref, out_ref) in enumerate(zip(prompt_refs, out_refs)):
+        wanted = wanted_prompts(seq, rows, prompt_ref)
+        sources = [
+            (stay_ref[i], wanted == group * key_rows // PLEN),
+            (cross_ref[i + 1], wanted == (group ^ 1) * key_rows // PLEN),
+        ]
+        logs = []
+        for h in range(heads):
+            part = slice(h * HEAD_DIM, (h + 1) * HEAD_DIM)
+            value, log = blend(
+                [jnp.where(here, unpack_log(x[:, at:], h), NEG) for x, here in sources],
+                [x[:, part].astype(F32) for x, _ in sources],
+            )
+            out_ref[:, part] = value.astype(BF16)
+            logs.append(log)
+        out_ref[:, at:] = pack_logs(logs, rows)
+
+
+def project_kernel(heads, seq, key_rows, count, wide, prompt_ref, own_ref, cross_ref, *refs):
+    got_refs, weight_ref, refs = refs[:count], refs[count], refs[count + 1 :]
+    send_left_ref, keep_left_ref, keep_right_ref = refs[:3]
+    send_right_refs, (attended_ref, partial_ref, near_ref, sems) = refs[3:-4], refs[-4:]
     rows = own_ref.shape[0]
-    wanted = wanted_prompts(seq, rows, prompt_ref)
-    group = lax.axis_index("group")
-    holders = [(group ^ d) * key_rows // PLEN for d in range(group_size - 1, 0, -1)]
+    blocks, share = partial_ref.shape[:2]
+    half = send_left_ref.shape[2]
+    copies = [
+        pltpu.make_async_copy(
+            weight_ref.at[:, pl.ds(n * wide, wide)], near_ref.at[:, pl.ds(n * wide, wide)], sems.at[n]
+        )
+        for n in range(2 * half // wide)
+    ]
+    for copy in copies:
+        copy.start()
+    here = wanted_prompts(seq, rows, prompt_ref) == (lax.axis_index("group") ^ 1) * key_rows // PLEN
+    at = heads * HEAD_DIM
     for h in range(heads):
         part = slice(h * HEAD_DIM, (h + 1) * HEAD_DIM)
-        at = heads * HEAD_DIM
         logs = [own_ref[:, at + h : at + h + 1]]
-        values = [own_ref[:, part]]
-        for holder, ref in zip(holders, got_refs):
-            three = ref[:, at : at + 128].astype(F32)
-            log = (
-                three[:, 3 * h : 3 * h + 1]
-                + three[:, 3 * h + 1 : 3 * h + 2]
-                + three[:, 3 * h + 2 : 3 * h + 3]
-            )
-            logs.append(jnp.where(wanted == holder, log, NEG))
-            values.append(ref[:, part].astype(F32))
-        peak = functools.reduce(jnp.maximum, logs)
-        loads = [jnp.exp(log - peak) for log in logs]
-        total = functools.reduce(jnp.add, loads)
-        mixed = functools.reduce(jnp.add, [w * v for w, v in zip(loads, values)])
-        attended_ref[:, part] = (mixed / total).astype(BF16)
+        logs.append(jnp.where(here, unpack_log(cross_ref[0, :, at:], h), NEG))
+        logs += [unpack_log(ref[:, at:], h) for ref in got_refs]
+        values = [own_ref[:, part], cross_ref[0, :, part].astype(F32)]
+        values += [ref[:, part].astype(F32) for ref in got_refs]
+        attended_ref[:, part] = blend(logs, values)[0].astype(BF16)
 
     me = lax.axis_index("tensor")
-    blocks = rows // share
-    half = send_left_ref.shape[2]
-
-    def multiply(columns):
-        partial = jnp.dot(attended_ref[...], weight_ref[:, columns], preferred_element_type=F32)
+    for n, copy in enumerate(copies):
+        copy.wait()
+        start = n * wide % half
+        columns = slice(start, start + wide)
+        partial = jnp.dot(
+            attended_ref[...], near_ref[:, n * wide : (n + 1) * wide], preferred_element_type=F32
+        )
         for b in range(blocks):
             partial_ref[b] = partial[b * share : (b + 1) * share]
-
-    @pl.loop(0, half // wide)
-    def _(n):
-        columns = pl.ds(pl.multiple_of(n * wide, 128), wide)
-        multiply(columns)
-        for d in range(0, blocks, 2):
-            keep_left_ref[d // 2, :, columns] = partial_ref[me ^ d]
-            send_left_ref[d // 2, :, columns] = partial_ref[me ^ (d + 1)].astype(BF16)
-
-    @pl.loop(0, half // wide)
-    def _(n):
-        columns = pl.ds(pl.multiple_of(n * wide, 128), wide)
-        multiply(pl.ds(pl.multiple_of(half + n * wide, 128), wide))
         for d in range(blocks):
             block = partial_ref[me ^ d]
-            if d < 2:
+            if n * wide < half:
+                if d % 2:
+                    send_left_ref[d // 2, :, columns] = block.astype(BF16)
+                else:
+                    keep_left_ref[d // 2, :, columns] = block
+            elif d < 2:
                 keep_right_ref[d, :, columns] = block
             else:
                 send_right_refs[d // 2 - 1][d % 2, :, columns] = block.astype(BF16)
@@ -428,9 +454,20 @@
     vocab = lm_weight.shape[1]
     i32 = jnp.int32
 
-    distances = list(range(group_size - 1, 0, -1))
-    queries = [swap(resp_query, "group", d, group_size) for d in distances]
     wanted = targets.reshape(-1, share, 1)
+    above = list(range(2, group_size, 2))
+    far_queries = [swap(resp_query, "group", a, group_size) for a in above[::-1]][::-1]
+    far_prompts = [swap(prompt_of, "group", a, group_size) for a in above]
+    near_queries = [swap(resp_query, "group", 1, group_size)]
+    far_queries = pl.pallas_call(
+        functools.partial(pass_kernel, len(above)),
+        out_shape=[jax.ShapeDtypeStruct(x.shape, x.dtype) for x in far_queries],
+        in_specs=[vmem()] * len(above) + [anywhere()] * (1 + len(above)),
+        out_specs=[vmem()] * len(above),
+        compiler_params=params(1),
+        name="pass",
+    )(*map(held, far_queries), wanted, *far_prompts)
+    near_queries += [swap(x, "group", 1, group_size) for x in far_queries]
     inputs = (resp_query, resp_key, resp_value, prompt_keys, prompt_values)
     loaded = pl.pallas_call(
         functools.partial(load_kernel, len(inputs)),
@@ -441,41 +478,40 @@
         compiler_params=params(1),
         cost_estimate=cost(moved=2 * MIB),
         name="load",
-    )(wanted, *map(stored, inputs))
+    )(far_queries[0], *map(stored, inputs))
     query, own_keys, own_values, keys, values = map(held, loaded)
-    answers = pl.pallas_call(
-        functools.partial(prefix_kernel, heads, len(distances)),
-        out_shape=[jax.ShapeDtypeStruct((rows, span + 128), BF16)] * len(distances),
-        in_specs=[vmem()] * (len(distances) + 2),
-        out_specs=[vmem()] * len(distances),
+    packed = (rows, span + 128)
+    queries = near_queries + list(far_queries)
+    cross, stay = pl.pallas_call(
+        functools.partial(prefix_kernel, heads, len(queries)),
+        out_shape=[
+            jax.ShapeDtypeStruct((len(near_queries), *packed), BF16),
+            jax.ShapeDtypeStruct((len(above), *packed), BF16),
+        ],
+        in_specs=[vmem()] * (len(queries) + 2),
+        out_specs=[vmem()] * 2,
         compiler_params=params(8),
         name="prefix_attention",
     )(*map(held, queries), keys, values)
-    got = [swap(x, "group", d, group_size) for x, d in zip(answers, distances)]
-    own, live, weight = pl.pallas_call(
+    cross = swap(cross, "group", 1, group_size)
+    merged = pl.pallas_call(
+        functools.partial(merge_kernel, heads, seq, key_rows, len(above)),
+        out_shape=[jax.ShapeDtypeStruct(packed, BF16)] * len(above),
+        in_specs=[smem()] * len(above) + [vmem()] * 2,
+        out_specs=[vmem()] * len(above),
+        compiler_params=params(4),
+        name="merge",
+    )(*far_prompts, held(stay), held(cross))
+    got = [swap(x, "group", a, group_size) for x, a in zip(merged, above)]
+    own, live = pl.pallas_call(
         functools.partial(own_kernel, heads, seq, share),
-        out_shape=[
-            jax.ShapeDtypeStruct((rows, span + 128), F32),
-            jax.ShapeDtypeStruct((8, 128), F32),
-            pltpu.VMEM(out_weight.shape, BF16),
-        ],
-        in_specs=[smem()] * 2 + [vmem()] * 5 + [anywhere()] * 2,
-        out_specs=[vmem()] * 3,
-        scratch_shapes=[pltpu.SemaphoreType.DMA((4,))],
+        out_shape=[jax.ShapeDtypeStruct(packed, F32), jax.ShapeDtypeStruct((8, 128), F32)],
+        in_specs=[smem()] * 2 + [vmem()] * 5 + [anywhere()],
+        out_specs=[vmem()] * 2,
         compiler_params=params(6),
-        cost_estimate=cost(moved=8 * MIB),
+        cost_estimate=cost(moved=4 * MIB),
         name="own_attention",
-    )(
-        stored(lengths),
-        stored(prompt_of),
-        query,
-        own_keys,
-        own_values,
-        keys,
-        values,
-        stored(out_weight),
-        answers[0],
-    )
+    )(stored(lengths), stored(prompt_of), query, own_keys, own_values, keys, values, merged[0])
 
     def fetch(source, start, count, gate):
         return held(
@@ -496,22 +532,24 @@
     wide = 1280 if half % 1280 == 0 else half
     pairs = tensor_size // 2
     send_left, keep_left, keep_right, *rest = pl.pallas_call(
-        functools.partial(project_kernel, heads, seq, share, wide, group_size, key_rows),
+        functools.partial(project_kernel, heads, seq, key_rows, len(got), wide),
         out_shape=[
             jax.ShapeDtypeStruct((pairs, share, half), BF16),
             jax.ShapeDtypeStruct((pairs, share, half), F32),
             jax.ShapeDtypeStruct((2, share, half), F32),
         ]
         + [jax.ShapeDtypeStruct((2, share, half), BF16)] * (pairs - 1),
-        in_specs=[smem()] + [vmem()] * (2 + len(distances)),
+        in_specs=[smem()] + [vmem()] * (2 + len(got)) + [anywhere()],
         out_specs=[vmem()] * (2 + pairs),
         scratch_shapes=[
             pltpu.VMEM((rows, span), BF16),
             pltpu.VMEM((tensor_size, share, wide), F32),
+            pltpu.VMEM(out_weight.shape, BF16),
+            pltpu.SemaphoreType.DMA((depth // wide,)),
         ],
-        compiler_params=params(6),
+        compiler_params=params(10),
         name="project",
-    )(stored(prompt_of), *map(held, (own, *got)), held(weight))
+    )(stored(prompt_of), *map(held, (own, cross, *got)), stored(out_weight))
 
     far = list(range(2, tensor_size, 2))
     got_left = swap(send_left, "tensor", 1, tensor_size)
@@ -550,7 +588,6 @@
         *map(held, (left[0], *got_left, right[0], got_right)),
     )
 
-    above = list(range(2, group_size, 2))
     order = [0] + far
     here = [(g, x) for g in [0] + above for x in (0, 1)]
     column = [swap(normed, "tensor", d, tensor_size) for d in far[::-1]]
@@ -592,7 +629,7 @@
         halves.append((tokens, swap(tokens, "group", 1, group_size)))
     spots = [(g + c, t + x) for c in (0, 1) for g, x in here for t in order]
     total_rows = 2 * tokens.shape[0]
-    narrow = 3072 if vocab % 3072 == 0 else vocab
+    narrow = 1536 if vocab % 1536 == 0 else vocab
     limit = 10 if total_rows <= 256 else 24
     work = 2 * total_rows * (half) * vocab
     first, last = pl.pallas_call(
@@ -609,7 +646,7 @@
         name="logits_first",
     )(*map(held, (*halves[0], first_quarter, second_quarter)), stored(lm_weight))
     stats = pl.pallas_call(
-        functools.partial(logits_kernel, narrow, spots, tensor_size),
+        functools.partial(logits_kernel, vocab, spots, tensor_size),
         out_shape=jax.ShapeDtypeStruct((len(spots), 1, 128), F32),
         in_specs=[vmem()] * 6,
         out_specs=vmem(),

time: 84.4 us -> 84.1 us (level)
  waiting for transfers between devices: 16.9 us -> 21.5 us
  Pallas kernels: 31.8 us -> 29.2 us
  starting transfers between devices: 25.4 us -> 23.1 us
    ppermute x23, waiting for transfers between devices: 16.9 us -> 21.5 us  [swap(): return lax.ppermute(x, axis, [(i, i ^ distance) for i in range(size)])]
    pallas_call x1, Pallas kernels: 6.77 us -> 4.52 us  [local(): pl.pallas_call(functools.partial(first_kernel, narrow), out_shape=[pltpu....]
    ppermute x23, starting transfers between devices: 25.4 us -> 23.1 us  [swap(): return lax.ppermute(x, axis, [(i, i ^ distance) for i in range(size)])]
    pallas_call x1, Pallas kernels: 3.54 us -> 1.33 us  [local(): pl.pallas_call(functools.partial(own_kernel, heads, seq, share), out_shap...]
    pallas_call x3 -> x5, Pallas kernels: 9.13 us -> 11 us  [the longest x1 5.01 us: local(): pl.pallas_call(functools.partial(logits_kernel, vocab, spots, tensor_size...]
  transfers between devices with their start and end apart: 23 -> 23, of which waited for: 10 -> 11; matrix products, arithmetic and copies ran while one was open for 1% -> 1% of each run, Pallas kernels for 26% -> 21%
where the time goes in v7:
time: 84.1 us; the launch traced here: 83.9 us
  Pallas kernels  29.2 us (35%)
  starting transfers between devices  23.1 us (27%)
  waiting for transfers between devices  21.5 us (26%)
  blocking collectives  8.81 us (10%)
  local copies, waits for them, and re-layouts  0.92 us (1%)
    ppermute x23, starting transfers between devices, swap(): return lax.ppermute(x, axis, [(i, i ^ distance) for i in range(size)])  23.1 us
    ppermute x23, waiting for transfers between devices, swap(): return lax.ppermute(x, axis, [(i, i ^ distance) for i in range(size)])  21.5 us
    pallas_call x3, Pallas kernels, fetch(): pl.pallas_call(functools.partial(fetch_kernel, start), out_shape=pltpu.VM...  10 us
    all_to_all x1, blocking collectives, local(): stats = lax.all_to_all(stats, ('group', 'tensor'), 0, 0, tiled=True)  8.81 us
    pallas_call x1, Pallas kernels, local(): pl.pallas_call(functools.partial(logits_kernel, vocab, spots, tensor_size...  5.01 us
    pallas_call x1, Pallas kernels, local(): pl.pallas_call(functools.partial(first_kernel, narrow), out_shape=[pltpu....  4.52 us
    pallas_call x1, Pallas kernels, local(): pl.pallas_call(functools.partial(project_kernel, heads, seq, key_rows, le...  4.27 us
  transfers between devices with their start and end apart: 23, of which 11 were waited for; matrix products, arithmetic and copies ran while one was open for 1% of the time, Pallas kernels for 21%

profile of v7, /device:TPU:0, one launch (start us, length us, event | category | flops | bytes accessed | tf_op | source)
XLA Modules:
  0.0 83.9 jit_solution(3410476802047709412)
XLA Ops:
  0.0 3.0 %collective-permute-start = (bf16[64,512]{1,0:T(8,128)(2,1)}, bf16[64,512]{1,0:T(8,128)(2,1)S(1)}, u32[]{:S(2)}, u32[]{:S(2)}) collective-permute-start(bf16[64,512]{1,0:T(8,128)(2,1)} %refs_0_.1), channel_id=1, source_target_pairs={{0,16},{8,24},{16,0},{24,8},{1,17},{9,25},{17,1},{25,9},{2,18},{10... | collective-permute-start | bytes 196616 | tf_op jit(solution)/shard_map/ppermute | solution.py:47
  3.1 0.9 %reshape.16.refs_1_.target_ref = s32[32,8,1]{2,1,0:T(8,128)S(1)} reshape(s32[256]{0:T(256)} %param.23) | data formatting | bytes 2048 | tf_op jit(solution)/shard_map/reshape | solution.py:457
  4.0 2.6 %collective-permute-done.1.refs_2_.refs_0_ = s32[2]{0:T(128)S(1)} collective-permute-done((s32[2]{0:T(128)}, s32[2]{0:T(128)S(1)}, u32[]{:S(2)}, u32[]{:S(2)}) %collective-permute-start.1) | collective-permute-done | bytes 40 | tf_op jit(solution)/shard_map/ppermute | solution.py:47
  6.7 1.4 %load.1 = (bf16[64,512]{1,0:T(8,128)(2,1)S(1)}, bf16[64,512]{1,0:T(8,128)(2,1)S(1)}, bf16[64,512]{1,0:T(8,128)(2,1)S(1)}, bf16[512,512]{1,0:T(8,128)(2,1)S(1)}, bf16[512,512]{1,0:T(8,128)(2,1)S(1)}) custom-call(bf16[64,512]{1,0:T(8,128)(2,1)S(1)} %pass.1.gate_ref.refs_2_, bf16[64,512]{1,0:T(8,128)(2,1)} %refs_0_.1, bf16[64,512]{1,0:T(8,128)(2,1)} %refs_1_.2, ...), custom_call_target="tpu_custom_call" | custom-call | bytes 2097152 | tf_op jit(solution)/shard_map/load/pallas_call | solution.py:472
  8.1 0.9 %prefix_attention.1 = (bf16[2,64,640]{2,1,0:T(8,128)(2,1)S(1)}, bf16[1,64,640]{2,1,0:T(8,128)(2,1)S(1)}) custom-call(bf16[64,512]{1,0:T(8,128)(2,1)S(1)} %collective-permute-done.2.refs_0_, bf16[64,512]{1,0:T(8,128)(2,1)S(1)} %collective-permute-done.3.refs_1_, bf16[64,512]{1,0:T(8,128)(2,1)S(1)} %pass.1.gate_ref.refs_2_, ...), custom_call_target="tpu_custom_call" | custom-call | tf_op jit(solution)/shard_map/prefix_attention/pallas_call | solution.py:485
  9.5 1.0 %collective-permute-done.4.refs_2_.cross_ref = bf16[2,64,640]{2,1,0:T(8,128)(2,1)S(1)} collective-permute-done((bf16[2,64,640]{2,1,0:T(8,128)(2,1)S(1)}, bf16[2,64,640]{2,1,0:T(8,128)(2,1)S(1)}, u32[]{:S(2)}, u32[]{:S(2)}) %collective-permute-start.4) | collective-permute-done | bytes 163872 | tf_op jit(solution)/shard_map/ppermute | solution.py:47
  10.6 0.9 %merge.1.gate_ref = bf16[64,640]{1,0:T(8,128)(2,1)S(1)} custom-call(s32[2]{0:T(128)S(1)} %collective-permute-done.1.refs_2_.refs_0_, bf16[1,64,640]{2,1,0:T(8,128)(2,1)S(1)} %get-tuple-element.35.refs_1_, bf16[2,64,640]{2,1,0:T(8,128)(2,1)S(1)} %collective-permute-done.4.refs_2_.cross_ref), custom_call_target="tpu_custom_call" | custom-call | tf_op jit(solution)/shard_map/merge/pallas_call | solution.py:497
  11.4 0.9 %collective-permute-start.5 = (bf16[64,640]{1,0:T(8,128)(2,1)S(1)}, bf16[64,640]{1,0:T(8,128)(2,1)S(1)}, u32[]{:S(2)}, u32[]{:S(2)}) collective-permute-start(bf16[64,640]{1,0:T(8,128)(2,1)S(1)} %merge.1.gate_ref), channel_id=1, source_target_pairs={{0,16},{8,24},{16,0},{24,8},{1,17},{9,25},{17,1},{25,9},{2,18},{10... | collective-permute-start | bytes 245768 | tf_op jit(solution)/shard_map/ppermute | solution.py:47
  12.4 1.3 %own_attention.1 = (f32[64,640]{1,0:T(8,128)S(1)}, f32[8,128]{1,0:T(8,128)S(1)}) custom-call(s32[2]{0:T(128)} %lengths_ref.1, s32[2]{0:T(128)} %prompt_ref.3, bf16[64,512]{1,0:T(8,128)(2,1)S(1)} %get-tuple-element.30.q_ref, bf16[64,512]{1,0:T(8,128)(2,1)S(1)} %get-tuple-element.31.rk_ref, bf16[64,512]{1,0:T(8,128)(2,1)S(1)} %get-tuple-element.32.rv_ref, ...), custom_call_target="tpu_custom_call" | custom-call | bytes 4194304 | tf_op jit(solution)/shard_map/own_attention/pallas_call | solution.py:506
  13.7 2.5 %collective-permute-done.5.refs_0_ = bf16[64,640]{1,0:T(8,128)(2,1)S(1)} collective-permute-done((bf16[64,640]{1,0:T(8,128)(2,1)S(1)}, bf16[64,640]{1,0:T(8,128)(2,1)S(1)}, u32[]{:S(2)}, u32[]{:S(2)}) %collective-permute-start.5) | collective-permute-done | bytes 81952 | tf_op jit(solution)/shard_map/ppermute | solution.py:47
  16.2 4.3 %project.1 = (bf16[4,8,2560]{2,1,0:T(8,128)(2,1)S(1)}, f32[4,8,2560]{2,1,0:T(8,128)S(1)}, f32[2,8,2560]{2,1,0:T(8,128)S(1)}, bf16[2,8,2560]{2,1,0:T(8,128)(2,1)S...) custom-call(s32[2]{0:T(128)} %prompt_ref.3, f32[64,640]{1,0:T(8,128)S(1)} %get-tuple-element.38.own_ref, ...), custom_call_target="tpu_custom_call" | custom-call | tf_op jit(solution)/shard_map/project/pallas_call | solution.py:534
  20.5 1.6 %collective-permute-start.6 = (bf16[4,8,2560]{2,1,0:T(8,128)(2,1)S(1)}, bf16[4,8,2560]{2,1,0:T(8,128)(2,1)S(1)}, u32[]{:S(2)}, u32[]{:S(2)}) collective-permute-start(bf16[4,8,2560]{2,1,0:T(8,128)(2,1)S(1)} %get-tuple-element.40), channel_id=1, source_target_pairs={{0,1},{1,0},{2,3},{3,2},{4,5},{5,4},{6,7},{7,6},{8,9},{9,8},{10,11... | collective-permute-start | bytes 491528 | tf_op jit(solution)/shard_map/ppermute | solution.py:47
  22.1 3.6 %collective-permute-start.10 = (bf16[2,8,2560]{2,1,0:T(8,128)(2,1)S(1)}, bf16[2,8,2560]{2,1,0:T(8,128)(2,1)S(1)}, u32[]{:S(2)}, u32[]{:S(2)}) collective-permute-start(bf16[2,8,2560]{2,1,0:T(8,128)(2,1)S(1)} %get-tuple-element.46), channel_id=1, source_target_pairs={{0,6},{1,7},{2,4},{3,5},{4,2},{5,3},{6,0},{7,1},{8,14},{9,15},{10,... | collective-permute-start | bytes 245768 | tf_op jit(solution)/shard_map/ppermute | solution.py:47
  26.5 3.7 %collective-permute-start.7 = (bf16[8,2560]{1,0:T(8,128)(2,1)S(1)}, bf16[8,2560]{1,0:T(8,128)(2,1)S(1)}, u32[]{:S(2)}, u32[]{:S(2)}) collective-permute-start(bf16[8,2560]{1,0:T(8,128)(2,1)S(1)} %get-tuple-element.42), channel_id=1, source_target_pairs={{0,6},{1,7},{2,4},{3,5},{4,2},{5,3},{6,0},{7,1},{8,14},{9,15},{10,... | collective-permute-start | bytes 122888 | tf_op jit(solution)/shard_map/ppermute | solution.py:47
  30.2 2.1 %collective-permute-start.9 = (bf16[8,2560]{1,0:T(8,128)(2,1)S(1)}, bf16[8,2560]{1,0:T(8,128)(2,1)S(1)}, u32[]{:S(2)}, u32[]{:S(2)}) collective-permute-start(bf16[8,2560]{1,0:T(8,128)(2,1)S(1)} %get-tuple-element.44.gate_ref), channel_id=1, source_target_pairs={{0,2},{1,3},{2,0},{3,1},{4,6},{5,7},{6,4},{7,5},{8,10},{9,11},{10,... | collective-permute-start | bytes 122888 | tf_op jit(solution)/shard_map/ppermute | solution.py:47
  32.2 1.8 %collective-permute-done.11.refs_1_ = bf16[2,8,2560]{2,1,0:T(8,128)(2,1)S(1)} collective-permute-done((bf16[2,8,2560]{2,1,0:T(8,128)(2,1)S(1)}, bf16[2,8,2560]{2,1,0:T(8,128)(2,1)S(1)}, u32[]{:S(2)}, u32[]{:S(2)}) %collective-permute-start.11) | collective-permute-done | bytes 81952 | tf_op jit(solution)/shard_map/ppermute | solution.py:47
  34.3 1.2 %collective-permute-done.8.refs_2_ = bf16[8,2560]{1,0:T(8,128)(2,1)S(1)} collective-permute-done((bf16[8,2560]{1,0:T(8,128)(2,1)S(1)}, bf16[8,2560]{1,0:T(8,128)(2,1)S(1)}, u32[]{:S(2)}, u32[]{:S(2)}) %collective-permute-start.8) | collective-permute-done | bytes 40992 | tf_op jit(solution)/shard_map/ppermute | solution.py:47
  35.5 2.7 %collective-permute-done.13.refs_5_ = bf16[8,2560]{1,0:T(8,128)(2,1)S(1)} collective-permute-done((bf16[8,2560]{1,0:T(8,128)(2,1)S(1)}, bf16[8,2560]{1,0:T(8,128)(2,1)S(1)}, u32[]{:S(2)}, u32[]{:S(2)}) %collective-permute-start.13) | collective-permute-done | bytes 40992 | tf_op jit(solution)/shard_map/ppermute | solution.py:47
  38.8 3.3 %collective-permute-start.15 = (bf16[8,5120]{1,0:T(8,128)(2,1)S(1)}, bf16[8,5120]{1,0:T(8,128)(2,1)S(1)}, u32[]{:S(2)}, u32[]{:S(2)}) collective-permute-start(bf16[8,5120]{1,0:T(8,128)(2,1)S(1)} %norm.1.gate_ref.refs_0_), channel_id=1, source_target_pairs={{0,4},{1,5},{2,6},{3,7},{4,0},{5,1},{6,2},{7,3},{8,12},{9,13},{10,... | collective-permute-start | bytes 245768 | tf_op jit(solution)/shard_map/ppermute | solution.py:47
  42.8 3.3 %fetch.3.refs_4_.weight_ref = bf16[1280,3072]{1,0:T(8,128)(2,1)S(1)} custom-call(bf16[5120,3072]{1,0:T(8,128)(2,1)} %source_ref.7, bf16[8,5120]{1,0:T(8,128)(2,1)S(1)} %norm.1.gate_ref.refs_0_), custom_call_target="tpu_custom_call" | custom-call | bytes 7864320 | tf_op jit(solution)/shard_map/fetch/pallas_call | solution.py:518
  46.1 2.2 %collective-permute-done.16.refs_3_ = bf16[8,5120]{1,0:T(8,128)(2,1)S(1)} collective-permute-done((bf16[8,5120]{1,0:T(8,128)(2,1)S(1)}, bf16[8,5120]{1,0:T(8,128)(2,1)S(1)}, u32[]{:S(2)}, u32[]{:S(2)}) %collective-permute-start.16) | collective-permute-done | bytes 81952 | tf_op jit(solution)/shard_map/ppermute | solution.py:47
  48.5 0.9 %collective-permute-start.20 = (bf16[4,8,2560]{2,1,0:T(8,128)(2,1)S(1)}, bf16[4,8,2560]{2,1,0:T(8,128)(2,1)S(1)}, u32[]{:S(2)}, u32[]{:S(2)}) collective-permute-start(bf16[4,8,2560]{2,1,0:T(8,128)(2,1)S(1)} %get-tuple-element.53), channel_id=1, source_target_pairs={{0,16},{8,24},{16,0},{24,8},{1,17},{9,25},{17,1},{25,9},{2,18},{10... | collective-permute-start | bytes 491528 | tf_op jit(solution)/shard_map/ppermute | solution.py:47
  49.4 3.3 %fetch.4.refs_2_.weight_ref = bf16[1280,3072]{1,0:T(8,128)(2,1)S(1)} custom-call(bf16[5120,3072]{1,0:T(8,128)(2,1)} %source_ref.7, bf16[4,8,2560]{2,1,0:T(8,128)(2,1)S(1)} %get-tuple-element.51.gate_ref.refs_0_), custom_call_target="tpu_custom_call" | custom-call | bytes 7864320 | tf_op jit(solution)/shard_map/fetch/pallas_call | solution.py:518
  52.7 2.8 %collective-permute-done.17.refs_1_ = bf16[4,8,2560]{2,1,0:T(8,128)(2,1)S(1)} collective-permute-done((bf16[4,8,2560]{2,1,0:T(8,128)(2,1)S(1)}, bf16[4,8,2560]{2,1,0:T(8,128)(2,1)S(1)}, u32[]{:S(2)}, u32[]{:S(2)}) %collective-permute-start.17) | collective-permute-done | bytes 163872 | tf_op jit(solution)/shard_map/ppermute | solution.py:47
  55.6 0.9 %collective-permute-start.18 = (bf16[8,8,2560]{2,1,0:T(8,128)(2,1)S(1)}, bf16[8,8,2560]{2,1,0:T(8,128)(2,1)S(1)}, u32[]{:S(2)}, u32[]{:S(2)}) collective-permute-start(bf16[8,8,2560]{2,1,0:T(8,128)(2,1)S(1)} %join.2.gate_ref.refs_0_), channel_id=1, source_target_pairs={{0,16},{8,24},{16,0},{24,8},{1,17},{9,25},{17,1},{25,9},{2,18},{10... | collective-permute-start | bytes 983048 | tf_op jit(solution)/shard_map/ppermute | solution.py:47
  56.6 3.3 %fetch.5.refs_2_.next_ref = bf16[1280,3072]{1,0:T(8,128)(2,1)S(1)} custom-call(bf16[5120,3072]{1,0:T(8,128)(2,1)} %source_ref.7, bf16[8,8,2560]{2,1,0:T(8,128)(2,1)S(1)} %join.2.gate_ref.refs_0_), custom_call_target="tpu_custom_call" | custom-call | bytes 7864320 | tf_op jit(solution)/shard_map/fetch/pallas_call | solution.py:518
  60.0 2.7 %collective-permute-done.18.refs_1_ = bf16[8,8,2560]{2,1,0:T(8,128)(2,1)S(1)} collective-permute-done((bf16[8,8,2560]{2,1,0:T(8,128)(2,1)S(1)}, bf16[8,8,2560]{2,1,0:T(8,128)(2,1)S(1)}, u32[]{:S(2)}, u32[]{:S(2)}) %collective-permute-start.18) | collective-permute-done | bytes 327712 | tf_op jit(solution)/shard_map/ppermute | solution.py:47
  62.8 0.8 collective-permute-done.21
  63.9 1.1 %collective-permute-done.19.right_ref = bf16[128,2560]{1,0:T(8,128)(2,1)S(1)} collective-permute-done((bf16[128,2560]{1,0:T(8,128)(2,1)S(1)}, bf16[128,2560]{1,0:T(8,128)(2,1)S(1)}, u32[]{:S(2)}, u32[]{:S(2)}) %collective-permute-start.19) | collective-permute-done | bytes 655392 | tf_op jit(solution)/shard_map/ppermute | solution.py:47
  64.9 4.5 %logits_first.1 = (f32[256,3072]{1,0:T(8,128)S(1)}, bf16[1280,3072]{1,0:T(8,128)(2,1)S(1)}) custom-call(bf16[128,2560]{1,0:T(8,128)(2,1)S(1)} %bitcast.5, bf16[128,2560]{1,0:T(8,128)(2,1)S(1)} %collective-permute-done.19.right_ref, bf16[1280,3072]{1,0:T(8,128)(2,1)S(1)} %fetch.4.refs_2_.weight_ref, bf16[1280,3072]{1,0:T(8,128)(2,1)S(1)} %fetch.5.refs_2_.next_ref, ...), custom_call_target="tpu_custom_call" | custom-call | flops 4026531840 | tf_op jit(solution)/shard_map/logits_first/pallas_call | solution.py:635
  69.5 5.0 %logits.1 = f32[32,1,128]{2,1,0:T(1,128)S(1)} custom-call(f32[256,3072]{1,0:T(8,128)S(1)} %get-tuple-element.52.sum_in_ref, bf16[128,2560]{1,0:T(8,128)(2,1)S(1)} %maximum_bitcast_fusion.left_ref, bf16[128,2560]{1,0:T(8,128)(2,1)S(1)} %collective-permute-done.22.right_ref, s32[32,8,1]{2,1,0:T(8,128)S(1)} %reshape.16.refs_1_.target_ref, ...), custom_call_target="tpu_custom_call" | custom-call | flops 4026531840 | tf_op jit(solution)/shard_map/logits/pallas_call | solution.py:648
  74.5 8.8 %all_to_all.5.stats_ref = f32[32,1,128]{2,1,0:T(1,128)S(1)} all-to-all(f32[32,1,128]{2,1,0:T(1,128)S(1)} %logits.1), channel_id=1, replica_groups=mesh['group'=4,'tensor'=8] {'group','tensor'}, dimensions={0} | all-to-all | bytes 32768 | tf_op jit(solution)/shard_map/all_to_all | solution.py:661
  (42 shorter events, 4.2 us)
Async XLA Ops:
  0.0 34.2 %copy-start.1 = (bf16[5120]{0:T(1024)(128)(2,1)S(1)}, bf16[5120]{0:T(1024)(128)(2,1)}, u32[]{:S(2)}) copy-start(bf16[5120]{0:T(1024)(128)(2,1)} %param.21) | copy-start | bytes 30724
  0.0 38.2 %copy-start = (bf16[64,5120]{1,0:T(8,128)(2,1)S(1)}, bf16[64,5120]{1,0:T(8,128)(2,1)}, u32[]{:S(2)}) copy-start(bf16[64,5120]{1,0:T(8,128)(2,1)} %param.19) | copy-start | bytes 1966084
  0.0 6.6 %collective-permute-start = (bf16[64,512]{1,0:T(8,128)(2,1)}, bf16[64,512]{1,0:T(8,128)(2,1)S(1)}, u32[]{:S(2)}, u32[]{:S(2)}) collective-permute-start(bf16[64,512]{1,0:T(8,128)(2,1)} %refs_0_.1), channel_id=1, source_target_pairs={{0,16},{8,24},{16,0},{24,8},{1,17},{9,25},{17,1},{25,9},{2,18},{10... | collective-permute-start | bytes 196616 | tf_op jit(solution)/shard_map/ppermute | solution.py:47
  3.0 5.1 %collective-permute-start.2 = (bf16[64,512]{1,0:T(8,128)(2,1)}, bf16[64,512]{1,0:T(8,128)(2,1)S(1)}, u32[]{:S(2)}, u32[]{:S(2)}) collective-permute-start(bf16[64,512]{1,0:T(8,128)(2,1)} %refs_0_.1), channel_id=1, source_target_pairs={{0,8},{8,0},{16,24},{24,16},{1,9},{9,1},{17,25},{25,17},{2,10},{10... | collective-permute-start | bytes 196616 | tf_op jit(solution)/shard_map/ppermute | solution.py:47
  3.0 3.7 %collective-permute-start.1 = (s32[2]{0:T(128)}, s32[2]{0:T(128)S(1)}, u32[]{:S(2)}, u32[]{:S(2)}) collective-permute-start(s32[2]{0:T(128)} %prompt_ref.3), channel_id=1, source_target_pairs={{0,16},{8,24},{16,0},{24,8},{1,17},{9,25},{17,1},{25,9},{2,18},{10... | collective-permute-start | bytes 32 | tf_op jit(solution)/shard_map/ppermute | solution.py:47
  6.7 1.5 %collective-permute-start.3 = (bf16[64,512]{1,0:T(8,128)(2,1)S(1)}, bf16[64,512]{1,0:T(8,128)(2,1)S(1)}, u32[]{:S(2)}, u32[]{:S(2)}) collective-permute-start(bf16[64,512]{1,0:T(8,128)(2,1)S(1)} %pass.1.gate_ref.refs_2_), channel_id=1, source_target_pairs={{0,8},{8,0},{16,24},{24,16},{1,9},{9,1},{17,25},{25,17},{2,10},{10... | collective-permute-start | bytes 196616 | tf_op jit(solution)/shard_map/ppermute | solution.py:47
  9.0 1.6 %collective-permute-start.4 = (bf16[2,64,640]{2,1,0:T(8,128)(2,1)S(1)}, bf16[2,64,640]{2,1,0:T(8,128)(2,1)S(1)}, u32[]{:S(2)}, u32[]{:S(2)}) collective-permute-start(bf16[2,64,640]{2,1,0:T(8,128)(2,1)S(1)} %get-tuple-element.36), channel_id=1, source_target_pairs={{0,8},{8,0},{16,24},{24,16},{1,9},{9,1},{17,25},{25,17},{2,10},{10... | collective-permute-start | bytes 491528 | tf_op jit(solution)/shard_map/ppermute | solution.py:47
  11.4 4.8 %collective-permute-start.5 = (bf16[64,640]{1,0:T(8,128)(2,1)S(1)}, bf16[64,640]{1,0:T(8,128)(2,1)S(1)}, u32[]{:S(2)}, u32[]{:S(2)}) collective-permute-start(bf16[64,640]{1,0:T(8,128)(2,1)S(1)} %merge.1.gate_ref), channel_id=1, source_target_pairs={{0,16},{8,24},{16,0},{24,8},{1,17},{9,25},{17,1},{25,9},{2,18},{10... | collective-permute-start | bytes 245768 | tf_op jit(solution)/shard_map/ppermute | solution.py:47
  20.5 5.9 %collective-permute-start.6 = (bf16[4,8,2560]{2,1,0:T(8,128)(2,1)S(1)}, bf16[4,8,2560]{2,1,0:T(8,128)(2,1)S(1)}, u32[]{:S(2)}, u32[]{:S(2)}) collective-permute-start(bf16[4,8,2560]{2,1,0:T(8,128)(2,1)S(1)} %get-tuple-element.40), channel_id=1, source_target_pairs={{0,1},{1,0},{2,3},{3,2},{4,5},{5,4},{6,7},{7,6},{8,9},{9,8},{10,11... | collective-permute-start | bytes 491528 | tf_op jit(solution)/shard_map/ppermute | solution.py:47
  22.1 8.1 %collective-permute-start.10 = (bf16[2,8,2560]{2,1,0:T(8,128)(2,1)S(1)}, bf16[2,8,2560]{2,1,0:T(8,128)(2,1)S(1)}, u32[]{:S(2)}, u32[]{:S(2)}) collective-permute-start(bf16[2,8,2560]{2,1,0:T(8,128)(2,1)S(1)} %get-tuple-element.46), channel_id=1, source_target_pairs={{0,6},{1,7},{2,4},{3,5},{4,2},{5,3},{6,0},{7,1},{8,14},{9,15},{10,... | collective-permute-start | bytes 245768 | tf_op jit(solution)/shard_map/ppermute | solution.py:47
  25.7 8.4 %collective-permute-start.11 = (bf16[2,8,2560]{2,1,0:T(8,128)(2,1)S(1)}, bf16[2,8,2560]{2,1,0:T(8,128)(2,1)S(1)}, u32[]{:S(2)}, u32[]{:S(2)}) collective-permute-start(bf16[2,8,2560]{2,1,0:T(8,128)(2,1)S(1)} %get-tuple-element.47), channel_id=1, source_target_pairs={{0,4},{1,5},{2,6},{3,7},{4,0},{5,1},{6,2},{7,3},{8,12},{9,13},{10,... | collective-permute-start | bytes 245768 | tf_op jit(solution)/shard_map/ppermute | solution.py:47
  25.7 8.4 %collective-permute-start.12 = (bf16[2,8,2560]{2,1,0:T(8,128)(2,1)S(1)}, bf16[2,8,2560]{2,1,0:T(8,128)(2,1)S(1)}, u32[]{:S(2)}, u32[]{:S(2)}) collective-permute-start(bf16[2,8,2560]{2,1,0:T(8,128)(2,1)S(1)} %get-tuple-element.48), channel_id=1, source_target_pairs={{0,2},{1,3},{2,0},{3,1},{4,6},{5,7},{6,4},{7,5},{8,10},{9,11},{10,... | collective-permute-start | bytes 245768 | tf_op jit(solution)/shard_map/ppermute | solution.py:47
  26.5 7.8 %collective-permute-start.7 = (bf16[8,2560]{1,0:T(8,128)(2,1)S(1)}, bf16[8,2560]{1,0:T(8,128)(2,1)S(1)}, u32[]{:S(2)}, u32[]{:S(2)}) collective-permute-start(bf16[8,2560]{1,0:T(8,128)(2,1)S(1)} %get-tuple-element.42), channel_id=1, source_target_pairs={{0,6},{1,7},{2,4},{3,5},{4,2},{5,3},{6,0},{7,1},{8,14},{9,15},{10,... | collective-permute-start | bytes 122888 | tf_op jit(solution)/shard_map/ppermute | solution.py:47
  30.2 5.3 %collective-permute-start.8 = (bf16[8,2560]{1,0:T(8,128)(2,1)S(1)}, bf16[8,2560]{1,0:T(8,128)(2,1)S(1)}, u32[]{:S(2)}, u32[]{:S(2)}) collective-permute-start(bf16[8,2560]{1,0:T(8,128)(2,1)S(1)} %get-tuple-element.43), channel_id=1, source_target_pairs={{0,4},{1,5},{2,6},{3,7},{4,0},{5,1},{6,2},{7,3},{8,12},{9,13},{10,... | collective-permute-start | bytes 122888 | tf_op jit(solution)/shard_map/ppermute | solution.py:47
  30.2 5.3 %collective-permute-start.9 = (bf16[8,2560]{1,0:T(8,128)(2,1)S(1)}, bf16[8,2560]{1,0:T(8,128)(2,1)S(1)}, u32[]{:S(2)}, u32[]{:S(2)}) collective-permute-start(bf16[8,2560]{1,0:T(8,128)(2,1)S(1)} %get-tuple-element.44.gate_ref), channel_id=1, source_target_pairs={{0,2},{1,3},{2,0},{3,1},{4,6},{5,7},{6,4},{7,5},{8,10},{9,11},{10,... | collective-permute-start | bytes 122888 | tf_op jit(solution)/shard_map/ppermute | solution.py:47
  34.1 4.1 %collective-permute-start.13 = (bf16[8,2560]{1,0:T(8,128)(2,1)S(1)}, bf16[8,2560]{1,0:T(8,128)(2,1)S(1)}, u32[]{:S(2)}, u32[]{:S(2)}) collective-permute-start(bf16[8,2560]{1,0:T(8,128)(2,1)S(1)} %get-tuple-element.50), channel_id=1, source_target_pairs={{0,1},{1,0},{2,3},{3,2},{4,5},{5,4},{6,7},{7,6},{8,9},{9,8},{10,11... | collective-permute-start | bytes 122888 | tf_op jit(solution)/shard_map/ppermute | solution.py:47
  38.3 7.8 %collective-permute-start.14 = (bf16[8,5120]{1,0:T(8,128)(2,1)S(1)}, bf16[8,5120]{1,0:T(8,128)(2,1)S(1)}, u32[]{:S(2)}, u32[]{:S(2)}) collective-permute-start(bf16[8,5120]{1,0:T(8,128)(2,1)S(1)} %norm.1.gate_ref.refs_0_), channel_id=1, source_target_pairs={{0,2},{1,3},{2,0},{3,1},{4,6},{5,7},{6,4},{7,5},{8,10},{9,11},{10,... | collective-permute-start | bytes 245768 | tf_op jit(solution)/shard_map/ppermute | solution.py:47
  38.8 7.4 %collective-permute-start.15 = (bf16[8,5120]{1,0:T(8,128)(2,1)S(1)}, bf16[8,5120]{1,0:T(8,128)(2,1)S(1)}, u32[]{:S(2)}, u32[]{:S(2)}) collective-permute-start(bf16[8,5120]{1,0:T(8,128)(2,1)S(1)} %norm.1.gate_ref.refs_0_), channel_id=1, source_target_pairs={{0,4},{1,5},{2,6},{3,7},{4,0},{5,1},{6,2},{7,3},{8,12},{9,13},{10,... | collective-permute-start | bytes 245768 | tf_op jit(solution)/shard_map/ppermute | solution.py:47
  42.1 6.2 %collective-permute-start.16 = (bf16[8,5120]{1,0:T(8,128)(2,1)S(1)}, bf16[8,5120]{1,0:T(8,128)(2,1)S(1)}, u32[]{:S(2)}, u32[]{:S(2)}) collective-permute-start(bf16[8,5120]{1,0:T(8,128)(2,1)S(1)} %norm.1.gate_ref.refs_0_), channel_id=1, source_target_pairs={{0,6},{1,7},{2,4},{3,5},{4,2},{5,3},{6,0},{7,1},{8,14},{9,15},{10,... | collective-permute-start | bytes 245768 | tf_op jit(solution)/shard_map/ppermute | solution.py:47
  48.4 7.1 %collective-permute-start.17 = (bf16[4,8,2560]{2,1,0:T(8,128)(2,1)S(1)}, bf16[4,8,2560]{2,1,0:T(8,128)(2,1)S(1)}, u32[]{:S(2)}, u32[]{:S(2)}) collective-permute-start(bf16[4,8,2560]{2,1,0:T(8,128)(2,1)S(1)} %get-tuple-element.51.gate_ref.refs_0_), channel_id=1, source_target_pairs={{0,1},{1,0},{2,3},{3,2},{4,5},{5,4},{6,7},{7,6},{8,9},{9,8},{10,11... | collective-permute-start | bytes 491528 | tf_op jit(solution)/shard_map/ppermute | solution.py:47
  48.5 8.0 %collective-permute-start.20 = (bf16[4,8,2560]{2,1,0:T(8,128)(2,1)S(1)}, bf16[4,8,2560]{2,1,0:T(8,128)(2,1)S(1)}, u32[]{:S(2)}, u32[]{:S(2)}) collective-permute-start(bf16[4,8,2560]{2,1,0:T(8,128)(2,1)S(1)} %get-tuple-element.53), channel_id=1, source_target_pairs={{0,16},{8,24},{16,0},{24,8},{1,17},{9,25},{17,1},{25,9},{2,18},{10... | collective-permute-start | bytes 491528 | tf_op jit(solution)/shard_map/ppermute | solution.py:47
  55.6 7.1 %collective-permute-start.18 = (bf16[8,8,2560]{2,1,0:T(8,128)(2,1)S(1)}, bf16[8,8,2560]{2,1,0:T(8,128)(2,1)S(1)}, u32[]{:S(2)}, u32[]{:S(2)}) collective-permute-start(bf16[8,8,2560]{2,1,0:T(8,128)(2,1)S(1)} %join.2.gate_ref.refs_0_), channel_id=1, source_target_pairs={{0,16},{8,24},{16,0},{24,8},{1,17},{9,25},{17,1},{25,9},{2,18},{10... | collective-permute-start | bytes 983048 | tf_op jit(solution)/shard_map/ppermute | solution.py:47
  56.5 7.1 %collective-permute-start.21 = (bf16[8,8,2560]{2,1,0:T(8,128)(2,1)S(1)}, bf16[8,8,2560]{2,1,0:T(8,128)(2,1)S(1)}, u32[]{:S(2)}, u32[]{:S(2)}) collective-permute-start(bf16[8,8,2560]{2,1,0:T(8,128)(2,1)S(1)} %pad_maximum_fusion), channel_id=1, source_target_pairs={{0,1},{1,0},{2,3},{3,2},{4,5},{5,4},{6,7},{7,6},{8,9},{9,8},{10,11... | collective-permute-start | bytes 983048 | tf_op jit(solution)/shard_map/ppermute | solution.py:47
  62.8 2.2 %collective-permute-start.19 = (bf16[128,2560]{1,0:T(8,128)(2,1)S(1)}, bf16[128,2560]{1,0:T(8,128)(2,1)S(1)}, u32[]{:S(2)}, u32[]{:S(2)}) collective-permute-start(bf16[128,2560]{1,0:T(8,128)(2,1)S(1)} %bitcast.4), channel_id=1, source_target_pairs={{0,8},{8,0},{16,24},{24,16},{1,9},{9,1},{17,25},{25,17},{2,10},{10... | collective-permute-start | bytes 1966088 | tf_op jit(solution)/shard_map/ppermute | solution.py:47
  63.8 5.7 %collective-permute-start.22 = (bf16[128,2560]{1,0:T(8,128)(2,1)S(1)}, bf16[128,2560]{1,0:T(8,128)(2,1)S(1)}, u32[]{:S(2)}, u32[]{:S(2)}) collective-permute-start(bf16[128,2560]{1,0:T(8,128)(2,1)S(1)} %maximum_bitcast_fusion.left_ref), channel_id=1, source_target_pairs={{0,8},{8,0},{16,24},{24,16},{1,9},{9,1},{17,25},{25,17},{2,10},{10... | collective-permute-start | bytes 1966088 | tf_op jit(solution)/shard_map/ppermute | solution.py:47

commit v8 on v6

--- a/solution.py
+++ b/solution.py
@@ -82,6 +82,11 @@
         for part, value in enumerate((first, second, third)):
             packed = jnp.where(lane == 3 * head + part, value, packed)
     return packed.astype(BF16)
+
+
+def pass_kernel(count, *refs):
+    for ref, out_ref in zip(refs, refs[-count:]):
+        out_ref[...] = ref[...]
 
 
 def load_kernel(count, gate_ref, *refs):
@@ -428,9 +433,23 @@
     vocab = lm_weight.shape[1]
     i32 = jnp.int32
 
+    wanted = targets.reshape(-1, share, 1)
+    above = list(range(2, group_size, 2))
     distances = list(range(group_size - 1, 0, -1))
-    queries = [swap(resp_query, "group", d, group_size) for d in distances]
-    wanted = targets.reshape(-1, share, 1)
+    far_queries = [swap(resp_query, "group", a, group_size) for a in above]
+    queries = {1: swap(resp_query, "group", 1, group_size)}
+    far_queries = pl.pallas_call(
+        functools.partial(pass_kernel, len(above)),
+        out_shape=[jax.ShapeDtypeStruct(x.shape, x.dtype) for x in far_queries],
+        in_specs=[vmem()] * len(above) + [anywhere()],
+        out_specs=[vmem()] * len(above),
+        compiler_params=params(1),
+        name="pass",
+    )(*map(held, far_queries), wanted)
+    for a, x in zip(above, far_queries):
+        queries[a] = x
+        queries[a + 1] = swap(x, "group", 1, group_size)
+    queries = [queries[d] for d in distances]
     inputs = (resp_query, resp_key, resp_value, prompt_keys, prompt_values)
     loaded = pl.pallas_call(
         functools.partial(load_kernel, len(inputs)),
@@ -441,7 +460,7 @@
         compiler_params=params(1),
         cost_estimate=cost(moved=2 * MIB),
         name="load",
-    )(wanted, *map(stored, inputs))
+    )(far_queries[0], *map(stored, inputs))
     query, own_keys, own_values, keys, values = map(held, loaded)
     answers = pl.pallas_call(
         functools.partial(prefix_kernel, heads, len(distances)),
@@ -550,7 +569,6 @@
         *map(held, (left[0], *got_left, right[0], got_right)),
     )
 
-    above = list(range(2, group_size, 2))
     order = [0] + far
     here = [(g, x) for g in [0] + above for x in (0, 1)]
     column = [swap(normed, "tensor", d, tensor_size) for d in far[::-1]]
@@ -592,7 +610,7 @@
         halves.append((tokens, swap(tokens, "group", 1, group_size)))
     spots = [(g + c, t + x) for c in (0, 1) for g, x in here for t in order]
     total_rows = 2 * tokens.shape[0]
-    narrow = 3072 if vocab % 3072 == 0 else vocab
+    narrow = 1536 if vocab % 1536 == 0 else vocab
     limit = 10 if total_rows <= 256 else 24
     work = 2 * total_rows * (half) * vocab
     first, last = pl.pallas_call(
@@ -609,7 +627,7 @@
         name="logits_first",
     )(*map(held, (*halves[0], first_quarter, second_quarter)), stored(lm_weight))
     stats = pl.pallas_call(
-        functools.partial(logits_kernel, narrow, spots, tensor_size),
+        functools.partial(logits_kernel, vocab, spots, tensor_size),
         out_shape=jax.ShapeDtypeStruct((len(spots), 1, 128), F32),
         in_specs=[vmem()] * 6,
         out_specs=vmem(),

time: 84.4 us -> 82 us (0.972)
  Pallas kernels: 31.8 us -> 29.6 us
    pallas_call x1, Pallas kernels: 6.77 us -> 4.52 us  [local(): pl.pallas_call(functools.partial(first_kernel, narrow), out_shape=[pltpu....]
    pallas_call x1 -> x2, Pallas kernels: 5.01 us -> 5.02 us  [the longest x1 5.01 us: local(): pl.pallas_call(functools.partial(logits_kernel, vocab, spots, tensor_size...]
  transfers between devices with their start and end apart: 23 -> 23, of which waited for: 10 -> 10; matrix products, arithmetic and copies ran while one was open for 1% -> 1% of each run, Pallas kernels for 26% -> 24%
where the time goes in v8:
time: 82 us; the launch traced here: 81.8 us
  Pallas kernels  29.6 us (36%)
  starting transfers between devices  25.1 us (31%)
  waiting for transfers between devices  16.9 us (21%)
  blocking collectives  8.92 us (11%)
  local copies, waits for them, and re-layouts  0.92 us (1%)
    ppermute x23, starting transfers between devices, swap(): return lax.ppermute(x, axis, [(i, i ^ distance) for i in range(size)])  25.1 us
    ppermute x23, waiting for transfers between devices, swap(): return lax.ppermute(x, axis, [(i, i ^ distance) for i in range(size)])  16.9 us
    pallas_call x3, Pallas kernels, fetch(): pl.pallas_call(functools.partial(fetch_kernel, start), out_shape=pltpu.VM...  10 us
    all_to_all x1, blocking collectives, local(): stats = lax.all_to_all(stats, ('group', 'tensor'), 0, 0, tiled=True)  8.92 us
    pallas_call x1, Pallas kernels, local(): pl.pallas_call(functools.partial(logits_kernel, vocab, spots, tensor_size...  5.01 us
    pallas_call x1, Pallas kernels, local(): pl.pallas_call(functools.partial(first_kernel, narrow), out_shape=[pltpu....  4.52 us
    pallas_call x1, Pallas kernels, local(): pl.pallas_call(functools.partial(own_kernel, heads, seq, share), out_shap...  3.54 us
    pallas_call x1, Pallas kernels, local(): pl.pallas_call(functools.partial(project_kernel, heads, seq, share, wide,...  3.27 us
  transfers between devices with their start and end apart: 23, of which 10 were waited for; matrix products, arithmetic and copies ran while one was open for 1% of the time, Pallas kernels for 24%

profile of v8, /device:TPU:0, one launch (start us, length us, event | category | flops | bytes accessed | tf_op | source)
XLA Modules:
  0.0 81.8 jit_solution(10591021965966841078)
XLA Ops:
  0.0 3.0 %collective-permute-start = (bf16[64,512]{1,0:T(8,128)(2,1)}, bf16[64,512]{1,0:T(8,128)(2,1)S(1)}, u32[]{:S(2)}, u32[]{:S(2)}) collective-permute-start(bf16[64,512]{1,0:T(8,128)(2,1)} %refs_0_.1), channel_id=1, source_target_pairs={{0,16},{8,24},{16,0},{24,8},{1,17},{9,25},{17,1},{25,9},{2,18},{10... | collective-permute-start | bytes 196616 | tf_op jit(solution)/shard_map/ppermute | solution.py:47
  3.0 0.9 %reshape.16.refs_1_.target_ref = s32[32,8,1]{2,1,0:T(8,128)S(1)} reshape(s32[256]{0:T(256)} %param.23) | data formatting | bytes 2048 | tf_op jit(solution)/shard_map/reshape | solution.py:436
  3.9 1.6 %collective-permute-done.refs_0_ = bf16[64,512]{1,0:T(8,128)(2,1)S(1)} collective-permute-done((bf16[64,512]{1,0:T(8,128)(2,1)}, bf16[64,512]{1,0:T(8,128)(2,1)S(1)}, u32[]{:S(2)}, u32[]{:S(2)}) %collective-permute-start) | collective-permute-done | bytes 65568 | tf_op jit(solution)/shard_map/ppermute | solution.py:47
  5.5 1.4 %load.1 = (bf16[64,512]{1,0:T(8,128)(2,1)S(1)}, bf16[64,512]{1,0:T(8,128)(2,1)S(1)}, bf16[64,512]{1,0:T(8,128)(2,1)S(1)}, bf16[512,512]{1,0:T(8,128)(2,1)S(1)}, bf16[512,512]{1,0:T(8,128)(2,1)S(1)}) custom-call(bf16[64,512]{1,0:T(8,128)(2,1)S(1)} %pass.1.gate_ref.refs_1_, bf16[64,512]{1,0:T(8,128)(2,1)} %refs_0_.1, bf16[64,512]{1,0:T(8,128)(2,1)} %refs_1_.1, ...), custom_call_target="tpu_custom_call" | custom-call | bytes 2097152 | tf_op jit(solution)/shard_map/load/pallas_call | solution.py:454
  7.0 0.9 %prefix_attention.1 = (bf16[64,640]{1,0:T(8,128)(2,1)S(1)}, bf16[64,640]{1,0:T(8,128)(2,1)S(1)}, bf16[64,640]{1,0:T(8,128)(2,1)S(1)}) custom-call(bf16[64,512]{1,0:T(8,128)(2,1)S(1)} %collective-permute-done.1.refs_0_, bf16[64,512]{1,0:T(8,128)(2,1)S(1)} %pass.1.gate_ref.refs_1_, bf16[64,512]{1,0:T(8,128)(2,1)S(1)} %collective-permute-done.2.refs_2_, ...), custom_call_target="tpu_custom_call" | custom-call | tf_op jit(solution)/shard_map/prefix_attention/pallas_call | solution.py:465
  7.8 2.1 %collective-permute-start.3 = (bf16[64,640]{1,0:T(8,128)(2,1)S(1)}, bf16[64,640]{1,0:T(8,128)(2,1)S(1)}, u32[]{:S(2)}, u32[]{:S(2)}) collective-permute-start(bf16[64,640]{1,0:T(8,128)(2,1)S(1)} %get-tuple-element.37.gate_ref), channel_id=1, source_target_pairs={{0,24},{8,16},{16,8},{24,0},{1,25},{9,17},{17,9},{25,1},{2,26},{10... | collective-permute-start | bytes 245768 | tf_op jit(solution)/shard_map/ppermute | solution.py:47
  10.2 3.5 %own_attention.1 = (f32[64,640]{1,0:T(8,128)S(1)}, f32[8,128]{1,0:T(8,128)S(1)}, bf16[512,5120]{1,0:T(8,128)(2,1)S(1)}) custom-call(s32[2]{0:T(128)} %lengths_ref.1, s32[2]{0:T(128)} %prompt_ref.3, bf16[64,512]{1,0:T(8,128)(2,1)S(1)} %get-tuple-element.32.q_ref, bf16[64,512]{1,0:T(8,128)(2,1)S(1)} %get-tuple-element.33.rk_ref, ...), custom_call_target="tpu_custom_call" | custom-call | bytes 8388608 | tf_op jit(solution)/shard_map/own_attention/pallas_call | solution.py:474
  13.7 1.0 %collective-permute-done.4.refs_1_ = bf16[64,640]{1,0:T(8,128)(2,1)S(1)} collective-permute-done((bf16[64,640]{1,0:T(8,128)(2,1)S(1)}, bf16[64,640]{1,0:T(8,128)(2,1)S(1)}, u32[]{:S(2)}, u32[]{:S(2)}) %collective-permute-start.4) | collective-permute-done | bytes 81952 | tf_op jit(solution)/shard_map/ppermute | solution.py:47
  14.7 3.3 %project.1 = (bf16[4,8,2560]{2,1,0:T(8,128)(2,1)S(1)}, f32[4,8,2560]{2,1,0:T(8,128)S(1)}, f32[2,8,2560]{2,1,0:T(8,128)S(1)}, bf16[2,8,2560]{2,1,0:T(8,128)(2,1)S...) custom-call(s32[2]{0:T(128)} %prompt_ref.3, f32[64,640]{1,0:T(8,128)S(1)} %get-tuple-element.39.own_ref, ...), custom_call_target="tpu_custom_call" | custom-call | tf_op jit(solution)/shard_map/project/pallas_call | solution.py:517
  18.0 1.7 %collective-permute-start.6 = (bf16[4,8,2560]{2,1,0:T(8,128)(2,1)S(1)}, bf16[4,8,2560]{2,1,0:T(8,128)(2,1)S(1)}, u32[]{:S(2)}, u32[]{:S(2)}) collective-permute-start(bf16[4,8,2560]{2,1,0:T(8,128)(2,1)S(1)} %get-tuple-element.44), channel_id=1, source_target_pairs={{0,1},{1,0},{2,3},{3,2},{4,5},{5,4},{6,7},{7,6},{8,9},{9,8},{10,11... | collective-permute-start | bytes 491528 | tf_op jit(solution)/shard_map/ppermute | solution.py:47
  19.7 3.6 %collective-permute-start.10 = (bf16[2,8,2560]{2,1,0:T(8,128)(2,1)S(1)}, bf16[2,8,2560]{2,1,0:T(8,128)(2,1)S(1)}, u32[]{:S(2)}, u32[]{:S(2)}) collective-permute-start(bf16[2,8,2560]{2,1,0:T(8,128)(2,1)S(1)} %get-tuple-element.50), channel_id=1, source_target_pairs={{0,6},{1,7},{2,4},{3,5},{4,2},{5,3},{6,0},{7,1},{8,14},{9,15},{10,... | collective-permute-start | bytes 245768 | tf_op jit(solution)/shard_map/ppermute | solution.py:47
  23.3 0.8 collective-permute-start.12
  24.2 3.7 %collective-permute-start.7 = (bf16[8,2560]{1,0:T(8,128)(2,1)S(1)}, bf16[8,2560]{1,0:T(8,128)(2,1)S(1)}, u32[]{:S(2)}, u32[]{:S(2)}) collective-permute-start(bf16[8,2560]{1,0:T(8,128)(2,1)S(1)} %get-tuple-element.46), channel_id=1, source_target_pairs={{0,6},{1,7},{2,4},{3,5},{4,2},{5,3},{6,0},{7,1},{8,14},{9,15},{10,... | collective-permute-start | bytes 122888 | tf_op jit(solution)/shard_map/ppermute | solution.py:47
  27.8 1.9 %collective-permute-start.9 = (bf16[8,2560]{1,0:T(8,128)(2,1)S(1)}, bf16[8,2560]{1,0:T(8,128)(2,1)S(1)}, u32[]{:S(2)}, u32[]{:S(2)}) collective-permute-start(bf16[8,2560]{1,0:T(8,128)(2,1)S(1)} %get-tuple-element.48.gate_ref), channel_id=1, source_target_pairs={{0,2},{1,3},{2,0},{3,1},{4,6},{5,7},{6,4},{7,5},{8,10},{9,11},{10,... | collective-permute-start | bytes 122888 | tf_op jit(solution)/shard_map/ppermute | solution.py:47
  29.7 2.1 %collective-permute-done.11.refs_1_ = bf16[2,8,2560]{2,1,0:T(8,128)(2,1)S(1)} collective-permute-done((bf16[2,8,2560]{2,1,0:T(8,128)(2,1)S(1)}, bf16[2,8,2560]{2,1,0:T(8,128)(2,1)S(1)}, u32[]{:S(2)}, u32[]{:S(2)}) %collective-permute-start.11) | collective-permute-done | bytes 81952 | tf_op jit(solution)/shard_map/ppermute | solution.py:47
  32.1 1.2 %collective-permute-done.8.refs_2_ = bf16[8,2560]{1,0:T(8,128)(2,1)S(1)} collective-permute-done((bf16[8,2560]{1,0:T(8,128)(2,1)S(1)}, bf16[8,2560]{1,0:T(8,128)(2,1)S(1)}, u32[]{:S(2)}, u32[]{:S(2)}) %collective-permute-start.8) | collective-permute-done | bytes 40992 | tf_op jit(solution)/shard_map/ppermute | solution.py:47
  33.3 2.7 %collective-permute-done.13.refs_5_ = bf16[8,2560]{1,0:T(8,128)(2,1)S(1)} collective-permute-done((bf16[8,2560]{1,0:T(8,128)(2,1)S(1)}, bf16[8,2560]{1,0:T(8,128)(2,1)S(1)}, u32[]{:S(2)}, u32[]{:S(2)}) %collective-permute-start.13) | collective-permute-done | bytes 40992 | tf_op jit(solution)/shard_map/ppermute | solution.py:47
  36.6 3.3 %collective-permute-start.15 = (bf16[8,5120]{1,0:T(8,128)(2,1)S(1)}, bf16[8,5120]{1,0:T(8,128)(2,1)S(1)}, u32[]{:S(2)}, u32[]{:S(2)}) collective-permute-start(bf16[8,5120]{1,0:T(8,128)(2,1)S(1)} %norm.1.gate_ref.refs_0_), channel_id=1, source_target_pairs={{0,4},{1,5},{2,6},{3,7},{4,0},{5,1},{6,2},{7,3},{8,12},{9,13},{10,... | collective-permute-start | bytes 245768 | tf_op jit(solution)/shard_map/ppermute | solution.py:47
  39.9 0.6 collective-permute-start.16
  40.6 3.3 %fetch.3.refs_4_.weight_ref = bf16[1280,3072]{1,0:T(8,128)(2,1)S(1)} custom-call(bf16[5120,3072]{1,0:T(8,128)(2,1)} %source_ref.9, bf16[8,5120]{1,0:T(8,128)(2,1)S(1)} %norm.1.gate_ref.refs_0_), custom_call_target="tpu_custom_call" | custom-call | bytes 7864320 | tf_op jit(solution)/shard_map/fetch/pallas_call | solution.py:501
  43.9 2.2 %collective-permute-done.16.refs_3_ = bf16[8,5120]{1,0:T(8,128)(2,1)S(1)} collective-permute-done((bf16[8,5120]{1,0:T(8,128)(2,1)S(1)}, bf16[8,5120]{1,0:T(8,128)(2,1)S(1)}, u32[]{:S(2)}, u32[]{:S(2)}) %collective-permute-start.16) | collective-permute-done | bytes 81952 | tf_op jit(solution)/shard_map/ppermute | solution.py:47
  46.3 1.6 %collective-permute-start.20 = (bf16[4,8,2560]{2,1,0:T(8,128)(2,1)S(1)}, bf16[4,8,2560]{2,1,0:T(8,128)(2,1)S(1)}, u32[]{:S(2)}, u32[]{:S(2)}) collective-permute-start(bf16[4,8,2560]{2,1,0:T(8,128)(2,1)S(1)} %get-tuple-element.57), channel_id=1, source_target_pairs={{0,16},{8,24},{16,0},{24,8},{1,17},{9,25},{17,1},{25,9},{2,18},{10... | collective-permute-start | bytes 491528 | tf_op jit(solution)/shard_map/ppermute | solution.py:47
  47.8 3.3 %fetch.4.refs_2_.weight_ref = bf16[1280,3072]{1,0:T(8,128)(2,1)S(1)} custom-call(bf16[5120,3072]{1,0:T(8,128)(2,1)} %source_ref.9, bf16[4,8,2560]{2,1,0:T(8,128)(2,1)S(1)} %get-tuple-element.55.gate_ref.refs_0_), custom_call_target="tpu_custom_call" | custom-call | bytes 7864320 | tf_op jit(solution)/shard_map/fetch/pallas_call | solution.py:501
  51.2 2.1 %collective-permute-done.17.refs_1_ = bf16[4,8,2560]{2,1,0:T(8,128)(2,1)S(1)} collective-permute-done((bf16[4,8,2560]{2,1,0:T(8,128)(2,1)S(1)}, bf16[4,8,2560]{2,1,0:T(8,128)(2,1)S(1)}, u32[]{:S(2)}, u32[]{:S(2)}) %collective-permute-start.17) | collective-permute-done | bytes 163872 | tf_op jit(solution)/shard_map/ppermute | solution.py:47
  53.3 1.6 %collective-permute-start.18 = (bf16[8,8,2560]{2,1,0:T(8,128)(2,1)S(1)}, bf16[8,8,2560]{2,1,0:T(8,128)(2,1)S(1)}, u32[]{:S(2)}, u32[]{:S(2)}) collective-permute-start(bf16[8,8,2560]{2,1,0:T(8,128)(2,1)S(1)} %join.2.gate_ref.refs_0_), channel_id=1, source_target_pairs={{0,16},{8,24},{16,0},{24,8},{1,17},{9,25},{17,1},{25,9},{2,18},{10... | collective-permute-start | bytes 983048 | tf_op jit(solution)/shard_map/ppermute | solution.py:47
  55.1 3.3 %fetch.5.refs_2_.next_ref = bf16[1280,3072]{1,0:T(8,128)(2,1)S(1)} custom-call(bf16[5120,3072]{1,0:T(8,128)(2,1)} %source_ref.9, bf16[8,8,2560]{2,1,0:T(8,128)(2,1)S(1)} %join.2.gate_ref.refs_0_), custom_call_target="tpu_custom_call" | custom-call | bytes 7864320 | tf_op jit(solution)/shard_map/fetch/pallas_call | solution.py:501
  58.4 2.1 %collective-permute-done.18.refs_1_ = bf16[8,8,2560]{2,1,0:T(8,128)(2,1)S(1)} collective-permute-done((bf16[8,8,2560]{2,1,0:T(8,128)(2,1)S(1)}, bf16[8,8,2560]{2,1,0:T(8,128)(2,1)S(1)}, u32[]{:S(2)}, u32[]{:S(2)}) %collective-permute-start.18) | collective-permute-done | bytes 327712 | tf_op jit(solution)/shard_map/ppermute | solution.py:47
  60.6 1.5 %collective-permute-done.21 = bf16[8,8,2560]{2,1,0:T(8,128)(2,1)S(1)} collective-permute-done((bf16[8,8,2560]{2,1,0:T(8,128)(2,1)S(1)}, bf16[8,8,2560]{2,1,0:T(8,128)(2,1)S(1)}, u32[]{:S(2)}, u32[]{:S(2)}) %collective-permute-start.21) | collective-permute-done | bytes 327712 | tf_op jit(solution)/shard_map/ppermute | solution.py:47
  62.7 4.5 %logits_first.1 = (f32[256,3072]{1,0:T(8,128)S(1)}, bf16[1280,3072]{1,0:T(8,128)(2,1)S(1)}) custom-call(bf16[128,2560]{1,0:T(8,128)(2,1)S(1)} %bitcast.5, bf16[128,2560]{1,0:T(8,128)(2,1)S(1)} %collective-permute-done.19.right_ref, bf16[1280,3072]{1,0:T(8,128)(2,1)S(1)} %fetch.4.refs_2_.weight_ref, bf16[1280,3072]{1,0:T(8,128)(2,1)S(1)} %fetch.5.refs_2_.next_ref, ...), custom_call_target="tpu_custom_call" | custom-call | flops 4026531840 | tf_op jit(solution)/shard_map/logits_first/pallas_call | solution.py:616
  67.2 5.0 %logits.1 = f32[32,1,128]{2,1,0:T(1,128)S(1)} custom-call(f32[256,3072]{1,0:T(8,128)S(1)} %get-tuple-element.56.sum_in_ref, bf16[128,2560]{1,0:T(8,128)(2,1)S(1)} %maximum_bitcast_fusion.left_ref, bf16[128,2560]{1,0:T(8,128)(2,1)S(1)} %collective-permute-done.22.right_ref, s32[32,8,1]{2,1,0:T(8,128)S(1)} %reshape.16.refs_1_.target_ref, ...), custom_call_target="tpu_custom_call" | custom-call | flops 4026531840 | tf_op jit(solution)/shard_map/logits/pallas_call | solution.py:629
  72.2 8.9 %all_to_all.5.stats_ref = f32[32,1,128]{2,1,0:T(1,128)S(1)} all-to-all(f32[32,1,128]{2,1,0:T(1,128)S(1)} %logits.1), channel_id=1, replica_groups=mesh['group'=4,'tensor'=8] {'group','tensor'}, dimensions={0} | all-to-all | bytes 32768 | tf_op jit(solution)/shard_map/all_to_all | solution.py:642
  81.2 0.6 final.1
  (41 shorter events, 2.0 us)
Async XLA Ops:
  0.0 5.4 %collective-permute-start = (bf16[64,512]{1,0:T(8,128)(2,1)}, bf16[64,512]{1,0:T(8,128)(2,1)S(1)}, u32[]{:S(2)}, u32[]{:S(2)}) collective-permute-start(bf16[64,512]{1,0:T(8,128)(2,1)} %refs_0_.1), channel_id=1, source_target_pairs={{0,16},{8,24},{16,0},{24,8},{1,17},{9,25},{17,1},{25,9},{2,18},{10... | collective-permute-start | bytes 196616 | tf_op jit(solution)/shard_map/ppermute | solution.py:47
  3.0 4.0 %collective-permute-start.2 = (bf16[64,512]{1,0:T(8,128)(2,1)}, bf16[64,512]{1,0:T(8,128)(2,1)S(1)}, u32[]{:S(2)}, u32[]{:S(2)}) collective-permute-start(bf16[64,512]{1,0:T(8,128)(2,1)} %refs_0_.1), channel_id=1, source_target_pairs={{0,8},{8,0},{16,24},{24,16},{1,9},{9,1},{17,25},{25,17},{2,10},{10... | collective-permute-start | bytes 196616 | tf_op jit(solution)/shard_map/ppermute | solution.py:47
  5.4 26.6 %copy-start.1 = (bf16[5120]{0:T(1024)(128)(2,1)S(1)}, bf16[5120]{0:T(1024)(128)(2,1)}, u32[]{:S(2)}) copy-start(bf16[5120]{0:T(1024)(128)(2,1)} %param.21) | copy-start | bytes 30724
  5.4 30.5 %copy-start = (bf16[64,5120]{1,0:T(8,128)(2,1)S(1)}, bf16[64,5120]{1,0:T(8,128)(2,1)}, u32[]{:S(2)}) copy-start(bf16[64,5120]{1,0:T(8,128)(2,1)} %param.19) | copy-start | bytes 1966084
  5.4 1.5 %collective-permute-start.1 = (bf16[64,512]{1,0:T(8,128)(2,1)S(1)}, bf16[64,512]{1,0:T(8,128)(2,1)S(1)}, u32[]{:S(2)}, u32[]{:S(2)}) collective-permute-start(bf16[64,512]{1,0:T(8,128)(2,1)S(1)} %pass.1.gate_ref.refs_1_), channel_id=1, source_target_pairs={{0,8},{8,0},{16,24},{24,16},{1,9},{9,1},{17,25},{25,17},{2,10},{10... | collective-permute-start | bytes 196616 | tf_op jit(solution)/shard_map/ppermute | solution.py:47
  7.8 5.9 %collective-permute-start.3 = (bf16[64,640]{1,0:T(8,128)(2,1)S(1)}, bf16[64,640]{1,0:T(8,128)(2,1)S(1)}, u32[]{:S(2)}, u32[]{:S(2)}) collective-permute-start(bf16[64,640]{1,0:T(8,128)(2,1)S(1)} %get-tuple-element.37.gate_ref), channel_id=1, source_target_pairs={{0,24},{8,16},{16,8},{24,0},{1,25},{9,17},{17,9},{25,1},{2,26},{10... | collective-permute-start | bytes 245768 | tf_op jit(solution)/shard_map/ppermute | solution.py:47
  10.0 4.8 %collective-permute-start.4 = (bf16[64,640]{1,0:T(8,128)(2,1)S(1)}, bf16[64,640]{1,0:T(8,128)(2,1)S(1)}, u32[]{:S(2)}, u32[]{:S(2)}) collective-permute-start(bf16[64,640]{1,0:T(8,128)(2,1)S(1)} %get-tuple-element.40), channel_id=1, source_target_pairs={{0,16},{8,24},{16,0},{24,8},{1,17},{9,25},{17,1},{25,9},{2,18},{10... | collective-permute-start | bytes 245768 | tf_op jit(solution)/shard_map/ppermute | solution.py:47
  10.0 4.7 %collective-permute-start.5 = (bf16[64,640]{1,0:T(8,128)(2,1)S(1)}, bf16[64,640]{1,0:T(8,128)(2,1)S(1)}, u32[]{:S(2)}, u32[]{:S(2)}) collective-permute-start(bf16[64,640]{1,0:T(8,128)(2,1)S(1)} %get-tuple-element.41), channel_id=1, source_target_pairs={{0,8},{8,0},{16,24},{24,16},{1,9},{9,1},{17,25},{25,17},{2,10},{10... | collective-permute-start | bytes 245768 | tf_op jit(solution)/shard_map/ppermute | solution.py:47
  18.0 6.1 %collective-permute-start.6 = (bf16[4,8,2560]{2,1,0:T(8,128)(2,1)S(1)}, bf16[4,8,2560]{2,1,0:T(8,128)(2,1)S(1)}, u32[]{:S(2)}, u32[]{:S(2)}) collective-permute-start(bf16[4,8,2560]{2,1,0:T(8,128)(2,1)S(1)} %get-tuple-element.44), channel_id=1, source_target_pairs={{0,1},{1,0},{2,3},{3,2},{4,5},{5,4},{6,7},{7,6},{8,9},{9,8},{10,11... | collective-permute-start | bytes 491528 | tf_op jit(solution)/shard_map/ppermute | solution.py:47
  19.7 8.1 %collective-permute-start.10 = (bf16[2,8,2560]{2,1,0:T(8,128)(2,1)S(1)}, bf16[2,8,2560]{2,1,0:T(8,128)(2,1)S(1)}, u32[]{:S(2)}, u32[]{:S(2)}) collective-permute-start(bf16[2,8,2560]{2,1,0:T(8,128)(2,1)S(1)} %get-tuple-element.50), channel_id=1, source_target_pairs={{0,6},{1,7},{2,4},{3,5},{4,2},{5,3},{6,0},{7,1},{8,14},{9,15},{10,... | collective-permute-start | bytes 245768 | tf_op jit(solution)/shard_map/ppermute | solution.py:47
  23.3 8.5 %collective-permute-start.11 = (bf16[2,8,2560]{2,1,0:T(8,128)(2,1)S(1)}, bf16[2,8,2560]{2,1,0:T(8,128)(2,1)S(1)}, u32[]{:S(2)}, u32[]{:S(2)}) collective-permute-start(bf16[2,8,2560]{2,1,0:T(8,128)(2,1)S(1)} %get-tuple-element.51), channel_id=1, source_target_pairs={{0,4},{1,5},{2,6},{3,7},{4,0},{5,1},{6,2},{7,3},{8,12},{9,13},{10,... | collective-permute-start | bytes 245768 | tf_op jit(solution)/shard_map/ppermute | solution.py:47
  23.3 8.5 %collective-permute-start.12 = (bf16[2,8,2560]{2,1,0:T(8,128)(2,1)S(1)}, bf16[2,8,2560]{2,1,0:T(8,128)(2,1)S(1)}, u32[]{:S(2)}, u32[]{:S(2)}) collective-permute-start(bf16[2,8,2560]{2,1,0:T(8,128)(2,1)S(1)} %get-tuple-element.52), channel_id=1, source_target_pairs={{0,2},{1,3},{2,0},{3,1},{4,6},{5,7},{6,4},{7,5},{8,10},{9,11},{10,... | collective-permute-start | bytes 245768 | tf_op jit(solution)/shard_map/ppermute | solution.py:47
  24.2 7.9 %collective-permute-start.7 = (bf16[8,2560]{1,0:T(8,128)(2,1)S(1)}, bf16[8,2560]{1,0:T(8,128)(2,1)S(1)}, u32[]{:S(2)}, u32[]{:S(2)}) collective-permute-start(bf16[8,2560]{1,0:T(8,128)(2,1)S(1)} %get-tuple-element.46), channel_id=1, source_target_pairs={{0,6},{1,7},{2,4},{3,5},{4,2},{5,3},{6,0},{7,1},{8,14},{9,15},{10,... | collective-permute-start | bytes 122888 | tf_op jit(solution)/shard_map/ppermute | solution.py:47
  27.8 5.4 %collective-permute-start.8 = (bf16[8,2560]{1,0:T(8,128)(2,1)S(1)}, bf16[8,2560]{1,0:T(8,128)(2,1)S(1)}, u32[]{:S(2)}, u32[]{:S(2)}) collective-permute-start(bf16[8,2560]{1,0:T(8,128)(2,1)S(1)} %get-tuple-element.47), channel_id=1, source_target_pairs={{0,4},{1,5},{2,6},{3,7},{4,0},{5,1},{6,2},{7,3},{8,12},{9,13},{10,... | collective-permute-start | bytes 122888 | tf_op jit(solution)/shard_map/ppermute | solution.py:47
  27.8 5.4 %collective-permute-start.9 = (bf16[8,2560]{1,0:T(8,128)(2,1)S(1)}, bf16[8,2560]{1,0:T(8,128)(2,1)S(1)}, u32[]{:S(2)}, u32[]{:S(2)}) collective-permute-start(bf16[8,2560]{1,0:T(8,128)(2,1)S(1)} %get-tuple-element.48.gate_ref), channel_id=1, source_target_pairs={{0,2},{1,3},{2,0},{3,1},{4,6},{5,7},{6,4},{7,5},{8,10},{9,11},{10,... | collective-permute-start | bytes 122888 | tf_op jit(solution)/shard_map/ppermute | solution.py:47
  31.9 4.1 %collective-permute-start.13 = (bf16[8,2560]{1,0:T(8,128)(2,1)S(1)}, bf16[8,2560]{1,0:T(8,128)(2,1)S(1)}, u32[]{:S(2)}, u32[]{:S(2)}) collective-permute-start(bf16[8,2560]{1,0:T(8,128)(2,1)S(1)} %get-tuple-element.54), channel_id=1, source_target_pairs={{0,1},{1,0},{2,3},{3,2},{4,5},{5,4},{6,7},{7,6},{8,9},{9,8},{10,11... | collective-permute-start | bytes 122888 | tf_op jit(solution)/shard_map/ppermute | solution.py:47
  36.1 7.8 %collective-permute-start.14 = (bf16[8,5120]{1,0:T(8,128)(2,1)S(1)}, bf16[8,5120]{1,0:T(8,128)(2,1)S(1)}, u32[]{:S(2)}, u32[]{:S(2)}) collective-permute-start(bf16[8,5120]{1,0:T(8,128)(2,1)S(1)} %norm.1.gate_ref.refs_0_), channel_id=1, source_target_pairs={{0,2},{1,3},{2,0},{3,1},{4,6},{5,7},{6,4},{7,5},{8,10},{9,11},{10,... | collective-permute-start | bytes 245768 | tf_op jit(solution)/shard_map/ppermute | solution.py:47
  36.6 7.4 %collective-permute-start.15 = (bf16[8,5120]{1,0:T(8,128)(2,1)S(1)}, bf16[8,5120]{1,0:T(8,128)(2,1)S(1)}, u32[]{:S(2)}, u32[]{:S(2)}) collective-permute-start(bf16[8,5120]{1,0:T(8,128)(2,1)S(1)} %norm.1.gate_ref.refs_0_), channel_id=1, source_target_pairs={{0,4},{1,5},{2,6},{3,7},{4,0},{5,1},{6,2},{7,3},{8,12},{9,13},{10,... | collective-permute-start | bytes 245768 | tf_op jit(solution)/shard_map/ppermute | solution.py:47
  39.9 6.2 %collective-permute-start.16 = (bf16[8,5120]{1,0:T(8,128)(2,1)S(1)}, bf16[8,5120]{1,0:T(8,128)(2,1)S(1)}, u32[]{:S(2)}, u32[]{:S(2)}) collective-permute-start(bf16[8,5120]{1,0:T(8,128)(2,1)S(1)} %norm.1.gate_ref.refs_0_), channel_id=1, source_target_pairs={{0,6},{1,7},{2,4},{3,5},{4,2},{5,3},{6,0},{7,1},{8,14},{9,15},{10,... | collective-permute-start | bytes 245768 | tf_op jit(solution)/shard_map/ppermute | solution.py:47
  46.2 7.1 %collective-permute-start.17 = (bf16[4,8,2560]{2,1,0:T(8,128)(2,1)S(1)}, bf16[4,8,2560]{2,1,0:T(8,128)(2,1)S(1)}, u32[]{:S(2)}, u32[]{:S(2)}) collective-permute-start(bf16[4,8,2560]{2,1,0:T(8,128)(2,1)S(1)} %get-tuple-element.55.gate_ref.refs_0_), channel_id=1, source_target_pairs={{0,1},{1,0},{2,3},{3,2},{4,5},{5,4},{6,7},{7,6},{8,9},{9,8},{10,11... | collective-permute-start | bytes 491528 | tf_op jit(solution)/shard_map/ppermute | solution.py:47
  46.3 8.7 %collective-permute-start.20 = (bf16[4,8,2560]{2,1,0:T(8,128)(2,1)S(1)}, bf16[4,8,2560]{2,1,0:T(8,128)(2,1)S(1)}, u32[]{:S(2)}, u32[]{:S(2)}) collective-permute-start(bf16[4,8,2560]{2,1,0:T(8,128)(2,1)S(1)} %get-tuple-element.57), channel_id=1, source_target_pairs={{0,16},{8,24},{16,0},{24,8},{1,17},{9,25},{17,1},{25,9},{2,18},{10... | collective-permute-start | bytes 491528 | tf_op jit(solution)/shard_map/ppermute | solution.py:47
  53.3 7.1 %collective-permute-start.18 = (bf16[8,8,2560]{2,1,0:T(8,128)(2,1)S(1)}, bf16[8,8,2560]{2,1,0:T(8,128)(2,1)S(1)}, u32[]{:S(2)}, u32[]{:S(2)}) collective-permute-start(bf16[8,8,2560]{2,1,0:T(8,128)(2,1)S(1)} %join.2.gate_ref.refs_0_), channel_id=1, source_target_pairs={{0,16},{8,24},{16,0},{24,8},{1,17},{9,25},{17,1},{25,9},{2,18},{10... | collective-permute-start | bytes 983048 | tf_op jit(solution)/shard_map/ppermute | solution.py:47
  55.0 7.1 %collective-permute-start.21 = (bf16[8,8,2560]{2,1,0:T(8,128)(2,1)S(1)}, bf16[8,8,2560]{2,1,0:T(8,128)(2,1)S(1)}, u32[]{:S(2)}, u32[]{:S(2)}) collective-permute-start(bf16[8,8,2560]{2,1,0:T(8,128)(2,1)S(1)} %pad_maximum_fusion), channel_id=1, source_target_pairs={{0,1},{1,0},{2,3},{3,2},{4,5},{5,4},{6,7},{7,6},{8,9},{9,8},{10,11... | collective-permute-start | bytes 983048 | tf_op jit(solution)/shard_map/ppermute | solution.py:47
  60.5 2.2 %collective-permute-start.19 = (bf16[128,2560]{1,0:T(8,128)(2,1)S(1)}, bf16[128,2560]{1,0:T(8,128)(2,1)S(1)}, u32[]{:S(2)}, u32[]{:S(2)}) collective-permute-start(bf16[128,2560]{1,0:T(8,128)(2,1)S(1)} %bitcast.4), channel_id=1, source_target_pairs={{0,8},{8,0},{16,24},{24,16},{1,9},{9,1},{17,25},{25,17},{2,10},{10... | collective-permute-start | bytes 1966088 | tf_op jit(solution)/shard_map/ppermute | solution.py:47
  62.2 5.0 %collective-permute-start.22 = (bf16[128,2560]{1,0:T(8,128)(2,1)S(1)}, bf16[128,2560]{1,0:T(8,128)(2,1)S(1)}, u32[]{:S(2)}, u32[]{:S(2)}) collective-permute-start(bf16[128,2560]{1,0:T(8,128)(2,1)S(1)} %maximum_bitcast_fusion.left_ref), channel_id=1, source_target_pairs={{0,8},{8,0},{16,24},{24,16},{1,9},{9,1},{17,25},{25,17},{2,10},{10... | collective-permute-start | bytes 1966088 | tf_op jit(solution)/shard_map/ppermute | solution.py:47

commit v9 on v8

--- a/solution.py
+++ b/solution.py
@@ -189,10 +189,10 @@
         out_refs[i][:, heads * HEAD_DIM :] = pack_logs([log[rung] for _, log in found], rows)
 
 
-def project_kernel(heads, seq, share, wide, group_size, key_rows, prompt_ref, own_ref, *refs):
+def project_kernel(heads, seq, wide, group_size, key_rows, prompt_ref, own_ref, *refs):
     got_refs, refs = refs[: group_size - 1], refs[group_size - 1 :]
-    weight_ref, send_left_ref, keep_left_ref, keep_right_ref = refs[:4]
-    send_right_refs, (attended_ref, partial_ref) = refs[4:-2], refs[-2:]
+    weight_ref, send_left_ref, keep_left_ref, send_right_ref, keep_right_ref = refs[:5]
+    attended_ref, partial_ref = refs[5:]
     rows = own_ref.shape[0]
     wanted = wanted_prompts(seq, rows, prompt_ref)
     group = lax.axis_index("group")
@@ -217,47 +217,49 @@
         mixed = functools.reduce(jnp.add, [w * v for w, v in zip(loads, values)])
         attended_ref[:, part] = (mixed / total).astype(BF16)
 
-    me = lax.axis_index("tensor")
-    blocks = rows // share
+    me = lax.axis_index("tensor") % 4
+    block = rows // 4
     half = send_left_ref.shape[2]
 
     def multiply(columns):
         partial = jnp.dot(attended_ref[...], weight_ref[:, columns], preferred_element_type=F32)
-        for b in range(blocks):
-            partial_ref[b] = partial[b * share : (b + 1) * share]
+        for b in range(4):
+            partial_ref[b] = partial[b * block : (b + 1) * block]
 
     @pl.loop(0, half // wide)
     def _(n):
         columns = pl.ds(pl.multiple_of(n * wide, 128), wide)
         multiply(columns)
-        for d in range(0, blocks, 2):
-            keep_left_ref[d // 2, :, columns] = partial_ref[me ^ d]
-            send_left_ref[d // 2, :, columns] = partial_ref[me ^ (d + 1)].astype(BF16)
+        for i in range(2):
+            keep_left_ref[i, :, columns] = partial_ref[me ^ (2 * i)]
+            send_left_ref[i, :, columns] = partial_ref[me ^ (2 * i + 1)].astype(BF16)
 
     @pl.loop(0, half // wide)
     def _(n):
         columns = pl.ds(pl.multiple_of(n * wide, 128), wide)
         multiply(pl.ds(pl.multiple_of(half + n * wide, 128), wide))
-        for d in range(blocks):
-            block = partial_ref[me ^ d]
-            if d < 2:
-                keep_right_ref[d, :, columns] = block
-            else:
-                send_right_refs[d // 2 - 1][d % 2, :, columns] = block.astype(BF16)
-
-
-def fold_left_kernel(keep_ref, got_ref, *out_refs):
-    for i, ref in enumerate(out_refs):
-        ref[...] = (keep_ref[i] + got_ref[i].astype(F32)).astype(ref.dtype)
-
-
-def fold_right_kernel(gate_ref, keep_ref, *refs):
-    got_refs, out_refs = refs[:-2], refs[-2:]
-    for i, ref in enumerate(out_refs):
-        total = keep_ref[i]
-        for got_ref in got_refs:
-            total = total + got_ref[i].astype(F32)
-        ref[...] = total.astype(ref.dtype)
+        for i in range(2):
+            keep_right_ref[i, :, columns] = partial_ref[me ^ i]
+            send_right_ref[i, :, columns] = partial_ref[me ^ (i + 2)].astype(BF16)
+
+
+def fold_kernel(keep_ref, got_ref, own_ref, send_ref):
+    own_ref[...] = keep_ref[0] + got_ref[0].astype(F32)
+    send_ref[...] = (keep_ref[1] + got_ref[1].astype(F32)).astype(BF16)
+
+
+def side_kernel(left_ref, got_left_ref, right_ref, got_right_ref, own_ref, send_ref):
+    half = left_ref.shape[1]
+    for i, (ref, got_ref) in enumerate(((left_ref, got_left_ref), (right_ref, got_right_ref))):
+        total = ref[...] + got_ref[...].astype(F32)
+        own_ref[:, i * half : (i + 1) * half] = total
+        send_ref[:, i * half : (i + 1) * half] = total.astype(BF16)
+
+
+def add_kernel(own_ref, got_ref, out_ref, send_ref):
+    total = own_ref[...] + got_ref[...].astype(F32)
+    out_ref[...] = total
+    send_ref[...] = total.astype(BF16)
 
 
 def fetch_kernel(start, source_ref, gate_ref, out_ref, sems):
@@ -276,21 +278,11 @@
             out_ref[i] = ref[:, half * width : (half + 1) * width]
 
 
-def norm_kernel(far_count, residual_ref, gain_ref, *refs):
-    left_refs, right_refs, out_ref = refs[: 1 + far_count], refs[1 + far_count : -1], refs[-1]
-    residual = residual_ref[lax.axis_index("tensor")].astype(F32)
-    width = residual.shape[1] // 2
-    halves = []
-    for i, terms in enumerate((left_refs, right_refs)):
-        hidden = residual[:, i * width : (i + 1) * width]
-        for ref in terms:
-            hidden = hidden + ref[...].astype(F32)
-        halves.append(hidden)
-    squares = sum(jnp.sum(hidden * hidden, axis=-1, keepdims=True) for hidden in halves)
-    scale = lax.rsqrt(squares / residual.shape[1] + 1e-06)
-    for i, hidden in enumerate(halves):
-        columns = slice(i * width, (i + 1) * width)
-        out_ref[:, columns] = (hidden * scale * gain_ref[:, columns].astype(F32)).astype(BF16)
+def norm_kernel(residual_ref, gain_ref, first_gate_ref, second_gate_ref, own_ref, got_ref, out_ref):
+    hidden = residual_ref[lax.axis_index("tensor") % 4].astype(F32)
+    hidden = hidden + (own_ref[...] + got_ref[...].astype(F32))
+    squares = jnp.mean(hidden * hidden, axis=-1, keepdims=True)
+    out_ref[...] = (hidden * lax.rsqrt(squares + 1e-06) * gain_ref[...].astype(F32)).astype(BF16)
 
 
 def join_kernel(count, *refs):
@@ -353,7 +345,10 @@
     share = target_ref.shape[1]
     group, tensor = lax.axis_index("group"), lax.axis_index("tensor")
     vocab = weight_ref.shape[1]
-    places = [(group ^ g) * tensor_size + (tensor ^ t) for g, t in spots]
+    shares = tensor_size // 4
+    places = [
+        (group ^ g) * tensor_size + shares * ((tensor % 4) ^ d) + i for g, d in spots for i in range(shares)
+    ]
     for i, place in enumerate(places):
         wanted_ref[i * share : (i + 1) * share] = target_ref[place]
     wanted = wanted_ref[...] - (group * tensor_size + tensor) * vocab
@@ -513,81 +508,80 @@
     half = depth // 2
     quarter = depth // 4
     wide = 1280 if half % 1280 == 0 else half
-    pairs = tensor_size // 2
-    send_left, keep_left, keep_right, *rest = pl.pallas_call(
-        functools.partial(project_kernel, heads, seq, share, wide, group_size, key_rows),
+    block = rows // 4
+    send_left, keep_left, send_right, keep_right = pl.pallas_call(
+        functools.partial(project_kernel, heads, seq, wide, group_size, key_rows),
         out_shape=[
-            jax.ShapeDtypeStruct((pairs, share, half), BF16),
-            jax.ShapeDtypeStruct((pairs, share, half), F32),
-            jax.ShapeDtypeStruct((2, share, half), F32),
+            jax.ShapeDtypeStruct((2, block, half), BF16),
+            jax.ShapeDtypeStruct((2, block, half), F32),
         ]
-        + [jax.ShapeDtypeStruct((2, share, half), BF16)] * (pairs - 1),
+        * 2,
         in_specs=[smem()] + [vmem()] * (2 + len(distances)),
-        out_specs=[vmem()] * (2 + pairs),
+        out_specs=[vmem()] * 4,
         scratch_shapes=[
             pltpu.VMEM((rows, span), BF16),
-            pltpu.VMEM((tensor_size, share, wide), F32),
+            pltpu.VMEM((4, block, wide), F32),
         ],
         compiler_params=params(6),
         name="project",
     )(stored(prompt_of), *map(held, (own, *got)), held(weight))
 
-    far = list(range(2, tensor_size, 2))
+    def add(kernel, name, size, *operands):
+        return pl.pallas_call(
+            kernel,
+            out_shape=[jax.ShapeDtypeStruct(size, F32), jax.ShapeDtypeStruct(size, BF16)],
+            in_specs=[vmem()] * len(operands),
+            out_specs=[vmem()] * 2,
+            compiler_params=params(2),
+            name=name,
+        )(*map(held, operands))
+
     got_left = swap(send_left, "tensor", 1, tensor_size)
-    got_right = [swap(x, "tensor", d, tensor_size) for x, d in zip(rest[::-1], far[::-1])]
-    left = pl.pallas_call(
-        fold_left_kernel,
-        out_shape=[jax.ShapeDtypeStruct((share, half), F32)]
-        + [jax.ShapeDtypeStruct((share, half), BF16)] * len(far),
-        in_specs=[vmem()] * 2,
-        out_specs=[vmem()] * (1 + len(far)),
-        compiler_params=params(2),
-        name="fold_left",
-    )(held(keep_left), held(got_left))
-    got_left = [swap(x, "tensor", d, tensor_size) for x, d in zip(left[:0:-1], far[::-1])]
-    right = pl.pallas_call(
-        fold_right_kernel,
-        out_shape=[
-            jax.ShapeDtypeStruct((share, half), F32),
-            jax.ShapeDtypeStruct((share, half), BF16),
-        ],
-        in_specs=[anywhere()] + [vmem()] * (1 + len(far)),
-        out_specs=[vmem()] * 2,
-        compiler_params=params(2),
-        name="fold_right",
-    )(left[1], *map(held, (keep_right, *got_right)))
-    got_right = swap(right[1], "tensor", 1, tensor_size)
+    got_right = swap(send_right, "tensor", 2, tensor_size)
+    left, send_left = add(fold_kernel, "fold_left", (block, half), keep_left, got_left)
+    right, send_right = add(fold_kernel, "fold_right", (block, half), keep_right, got_right)
+    got_left = swap(send_left, "tensor", 2, tensor_size)
+    got_right = swap(send_right, "tensor", 1, tensor_size)
+    total, send = add(side_kernel, "side", (block, depth), left, got_left, right, got_right)
+    first_quarter = fetch(lm_weight, 0, quarter, send)
+    second_quarter = fetch(lm_weight, quarter, quarter, send)
+    far = 4
+    while 2 * far < tensor_size:
+        total, send = add(
+            add_kernel, "add", (block, depth), total, swap(send, "tensor", far, tensor_size)
+        )
+        far = 2 * far
     normed = pl.pallas_call(
-        functools.partial(norm_kernel, len(far)),
-        out_shape=jax.ShapeDtypeStruct((share, depth), BF16),
-        in_specs=[vmem()] * (5 + len(far)),
+        norm_kernel,
+        out_shape=jax.ShapeDtypeStruct((block, depth), BF16),
+        in_specs=[vmem()] * 2 + [anywhere()] * 2 + [vmem()] * 2,
         out_specs=vmem(),
         compiler_params=params(4),
         name="norm",
     )(
-        *map(held, (residual.reshape(tensor_size, share, depth), norm_gain[None])),
-        *map(held, (left[0], *got_left, right[0], got_right)),
+        *map(held, (residual.reshape(4, block, depth), norm_gain[None])),
+        first_quarter,
+        second_quarter,
+        *map(held, (total, swap(send, "tensor", far, tensor_size))),
     )
 
-    order = [0] + far
+    order = [0, 2]
     here = [(g, x) for g in [0] + above for x in (0, 1)]
-    column = [swap(normed, "tensor", d, tensor_size) for d in far[::-1]]
-    column = [normed] + column[::-1]
-    third = fetch(lm_weight, 2 * quarter, quarter, normed)
+    column = [normed, swap(normed, "tensor", 2, tensor_size)]
     columns = pl.pallas_call(
         functools.partial(column_kernel, len(column)),
-        out_shape=[jax.ShapeDtypeStruct((len(column), share, half), BF16)] * 2,
-        in_specs=[vmem()] * len(column) + [anywhere()],
+        out_shape=[jax.ShapeDtypeStruct((len(column), block, half), BF16)] * 2,
+        in_specs=[vmem()] * len(column),
         out_specs=[vmem()] * 2,
         compiler_params=params(2),
         name="column",
-    )(*map(held, column), third)
+    )(*map(held, column))
 
     def join(pieces, gate):
         blocks = sum(x.shape[0] for x in pieces)
         return pl.pallas_call(
             functools.partial(join_kernel, len(pieces)),
-            out_shape=jax.ShapeDtypeStruct((blocks, share, half), BF16),
+            out_shape=jax.ShapeDtypeStruct((blocks, block, half), BF16),
             in_specs=[vmem()] * len(pieces) + [anywhere()],
             out_specs=vmem(),
             compiler_params=params(2),
@@ -596,16 +590,15 @@
 
     left, right = columns
     got_left = swap(left, "tensor", 1, tensor_size)
-    first_quarter = fetch(lm_weight, 0, quarter, left)
+    third = fetch(lm_weight, 2 * quarter, quarter, left)
     right = [right] + [swap(right, "group", d, group_size) for d in above]
-    left = join([left, got_left], first_quarter)
+    left = join([left, got_left], third)
     got_left = [swap(left, "group", d, group_size) for d in above]
-    second_quarter = fetch(lm_weight, quarter, quarter, left)
     across = swap(jnp.concatenate(right), "tensor", 1, tensor_size)
     across = jnp.split(across, len(right))
     right = [x for pair in zip(right, across) for x in pair]
     halves = []
-    for tokens in (join([left] + got_left, second_quarter), jnp.concatenate(right)):
+    for tokens in (jnp.concatenate([left] + got_left), jnp.concatenate(right)):
         tokens = tokens.reshape(-1, half)
         halves.append((tokens, swap(tokens, "group", 1, group_size)))
     spots = [(g + c, t + x) for c in (0, 1) for g, x in here for t in order]
@@ -628,7 +621,7 @@
     )(*map(held, (*halves[0], first_quarter, second_quarter)), stored(lm_weight))
     stats = pl.pallas_call(
         functools.partial(logits_kernel, vocab, spots, tensor_size),
-        out_shape=jax.ShapeDtypeStruct((len(spots), 1, 128), F32),
+        out_shape=jax.ShapeDtypeStruct((group_size * tensor_size, 1, 128), F32),
         in_specs=[vmem()] * 6,
         out_specs=vmem(),
         scratch_shapes=[pltpu.VMEM((total_rows, half), BF16)]

time: 82 us -> 81.9 us (level)
  starting transfers between devices: 25.1 us -> 21.1 us
  waiting for transfers between devices: 16.9 us -> 19.5 us
  blocking collectives: 8.92 us -> 10.2 us
    ppermute x23 -> x18, starting transfers between devices: 25.1 us -> 21.1 us  [swap(): return lax.ppermute(x, axis, [(i, i ^ distance) for i in range(size)])]
    ppermute x23 -> x18, waiting for transfers between devices: 16.9 us -> 19.5 us  [swap(): return lax.ppermute(x, axis, [(i, i ^ distance) for i in range(size)])]
    all_to_all x1, blocking collectives: 8.92 us -> 10.2 us  [local(): stats = lax.all_to_all(stats, ('group', 'tensor'), 0, 0, tiled=True)]
    pallas_call x4 -> x5, Pallas kernels: 3.5 us -> 3.58 us  [the longest x1 3.27 us: local(): pl.pallas_call(functools.partial(project_kernel, heads, seq, wide, group_...]
  transfers between devices with their start and end apart: 23 -> 18, of which waited for: 10 -> 9; matrix products, arithmetic and copies ran while one was open for 1% -> 1% of each run, Pallas kernels for 24% -> 24%
where the time goes in v9:
time: 81.9 us; the launch traced here: 81.7 us
  Pallas kernels  29.6 us (36%)
  starting transfers between devices  21.1 us (26%)
  waiting for transfers between devices  19.5 us (24%)
  blocking collectives  10.2 us (12%)
  local copies, waits for them, and re-layouts  0.92 us (1%)
    ppermute x18, starting transfers between devices, swap(): return lax.ppermute(x, axis, [(i, i ^ distance) for i in range(size)])  21.1 us
    ppermute x18, waiting for transfers between devices, swap(): return lax.ppermute(x, axis, [(i, i ^ distance) for i in range(size)])  19.5 us
    all_to_all x1, blocking collectives, local(): stats = lax.all_to_all(stats, ('group', 'tensor'), 0, 0, tiled=True)  10.2 us
    pallas_call x3, Pallas kernels, fetch(): pl.pallas_call(functools.partial(fetch_kernel, start), out_shape=pltpu.VM...  10.1 us
    pallas_call x1, Pallas kernels, local(): pl.pallas_call(functools.partial(logits_kernel, vocab, spots, tensor_size...  5 us
    pallas_call x1, Pallas kernels, local(): pl.pallas_call(functools.partial(first_kernel, narrow), out_shape=[pltpu....  4.52 us
    pallas_call x1, Pallas kernels, local(): pl.pallas_call(functools.partial(own_kernel, heads, seq, share), out_shap...  3.54 us
    pallas_call x1, Pallas kernels, local(): pl.pallas_call(functools.partial(project_kernel, heads, seq, wide, group_...  3.27 us
  transfers between devices with their start and end apart: 18, of which 9 were waited for; matrix products, arithmetic and copies ran while one was open for 1% of the time, Pallas kernels for 24%

profile of v9, /device:TPU:0, one launch (start us, length us, event | category | flops | bytes accessed | tf_op | source)
XLA Modules:
  0.0 81.7 jit_solution(3128719536266214712)
XLA Ops:
  0.0 3.0 %collective-permute-start = (bf16[64,512]{1,0:T(8,128)(2,1)}, bf16[64,512]{1,0:T(8,128)(2,1)S(1)}, u32[]{:S(2)}, u32[]{:S(2)}) collective-permute-start(bf16[64,512]{1,0:T(8,128)(2,1)} %refs_0_.1), channel_id=1, source_target_pairs={{0,16},{8,24},{16,0},{24,8},{1,17},{9,25},{17,1},{25,9},{2,18},{10... | collective-permute-start | bytes 196616 | tf_op jit(solution)/shard_map/ppermute | solution.py:47
  3.0 0.9 %reshape.16.refs_1_.target_ref = s32[32,8,1]{2,1,0:T(8,128)S(1)} reshape(s32[256]{0:T(256)} %param.23) | data formatting | bytes 2048 | tf_op jit(solution)/shard_map/reshape | solution.py:431
  3.9 1.6 %collective-permute-done.refs_0_ = bf16[64,512]{1,0:T(8,128)(2,1)S(1)} collective-permute-done((bf16[64,512]{1,0:T(8,128)(2,1)}, bf16[64,512]{1,0:T(8,128)(2,1)S(1)}, u32[]{:S(2)}, u32[]{:S(2)}) %collective-permute-start) | collective-permute-done | bytes 65568 | tf_op jit(solution)/shard_map/ppermute | solution.py:47
  5.5 1.4 %load.1 = (bf16[64,512]{1,0:T(8,128)(2,1)S(1)}, bf16[64,512]{1,0:T(8,128)(2,1)S(1)}, bf16[64,512]{1,0:T(8,128)(2,1)S(1)}, bf16[512,512]{1,0:T(8,128)(2,1)S(1)}, bf16[512,512]{1,0:T(8,128)(2,1)S(1)}) custom-call(bf16[64,512]{1,0:T(8,128)(2,1)S(1)} %pass.1.gate_ref.refs_1_, bf16[64,512]{1,0:T(8,128)(2,1)} %refs_0_.1, bf16[64,512]{1,0:T(8,128)(2,1)} %refs_1_.1, ...), custom_call_target="tpu_custom_call" | custom-call | bytes 2097152 | tf_op jit(solution)/shard_map/load/pallas_call | solution.py:449
  6.9 0.9 %prefix_attention.1 = (bf16[64,640]{1,0:T(8,128)(2,1)S(1)}, bf16[64,640]{1,0:T(8,128)(2,1)S(1)}, bf16[64,640]{1,0:T(8,128)(2,1)S(1)}) custom-call(bf16[64,512]{1,0:T(8,128)(2,1)S(1)} %collective-permute-done.1.refs_0_, bf16[64,512]{1,0:T(8,128)(2,1)S(1)} %pass.1.gate_ref.refs_1_, bf16[64,512]{1,0:T(8,128)(2,1)S(1)} %collective-permute-done.2.refs_2_, ...), custom_call_target="tpu_custom_call" | custom-call | tf_op jit(solution)/shard_map/prefix_attention/pallas_call | solution.py:460
  7.8 2.2 %collective-permute-start.3 = (bf16[64,640]{1,0:T(8,128)(2,1)S(1)}, bf16[64,640]{1,0:T(8,128)(2,1)S(1)}, u32[]{:S(2)}, u32[]{:S(2)}) collective-permute-start(bf16[64,640]{1,0:T(8,128)(2,1)S(1)} %get-tuple-element.35.gate_ref), channel_id=1, source_target_pairs={{0,24},{8,16},{16,8},{24,0},{1,25},{9,17},{17,9},{25,1},{2,26},{10... | collective-permute-start | bytes 245768 | tf_op jit(solution)/shard_map/ppermute | solution.py:47
  10.1 3.5 %own_attention.1 = (f32[64,640]{1,0:T(8,128)S(1)}, f32[8,128]{1,0:T(8,128)S(1)}, bf16[512,5120]{1,0:T(8,128)(2,1)S(1)}) custom-call(s32[2]{0:T(128)} %lengths_ref.1, s32[2]{0:T(128)} %prompt_ref.3, bf16[64,512]{1,0:T(8,128)(2,1)S(1)} %get-tuple-element.30.q_ref, bf16[64,512]{1,0:T(8,128)(2,1)S(1)} %get-tuple-element.31.rk_ref, ...), custom_call_target="tpu_custom_call" | custom-call | bytes 8388608 | tf_op jit(solution)/shard_map/own_attention/pallas_call | solution.py:469
  13.7 1.0 %collective-permute-done.4.refs_1_ = bf16[64,640]{1,0:T(8,128)(2,1)S(1)} collective-permute-done((bf16[64,640]{1,0:T(8,128)(2,1)S(1)}, bf16[64,640]{1,0:T(8,128)(2,1)S(1)}, u32[]{:S(2)}, u32[]{:S(2)}) %collective-permute-start.4) | collective-permute-done | bytes 81952 | tf_op jit(solution)/shard_map/ppermute | solution.py:47
  14.7 3.3 %project.1 = (bf16[2,16,2560]{2,1,0:T(8,128)(2,1)S(1)}, f32[2,16,2560]{2,1,0:T(8,128)S(1)}, bf16[2,16,2560]{2,1,0:T(8,128)(2,1)S(1)}, f32[2,16,2560]{2,1,0:T(8,128)S(1)}) custom-call(s32[2]{0:T(128)} %prompt_ref.3, f32[64,640]{1,0:T(8,128)S(1)} %get-tuple-element.37.own_ref, bf16[64,640]{1,0:T(8,128)(2,1)S(1)} %collective-permute-done.3.refs_0_, ...), custom_call_target="tpu_custom_call" | custom-call | tf_op jit(solution)/shard_map/project/pallas_call | solution.py:512
  18.0 1.7 %collective-permute-start.6 = (bf16[2,16,2560]{2,1,0:T(8,128)(2,1)S(1)}, bf16[2,16,2560]{2,1,0:T(8,128)(2,1)S(1)}, u32[]{:S(2)}, u32[]{:S(2)}) collective-permute-start(bf16[2,16,2560]{2,1,0:T(8,128)(2,1)S(1)} %get-tuple-element.42), channel_id=1, source_target_pairs={{0,1},{1,0},{2,3},{3,2},{4,5},{5,4},{6,7},{7,6},{8,9},{9,8},{10,11... | collective-permute-start | bytes 491528 | tf_op jit(solution)/shard_map/ppermute | solution.py:47
  19.7 1.6 %collective-permute-start.8 = (bf16[2,16,2560]{2,1,0:T(8,128)(2,1)S(1)}, bf16[2,16,2560]{2,1,0:T(8,128)(2,1)S(1)}, u32[]{:S(2)}, u32[]{:S(2)}) collective-permute-start(bf16[2,16,2560]{2,1,0:T(8,128)(2,1)S(1)} %get-tuple-element.46), channel_id=1, source_target_pairs={{0,2},{1,3},{2,0},{3,1},{4,6},{5,7},{6,4},{7,5},{8,10},{9,11},{10,... | collective-permute-start | bytes 491528 | tf_op jit(solution)/shard_map/ppermute | solution.py:47
  21.3 2.5 %collective-permute-done.6.got_ref = bf16[2,16,2560]{2,1,0:T(8,128)(2,1)S(1)} collective-permute-done((bf16[2,16,2560]{2,1,0:T(8,128)(2,1)S(1)}, bf16[2,16,2560]{2,1,0:T(8,128)(2,1)S(1)}, u32[]{:S(2)}, u32[]{:S(2)}) %collective-permute-start.6) | collective-permute-done | bytes 163872 | tf_op jit(solution)/shard_map/ppermute | solution.py:47
  23.8 1.9 %collective-permute-start.7 = (bf16[16,2560]{1,0:T(8,128)(2,1)S(1)}, bf16[16,2560]{1,0:T(8,128)(2,1)S(1)}, u32[]{:S(2)}, u32[]{:S(2)}) collective-permute-start(bf16[16,2560]{1,0:T(8,128)(2,1)S(1)} %get-tuple-element.44), channel_id=1, source_target_pairs={{0,2},{1,3},{2,0},{3,1},{4,6},{5,7},{6,4},{7,5},{8,10},{9,11},{10,... | collective-permute-start | bytes 245768 | tf_op jit(solution)/shard_map/ppermute | solution.py:47
  25.7 1.6 %collective-permute-start.9 = (bf16[16,2560]{1,0:T(8,128)(2,1)S(1)}, bf16[16,2560]{1,0:T(8,128)(2,1)S(1)}, u32[]{:S(2)}, u32[]{:S(2)}) collective-permute-start(bf16[16,2560]{1,0:T(8,128)(2,1)S(1)} %get-tuple-element.48), channel_id=1, source_target_pairs={{0,1},{1,0},{2,3},{3,2},{4,5},{5,4},{6,7},{7,6},{8,9},{9,8},{10,11... | collective-permute-start | bytes 245768 | tf_op jit(solution)/shard_map/ppermute | solution.py:47
  27.3 1.0 %collective-permute-done.7.got_left_ref = bf16[16,2560]{1,0:T(8,128)(2,1)S(1)} collective-permute-done((bf16[16,2560]{1,0:T(8,128)(2,1)S(1)}, bf16[16,2560]{1,0:T(8,128)(2,1)S(1)}, u32[]{:S(2)}, u32[]{:S(2)}) %collective-permute-start.7) | collective-permute-done | bytes 81952 | tf_op jit(solution)/shard_map/ppermute | solution.py:47
  28.3 1.9 %collective-permute-done.9.got_right_ref = bf16[16,2560]{1,0:T(8,128)(2,1)S(1)} collective-permute-done((bf16[16,2560]{1,0:T(8,128)(2,1)S(1)}, bf16[16,2560]{1,0:T(8,128)(2,1)S(1)}, u32[]{:S(2)}, u32[]{:S(2)}) %collective-permute-start.9) | collective-permute-done | bytes 81952 | tf_op jit(solution)/shard_map/ppermute | solution.py:47
  30.3 2.7 %collective-permute-start.10 = (bf16[16,5120]{1,0:T(8,128)(2,1)S(1)}, bf16[16,5120]{1,0:T(8,128)(2,1)S(1)}, u32[]{:S(2)}, u32[]{:S(2)}) collective-permute-start(bf16[16,5120]{1,0:T(8,128)(2,1)S(1)} %get-tuple-element.49.gate_ref), channel_id=1, source_target_pairs={{0,4},{1,5},{2,6},{3,7},{4,0},{5,1},{6,2},{7,3},{8,12},{9,13},{10,... | collective-permute-start | bytes 491528 | tf_op jit(solution)/shard_map/ppermute | solution.py:47
  32.9 3.3 %fetch.3.first_gate_ref.weight_ref = bf16[1280,3072]{1,0:T(8,128)(2,1)S(1)} custom-call(bf16[5120,3072]{1,0:T(8,128)(2,1)} %source_ref.9, bf16[16,5120]{1,0:T(8,128)(2,1)S(1)} %get-tuple-element.49.gate_ref), custom_call_target="tpu_custom_call" | custom-call | bytes 7864320 | tf_op jit(solution)/shard_map/fetch/pallas_call | solution.py:496
  36.3 3.4 %fetch.4.second_gate_ref.next_ref = bf16[1280,3072]{1,0:T(8,128)(2,1)S(1)} custom-call(bf16[5120,3072]{1,0:T(8,128)(2,1)} %source_ref.9, bf16[16,5120]{1,0:T(8,128)(2,1)S(1)} %get-tuple-element.49.gate_ref), custom_call_target="tpu_custom_call" | custom-call | bytes 7864320 | tf_op jit(solution)/shard_map/fetch/pallas_call | solution.py:496
  39.9 1.2 %collective-permute-start.11 = (bf16[16,5120]{1,0:T(8,128)(2,1)S(1)}, bf16[16,5120]{1,0:T(8,128)(2,1)S(1)}, u32[]{:S(2)}, u32[]{:S(2)}) collective-permute-start(bf16[16,5120]{1,0:T(8,128)(2,1)S(1)} %norm.1.refs_0_), channel_id=1, source_target_pairs={{0,2},{1,3},{2,0},{3,1},{4,6},{5,7},{6,4},{7,5},{8,10},{9,11},{10,... | collective-permute-start | bytes 491528 | tf_op jit(solution)/shard_map/ppermute | solution.py:47
  41.1 4.2 %collective-permute-done.11.refs_1_ = bf16[16,5120]{1,0:T(8,128)(2,1)S(1)} collective-permute-done((bf16[16,5120]{1,0:T(8,128)(2,1)S(1)}, bf16[16,5120]{1,0:T(8,128)(2,1)S(1)}, u32[]{:S(2)}, u32[]{:S(2)}) %collective-permute-start.11) | collective-permute-done | bytes 163872 | tf_op jit(solution)/shard_map/ppermute | solution.py:47
  45.4 1.6 %collective-permute-start.12 = (bf16[2,16,2560]{2,1,0:T(8,128)(2,1)S(1)}, bf16[2,16,2560]{2,1,0:T(8,128)(2,1)S(1)}, u32[]{:S(2)}, u32[]{:S(2)}) collective-permute-start(bf16[2,16,2560]{2,1,0:T(8,128)(2,1)S(1)} %get-tuple-element.51.gate_ref.refs_0_), channel_id=1, source_target_pairs={{0,1},{1,0},{2,3},{3,2},{4,5},{5,4},{6,7},{7,6},{8,9},{9,8},{10,11... | collective-permute-start | bytes 491528 | tf_op jit(solution)/shard_map/ppermute | solution.py:47
  46.9 1.5 %collective-permute-start.15 = (bf16[2,16,2560]{2,1,0:T(8,128)(2,1)S(1)}, bf16[2,16,2560]{2,1,0:T(8,128)(2,1)S(1)}, u32[]{:S(2)}, u32[]{:S(2)}) collective-permute-start(bf16[2,16,2560]{2,1,0:T(8,128)(2,1)S(1)} %get-tuple-element.53), channel_id=1, source_target_pairs={{0,16},{8,24},{16,0},{24,8},{1,17},{9,25},{17,1},{25,9},{2,18},{10... | collective-permute-start | bytes 491528 | tf_op jit(solution)/shard_map/ppermute | solution.py:47
  48.4 3.3 %fetch.5.refs_2_.weight_ref = bf16[1280,3072]{1,0:T(8,128)(2,1)S(1)} custom-call(bf16[5120,3072]{1,0:T(8,128)(2,1)} %source_ref.9, bf16[2,16,2560]{2,1,0:T(8,128)(2,1)S(1)} %get-tuple-element.51.gate_ref.refs_0_), custom_call_target="tpu_custom_call" | custom-call | bytes 7864320 | tf_op jit(solution)/shard_map/fetch/pallas_call | solution.py:496
  51.8 0.8 collective-permute-start.13
  52.6 1.4 %collective-permute-done.15 = bf16[2,16,2560]{2,1,0:T(8,128)(2,1)S(1)} collective-permute-done((bf16[2,16,2560]{2,1,0:T(8,128)(2,1)S(1)}, bf16[2,16,2560]{2,1,0:T(8,128)(2,1)S(1)}, u32[]{:S(2)}, u32[]{:S(2)}) %collective-permute-start.15) | collective-permute-done | bytes 163872 | tf_op jit(solution)/shard_map/ppermute | solution.py:47
  54.0 1.2 %collective-permute-start.16 = (bf16[4,16,2560]{2,1,0:T(8,128)(2,1)S(1)}, bf16[4,16,2560]{2,1,0:T(8,128)(2,1)S(1)}, u32[]{:S(2)}, u32[]{:S(2)}) collective-permute-start(bf16[4,16,2560]{2,1,0:T(8,128)(2,1)S(1)} %pad_maximum_fusion.2), channel_id=1, source_target_pairs={{0,1},{1,0},{2,3},{3,2},{4,5},{5,4},{6,7},{7,6},{8,9},{9,8},{10,11... | collective-permute-start | bytes 983048 | tf_op jit(solution)/shard_map/ppermute | solution.py:47
  55.2 3.8 %collective-permute-done.13 = bf16[4,16,2560]{2,1,0:T(8,128)(2,1)S(1)} collective-permute-done((bf16[4,16,2560]{2,1,0:T(8,128)(2,1)S(1)}, bf16[4,16,2560]{2,1,0:T(8,128)(2,1)S(1)}, u32[]{:S(2)}, u32[]{:S(2)}) %collective-permute-start.13) | collective-permute-done | bytes 327712 | tf_op jit(solution)/shard_map/ppermute | solution.py:47
  59.1 2.1 %collective-permute-done.16 = bf16[4,16,2560]{2,1,0:T(8,128)(2,1)S(1)} collective-permute-done((bf16[4,16,2560]{2,1,0:T(8,128)(2,1)S(1)}, bf16[4,16,2560]{2,1,0:T(8,128)(2,1)S(1)}, u32[]{:S(2)}, u32[]{:S(2)}) %collective-permute-start.16) | collective-permute-done | bytes 327712 | tf_op jit(solution)/shard_map/ppermute | solution.py:47
  61.4 4.5 %logits_first.1 = (f32[256,3072]{1,0:T(8,128)S(1)}, bf16[1280,3072]{1,0:T(8,128)(2,1)S(1)}) custom-call(bf16[128,2560]{1,0:T(8,128)(2,1)S(1)} %bitcast.6, bf16[128,2560]{1,0:T(8,128)(2,1)S(1)} %collective-permute-done.14.right_ref, bf16[1280,3072]{1,0:T(8,128)(2,1)S(1)} %fetch.3.first_gate_ref.weight_ref, ...), custom_call_target="tpu_custom_call" | custom-call | flops 4026531840 | tf_op jit(solution)/shard_map/logits_first/pallas_call | solution.py:609
  65.9 5.0 %logits.1 = f32[32,1,128]{2,1,0:T(1,128)S(1)} custom-call(f32[256,3072]{1,0:T(8,128)S(1)} %get-tuple-element.52.sum_in_ref, bf16[128,2560]{1,0:T(8,128)(2,1)S(1)} %bitcast.4, bf16[128,2560]{1,0:T(8,128)(2,1)S(1)} %collective-permute-done.17.right_ref, s32[32,8,1]{2,1,0:T(8,128)S(1)} %reshape.16.refs_1_.target_ref, ...), custom_call_target="tpu_custom_call" | custom-call | flops 4026531840 | tf_op jit(solution)/shard_map/logits/pallas_call | solution.py:622
  70.9 10.2 %all_to_all.5.stats_ref = f32[32,1,128]{2,1,0:T(1,128)S(1)} all-to-all(f32[32,1,128]{2,1,0:T(1,128)S(1)} %logits.1), channel_id=1, replica_groups=mesh['group'=4,'tensor'=8] {'group','tensor'}, dimensions={0} | all-to-all | bytes 32768 | tf_op jit(solution)/shard_map/all_to_all | solution.py:635
  (32 shorter events, 1.6 us)
Async XLA Ops:
  0.0 5.4 %collective-permute-start = (bf16[64,512]{1,0:T(8,128)(2,1)}, bf16[64,512]{1,0:T(8,128)(2,1)S(1)}, u32[]{:S(2)}, u32[]{:S(2)}) collective-permute-start(bf16[64,512]{1,0:T(8,128)(2,1)} %refs_0_.1), channel_id=1, source_target_pairs={{0,16},{8,24},{16,0},{24,8},{1,17},{9,25},{17,1},{25,9},{2,18},{10... | collective-permute-start | bytes 196616 | tf_op jit(solution)/shard_map/ppermute | solution.py:47
  3.0 3.9 %collective-permute-start.2 = (bf16[64,512]{1,0:T(8,128)(2,1)}, bf16[64,512]{1,0:T(8,128)(2,1)S(1)}, u32[]{:S(2)}, u32[]{:S(2)}) collective-permute-start(bf16[64,512]{1,0:T(8,128)(2,1)} %refs_0_.1), channel_id=1, source_target_pairs={{0,8},{8,0},{16,24},{24,16},{1,9},{9,1},{17,25},{25,17},{2,10},{10... | collective-permute-start | bytes 196616 | tf_op jit(solution)/shard_map/ppermute | solution.py:47
  5.4 27.5 %copy-start.1 = (bf16[5120]{0:T(1024)(128)(2,1)S(1)}, bf16[5120]{0:T(1024)(128)(2,1)}, u32[]{:S(2)}) copy-start(bf16[5120]{0:T(1024)(128)(2,1)} %param.21) | copy-start | bytes 30724
  5.4 1.5 %collective-permute-start.1 = (bf16[64,512]{1,0:T(8,128)(2,1)S(1)}, bf16[64,512]{1,0:T(8,128)(2,1)S(1)}, u32[]{:S(2)}, u32[]{:S(2)}) collective-permute-start(bf16[64,512]{1,0:T(8,128)(2,1)S(1)} %pass.1.gate_ref.refs_1_), channel_id=1, source_target_pairs={{0,8},{8,0},{16,24},{24,16},{1,9},{9,1},{17,25},{25,17},{2,10},{10... | collective-permute-start | bytes 196616 | tf_op jit(solution)/shard_map/ppermute | solution.py:47
  7.8 5.9 %collective-permute-start.3 = (bf16[64,640]{1,0:T(8,128)(2,1)S(1)}, bf16[64,640]{1,0:T(8,128)(2,1)S(1)}, u32[]{:S(2)}, u32[]{:S(2)}) collective-permute-start(bf16[64,640]{1,0:T(8,128)(2,1)S(1)} %get-tuple-element.35.gate_ref), channel_id=1, source_target_pairs={{0,24},{8,16},{16,8},{24,0},{1,25},{9,17},{17,9},{25,1},{2,26},{10... | collective-permute-start | bytes 245768 | tf_op jit(solution)/shard_map/ppermute | solution.py:47
  10.0 4.7 %collective-permute-start.4 = (bf16[64,640]{1,0:T(8,128)(2,1)S(1)}, bf16[64,640]{1,0:T(8,128)(2,1)S(1)}, u32[]{:S(2)}, u32[]{:S(2)}) collective-permute-start(bf16[64,640]{1,0:T(8,128)(2,1)S(1)} %get-tuple-element.38), channel_id=1, source_target_pairs={{0,16},{8,24},{16,0},{24,8},{1,17},{9,25},{17,1},{25,9},{2,18},{10... | collective-permute-start | bytes 245768 | tf_op jit(solution)/shard_map/ppermute | solution.py:47
  10.0 4.7 %collective-permute-start.5 = (bf16[64,640]{1,0:T(8,128)(2,1)S(1)}, bf16[64,640]{1,0:T(8,128)(2,1)S(1)}, u32[]{:S(2)}, u32[]{:S(2)}) collective-permute-start(bf16[64,640]{1,0:T(8,128)(2,1)S(1)} %get-tuple-element.39), channel_id=1, source_target_pairs={{0,8},{8,0},{16,24},{24,16},{1,9},{9,1},{17,25},{25,17},{2,10},{10... | collective-permute-start | bytes 245768 | tf_op jit(solution)/shard_map/ppermute | solution.py:47
  18.0 5.8 %collective-permute-start.6 = (bf16[2,16,2560]{2,1,0:T(8,128)(2,1)S(1)}, bf16[2,16,2560]{2,1,0:T(8,128)(2,1)S(1)}, u32[]{:S(2)}, u32[]{:S(2)}) collective-permute-start(bf16[2,16,2560]{2,1,0:T(8,128)(2,1)S(1)} %get-tuple-element.42), channel_id=1, source_target_pairs={{0,1},{1,0},{2,3},{3,2},{4,5},{5,4},{6,7},{7,6},{8,9},{9,8},{10,11... | collective-permute-start | bytes 491528 | tf_op jit(solution)/shard_map/ppermute | solution.py:47
  19.7 6.0 %collective-permute-start.8 = (bf16[2,16,2560]{2,1,0:T(8,128)(2,1)S(1)}, bf16[2,16,2560]{2,1,0:T(8,128)(2,1)S(1)}, u32[]{:S(2)}, u32[]{:S(2)}) collective-permute-start(bf16[2,16,2560]{2,1,0:T(8,128)(2,1)S(1)} %get-tuple-element.46), channel_id=1, source_target_pairs={{0,2},{1,3},{2,0},{3,1},{4,6},{5,7},{6,4},{7,5},{8,10},{9,11},{10,... | collective-permute-start | bytes 491528 | tf_op jit(solution)/shard_map/ppermute | solution.py:47
  23.8 4.5 %collective-permute-start.7 = (bf16[16,2560]{1,0:T(8,128)(2,1)S(1)}, bf16[16,2560]{1,0:T(8,128)(2,1)S(1)}, u32[]{:S(2)}, u32[]{:S(2)}) collective-permute-start(bf16[16,2560]{1,0:T(8,128)(2,1)S(1)} %get-tuple-element.44), channel_id=1, source_target_pairs={{0,2},{1,3},{2,0},{3,1},{4,6},{5,7},{6,4},{7,5},{8,10},{9,11},{10,... | collective-permute-start | bytes 245768 | tf_op jit(solution)/shard_map/ppermute | solution.py:47
  25.7 4.5 %collective-permute-start.9 = (bf16[16,2560]{1,0:T(8,128)(2,1)S(1)}, bf16[16,2560]{1,0:T(8,128)(2,1)S(1)}, u32[]{:S(2)}, u32[]{:S(2)}) collective-permute-start(bf16[16,2560]{1,0:T(8,128)(2,1)S(1)} %get-tuple-element.48), channel_id=1, source_target_pairs={{0,1},{1,0},{2,3},{3,2},{4,5},{5,4},{6,7},{7,6},{8,9},{9,8},{10,11... | collective-permute-start | bytes 245768 | tf_op jit(solution)/shard_map/ppermute | solution.py:47
  30.3 9.5 %collective-permute-start.10 = (bf16[16,5120]{1,0:T(8,128)(2,1)S(1)}, bf16[16,5120]{1,0:T(8,128)(2,1)S(1)}, u32[]{:S(2)}, u32[]{:S(2)}) collective-permute-start(bf16[16,5120]{1,0:T(8,128)(2,1)S(1)} %get-tuple-element.49.gate_ref), channel_id=1, source_target_pairs={{0,4},{1,5},{2,6},{3,7},{4,0},{5,1},{6,2},{7,3},{8,12},{9,13},{10,... | collective-permute-start | bytes 491528 | tf_op jit(solution)/shard_map/ppermute | solution.py:47
  36.3 3.4 %copy-start = (bf16[64,5120]{1,0:T(8,128)(2,1)S(1)}, bf16[64,5120]{1,0:T(8,128)(2,1)}, u32[]{:S(2)}) copy-start(bf16[64,5120]{1,0:T(8,128)(2,1)} %param.19) | copy-start | bytes 1966084
  39.9 5.4 %collective-permute-start.11 = (bf16[16,5120]{1,0:T(8,128)(2,1)S(1)}, bf16[16,5120]{1,0:T(8,128)(2,1)S(1)}, u32[]{:S(2)}, u32[]{:S(2)}) collective-permute-start(bf16[16,5120]{1,0:T(8,128)(2,1)S(1)} %norm.1.refs_0_), channel_id=1, source_target_pairs={{0,2},{1,3},{2,0},{3,1},{4,6},{5,7},{6,4},{7,5},{8,10},{9,11},{10,... | collective-permute-start | bytes 491528 | tf_op jit(solution)/shard_map/ppermute | solution.py:47
  45.4 6.4 %collective-permute-start.12 = (bf16[2,16,2560]{2,1,0:T(8,128)(2,1)S(1)}, bf16[2,16,2560]{2,1,0:T(8,128)(2,1)S(1)}, u32[]{:S(2)}, u32[]{:S(2)}) collective-permute-start(bf16[2,16,2560]{2,1,0:T(8,128)(2,1)S(1)} %get-tuple-element.51.gate_ref.refs_0_), channel_id=1, source_target_pairs={{0,1},{1,0},{2,3},{3,2},{4,5},{5,4},{6,7},{7,6},{8,9},{9,8},{10,11... | collective-permute-start | bytes 491528 | tf_op jit(solution)/shard_map/ppermute | solution.py:47
  46.9 7.1 %collective-permute-start.15 = (bf16[2,16,2560]{2,1,0:T(8,128)(2,1)S(1)}, bf16[2,16,2560]{2,1,0:T(8,128)(2,1)S(1)}, u32[]{:S(2)}, u32[]{:S(2)}) collective-permute-start(bf16[2,16,2560]{2,1,0:T(8,128)(2,1)S(1)} %get-tuple-element.53), channel_id=1, source_target_pairs={{0,16},{8,24},{16,0},{24,8},{1,17},{9,25},{17,1},{25,9},{2,18},{10... | collective-permute-start | bytes 491528 | tf_op jit(solution)/shard_map/ppermute | solution.py:47
  51.8 7.1 %collective-permute-start.13 = (bf16[4,16,2560]{2,1,0:T(8,128)(2,1)S(1)}, bf16[4,16,2560]{2,1,0:T(8,128)(2,1)S(1)}, u32[]{:S(2)}, u32[]{:S(2)}) collective-permute-start(bf16[4,16,2560]{2,1,0:T(8,128)(2,1)S(1)} %join.1), channel_id=1, source_target_pairs={{0,16},{8,24},{16,0},{24,8},{1,17},{9,25},{17,1},{25,9},{2,18},{10... | collective-permute-start | bytes 983048 | tf_op jit(solution)/shard_map/ppermute | solution.py:47
  54.0 7.1 %collective-permute-start.16 = (bf16[4,16,2560]{2,1,0:T(8,128)(2,1)S(1)}, bf16[4,16,2560]{2,1,0:T(8,128)(2,1)S(1)}, u32[]{:S(2)}, u32[]{:S(2)}) collective-permute-start(bf16[4,16,2560]{2,1,0:T(8,128)(2,1)S(1)} %pad_maximum_fusion.2), channel_id=1, source_target_pairs={{0,1},{1,0},{2,3},{3,2},{4,5},{5,4},{6,7},{7,6},{8,9},{9,8},{10,11... | collective-permute-start | bytes 983048 | tf_op jit(solution)/shard_map/ppermute | solution.py:47
  59.0 2.3 %collective-permute-start.14 = (bf16[128,2560]{1,0:T(8,128)(2,1)S(1)}, bf16[128,2560]{1,0:T(8,128)(2,1)S(1)}, u32[]{:S(2)}, u32[]{:S(2)}) collective-permute-start(bf16[128,2560]{1,0:T(8,128)(2,1)S(1)} %bitcast.5), channel_id=1, source_target_pairs={{0,8},{8,0},{16,24},{24,16},{1,9},{9,1},{17,25},{25,17},{2,10},{10... | collective-permute-start | bytes 1966088 | tf_op jit(solution)/shard_map/ppermute | solution.py:47
  61.3 4.6 %collective-permute-start.17 = (bf16[128,2560]{1,0:T(8,128)(2,1)S(1)}, bf16[128,2560]{1,0:T(8,128)(2,1)S(1)}, u32[]{:S(2)}, u32[]{:S(2)}) collective-permute-start(bf16[128,2560]{1,0:T(8,128)(2,1)S(1)} %bitcast.3), channel_id=1, source_target_pairs={{0,8},{8,0},{16,24},{24,16},{1,9},{9,1},{17,25},{25,17},{2,10},{10... | collective-permute-start | bytes 1966088 | tf_op jit(solution)/shard_map/ppermute | solution.py:47

commit v10 on v9

--- a/solution.py
+++ b/solution.py
@@ -243,7 +243,8 @@
             send_right_ref[i, :, columns] = partial_ref[me ^ (i + 2)].astype(BF16)
 
 
-def fold_kernel(keep_ref, got_ref, own_ref, send_ref):
+def fold_kernel(keep_ref, got_ref, *refs):
+    own_ref, send_ref = refs[-2:]
     own_ref[...] = keep_ref[0] + got_ref[0].astype(F32)
     send_ref[...] = (keep_ref[1] + got_ref[1].astype(F32)).astype(BF16)
 
@@ -270,81 +271,71 @@
         copy.wait()
 
 
-def column_kernel(count, *refs):
-    terms, out_refs = refs[:count], refs[-2:]
-    width = out_refs[0].shape[2]
-    for i, ref in enumerate(terms):
-        for half, out_ref in enumerate(out_refs):
-            out_ref[i] = ref[:, half * width : (half + 1) * width]
-
-
-def norm_kernel(residual_ref, gain_ref, first_gate_ref, second_gate_ref, own_ref, got_ref, out_ref):
+def norm_kernel(residual_ref, gain_ref, gate_ref, own_ref, got_ref, *out_refs):
     hidden = residual_ref[lax.axis_index("tensor") % 4].astype(F32)
     hidden = hidden + (own_ref[...] + got_ref[...].astype(F32))
     squares = jnp.mean(hidden * hidden, axis=-1, keepdims=True)
-    out_ref[...] = (hidden * lax.rsqrt(squares + 1e-06) * gain_ref[...].astype(F32)).astype(BF16)
-
-
-def join_kernel(count, *refs):
-    out_ref = refs[-1]
+    normed = (hidden * lax.rsqrt(squares + 1e-06) * gain_ref[...].astype(F32)).astype(BF16)
     start = 0
-    for ref in refs[:count]:
-        out_ref[start : start + ref.shape[0]] = ref[...]
-        start += ref.shape[0]
-
-
-def quarter_dots(x_ref, weight_refs, columns):
-    depth = weight_refs[0].shape[0]
-    return functools.reduce(
-        jnp.add,
-        [
-            jnp.dot(x_ref[:, i * depth : (i + 1) * depth], ref[:, columns], preferred_element_type=F32)
-            for i, ref in enumerate(weight_refs)
-        ],
-    )
+    for ref in out_refs:
+        width = ref.shape[2]
+        ref[0] = normed[:, start : start + width]
+        start += width
+
+
+def place_tokens(x_ref, start, places, left_ref, right_ref):
+    block, width = left_ref.shape[1:]
+    for side, ref in enumerate((left_ref, right_ref)):
+        for i, place in enumerate(places):
+            row = (side * len(places) + i) * block
+            x_ref[row : row + block, start : start + width] = ref[place]
+
+
+def tokens_dot(x_ref, start, weight):
+    x = x_ref[:, start : start + weight.shape[0]]
+    return jnp.dot(x, weight, preferred_element_type=F32)
 
 
 def first_kernel(
-    narrow, left_ref, right_ref, weight_ref, next_ref, source_ref, out_ref, last_ref, x_ref, sems
+    narrow, places, left_ref, right_ref, weight_ref, source_ref, out_ref, last_ref, x_ref, sems
 ):
     copies = carried(source_ref, source_ref.shape[0] - last_ref.shape[0], last_ref, sems)
     for copy in copies:
         copy.start()
-    half = left_ref.shape[0]
-    x_ref[:half] = left_ref[...]
-    x_ref[half:] = right_ref[...]
+    place_tokens(x_ref, 0, places, left_ref, right_ref)
 
     @pl.loop(0, weight_ref.shape[1] // narrow)
     def _(n):
         columns = pl.ds(n * narrow if narrow % 128 else pl.multiple_of(n * narrow, 128), narrow)
-        out_ref[:, columns] = quarter_dots(x_ref, (weight_ref, next_ref), columns)
+        out_ref[:, columns] = tokens_dot(x_ref, 0, weight_ref[:, columns])
 
     for copy in copies:
         copy.wait()
 
 
 def logits_kernel(
-    narrow,
     spots,
     tensor_size,
+    orders,
     sum_in_ref,
     left_ref,
     right_ref,
+    next_left_ref,
+    next_right_ref,
     target_ref,
-    weight_ref,
-    next_ref,
-    out_ref,
-    x_ref,
-    peak_ref,
-    sum_ref,
-    pick_ref,
-    wanted_ref,
+    *refs,
 ):
-    half = left_ref.shape[0]
-    rows = 2 * half
+    weight_ref, last_ref, source_ref, out_ref, x_ref, near_ref, sems, wanted_ref = refs
+    rows = x_ref.shape[0]
+    width = left_ref.shape[2]
+    copies = carried(source_ref, source_ref.shape[0] - last_ref.shape[0] - near_ref.shape[0], near_ref, sems)
+    for copy in copies:
+        copy.start()
+    place_tokens(x_ref, 0, orders[0], left_ref, right_ref)
+    place_tokens(x_ref, width, orders[1], next_left_ref, next_right_ref)
     share = target_ref.shape[1]
     group, tensor = lax.axis_index("group"), lax.axis_index("tensor")
-    vocab = weight_ref.shape[1]
+    vocab = sum_in_ref.shape[1]
     shares = tensor_size // 4
     places = [
         (group ^ g) * tensor_size + shares * ((tensor % 4) ^ d) + i for g, d in spots for i in range(shares)
@@ -353,37 +344,26 @@
         wanted_ref[i * share : (i + 1) * share] = target_ref[place]
     wanted = wanted_ref[...] - (group * tensor_size + tensor) * vocab
     wanted_ref[...] = jnp.where((wanted >= 0) & (wanted < vocab), wanted, -1)
-    x_ref[:half] = left_ref[...]
-    x_ref[half:] = right_ref[...]
-    peak_ref[...] = jnp.full_like(peak_ref, NEG)
-    sum_ref[...] = jnp.zeros_like(sum_ref)
-    pick_ref[...] = jnp.zeros_like(pick_ref)
-
-    @pl.loop(0, weight_ref.shape[1] // narrow)
-    def _(n):
-        columns = pl.ds(n * narrow if narrow % 128 else pl.multiple_of(n * narrow, 128), narrow)
-        logits = sum_in_ref[:, columns] + quarter_dots(x_ref, (weight_ref, next_ref), columns)
-        parts = [logits[:, c : c + 128] for c in range(0, narrow, 128)]
-        if narrow % 128:
-            spare = jnp.full((rows, 128 - narrow % 128), NEG, F32)
-            parts[-1] = jnp.concatenate([parts[-1], spare], axis=1)
-        lane = lax.broadcasted_iota(jnp.int32, (rows, 128), 1) + n * narrow
-        peak = peak_ref[...]
-        higher = functools.reduce(jnp.maximum, parts, peak)
-        total = sum_ref[...] * jnp.exp(peak - higher)
-        picked = pick_ref[...]
-        target = wanted_ref[...]
-        for c, part in enumerate(parts):
-            total = total + jnp.exp(part - higher)
-            picked = picked + jnp.where(lane + c * 128 == target, part, 0.0)
-        peak_ref[...] = higher
-        sum_ref[...] = total
-        pick_ref[...] = picked
-
-    higher = peak_ref[...]
+    logits = sum_in_ref[...] + tokens_dot(x_ref, 0, weight_ref[...])
+    logits = logits + tokens_dot(x_ref, width, last_ref[...])
+    for copy in copies:
+        copy.wait()
+    logits = logits + tokens_dot(x_ref, width - near_ref.shape[0], near_ref[...])
+    parts = [logits[:, c : c + 128] for c in range(0, vocab, 128)]
+    if vocab % 128:
+        spare = jnp.full((rows, 128 - vocab % 128), NEG, F32)
+        parts[-1] = jnp.concatenate([parts[-1], spare], axis=1)
+    lane = lax.broadcasted_iota(jnp.int32, (rows, 128), 1)
+    target = wanted_ref[...]
+    higher = functools.reduce(jnp.maximum, parts)
+    total = jnp.zeros((rows, 128), F32)
+    picked = jnp.zeros((rows, 128), F32)
+    for c, part in enumerate(parts):
+        total = total + jnp.exp(part - higher)
+        picked = picked + jnp.where(lane + c * 128 == target, part, 0.0)
     peak = jnp.max(higher, axis=1, keepdims=True)
-    sums = jnp.sum(sum_ref[...] * jnp.exp(higher - peak), axis=1, keepdims=True)
-    pick = jnp.sum(pick_ref[...], axis=1, keepdims=True)
+    sums = jnp.sum(total * jnp.exp(higher - peak), axis=1, keepdims=True)
+    pick = jnp.sum(picked, axis=1, keepdims=True)
     row = lax.broadcasted_iota(jnp.int32, (rows, 128), 0)
     lane = lax.broadcasted_iota(jnp.int32, (rows, 128), 1)
     three = jnp.where(lane // share == 0, peak, jnp.where(lane // share == 1, sums, pick))
@@ -506,7 +486,6 @@
         )
 
     half = depth // 2
-    quarter = depth // 4
     wide = 1280 if half % 1280 == 0 else half
     block = rows // 4
     send_left, keep_left, send_right, keep_right = pl.pallas_call(
@@ -526,25 +505,29 @@
         name="project",
     )(stored(prompt_of), *map(held, (own, *got)), held(weight))
 
-    def add(kernel, name, size, *operands):
+    def add(kernel, name, size, *operands, gates=()):
         return pl.pallas_call(
             kernel,
             out_shape=[jax.ShapeDtypeStruct(size, F32), jax.ShapeDtypeStruct(size, BF16)],
-            in_specs=[vmem()] * len(operands),
+            in_specs=[vmem()] * len(operands) + [anywhere()] * len(gates),
             out_specs=[vmem()] * 2,
             compiler_params=params(2),
             name=name,
-        )(*map(held, operands))
+        )(*map(held, operands), *gates)
+
+    unit = depth // 20
+    widths = [7 * unit, 7 * unit, 6 * unit]
+    second_rows = 4 * unit
+    second_weight = fetch(lm_weight, widths[0], second_rows, send_left)
 
     got_left = swap(send_left, "tensor", 1, tensor_size)
     got_right = swap(send_right, "tensor", 2, tensor_size)
-    left, send_left = add(fold_kernel, "fold_left", (block, half), keep_left, got_left)
+    left, send_left = add(fold_kernel, "fold_left", (block, half), keep_left, got_left, gates=(second_weight,))
     right, send_right = add(fold_kernel, "fold_right", (block, half), keep_right, got_right)
     got_left = swap(send_left, "tensor", 2, tensor_size)
     got_right = swap(send_right, "tensor", 1, tensor_size)
     total, send = add(side_kernel, "side", (block, depth), left, got_left, right, got_right)
-    first_quarter = fetch(lm_weight, 0, quarter, send)
-    second_quarter = fetch(lm_weight, quarter, quarter, send)
+    first_weight = fetch(lm_weight, 0, widths[0], send)
     far = 4
     while 2 * far < tensor_size:
         total, send = add(
@@ -553,84 +536,73 @@
         far = 2 * far
     normed = pl.pallas_call(
         norm_kernel,
-        out_shape=jax.ShapeDtypeStruct((block, depth), BF16),
-        in_specs=[vmem()] * 2 + [anywhere()] * 2 + [vmem()] * 2,
-        out_specs=vmem(),
+        out_shape=[jax.ShapeDtypeStruct((1, block, width), BF16) for width in widths],
+        in_specs=[vmem()] * 2 + [anywhere()] + [vmem()] * 2,
+        out_specs=[vmem()] * len(widths),
         compiler_params=params(4),
         name="norm",
     )(
         *map(held, (residual.reshape(4, block, depth), norm_gain[None])),
-        first_quarter,
-        second_quarter,
+        first_weight,
         *map(held, (total, swap(send, "tensor", far, tensor_size))),
     )
 
-    order = [0, 2]
-    here = [(g, x) for g in [0] + above for x in (0, 1)]
-    column = [normed, swap(normed, "tensor", 2, tensor_size)]
-    columns = pl.pallas_call(
-        functools.partial(column_kernel, len(column)),
-        out_shape=[jax.ShapeDtypeStruct((len(column), block, half), BF16)] * 2,
-        in_specs=[vmem()] * len(column),
-        out_specs=[vmem()] * 2,
-        compiler_params=params(2),
-        name="column",
-    )(*map(held, column))
-
-    def join(pieces, gate):
-        blocks = sum(x.shape[0] for x in pieces)
-        return pl.pallas_call(
-            functools.partial(join_kernel, len(pieces)),
-            out_shape=jax.ShapeDtypeStruct((blocks, block, half), BF16),
-            in_specs=[vmem()] * len(pieces) + [anywhere()],
-            out_specs=vmem(),
-            compiler_params=params(2),
-            name="join",
-        )(*map(held, pieces), gate)
-
-    left, right = columns
-    got_left = swap(left, "tensor", 1, tensor_size)
-    third = fetch(lm_weight, 2 * quarter, quarter, left)
-    right = [right] + [swap(right, "group", d, group_size) for d in above]
-    left = join([left, got_left], third)
-    got_left = [swap(left, "group", d, group_size) for d in above]
-    across = swap(jnp.concatenate(right), "tensor", 1, tensor_size)
-    across = jnp.split(across, len(right))
-    right = [x for pair in zip(right, across) for x in pair]
-    halves = []
-    for tokens in (jnp.concatenate([left] + got_left), jnp.concatenate(right)):
-        tokens = tokens.reshape(-1, half)
-        halves.append((tokens, swap(tokens, "group", 1, group_size)))
-    spots = [(g + c, t + x) for c in (0, 1) for g, x in here for t in order]
-    total_rows = 2 * tokens.shape[0]
+    axes = {
+        "x": [("tensor", 1)],
+        "z": [("tensor", 2)],
+        "y": [("group", d) for d in above],
+    }
+    arrays, labels = list(normed), [[(0, 0)] for _ in normed]
+    for stage in range(3):
+        for n, route in enumerate(("zxy", "xyz", "yzx")):
+            x, steps = arrays[n], axes[route[stage]]
+            got = [
+                swap(x, axis, d, group_size if axis == "group" else tensor_size) for axis, d in steps
+            ]
+            labels[n] = labels[n] + [
+                (g + d, t) if axis == "group" else (g, t + d) for axis, d in steps for g, t in labels[n]
+            ]
+            arrays[n] = (x, got) if stage == 2 else jnp.concatenate([x] + got)
+    arrays = [jnp.concatenate([x] + got) for x, got in arrays]
+    others = [swap(x, "group", 1, group_size) for x in arrays]
+    spots = [(g + c, t) for c in (0, 1) for g, t in labels[0]]
+    orders = [tuple(order.index(label) for label in labels[0]) for order in labels]
+    total_rows = len(spots) * block
     narrow = 1536 if vocab % 1536 == 0 else vocab
     limit = 10 if total_rows <= 256 else 24
-    work = 2 * total_rows * (half) * vocab
     first, last = pl.pallas_call(
-        functools.partial(first_kernel, narrow),
-        out_shape=[pltpu.VMEM((total_rows, vocab), F32), pltpu.VMEM((quarter, vocab), BF16)],
-        in_specs=[vmem()] * 4 + [anywhere()],
+        functools.partial(first_kernel, narrow, orders[0]),
+        out_shape=[pltpu.VMEM((total_rows, vocab), F32), pltpu.VMEM((widths[2], vocab), BF16)],
+        in_specs=[vmem()] * 3 + [anywhere()],
         out_specs=[vmem()] * 2,
         scratch_shapes=[
-            pltpu.VMEM((total_rows, half), BF16),
+            pltpu.VMEM((total_rows, widths[0]), BF16),
             pltpu.SemaphoreType.DMA((4,)),
         ],
         compiler_params=params(limit),
-        cost_estimate=cost(flops=work),
+        cost_estimate=cost(flops=2 * total_rows * widths[0] * vocab),
         name="logits_first",
-    )(*map(held, (*halves[0], first_quarter, second_quarter)), stored(lm_weight))
+    )(*map(held, (arrays[0], others[0], first_weight)), stored(lm_weight))
     stats = pl.pallas_call(
-        functools.partial(logits_kernel, vocab, spots, tensor_size),
+        functools.partial(logits_kernel, spots, tensor_size, orders[1:]),
         out_shape=jax.ShapeDtypeStruct((group_size * tensor_size, 1, 128), F32),
-        in_specs=[vmem()] * 6,
+        in_specs=[vmem()] * 8 + [anywhere()],
         out_specs=vmem(),
-        scratch_shapes=[pltpu.VMEM((total_rows, half), BF16)]
-        + [pltpu.VMEM((total_rows, 128), F32)] * 3
-        + [pltpu.VMEM((total_rows, 1), i32)],
-        compiler_params=params(limit),
-        cost_estimate=cost(flops=work),
+        scratch_shapes=[
+            pltpu.VMEM((total_rows, widths[1] + widths[2]), BF16),
+            pltpu.VMEM((widths[1] - second_rows, vocab), BF16),
+            pltpu.SemaphoreType.DMA((4,)),
+            pltpu.VMEM((total_rows, 1), i32),
+        ],
+        compiler_params=params(limit + 6),
+        cost_estimate=cost(flops=2 * total_rows * (widths[1] + widths[2]) * vocab),
         name="logits",
-    )(*map(held, (first, *halves[1])), wanted, held(third), held(last))
+    )(
+        *map(held, (first, arrays[1], others[1], arrays[2], others[2])),
+        wanted,
+        *map(held, (second_weight, last)),
+        stored(lm_weight),
+    )
 
     stats = lax.all_to_all(stats, ("group", "tensor"), 0, 0, tiled=True)
     return pl.pallas_call(

time: 81.9 us -> 84.1 us (1.027)
  starting transfers between devices: 21.1 us -> 26.4 us
  waiting for transfers between devices: 19.5 us -> 15.3 us
  blocking collectives: 10.2 us -> 11.2 us
    ppermute x18 -> x23, starting transfers between devices: 21.1 us -> 26.4 us  [swap(): return lax.ppermute(x, axis, [(i, i ^ distance) for i in range(size)])]
    ppermute x18 -> x23, waiting for transfers between devices: 19.5 us -> 15.3 us  [swap(): return lax.ppermute(x, axis, [(i, i ^ distance) for i in range(size)])]
    pallas_call x3 -> x2, Pallas kernels: 10.1 us -> 7.17 us  [fetch(): pl.pallas_call(functools.partial(fetch_kernel, start), out_shape=pltpu.VM...]
    pallas_call x5 -> x3, Pallas kernels: 9.77 us -> 12.7 us  [the longest x1 8.66 us: local(): pl.pallas_call(functools.partial(logits_kernel, spots, tensor_size, order...]
    all_to_all x1, blocking collectives: 10.2 us -> 11.2 us  [local(): stats = lax.all_to_all(stats, ('group', 'tensor'), 0, 0, tiled=True)]
  transfers between devices with their start and end apart: 18 -> 23, of which waited for: 9 -> 10; matrix products, arithmetic and copies ran while one was open for 1% -> 1% of each run, Pallas kernels for 24% -> 19%
where the time goes in v10:
time: 84.1 us; the launch traced here: 83.9 us
  Pallas kernels  29.6 us (35%)
  starting transfers between devices  26.4 us (31%)
  waiting for transfers between devices  15.3 us (18%)
  blocking collectives  11.2 us (13%)
  local copies, waits for them, and re-layouts  1.01 us (1%)
    ppermute x23, starting transfers between devices, swap(): return lax.ppermute(x, axis, [(i, i ^ distance) for i in range(size)])  26.4 us
    ppermute x23, waiting for transfers between devices, swap(): return lax.ppermute(x, axis, [(i, i ^ distance) for i in range(size)])  15.3 us
    all_to_all x1, blocking collectives, local(): stats = lax.all_to_all(stats, ('group', 'tensor'), 0, 0, tiled=True)  11.2 us
    pallas_call x1, Pallas kernels, local(): pl.pallas_call(functools.partial(logits_kernel, spots, tensor_size, order...  8.66 us
    pallas_call x2, Pallas kernels, fetch(): pl.pallas_call(functools.partial(fetch_kernel, start), out_shape=pltpu.VM...  7.17 us
    pallas_call x1, Pallas kernels, local(): pl.pallas_call(functools.partial(first_kernel, narrow, orders[0]), out_sh...  3.8 us
    pallas_call x1, Pallas kernels, local(): pl.pallas_call(functools.partial(own_kernel, heads, seq, share), out_shap...  3.54 us
    pallas_call x1, Pallas kernels, local(): pl.pallas_call(functools.partial(project_kernel, heads, seq, wide, group_...  3.27 us
  transfers between devices with their start and end apart: 23, of which 10 were waited for; matrix products, arithmetic and copies ran while one was open for 1% of the time, Pallas kernels for 19%

profile of v10, /device:TPU:0, one launch (start us, length us, event | category | flops | bytes accessed | tf_op | source)
XLA Modules:
  0.0 83.9 jit_solution(8985225934187679288)
XLA Ops:
  0.0 3.0 %collective-permute-start = (bf16[64,512]{1,0:T(8,128)(2,1)}, bf16[64,512]{1,0:T(8,128)(2,1)S(1)}, u32[]{:S(2)}, u32[]{:S(2)}) collective-permute-start(bf16[64,512]{1,0:T(8,128)(2,1)} %refs_0_.1), channel_id=1, source_target_pairs={{0,16},{8,24},{16,0},{24,8},{1,17},{9,25},{17,1},{25,9},{2,18},{10... | collective-permute-start | bytes 196616 | tf_op jit(solution)/shard_map/ppermute | solution.py:47
  3.0 0.9 %reshape.8.refs_1_.target_ref = s32[32,8,1]{2,1,0:T(8,128)S(1)} reshape(s32[256]{0:T(256)} %param.23) | data formatting | bytes 2048 | tf_op jit(solution)/shard_map/reshape | solution.py:411
  3.9 1.6 %collective-permute-done.refs_0_ = bf16[64,512]{1,0:T(8,128)(2,1)S(1)} collective-permute-done((bf16[64,512]{1,0:T(8,128)(2,1)}, bf16[64,512]{1,0:T(8,128)(2,1)S(1)}, u32[]{:S(2)}, u32[]{:S(2)}) %collective-permute-start) | collective-permute-done | bytes 65568 | tf_op jit(solution)/shard_map/ppermute | solution.py:47
  5.4 1.4 %load.1 = (bf16[64,512]{1,0:T(8,128)(2,1)S(1)}, bf16[64,512]{1,0:T(8,128)(2,1)S(1)}, bf16[64,512]{1,0:T(8,128)(2,1)S(1)}, bf16[512,512]{1,0:T(8,128)(2,1)S(1)}, bf16[512,512]{1,0:T(8,128)(2,1)S(1)}) custom-call(bf16[64,512]{1,0:T(8,128)(2,1)S(1)} %pass.1.gate_ref.refs_1_, bf16[64,512]{1,0:T(8,128)(2,1)} %refs_0_.1, bf16[64,512]{1,0:T(8,128)(2,1)} %refs_1_.1, ...), custom_call_target="tpu_custom_call" | custom-call | bytes 2097152 | tf_op jit(solution)/shard_map/load/pallas_call | solution.py:429
  7.7 2.2 %collective-permute-start.3 = (bf16[64,640]{1,0:T(8,128)(2,1)S(1)}, bf16[64,640]{1,0:T(8,128)(2,1)S(1)}, u32[]{:S(2)}, u32[]{:S(2)}) collective-permute-start(bf16[64,640]{1,0:T(8,128)(2,1)S(1)} %get-tuple-element.36.gate_ref), channel_id=1, source_target_pairs={{0,24},{8,16},{16,8},{24,0},{1,25},{9,17},{17,9},{25,1},{2,26},{10... | collective-permute-start | bytes 245768 | tf_op jit(solution)/shard_map/ppermute | solution.py:47
  10.1 3.5 %own_attention.1 = (f32[64,640]{1,0:T(8,128)S(1)}, f32[8,128]{1,0:T(8,128)S(1)}, bf16[512,5120]{1,0:T(8,128)(2,1)S(1)}) custom-call(s32[2]{0:T(128)} %lengths_ref.1, s32[2]{0:T(128)} %prompt_ref.3, bf16[64,512]{1,0:T(8,128)(2,1)S(1)} %get-tuple-element.31.q_ref, bf16[64,512]{1,0:T(8,128)(2,1)S(1)} %get-tuple-element.32.rk_ref, ...), custom_call_target="tpu_custom_call" | custom-call | bytes 8388608 | tf_op jit(solution)/shard_map/own_attention/pallas_call | solution.py:449
  13.6 1.0 %collective-permute-done.4.refs_1_ = bf16[64,640]{1,0:T(8,128)(2,1)S(1)} collective-permute-done((bf16[64,640]{1,0:T(8,128)(2,1)S(1)}, bf16[64,640]{1,0:T(8,128)(2,1)S(1)}, u32[]{:S(2)}, u32[]{:S(2)}) %collective-permute-start.4) | collective-permute-done | bytes 81952 | tf_op jit(solution)/shard_map/ppermute | solution.py:47
  14.6 3.3 %project.1 = (bf16[2,16,2560]{2,1,0:T(8,128)(2,1)S(1)}, f32[2,16,2560]{2,1,0:T(8,128)S(1)}, bf16[2,16,2560]{2,1,0:T(8,128)(2,1)S(1)}, f32[2,16,2560]{2,1,0:T(8,128)S(1)}) custom-call(s32[2]{0:T(128)} %prompt_ref.3, f32[64,640]{1,0:T(8,128)S(1)} %get-tuple-element.38.own_ref, bf16[64,640]{1,0:T(8,128)(2,1)S(1)} %collective-permute-done.3.refs_0_, ...), custom_call_target="tpu_custom_call" | custom-call | tf_op jit(solution)/shard_map/project/pallas_call | solution.py:491
  17.9 1.7 %collective-permute-start.6 = (bf16[2,16,2560]{2,1,0:T(8,128)(2,1)S(1)}, bf16[2,16,2560]{2,1,0:T(8,128)(2,1)S(1)}, u32[]{:S(2)}, u32[]{:S(2)}) collective-permute-start(bf16[2,16,2560]{2,1,0:T(8,128)(2,1)S(1)} %get-tuple-element.43.gate_ref), channel_id=1, source_target_pairs={{0,1},{1,0},{2,3},{3,2},{4,5},{5,4},{6,7},{7,6},{8,9},{9,8},{10,11... | collective-permute-start | bytes 491528 | tf_op jit(solution)/shard_map/ppermute | solution.py:47
  19.6 1.6 %collective-permute-start.8 = (bf16[2,16,2560]{2,1,0:T(8,128)(2,1)S(1)}, bf16[2,16,2560]{2,1,0:T(8,128)(2,1)S(1)}, u32[]{:S(2)}, u32[]{:S(2)}) collective-permute-start(bf16[2,16,2560]{2,1,0:T(8,128)(2,1)S(1)} %get-tuple-element.47), channel_id=1, source_target_pairs={{0,2},{1,3},{2,0},{3,1},{4,6},{5,7},{6,4},{7,5},{8,10},{9,11},{10,... | collective-permute-start | bytes 491528 | tf_op jit(solution)/shard_map/ppermute | solution.py:47
  21.2 2.9 %fetch.2.refs_0_ = bf16[1024,3072]{1,0:T(8,128)(2,1)S(1)} custom-call(bf16[5120,3072]{1,0:T(8,128)(2,1)} %refs_2_.3, bf16[2,16,2560]{2,1,0:T(8,128)(2,1)S(1)} %get-tuple-element.43.gate_ref), custom_call_target="tpu_custom_call" | custom-call | bytes 6291456 | tf_op jit(solution)/shard_map/fetch/pallas_call | solution.py:476
  24.1 1.5 %collective-permute-start.7 = (bf16[16,2560]{1,0:T(8,128)(2,1)S(1)}, bf16[16,2560]{1,0:T(8,128)(2,1)S(1)}, u32[]{:S(2)}, u32[]{:S(2)}) collective-permute-start(bf16[16,2560]{1,0:T(8,128)(2,1)S(1)} %get-tuple-element.45), channel_id=1, source_target_pairs={{0,2},{1,3},{2,0},{3,1},{4,6},{5,7},{6,4},{7,5},{8,10},{9,11},{10,... | collective-permute-start | bytes 245768 | tf_op jit(solution)/shard_map/ppermute | solution.py:47
  25.6 1.6 %collective-permute-start.9 = (bf16[16,2560]{1,0:T(8,128)(2,1)S(1)}, bf16[16,2560]{1,0:T(8,128)(2,1)S(1)}, u32[]{:S(2)}, u32[]{:S(2)}) collective-permute-start(bf16[16,2560]{1,0:T(8,128)(2,1)S(1)} %get-tuple-element.49), channel_id=1, source_target_pairs={{0,1},{1,0},{2,3},{3,2},{4,5},{5,4},{6,7},{7,6},{8,9},{9,8},{10,11... | collective-permute-start | bytes 245768 | tf_op jit(solution)/shard_map/ppermute | solution.py:47
  27.2 1.4 %collective-permute-done.7.got_left_ref = bf16[16,2560]{1,0:T(8,128)(2,1)S(1)} collective-permute-done((bf16[16,2560]{1,0:T(8,128)(2,1)S(1)}, bf16[16,2560]{1,0:T(8,128)(2,1)S(1)}, u32[]{:S(2)}, u32[]{:S(2)}) %collective-permute-start.7) | collective-permute-done | bytes 81952 | tf_op jit(solution)/shard_map/ppermute | solution.py:47
  28.6 1.5 %collective-permute-done.9.got_right_ref = bf16[16,2560]{1,0:T(8,128)(2,1)S(1)} collective-permute-done((bf16[16,2560]{1,0:T(8,128)(2,1)S(1)}, bf16[16,2560]{1,0:T(8,128)(2,1)S(1)}, u32[]{:S(2)}, u32[]{:S(2)}) %collective-permute-start.9) | collective-permute-done | bytes 81952 | tf_op jit(solution)/shard_map/ppermute | solution.py:47
  30.2 2.7 %collective-permute-start.10 = (bf16[16,5120]{1,0:T(8,128)(2,1)S(1)}, bf16[16,5120]{1,0:T(8,128)(2,1)S(1)}, u32[]{:S(2)}, u32[]{:S(2)}) collective-permute-start(bf16[16,5120]{1,0:T(8,128)(2,1)S(1)} %get-tuple-element.50.gate_ref), channel_id=1, source_target_pairs={{0,4},{1,5},{2,6},{3,7},{4,0},{5,1},{6,2},{7,3},{8,12},{9,13},{10,... | collective-permute-start | bytes 491528 | tf_op jit(solution)/shard_map/ppermute | solution.py:47
  32.9 4.3 %fetch.3.gate_ref.weight_ref = bf16[1792,3072]{1,0:T(8,128)(2,1)S(1)} custom-call(bf16[5120,3072]{1,0:T(8,128)(2,1)} %refs_2_.3, bf16[16,5120]{1,0:T(8,128)(2,1)S(1)} %get-tuple-element.50.gate_ref), custom_call_target="tpu_custom_call" | custom-call | bytes 11010048 | tf_op jit(solution)/shard_map/fetch/pallas_call | solution.py:476
  37.2 1.1 %collective-permute-done.10.got_ref = bf16[16,5120]{1,0:T(8,128)(2,1)S(1)} collective-permute-done((bf16[16,5120]{1,0:T(8,128)(2,1)S(1)}, bf16[16,5120]{1,0:T(8,128)(2,1)S(1)}, u32[]{:S(2)}, u32[]{:S(2)}) %collective-permute-start.10) | collective-permute-done | bytes 163872 | tf_op jit(solution)/shard_map/ppermute | solution.py:47
  38.8 1.2 %collective-permute-start.15 = (bf16[1,16,1792]{2,1,0:T(8,128)(2,1)S(1)}, bf16[1,16,1792]{2,1,0:T(8,128)(2,1)S(1)}, u32[]{:S(2)}, u32[]{:S(2)}) collective-permute-start(bf16[1,16,1792]{2,1,0:T(8,128)(2,1)S(1)} %get-tuple-element.54), channel_id=1, source_target_pairs={{0,1},{1,0},{2,3},{3,2},{4,5},{5,4},{6,7},{7,6},{8,9},{9,8},{10,11... | collective-permute-start | bytes 172040 | tf_op jit(solution)/shard_map/ppermute | solution.py:47
  40.0 1.5 %collective-permute-start.19 = (bf16[1,16,1536]{2,1,0:T(8,128)(2,1)S(1)}, bf16[1,16,1536]{2,1,0:T(8,128)(2,1)S(1)}, u32[]{:S(2)}, u32[]{:S(2)}) collective-permute-start(bf16[1,16,1536]{2,1,0:T(8,128)(2,1)S(1)} %get-tuple-element.55), channel_id=1, source_target_pairs={{0,16},{8,24},{16,0},{24,8},{1,17},{9,25},{17,1},{25,9},{2,18},{10... | collective-permute-start | bytes 147464 | tf_op jit(solution)/shard_map/ppermute | solution.py:47
  41.6 3.1 %collective-permute-done.19 = bf16[1,16,1536]{2,1,0:T(8,128)(2,1)S(1)} collective-permute-done((bf16[1,16,1536]{2,1,0:T(8,128)(2,1)S(1)}, bf16[1,16,1536]{2,1,0:T(8,128)(2,1)S(1)}, u32[]{:S(2)}, u32[]{:S(2)}) %collective-permute-start.19) | collective-permute-done | bytes 49184 | tf_op jit(solution)/shard_map/ppermute | solution.py:47
  44.7 1.6 %collective-permute-start.20 = (bf16[2,16,1536]{2,1,0:T(8,128)(2,1)S(1)}, bf16[2,16,1536]{2,1,0:T(8,128)(2,1)S(1)}, u32[]{:S(2)}, u32[]{:S(2)}) collective-permute-start(bf16[2,16,1536]{2,1,0:T(8,128)(2,1)S(1)} %pad_maximum_fusion.5), channel_id=1, source_target_pairs={{0,2},{1,3},{2,0},{3,1},{4,6},{5,7},{6,4},{7,5},{8,10},{9,11},{10,... | collective-permute-start | bytes 294920 | tf_op jit(solution)/shard_map/ppermute | solution.py:47
  46.3 1.1 %collective-permute-start.12 = (bf16[2,16,1792]{2,1,0:T(8,128)(2,1)S(1)}, bf16[2,16,1792]{2,1,0:T(8,128)(2,1)S(1)}, u32[]{:S(2)}, u32[]{:S(2)}) collective-permute-start(bf16[2,16,1792]{2,1,0:T(8,128)(2,1)S(1)} %pad_maximum_fusion.3), channel_id=1, source_target_pairs={{0,1},{1,0},{2,3},{3,2},{4,5},{5,4},{6,7},{7,6},{8,9},{9,8},{10,11... | collective-permute-start | bytes 344072 | tf_op jit(solution)/shard_map/ppermute | solution.py:47
  47.4 1.6 %collective-permute-start.16 = (bf16[2,16,1792]{2,1,0:T(8,128)(2,1)S(1)}, bf16[2,16,1792]{2,1,0:T(8,128)(2,1)S(1)}, u32[]{:S(2)}, u32[]{:S(2)}) collective-permute-start(bf16[2,16,1792]{2,1,0:T(8,128)(2,1)S(1)} %pad_maximum_fusion.4), channel_id=1, source_target_pairs={{0,16},{8,24},{16,0},{24,8},{1,17},{9,25},{17,1},{25,9},{2,18},{10... | collective-permute-start | bytes 344072 | tf_op jit(solution)/shard_map/ppermute | solution.py:47
  49.0 1.0 %collective-permute-done.20 = bf16[2,16,1536]{2,1,0:T(8,128)(2,1)S(1)} collective-permute-done((bf16[2,16,1536]{2,1,0:T(8,128)(2,1)S(1)}, bf16[2,16,1536]{2,1,0:T(8,128)(2,1)S(1)}, u32[]{:S(2)}, u32[]{:S(2)}) %collective-permute-start.20) | collective-permute-done | bytes 98336 | tf_op jit(solution)/shard_map/ppermute | solution.py:47
  51.2 1.6 %collective-permute-start.13 = (bf16[4,16,1792]{2,1,0:T(8,128)(2,1)S(1)}, bf16[4,16,1792]{2,1,0:T(8,128)(2,1)S(1)}, u32[]{:S(2)}, u32[]{:S(2)}) collective-permute-start(bf16[4,16,1792]{2,1,0:T(8,128)(2,1)S(1)} %pad_maximum_fusion), channel_id=1, source_target_pairs={{0,16},{8,24},{16,0},{24,8},{1,17},{9,25},{17,1},{25,9},{2,18},{10... | collective-permute-start | bytes 688136 | tf_op jit(solution)/shard_map/ppermute | solution.py:47
  52.8 2.0 %collective-permute-start.17 = (bf16[4,16,1792]{2,1,0:T(8,128)(2,1)S(1)}, bf16[4,16,1792]{2,1,0:T(8,128)(2,1)S(1)}, u32[]{:S(2)}, u32[]{:S(2)}) collective-permute-start(bf16[4,16,1792]{2,1,0:T(8,128)(2,1)S(1)} %pad_maximum_fusion.1), channel_id=1, source_target_pairs={{0,2},{1,3},{2,0},{3,1},{4,6},{5,7},{6,4},{7,5},{8,10},{9,11},{10,... | collective-permute-start | bytes 688136 | tf_op jit(solution)/shard_map/ppermute | solution.py:47
  54.8 2.5 %collective-permute-done.13 = bf16[4,16,1792]{2,1,0:T(8,128)(2,1)S(1)} collective-permute-done((bf16[4,16,1792]{2,1,0:T(8,128)(2,1)S(1)}, bf16[4,16,1792]{2,1,0:T(8,128)(2,1)S(1)}, u32[]{:S(2)}, u32[]{:S(2)}) %collective-permute-start.13) | collective-permute-done | bytes 229408 | tf_op jit(solution)/shard_map/ppermute | solution.py:47
  57.4 1.5 %collective-permute-done.17 = bf16[4,16,1792]{2,1,0:T(8,128)(2,1)S(1)} collective-permute-done((bf16[4,16,1792]{2,1,0:T(8,128)(2,1)S(1)}, bf16[4,16,1792]{2,1,0:T(8,128)(2,1)S(1)}, u32[]{:S(2)}, u32[]{:S(2)}) %collective-permute-start.17) | collective-permute-done | bytes 229408 | tf_op jit(solution)/shard_map/ppermute | solution.py:47
  59.6 3.8 %logits_first.1 = (f32[256,3072]{1,0:T(8,128)S(1)}, bf16[1536,3072]{1,0:T(8,128)(2,1)S(1)}) custom-call(bf16[8,16,1792]{2,1,0:T(8,128)(2,1)S(1)} %constant_dynamic-update-slice_fusion.left_ref, bf16[8,16,1792]{2,1,0:T(8,128)(2,1)S(1)} %collective-permute-done.14.right_ref, bf16[1792,3072]{1,0:T(8,128)(2,1)S(1)} %fetch.3.gate_ref.weight_ref, ...), custom_call_target="tpu_custom_call" | custom-call | flops 2818572288 | tf_op jit(solution)/shard_map/logits_first/pallas_call | solution.py:573
  63.4 8.7 %logits.1 = f32[32,1,128]{2,1,0:T(1,128)S(1)} custom-call(f32[256,3072]{1,0:T(8,128)S(1)} %get-tuple-element.53.sum_in_ref, bf16[8,16,1792]{2,1,0:T(8,128)(2,1)S(1)} %constant_dynamic-update-slice_fusion.4.left_ref, bf16[8,16,1792]{2,1,0:T(8,128)(2,1)S(1)} %collective-permute-done.18.right_ref, ...), custom_call_target="tpu_custom_call" | custom-call | flops 5234491392 | tf_op jit(solution)/shard_map/logits/pallas_call | solution.py:586
  72.1 11.2 %all_to_all.5.stats_ref = f32[32,1,128]{2,1,0:T(1,128)S(1)} all-to-all(f32[32,1,128]{2,1,0:T(1,128)S(1)} %logits.1), channel_id=1, replica_groups=mesh['group'=4,'tensor'=8] {'group','tensor'}, dimensions={0} | all-to-all | bytes 32768 | tf_op jit(solution)/shard_map/all_to_all | solution.py:607
  (52 shorter events, 4.3 us)
Async XLA Ops:
  0.0 5.4 %collective-permute-start = (bf16[64,512]{1,0:T(8,128)(2,1)}, bf16[64,512]{1,0:T(8,128)(2,1)S(1)}, u32[]{:S(2)}, u32[]{:S(2)}) collective-permute-start(bf16[64,512]{1,0:T(8,128)(2,1)} %refs_0_.1), channel_id=1, source_target_pairs={{0,16},{8,24},{16,0},{24,8},{1,17},{9,25},{17,1},{25,9},{2,18},{10... | collective-permute-start | bytes 196616 | tf_op jit(solution)/shard_map/ppermute | solution.py:47
  3.0 3.8 %collective-permute-start.2 = (bf16[64,512]{1,0:T(8,128)(2,1)}, bf16[64,512]{1,0:T(8,128)(2,1)S(1)}, u32[]{:S(2)}, u32[]{:S(2)}) collective-permute-start(bf16[64,512]{1,0:T(8,128)(2,1)} %refs_0_.1), channel_id=1, source_target_pairs={{0,8},{8,0},{16,24},{24,16},{1,9},{9,1},{17,25},{25,17},{2,10},{10... | collective-permute-start | bytes 196616 | tf_op jit(solution)/shard_map/ppermute | solution.py:47
  5.4 1.4 %collective-permute-start.1 = (bf16[64,512]{1,0:T(8,128)(2,1)S(1)}, bf16[64,512]{1,0:T(8,128)(2,1)S(1)}, u32[]{:S(2)}, u32[]{:S(2)}) collective-permute-start(bf16[64,512]{1,0:T(8,128)(2,1)S(1)} %pass.1.gate_ref.refs_1_), channel_id=1, source_target_pairs={{0,8},{8,0},{16,24},{24,16},{1,9},{9,1},{17,25},{25,17},{2,10},{10... | collective-permute-start | bytes 196616 | tf_op jit(solution)/shard_map/ppermute | solution.py:47
  7.7 5.9 %collective-permute-start.3 = (bf16[64,640]{1,0:T(8,128)(2,1)S(1)}, bf16[64,640]{1,0:T(8,128)(2,1)S(1)}, u32[]{:S(2)}, u32[]{:S(2)}) collective-permute-start(bf16[64,640]{1,0:T(8,128)(2,1)S(1)} %get-tuple-element.36.gate_ref), channel_id=1, source_target_pairs={{0,24},{8,16},{16,8},{24,0},{1,25},{9,17},{17,9},{25,1},{2,26},{10... | collective-permute-start | bytes 245768 | tf_op jit(solution)/shard_map/ppermute | solution.py:47
  9.9 4.8 %collective-permute-start.4 = (bf16[64,640]{1,0:T(8,128)(2,1)S(1)}, bf16[64,640]{1,0:T(8,128)(2,1)S(1)}, u32[]{:S(2)}, u32[]{:S(2)}) collective-permute-start(bf16[64,640]{1,0:T(8,128)(2,1)S(1)} %get-tuple-element.39), channel_id=1, source_target_pairs={{0,16},{8,24},{16,0},{24,8},{1,17},{9,25},{17,1},{25,9},{2,18},{10... | collective-permute-start | bytes 245768 | tf_op jit(solution)/shard_map/ppermute | solution.py:47
  9.9 4.7 %collective-permute-start.5 = (bf16[64,640]{1,0:T(8,128)(2,1)S(1)}, bf16[64,640]{1,0:T(8,128)(2,1)S(1)}, u32[]{:S(2)}, u32[]{:S(2)}) collective-permute-start(bf16[64,640]{1,0:T(8,128)(2,1)S(1)} %get-tuple-element.40), channel_id=1, source_target_pairs={{0,8},{8,0},{16,24},{24,16},{1,9},{9,1},{17,25},{25,17},{2,10},{10... | collective-permute-start | bytes 245768 | tf_op jit(solution)/shard_map/ppermute | solution.py:47
  17.9 6.1 %collective-permute-start.6 = (bf16[2,16,2560]{2,1,0:T(8,128)(2,1)S(1)}, bf16[2,16,2560]{2,1,0:T(8,128)(2,1)S(1)}, u32[]{:S(2)}, u32[]{:S(2)}) collective-permute-start(bf16[2,16,2560]{2,1,0:T(8,128)(2,1)S(1)} %get-tuple-element.43.gate_ref), channel_id=1, source_target_pairs={{0,1},{1,0},{2,3},{3,2},{4,5},{5,4},{6,7},{7,6},{8,9},{9,8},{10,11... | collective-permute-start | bytes 491528 | tf_op jit(solution)/shard_map/ppermute | solution.py:47
  19.6 6.0 %collective-permute-start.8 = (bf16[2,16,2560]{2,1,0:T(8,128)(2,1)S(1)}, bf16[2,16,2560]{2,1,0:T(8,128)(2,1)S(1)}, u32[]{:S(2)}, u32[]{:S(2)}) collective-permute-start(bf16[2,16,2560]{2,1,0:T(8,128)(2,1)S(1)} %get-tuple-element.47), channel_id=1, source_target_pairs={{0,2},{1,3},{2,0},{3,1},{4,6},{5,7},{6,4},{7,5},{8,10},{9,11},{10,... | collective-permute-start | bytes 491528 | tf_op jit(solution)/shard_map/ppermute | solution.py:47
  24.1 8.8 %copy-start.1 = (bf16[5120]{0:T(1024)(128)(2,1)S(1)}, bf16[5120]{0:T(1024)(128)(2,1)}, u32[]{:S(2)}) copy-start(bf16[5120]{0:T(1024)(128)(2,1)} %param.21) | copy-start | bytes 30724
  24.1 4.5 %collective-permute-start.7 = (bf16[16,2560]{1,0:T(8,128)(2,1)S(1)}, bf16[16,2560]{1,0:T(8,128)(2,1)S(1)}, u32[]{:S(2)}, u32[]{:S(2)}) collective-permute-start(bf16[16,2560]{1,0:T(8,128)(2,1)S(1)} %get-tuple-element.45), channel_id=1, source_target_pairs={{0,2},{1,3},{2,0},{3,1},{4,6},{5,7},{6,4},{7,5},{8,10},{9,11},{10,... | collective-permute-start | bytes 245768 | tf_op jit(solution)/shard_map/ppermute | solution.py:47
  25.6 4.5 %collective-permute-start.9 = (bf16[16,2560]{1,0:T(8,128)(2,1)S(1)}, bf16[16,2560]{1,0:T(8,128)(2,1)S(1)}, u32[]{:S(2)}, u32[]{:S(2)}) collective-permute-start(bf16[16,2560]{1,0:T(8,128)(2,1)S(1)} %get-tuple-element.49), channel_id=1, source_target_pairs={{0,1},{1,0},{2,3},{3,2},{4,5},{5,4},{6,7},{7,6},{8,9},{9,8},{10,11... | collective-permute-start | bytes 245768 | tf_op jit(solution)/shard_map/ppermute | solution.py:47
  30.2 8.1 %collective-permute-start.10 = (bf16[16,5120]{1,0:T(8,128)(2,1)S(1)}, bf16[16,5120]{1,0:T(8,128)(2,1)S(1)}, u32[]{:S(2)}, u32[]{:S(2)}) collective-permute-start(bf16[16,5120]{1,0:T(8,128)(2,1)S(1)} %get-tuple-element.50.gate_ref), channel_id=1, source_target_pairs={{0,4},{1,5},{2,6},{3,7},{4,0},{5,1},{6,2},{7,3},{8,12},{9,13},{10,... | collective-permute-start | bytes 491528 | tf_op jit(solution)/shard_map/ppermute | solution.py:47
  32.9 5.5 %copy-start = (bf16[64,5120]{1,0:T(8,128)(2,1)S(1)}, bf16[64,5120]{1,0:T(8,128)(2,1)}, u32[]{:S(2)}) copy-start(bf16[64,5120]{1,0:T(8,128)(2,1)} %param.19) | copy-start | bytes 1966084
  38.5 7.8 %collective-permute-start.11 = (bf16[1,16,1792]{2,1,0:T(8,128)(2,1)S(1)}, bf16[1,16,1792]{2,1,0:T(8,128)(2,1)S(1)}, u32[]{:S(2)}, u32[]{:S(2)}) collective-permute-start(bf16[1,16,1792]{2,1,0:T(8,128)(2,1)S(1)} %get-tuple-element.52), channel_id=1, source_target_pairs={{0,2},{1,3},{2,0},{3,1},{4,6},{5,7},{6,4},{7,5},{8,10},{9,11},{10,... | collective-permute-start | bytes 172040 | tf_op jit(solution)/shard_map/ppermute | solution.py:47
  38.8 8.6 %collective-permute-start.15 = (bf16[1,16,1792]{2,1,0:T(8,128)(2,1)S(1)}, bf16[1,16,1792]{2,1,0:T(8,128)(2,1)S(1)}, u32[]{:S(2)}, u32[]{:S(2)}) collective-permute-start(bf16[1,16,1792]{2,1,0:T(8,128)(2,1)S(1)} %get-tuple-element.54), channel_id=1, source_target_pairs={{0,1},{1,0},{2,3},{3,2},{4,5},{5,4},{6,7},{7,6},{8,9},{9,8},{10,11... | collective-permute-start | bytes 172040 | tf_op jit(solution)/shard_map/ppermute | solution.py:47
  40.0 4.6 %collective-permute-start.19 = (bf16[1,16,1536]{2,1,0:T(8,128)(2,1)S(1)}, bf16[1,16,1536]{2,1,0:T(8,128)(2,1)S(1)}, u32[]{:S(2)}, u32[]{:S(2)}) collective-permute-start(bf16[1,16,1536]{2,1,0:T(8,128)(2,1)S(1)} %get-tuple-element.55), channel_id=1, source_target_pairs={{0,16},{8,24},{16,0},{24,8},{1,17},{9,25},{17,1},{25,9},{2,18},{10... | collective-permute-start | bytes 147464 | tf_op jit(solution)/shard_map/ppermute | solution.py:47
  44.7 5.4 %collective-permute-start.20 = (bf16[2,16,1536]{2,1,0:T(8,128)(2,1)S(1)}, bf16[2,16,1536]{2,1,0:T(8,128)(2,1)S(1)}, u32[]{:S(2)}, u32[]{:S(2)}) collective-permute-start(bf16[2,16,1536]{2,1,0:T(8,128)(2,1)S(1)} %pad_maximum_fusion.5), channel_id=1, source_target_pairs={{0,2},{1,3},{2,0},{3,1},{4,6},{5,7},{6,4},{7,5},{8,10},{9,11},{10,... | collective-permute-start | bytes 294920 | tf_op jit(solution)/shard_map/ppermute | solution.py:47
  46.3 4.9 %collective-permute-start.12 = (bf16[2,16,1792]{2,1,0:T(8,128)(2,1)S(1)}, bf16[2,16,1792]{2,1,0:T(8,128)(2,1)S(1)}, u32[]{:S(2)}, u32[]{:S(2)}) collective-permute-start(bf16[2,16,1792]{2,1,0:T(8,128)(2,1)S(1)} %pad_maximum_fusion.3), channel_id=1, source_target_pairs={{0,1},{1,0},{2,3},{3,2},{4,5},{5,4},{6,7},{7,6},{8,9},{9,8},{10,11... | collective-permute-start | bytes 344072 | tf_op jit(solution)/shard_map/ppermute | solution.py:47
  47.4 5.4 %collective-permute-start.16 = (bf16[2,16,1792]{2,1,0:T(8,128)(2,1)S(1)}, bf16[2,16,1792]{2,1,0:T(8,128)(2,1)S(1)}, u32[]{:S(2)}, u32[]{:S(2)}) collective-permute-start(bf16[2,16,1792]{2,1,0:T(8,128)(2,1)S(1)} %pad_maximum_fusion.4), channel_id=1, source_target_pairs={{0,16},{8,24},{16,0},{24,8},{1,17},{9,25},{17,1},{25,9},{2,18},{10... | collective-permute-start | bytes 344072 | tf_op jit(solution)/shard_map/ppermute | solution.py:47
  50.1 8.9 %collective-permute-start.21 = (bf16[4,16,1536]{2,1,0:T(8,128)(2,1)S(1)}, bf16[4,16,1536]{2,1,0:T(8,128)(2,1)S(1)}, u32[]{:S(2)}, u32[]{:S(2)}) collective-permute-start(bf16[4,16,1536]{2,1,0:T(8,128)(2,1)S(1)} %pad_maximum_fusion.2), channel_id=1, source_target_pairs={{0,1},{1,0},{2,3},{3,2},{4,5},{5,4},{6,7},{7,6},{8,9},{9,8},{10,11... | collective-permute-start | bytes 589832 | tf_op jit(solution)/shard_map/ppermute | solution.py:47
  51.2 6.1 %collective-permute-start.13 = (bf16[4,16,1792]{2,1,0:T(8,128)(2,1)S(1)}, bf16[4,16,1792]{2,1,0:T(8,128)(2,1)S(1)}, u32[]{:S(2)}, u32[]{:S(2)}) collective-permute-start(bf16[4,16,1792]{2,1,0:T(8,128)(2,1)S(1)} %pad_maximum_fusion), channel_id=1, source_target_pairs={{0,16},{8,24},{16,0},{24,8},{1,17},{9,25},{17,1},{25,9},{2,18},{10... | collective-permute-start | bytes 688136 | tf_op jit(solution)/shard_map/ppermute | solution.py:47
  52.8 6.1 %collective-permute-start.17 = (bf16[4,16,1792]{2,1,0:T(8,128)(2,1)S(1)}, bf16[4,16,1792]{2,1,0:T(8,128)(2,1)S(1)}, u32[]{:S(2)}, u32[]{:S(2)}) collective-permute-start(bf16[4,16,1792]{2,1,0:T(8,128)(2,1)S(1)} %pad_maximum_fusion.1), channel_id=1, source_target_pairs={{0,2},{1,3},{2,0},{3,1},{4,6},{5,7},{6,4},{7,5},{8,10},{9,11},{10,... | collective-permute-start | bytes 688136 | tf_op jit(solution)/shard_map/ppermute | solution.py:47
  57.3 2.3 %collective-permute-start.14 = (bf16[8,16,1792]{2,1,0:T(8,128)(2,1)S(1)}, bf16[8,16,1792]{2,1,0:T(8,128)(2,1)S(1)}, u32[]{:S(2)}, u32[]{:S(2)}) collective-permute-start(bf16[8,16,1792]{2,1,0:T(8,128)(2,1)S(1)} %constant_dynamic-update-slice_fusion.left_ref), channel_id=1, source_target_pairs={{0,8},{8,0},{16,24},{24,16},{1,9},{9,1},{17,25},{25,17},{2,10},{10... | collective-permute-start | bytes 1376264 | tf_op jit(solution)/shard_map/ppermute | solution.py:47
  58.9 4.5 %collective-permute-start.18 = (bf16[8,16,1792]{2,1,0:T(8,128)(2,1)S(1)}, bf16[8,16,1792]{2,1,0:T(8,128)(2,1)S(1)}, u32[]{:S(2)}, u32[]{:S(2)}) collective-permute-start(bf16[8,16,1792]{2,1,0:T(8,128)(2,1)S(1)} %constant_dynamic-update-slice_fusion.4.left_ref), channel_id=1, source_target_pairs={{0,8},{8,0},{16,24},{24,16},{1,9},{9,1},{17,25},{25,17},{2,10},{10... | collective-permute-start | bytes 1376264 | tf_op jit(solution)/shard_map/ppermute | solution.py:47
  59.1 4.4 %collective-permute-start.22 = (bf16[8,16,1536]{2,1,0:T(8,128)(2,1)S(1)}, bf16[8,16,1536]{2,1,0:T(8,128)(2,1)S(1)}, u32[]{:S(2)}, u32[]{:S(2)}) collective-permute-start(bf16[8,16,1536]{2,1,0:T(8,128)(2,1)S(1)} %constant_dynamic-update-slice_fusion.8.next_left_ref), channel_id=1, source_target_pairs={{0,8},{8,0},{16,24},{24,16},{1,9},{9,1},{17,25},{25,17},{2,10},{10... | collective-permute-start | bytes 1179656 | tf_op jit(solution)/shard_map/ppermute | solution.py:47

commit v11 on v9

--- a/solution.py
+++ b/solution.py
@@ -106,6 +106,19 @@
     return [
         pltpu.make_async_copy(
             source_ref.at[pl.ds(start + i * rows, rows)], out_ref.at[pl.ds(i * rows, rows)], sems.at[i]
+        )
+        for i in range(count)
+    ]
+
+
+def column_copies(source_ref, start, out_ref, sems):
+    count = sems.shape[0]
+    width = out_ref.shape[1] // count
+    return [
+        pltpu.make_async_copy(
+            source_ref.at[:, pl.ds(start + i * width, width)],
+            out_ref.at[:, pl.ds(i * width, width)],
+            sems.at[i],
         )
         for i in range(count)
     ]
@@ -129,7 +142,7 @@
     weight_ref,
     sems,
 ):
-    copies = carried(source_ref, 0, weight_ref, sems)
+    copies = column_copies(source_ref, 0, weight_ref, sems)
     for copy in copies:
         copy.start()
     rows = q_ref.shape[0]
@@ -191,8 +204,11 @@
 
 def project_kernel(heads, seq, wide, group_size, key_rows, prompt_ref, own_ref, *refs):
     got_refs, refs = refs[: group_size - 1], refs[group_size - 1 :]
-    weight_ref, send_left_ref, keep_left_ref, send_right_ref, keep_right_ref = refs[:5]
-    attended_ref, partial_ref = refs[5:]
+    weight_ref, source_ref, send_left_ref, keep_left_ref, send_right_ref, keep_right_ref = refs[:6]
+    attended_ref, partial_ref, near_ref, sems = refs[6:]
+    copies = column_copies(source_ref, near_ref.shape[1], near_ref, sems)
+    for copy in copies:
+        copy.start()
     rows = own_ref.shape[0]
     wanted = wanted_prompts(seq, rows, prompt_ref)
     group = lax.axis_index("group")
@@ -221,29 +237,33 @@
     block = rows // 4
     half = send_left_ref.shape[2]
 
-    def multiply(columns):
-        partial = jnp.dot(attended_ref[...], weight_ref[:, columns], preferred_element_type=F32)
+    def multiply(ref, columns):
+        partial = jnp.dot(attended_ref[...], ref[:, columns], preferred_element_type=F32)
         for b in range(4):
             partial_ref[b] = partial[b * block : (b + 1) * block]
 
     @pl.loop(0, half // wide)
     def _(n):
         columns = pl.ds(pl.multiple_of(n * wide, 128), wide)
-        multiply(columns)
+        multiply(weight_ref, columns)
         for i in range(2):
             keep_left_ref[i, :, columns] = partial_ref[me ^ (2 * i)]
             send_left_ref[i, :, columns] = partial_ref[me ^ (2 * i + 1)].astype(BF16)
 
+    for copy in copies:
+        copy.wait()
+
     @pl.loop(0, half // wide)
     def _(n):
         columns = pl.ds(pl.multiple_of(n * wide, 128), wide)
-        multiply(pl.ds(pl.multiple_of(half + n * wide, 128), wide))
+        multiply(near_ref, columns)
         for i in range(2):
             keep_right_ref[i, :, columns] = partial_ref[me ^ i]
             send_right_ref[i, :, columns] = partial_ref[me ^ (i + 2)].astype(BF16)
 
 
-def fold_kernel(keep_ref, got_ref, own_ref, send_ref):
+def fold_kernel(keep_ref, got_ref, *refs):
+    own_ref, send_ref = refs[-2:]
     own_ref[...] = keep_ref[0] + got_ref[0].astype(F32)
     send_ref[...] = (keep_ref[1] + got_ref[1].astype(F32)).astype(BF16)
 
@@ -278,7 +298,7 @@
             out_ref[i] = ref[:, half * width : (half + 1) * width]
 
 
-def norm_kernel(residual_ref, gain_ref, first_gate_ref, second_gate_ref, own_ref, got_ref, out_ref):
+def norm_kernel(residual_ref, gain_ref, gate_ref, own_ref, got_ref, out_ref):
     hidden = residual_ref[lax.axis_index("tensor") % 4].astype(F32)
     hidden = hidden + (own_ref[...] + got_ref[...].astype(F32))
     squares = jnp.mean(hidden * hidden, axis=-1, keepdims=True)
@@ -294,14 +314,13 @@
 
 
 def quarter_dots(x_ref, weight_refs, columns):
-    depth = weight_refs[0].shape[0]
-    return functools.reduce(
-        jnp.add,
-        [
-            jnp.dot(x_ref[:, i * depth : (i + 1) * depth], ref[:, columns], preferred_element_type=F32)
-            for i, ref in enumerate(weight_refs)
-        ],
-    )
+    start, total = 0, None
+    for ref in weight_refs:
+        stop = start + ref.shape[0]
+        part = jnp.dot(x_ref[:, start:stop], ref[:, columns], preferred_element_type=F32)
+        total = part if total is None else total + part
+        start = stop
+    return total
 
 
 def first_kernel(
@@ -433,18 +452,6 @@
     distances = list(range(group_size - 1, 0, -1))
     far_queries = [swap(resp_query, "group", a, group_size) for a in above]
     queries = {1: swap(resp_query, "group", 1, group_size)}
-    far_queries = pl.pallas_call(
-        functools.partial(pass_kernel, len(above)),
-        out_shape=[jax.ShapeDtypeStruct(x.shape, x.dtype) for x in far_queries],
-        in_specs=[vmem()] * len(above) + [anywhere()],
-        out_specs=[vmem()] * len(above),
-        compiler_params=params(1),
-        name="pass",
-    )(*map(held, far_queries), wanted)
-    for a, x in zip(above, far_queries):
-        queries[a] = x
-        queries[a + 1] = swap(x, "group", 1, group_size)
-    queries = [queries[d] for d in distances]
     inputs = (resp_query, resp_key, resp_value, prompt_keys, prompt_values)
     loaded = pl.pallas_call(
         functools.partial(load_kernel, len(inputs)),
@@ -455,8 +462,20 @@
         compiler_params=params(1),
         cost_estimate=cost(moved=2 * MIB),
         name="load",
-    )(far_queries[0], *map(stored, inputs))
+    )(wanted, *map(stored, inputs))
     query, own_keys, own_values, keys, values = map(held, loaded)
+    far_queries = pl.pallas_call(
+        functools.partial(pass_kernel, len(above)),
+        out_shape=[jax.ShapeDtypeStruct(x.shape, x.dtype) for x in far_queries],
+        in_specs=[vmem()] * len(above) + [anywhere()],
+        out_specs=[vmem()] * len(above),
+        compiler_params=params(1),
+        name="pass",
+    )(*map(held, far_queries), loaded[0])
+    for a, x in zip(above, far_queries):
+        queries[a] = x
+        queries[a + 1] = swap(x, "group", 1, group_size)
+    queries = [queries[d] for d in distances]
     answers = pl.pallas_call(
         functools.partial(prefix_kernel, heads, len(distances)),
         out_shape=[jax.ShapeDtypeStruct((rows, span + 128), BF16)] * len(distances),
@@ -471,11 +490,11 @@
         out_shape=[
             jax.ShapeDtypeStruct((rows, span + 128), F32),
             jax.ShapeDtypeStruct((8, 128), F32),
-            pltpu.VMEM(out_weight.shape, BF16),
+            pltpu.VMEM((span, depth // 2), BF16),
         ],
         in_specs=[smem()] * 2 + [vmem()] * 5 + [anywhere()] * 2,
         out_specs=[vmem()] * 3,
-        scratch_shapes=[pltpu.SemaphoreType.DMA((4,))],
+        scratch_shapes=[pltpu.SemaphoreType.DMA((2,))],
         compiler_params=params(6),
         cost_estimate=cost(moved=8 * MIB),
         name="own_attention",
@@ -516,35 +535,39 @@
             jax.ShapeDtypeStruct((2, block, half), F32),
         ]
         * 2,
-        in_specs=[smem()] + [vmem()] * (2 + len(distances)),
+        in_specs=[smem()] + [vmem()] * (2 + len(distances)) + [anywhere()],
         out_specs=[vmem()] * 4,
         scratch_shapes=[
             pltpu.VMEM((rows, span), BF16),
             pltpu.VMEM((4, block, wide), F32),
+            pltpu.VMEM((span, half), BF16),
+            pltpu.SemaphoreType.DMA((2,)),
         ],
-        compiler_params=params(6),
+        compiler_params=params(8),
         name="project",
-    )(stored(prompt_of), *map(held, (own, *got)), held(weight))
-
-    def add(kernel, name, size, *operands):
+    )(stored(prompt_of), *map(held, (own, *got)), held(weight), stored(out_weight))
+
+    def add(kernel, name, size, *operands, gates=()):
         return pl.pallas_call(
             kernel,
             out_shape=[jax.ShapeDtypeStruct(size, F32), jax.ShapeDtypeStruct(size, BF16)],
-            in_specs=[vmem()] * len(operands),
+            in_specs=[vmem()] * len(operands) + [anywhere()] * len(gates),
             out_specs=[vmem()] * 2,
             compiler_params=params(2),
             name=name,
-        )(*map(held, operands))
+        )(*map(held, operands), *gates)
+
+    early_rows = 1024 if half > 1024 else half // 2
+    first_quarter = fetch(lm_weight, 0, early_rows, send_left)
 
     got_left = swap(send_left, "tensor", 1, tensor_size)
     got_right = swap(send_right, "tensor", 2, tensor_size)
-    left, send_left = add(fold_kernel, "fold_left", (block, half), keep_left, got_left)
+    left, send_left = add(fold_kernel, "fold_left", (block, half), keep_left, got_left, gates=(first_quarter,))
     right, send_right = add(fold_kernel, "fold_right", (block, half), keep_right, got_right)
     got_left = swap(send_left, "tensor", 2, tensor_size)
     got_right = swap(send_right, "tensor", 1, tensor_size)
     total, send = add(side_kernel, "side", (block, depth), left, got_left, right, got_right)
-    first_quarter = fetch(lm_weight, 0, quarter, send)
-    second_quarter = fetch(lm_weight, quarter, quarter, send)
+    second_quarter = fetch(lm_weight, early_rows, half - early_rows, send)
     far = 4
     while 2 * far < tensor_size:
         total, send = add(
@@ -554,13 +577,12 @@
     normed = pl.pallas_call(
         norm_kernel,
         out_shape=jax.ShapeDtypeStruct((block, depth), BF16),
-        in_specs=[vmem()] * 2 + [anywhere()] * 2 + [vmem()] * 2,
+        in_specs=[vmem()] * 2 + [anywhere()] + [vmem()] * 2,
         out_specs=vmem(),
         compiler_params=params(4),
         name="norm",
     )(
         *map(held, (residual.reshape(4, block, depth), norm_gain[None])),
-        first_quarter,
         second_quarter,
         *map(held, (total, swap(send, "tensor", far, tensor_size))),
     )
@@ -590,15 +612,15 @@
 
     left, right = columns
     got_left = swap(left, "tensor", 1, tensor_size)
+    right = [right] + [swap(right, "group", d, group_size) for d in above]
+    left = jnp.concatenate([left, got_left])
+    got_left = [swap(left, "group", d, group_size) for d in above]
     third = fetch(lm_weight, 2 * quarter, quarter, left)
-    right = [right] + [swap(right, "group", d, group_size) for d in above]
-    left = join([left, got_left], third)
-    got_left = [swap(left, "group", d, group_size) for d in above]
     across = swap(jnp.concatenate(right), "tensor", 1, tensor_size)
     across = jnp.split(across, len(right))
     right = [x for pair in zip(right, across) for x in pair]
     halves = []
-    for tokens in (jnp.concatenate([left] + got_left), jnp.concatenate(right)):
+    for tokens in (join([left] + got_left, third), jnp.concatenate(right)):
         tokens = tokens.reshape(-1, half)
         halves.append((tokens, swap(tokens, "group", 1, group_size)))
     spots = [(g + c, t + x) for c in (0, 1) for g, x in here for t in order]

time: 81.9 us -> 83 us (1.013)
  blocking collectives: 10.2 us -> 11.7 us
    all_to_all x1, blocking collectives: 10.2 us -> 11.7 us  [local(): stats = lax.all_to_all(stats, ('group', 'tensor'), 0, 0, tiled=True)]
  transfers between devices with their start and end apart: 18 -> 18, of which waited for: 9 -> 10; matrix products, arithmetic and copies ran while one was open for 1% -> 1% of each run, Pallas kernels for 24% -> 23%
where the time goes in v11:
time: 83 us; the launch traced here: 82.7 us
  Pallas kernels  29.6 us (36%)
  starting transfers between devices  21.2 us (26%)
  waiting for transfers between devices  18.9 us (23%)
  blocking collectives  11.7 us (14%)
  local copies, waits for them, and re-layouts  0.95 us (1%)
    ppermute x18, starting transfers between devices, swap(): return lax.ppermute(x, axis, [(i, i ^ distance) for i in range(size)])  21.2 us
    ppermute x18, waiting for transfers between devices, swap(): return lax.ppermute(x, axis, [(i, i ^ distance) for i in range(size)])  18.9 us
    all_to_all x1, blocking collectives, local(): stats = lax.all_to_all(stats, ('group', 'tensor'), 0, 0, tiled=True)  11.7 us
    pallas_call x3, Pallas kernels, fetch(): pl.pallas_call(functools.partial(fetch_kernel, start), out_shape=pltpu.VM...  10.1 us
    pallas_call x1, Pallas kernels, local(): pl.pallas_call(functools.partial(logits_kernel, vocab, spots, tensor_size...  5 us
    pallas_call x1, Pallas kernels, local(): pl.pallas_call(functools.partial(first_kernel, narrow), out_shape=[pltpu....  4.53 us
    pallas_call x1, Pallas kernels, local(): pl.pallas_call(functools.partial(project_kernel, heads, seq, wide, group_...  3.98 us
    pallas_call x1, Pallas kernels, local(): pl.pallas_call(functools.partial(own_kernel, heads, seq, share), out_shap...  2.86 us
  transfers between devices with their start and end apart: 18, of which 10 were waited for; matrix products, arithmetic and copies ran while one was open for 1% of the time, Pallas kernels for 23%

profile of v11, /device:TPU:0, one launch (start us, length us, event | category | flops | bytes accessed | tf_op | source)
XLA Modules:
  0.0 82.7 jit_solution(18000248882389222848)
XLA Ops:
  0.0 3.0 %collective-permute-start = (bf16[64,512]{1,0:T(8,128)(2,1)}, bf16[64,512]{1,0:T(8,128)(2,1)S(1)}, u32[]{:S(2)}, u32[]{:S(2)}) collective-permute-start(bf16[64,512]{1,0:T(8,128)(2,1)} %refs_0_.1), channel_id=1, source_target_pairs={{0,16},{8,24},{16,0},{24,8},{1,17},{9,25},{17,1},{25,9},{2,18},{10... | collective-permute-start | bytes 196616 | tf_op jit(solution)/shard_map/ppermute | solution.py:47
  3.0 0.9 %reshape.16.gate_ref.target_ref = s32[32,8,1]{2,1,0:T(8,128)S(1)} reshape(s32[256]{0:T(256)} %param.23) | data formatting | bytes 2048 | tf_op jit(solution)/shard_map/reshape | solution.py:450
  3.9 1.4 %load.1 = (bf16[64,512]{1,0:T(8,128)(2,1)S(1)}, bf16[64,512]{1,0:T(8,128)(2,1)S(1)}, bf16[64,512]{1,0:T(8,128)(2,1)S(1)}, bf16[512,512]{1,0:T(8,128)(2,1)S(1)}, bf16[512,512]{1,0:T(8,128)(2,1)S(1)}) custom-call(s32[32,8,1]{2,1,0:T(8,128)S(1)} %reshape.16.gate_ref.target_ref, bf16[64,512]{1,0:T(8,128)(2,1)} %refs_0_.1, bf16[64,512]{1,0:T(8,128)(2,1)} %refs_1_.1, ...), custom_call_target="tpu_custom_call" | custom-call | bytes 2097152 | tf_op jit(solution)/shard_map/load/pallas_call | solution.py:456
  5.8 0.9 %collective-permute-done.1.refs_0_ = bf16[64,512]{1,0:T(8,128)(2,1)S(1)} collective-permute-done((bf16[64,512]{1,0:T(8,128)(2,1)S(1)}, bf16[64,512]{1,0:T(8,128)(2,1)S(1)}, u32[]{:S(2)}, u32[]{:S(2)}) %collective-permute-start.1) | collective-permute-done | bytes 65568 | tf_op jit(solution)/shard_map/ppermute | solution.py:47
  6.7 0.9 %prefix_attention.1 = (bf16[64,640]{1,0:T(8,128)(2,1)S(1)}, bf16[64,640]{1,0:T(8,128)(2,1)S(1)}, bf16[64,640]{1,0:T(8,128)(2,1)S(1)}) custom-call(bf16[64,512]{1,0:T(8,128)(2,1)S(1)} %collective-permute-done.1.refs_0_, bf16[64,512]{1,0:T(8,128)(2,1)S(1)} %pass.1.refs_1_, bf16[64,512]{1,0:T(8,128)(2,1)S(1)} %collective-permute-done.2.refs_2_, ...), custom_call_target="tpu_custom_call" | custom-call | tf_op jit(solution)/shard_map/prefix_attention/pallas_call | solution.py:479
  7.6 1.8 %collective-permute-start.3 = (bf16[64,640]{1,0:T(8,128)(2,1)S(1)}, bf16[64,640]{1,0:T(8,128)(2,1)S(1)}, u32[]{:S(2)}, u32[]{:S(2)}) collective-permute-start(bf16[64,640]{1,0:T(8,128)(2,1)S(1)} %get-tuple-element.35.gate_ref), channel_id=1, source_target_pairs={{0,24},{8,16},{16,8},{24,0},{1,25},{9,17},{17,9},{25,1},{2,26},{10... | collective-permute-start | bytes 245768 | tf_op jit(solution)/shard_map/ppermute | solution.py:47
  9.7 2.9 %own_attention.1 = (f32[64,640]{1,0:T(8,128)S(1)}, f32[8,128]{1,0:T(8,128)S(1)}, bf16[512,2560]{1,0:T(8,128)(2,1)S(1)}) custom-call(s32[2]{0:T(128)} %lengths_ref.1, s32[2]{0:T(128)} %prompt_ref.3, bf16[64,512]{1,0:T(8,128)(2,1)S(1)} %get-tuple-element.30.refs_1_.q_ref, bf16[64,512]{1,0:T(8,128)(2,1)S(1)} %get-tuple-element.31.rk_ref, ...), custom_call_target="tpu_custom_call" | custom-call | bytes 8388608 | tf_op jit(solution)/shard_map/own_attention/pallas_call | solution.py:488
  12.6 1.5 %collective-permute-done.4.refs_1_ = bf16[64,640]{1,0:T(8,128)(2,1)S(1)} collective-permute-done((bf16[64,640]{1,0:T(8,128)(2,1)S(1)}, bf16[64,640]{1,0:T(8,128)(2,1)S(1)}, u32[]{:S(2)}, u32[]{:S(2)}) %collective-permute-start.4) | collective-permute-done | bytes 81952 | tf_op jit(solution)/shard_map/ppermute | solution.py:47
  14.2 4.0 %project.1 = (bf16[2,16,2560]{2,1,0:T(8,128)(2,1)S(1)}, f32[2,16,2560]{2,1,0:T(8,128)S(1)}, bf16[2,16,2560]{2,1,0:T(8,128)(2,1)S(1)}, f32[2,16,2560]{2,1,0:T(8,128)S(1)}) custom-call(s32[2]{0:T(128)} %prompt_ref.3, f32[64,640]{1,0:T(8,128)S(1)} %get-tuple-element.37.own_ref, bf16[64,640]{1,0:T(8,128)(2,1)S(1)} %collective-permute-done.3.refs_0_, ...), custom_call_target="tpu_custom_call" | custom-call | tf_op jit(solution)/shard_map/project/pallas_call | solution.py:531
  18.1 2.0 %collective-permute-start.6 = (bf16[2,16,2560]{2,1,0:T(8,128)(2,1)S(1)}, bf16[2,16,2560]{2,1,0:T(8,128)(2,1)S(1)}, u32[]{:S(2)}, u32[]{:S(2)}) collective-permute-start(bf16[2,16,2560]{2,1,0:T(8,128)(2,1)S(1)} %get-tuple-element.42.gate_ref), channel_id=1, source_target_pairs={{0,1},{1,0},{2,3},{3,2},{4,5},{5,4},{6,7},{7,6},{8,9},{9,8},{10,11... | collective-permute-start | bytes 491528 | tf_op jit(solution)/shard_map/ppermute | solution.py:47
  20.2 1.6 %collective-permute-start.8 = (bf16[2,16,2560]{2,1,0:T(8,128)(2,1)S(1)}, bf16[2,16,2560]{2,1,0:T(8,128)(2,1)S(1)}, u32[]{:S(2)}, u32[]{:S(2)}) collective-permute-start(bf16[2,16,2560]{2,1,0:T(8,128)(2,1)S(1)} %get-tuple-element.46), channel_id=1, source_target_pairs={{0,2},{1,3},{2,0},{3,1},{4,6},{5,7},{6,4},{7,5},{8,10},{9,11},{10,... | collective-permute-start | bytes 491528 | tf_op jit(solution)/shard_map/ppermute | solution.py:47
  21.7 2.9 %fetch.3.refs_0_.weight_ref = bf16[1024,3072]{1,0:T(8,128)(2,1)S(1)} custom-call(bf16[5120,3072]{1,0:T(8,128)(2,1)} %source_ref.9, bf16[2,16,2560]{2,1,0:T(8,128)(2,1)S(1)} %get-tuple-element.42.gate_ref), custom_call_target="tpu_custom_call" | custom-call | bytes 6291456 | tf_op jit(solution)/shard_map/fetch/pallas_call | solution.py:515
  24.7 1.6 %collective-permute-start.7 = (bf16[16,2560]{1,0:T(8,128)(2,1)S(1)}, bf16[16,2560]{1,0:T(8,128)(2,1)S(1)}, u32[]{:S(2)}, u32[]{:S(2)}) collective-permute-start(bf16[16,2560]{1,0:T(8,128)(2,1)S(1)} %get-tuple-element.44), channel_id=1, source_target_pairs={{0,2},{1,3},{2,0},{3,1},{4,6},{5,7},{6,4},{7,5},{8,10},{9,11},{10,... | collective-permute-start | bytes 245768 | tf_op jit(solution)/shard_map/ppermute | solution.py:47
  26.3 1.6 %collective-permute-start.9 = (bf16[16,2560]{1,0:T(8,128)(2,1)S(1)}, bf16[16,2560]{1,0:T(8,128)(2,1)S(1)}, u32[]{:S(2)}, u32[]{:S(2)}) collective-permute-start(bf16[16,2560]{1,0:T(8,128)(2,1)S(1)} %get-tuple-element.48), channel_id=1, source_target_pairs={{0,1},{1,0},{2,3},{3,2},{4,5},{5,4},{6,7},{7,6},{8,9},{9,8},{10,11... | collective-permute-start | bytes 245768 | tf_op jit(solution)/shard_map/ppermute | solution.py:47
  27.8 1.3 %collective-permute-done.7.got_left_ref = bf16[16,2560]{1,0:T(8,128)(2,1)S(1)} collective-permute-done((bf16[16,2560]{1,0:T(8,128)(2,1)S(1)}, bf16[16,2560]{1,0:T(8,128)(2,1)S(1)}, u32[]{:S(2)}, u32[]{:S(2)}) %collective-permute-start.7) | collective-permute-done | bytes 81952 | tf_op jit(solution)/shard_map/ppermute | solution.py:47
  29.2 1.6 %collective-permute-done.9.got_right_ref = bf16[16,2560]{1,0:T(8,128)(2,1)S(1)} collective-permute-done((bf16[16,2560]{1,0:T(8,128)(2,1)S(1)}, bf16[16,2560]{1,0:T(8,128)(2,1)S(1)}, u32[]{:S(2)}, u32[]{:S(2)}) %collective-permute-start.9) | collective-permute-done | bytes 81952 | tf_op jit(solution)/shard_map/ppermute | solution.py:47
  30.8 2.7 %collective-permute-start.10 = (bf16[16,5120]{1,0:T(8,128)(2,1)S(1)}, bf16[16,5120]{1,0:T(8,128)(2,1)S(1)}, u32[]{:S(2)}, u32[]{:S(2)}) collective-permute-start(bf16[16,5120]{1,0:T(8,128)(2,1)S(1)} %get-tuple-element.49.gate_ref), channel_id=1, source_target_pairs={{0,4},{1,5},{2,6},{3,7},{4,0},{5,1},{6,2},{7,3},{8,12},{9,13},{10,... | collective-permute-start | bytes 491528 | tf_op jit(solution)/shard_map/ppermute | solution.py:47
  33.5 3.9 %fetch.4.gate_ref.next_ref = bf16[1536,3072]{1,0:T(8,128)(2,1)S(1)} custom-call(bf16[5120,3072]{1,0:T(8,128)(2,1)} %source_ref.9, bf16[16,5120]{1,0:T(8,128)(2,1)S(1)} %get-tuple-element.49.gate_ref), custom_call_target="tpu_custom_call" | custom-call | bytes 9437184 | tf_op jit(solution)/shard_map/fetch/pallas_call | solution.py:515
  37.4 1.8 %collective-permute-done.10.got_ref = bf16[16,5120]{1,0:T(8,128)(2,1)S(1)} collective-permute-done((bf16[16,5120]{1,0:T(8,128)(2,1)S(1)}, bf16[16,5120]{1,0:T(8,128)(2,1)S(1)}, u32[]{:S(2)}, u32[]{:S(2)}) %collective-permute-start.10) | collective-permute-done | bytes 163872 | tf_op jit(solution)/shard_map/ppermute | solution.py:47
  39.5 5.3 %collective-permute-done.11.refs_1_ = bf16[16,5120]{1,0:T(8,128)(2,1)S(1)} collective-permute-done((bf16[16,5120]{1,0:T(8,128)(2,1)S(1)}, bf16[16,5120]{1,0:T(8,128)(2,1)S(1)}, u32[]{:S(2)}, u32[]{:S(2)}) %collective-permute-start.11) | collective-permute-done | bytes 163872 | tf_op jit(solution)/shard_map/ppermute | solution.py:47
  44.8 1.2 %collective-permute-start.12 = (bf16[2,16,2560]{2,1,0:T(8,128)(2,1)S(1)}, bf16[2,16,2560]{2,1,0:T(8,128)(2,1)S(1)}, u32[]{:S(2)}, u32[]{:S(2)}) collective-permute-start(bf16[2,16,2560]{2,1,0:T(8,128)(2,1)S(1)} %get-tuple-element.51), channel_id=1, source_target_pairs={{0,1},{1,0},{2,3},{3,2},{4,5},{5,4},{6,7},{7,6},{8,9},{9,8},{10,11... | collective-permute-start | bytes 491528 | tf_op jit(solution)/shard_map/ppermute | solution.py:47
  46.0 1.6 %collective-permute-start.15 = (bf16[2,16,2560]{2,1,0:T(8,128)(2,1)S(1)}, bf16[2,16,2560]{2,1,0:T(8,128)(2,1)S(1)}, u32[]{:S(2)}, u32[]{:S(2)}) collective-permute-start(bf16[2,16,2560]{2,1,0:T(8,128)(2,1)S(1)} %get-tuple-element.53), channel_id=1, source_target_pairs={{0,16},{8,24},{16,0},{24,8},{1,17},{9,25},{17,1},{25,9},{2,18},{10... | collective-permute-start | bytes 491528 | tf_op jit(solution)/shard_map/ppermute | solution.py:47
  47.6 3.8 %collective-permute-done.12 = bf16[2,16,2560]{2,1,0:T(8,128)(2,1)S(1)} collective-permute-done((bf16[2,16,2560]{2,1,0:T(8,128)(2,1)S(1)}, bf16[2,16,2560]{2,1,0:T(8,128)(2,1)S(1)}, u32[]{:S(2)}, u32[]{:S(2)}) %collective-permute-start.12) | collective-permute-done | bytes 163872 | tf_op jit(solution)/shard_map/ppermute | solution.py:47
  51.4 2.0 %collective-permute-start.13 = (bf16[4,16,2560]{2,1,0:T(8,128)(2,1)S(1)}, bf16[4,16,2560]{2,1,0:T(8,128)(2,1)S(1)}, u32[]{:S(2)}, u32[]{:S(2)}) collective-permute-start(bf16[4,16,2560]{2,1,0:T(8,128)(2,1)S(1)} %constant_dynamic-update-slice_fusion.gate_ref.refs_0_), channel_id=1, source_target_pairs={{0,16},{8,24},{16,0},{24,8},{1,17},{9,25},{17,1},{25,9},{2,18},{10... | collective-permute-start | bytes 983048 | tf_op jit(solution)/shard_map/ppermute | solution.py:47
  53.5 1.3 %collective-permute-start.16 = (bf16[4,16,2560]{2,1,0:T(8,128)(2,1)S(1)}, bf16[4,16,2560]{2,1,0:T(8,128)(2,1)S(1)}, u32[]{:S(2)}, u32[]{:S(2)}) collective-permute-start(bf16[4,16,2560]{2,1,0:T(8,128)(2,1)S(1)} %pad_maximum_fusion.1), channel_id=1, source_target_pairs={{0,1},{1,0},{2,3},{3,2},{4,5},{5,4},{6,7},{7,6},{8,9},{9,8},{10,11... | collective-permute-start | bytes 983048 | tf_op jit(solution)/shard_map/ppermute | solution.py:47
  54.8 3.3 %fetch.5.refs_2_.weight_ref = bf16[1280,3072]{1,0:T(8,128)(2,1)S(1)} custom-call(bf16[5120,3072]{1,0:T(8,128)(2,1)} %source_ref.9, bf16[4,16,2560]{2,1,0:T(8,128)(2,1)S(1)} %constant_dynamic-update-slice_fusion.gate_ref.refs_0_), custom_call_target="tpu_custom_call" | custom-call | bytes 7864320 | tf_op jit(solution)/shard_map/fetch/pallas_call | solution.py:515
  58.1 0.4 collective-permute-done.13.refs_1_
  58.7 1.9 %collective-permute-done.16 = bf16[4,16,2560]{2,1,0:T(8,128)(2,1)S(1)} collective-permute-done((bf16[4,16,2560]{2,1,0:T(8,128)(2,1)S(1)}, bf16[4,16,2560]{2,1,0:T(8,128)(2,1)S(1)}, u32[]{:S(2)}, u32[]{:S(2)}) %collective-permute-start.16) | collective-permute-done | bytes 327712 | tf_op jit(solution)/shard_map/ppermute | solution.py:47
  60.8 4.5 %logits_first.1 = (f32[256,3072]{1,0:T(8,128)S(1)}, bf16[1280,3072]{1,0:T(8,128)(2,1)S(1)}) custom-call(bf16[128,2560]{1,0:T(8,128)(2,1)S(1)} %bitcast.6, bf16[128,2560]{1,0:T(8,128)(2,1)S(1)} %collective-permute-done.14.right_ref, bf16[1024,3072]{1,0:T(8,128)(2,1)S(1)} %fetch.3.refs_0_.weight_ref, bf16[1536,3072]{1,0:T(8,128)(2,1)S(1)} %fetch.4.gate_ref.next_ref, ...), custom_call_target="tpu_custom_call" | custom-call | flops 4026531840 | tf_op jit(solution)/shard_map/logits_first/pallas_call | solution.py:631
  65.4 5.0 %logits.1 = f32[32,1,128]{2,1,0:T(1,128)S(1)} custom-call(f32[256,3072]{1,0:T(8,128)S(1)} %get-tuple-element.52.sum_in_ref, bf16[128,2560]{1,0:T(8,128)(2,1)S(1)} %bitcast.4, bf16[128,2560]{1,0:T(8,128)(2,1)S(1)} %collective-permute-done.17.right_ref, s32[32,8,1]{2,1,0:T(8,128)S(1)} %reshape.16.gate_ref.target_ref, ...), custom_call_target="tpu_custom_call" | custom-call | flops 4026531840 | tf_op jit(solution)/shard_map/logits/pallas_call | solution.py:644
  70.4 11.7 %all_to_all.5.stats_ref = f32[32,1,128]{2,1,0:T(1,128)S(1)} all-to-all(f32[32,1,128]{2,1,0:T(1,128)S(1)} %logits.1), channel_id=1, replica_groups=mesh['group'=4,'tensor'=8] {'group','tensor'}, dimensions={0} | all-to-all | bytes 32768 | tf_op jit(solution)/shard_map/all_to_all | solution.py:657
  82.1 0.6 final.1
  (33 shorter events, 1.7 us)
Async XLA Ops:
  0.0 5.4 %collective-permute-start = (bf16[64,512]{1,0:T(8,128)(2,1)}, bf16[64,512]{1,0:T(8,128)(2,1)S(1)}, u32[]{:S(2)}, u32[]{:S(2)}) collective-permute-start(bf16[64,512]{1,0:T(8,128)(2,1)} %refs_0_.1), channel_id=1, source_target_pairs={{0,16},{8,24},{16,0},{24,8},{1,17},{9,25},{17,1},{25,9},{2,18},{10... | collective-permute-start | bytes 196616 | tf_op jit(solution)/shard_map/ppermute | solution.py:47
  3.0 2.9 %collective-permute-start.2 = (bf16[64,512]{1,0:T(8,128)(2,1)}, bf16[64,512]{1,0:T(8,128)(2,1)S(1)}, u32[]{:S(2)}, u32[]{:S(2)}) collective-permute-start(bf16[64,512]{1,0:T(8,128)(2,1)} %refs_0_.1), channel_id=1, source_target_pairs={{0,8},{8,0},{16,24},{24,16},{1,9},{9,1},{17,25},{25,17},{2,10},{10... | collective-permute-start | bytes 196616 | tf_op jit(solution)/shard_map/ppermute | solution.py:47
  5.4 1.3 %collective-permute-start.1 = (bf16[64,512]{1,0:T(8,128)(2,1)S(1)}, bf16[64,512]{1,0:T(8,128)(2,1)S(1)}, u32[]{:S(2)}, u32[]{:S(2)}) collective-permute-start(bf16[64,512]{1,0:T(8,128)(2,1)S(1)} %pass.1.refs_1_), channel_id=1, source_target_pairs={{0,8},{8,0},{16,24},{24,16},{1,9},{9,1},{17,25},{25,17},{2,10},{10... | collective-permute-start | bytes 196616 | tf_op jit(solution)/shard_map/ppermute | solution.py:47
  7.6 5.0 %collective-permute-start.3 = (bf16[64,640]{1,0:T(8,128)(2,1)S(1)}, bf16[64,640]{1,0:T(8,128)(2,1)S(1)}, u32[]{:S(2)}, u32[]{:S(2)}) collective-permute-start(bf16[64,640]{1,0:T(8,128)(2,1)S(1)} %get-tuple-element.35.gate_ref), channel_id=1, source_target_pairs={{0,24},{8,16},{16,8},{24,0},{1,25},{9,17},{17,9},{25,1},{2,26},{10... | collective-permute-start | bytes 245768 | tf_op jit(solution)/shard_map/ppermute | solution.py:47
  9.4 4.8 %collective-permute-start.4 = (bf16[64,640]{1,0:T(8,128)(2,1)S(1)}, bf16[64,640]{1,0:T(8,128)(2,1)S(1)}, u32[]{:S(2)}, u32[]{:S(2)}) collective-permute-start(bf16[64,640]{1,0:T(8,128)(2,1)S(1)} %get-tuple-element.38), channel_id=1, source_target_pairs={{0,16},{8,24},{16,0},{24,8},{1,17},{9,25},{17,1},{25,9},{2,18},{10... | collective-permute-start | bytes 245768 | tf_op jit(solution)/shard_map/ppermute | solution.py:47
  9.7 4.5 %collective-permute-start.5 = (bf16[64,640]{1,0:T(8,128)(2,1)S(1)}, bf16[64,640]{1,0:T(8,128)(2,1)S(1)}, u32[]{:S(2)}, u32[]{:S(2)}) collective-permute-start(bf16[64,640]{1,0:T(8,128)(2,1)S(1)} %get-tuple-element.39), channel_id=1, source_target_pairs={{0,8},{8,0},{16,24},{24,16},{1,9},{9,1},{17,25},{25,17},{2,10},{10... | collective-permute-start | bytes 245768 | tf_op jit(solution)/shard_map/ppermute | solution.py:47
  18.1 6.5 %collective-permute-start.6 = (bf16[2,16,2560]{2,1,0:T(8,128)(2,1)S(1)}, bf16[2,16,2560]{2,1,0:T(8,128)(2,1)S(1)}, u32[]{:S(2)}, u32[]{:S(2)}) collective-permute-start(bf16[2,16,2560]{2,1,0:T(8,128)(2,1)S(1)} %get-tuple-element.42.gate_ref), channel_id=1, source_target_pairs={{0,1},{1,0},{2,3},{3,2},{4,5},{5,4},{6,7},{7,6},{8,9},{9,8},{10,11... | collective-permute-start | bytes 491528 | tf_op jit(solution)/shard_map/ppermute | solution.py:47
  20.2 13.3 %copy-start.1 = (bf16[5120]{0:T(1024)(128)(2,1)S(1)}, bf16[5120]{0:T(1024)(128)(2,1)}, u32[]{:S(2)}) copy-start(bf16[5120]{0:T(1024)(128)(2,1)} %param.21) | copy-start | bytes 30724
  20.2 6.1 %collective-permute-start.8 = (bf16[2,16,2560]{2,1,0:T(8,128)(2,1)S(1)}, bf16[2,16,2560]{2,1,0:T(8,128)(2,1)S(1)}, u32[]{:S(2)}, u32[]{:S(2)}) collective-permute-start(bf16[2,16,2560]{2,1,0:T(8,128)(2,1)S(1)} %get-tuple-element.46), channel_id=1, source_target_pairs={{0,2},{1,3},{2,0},{3,1},{4,6},{5,7},{6,4},{7,5},{8,10},{9,11},{10,... | collective-permute-start | bytes 491528 | tf_op jit(solution)/shard_map/ppermute | solution.py:47
  24.7 4.5 %collective-permute-start.7 = (bf16[16,2560]{1,0:T(8,128)(2,1)S(1)}, bf16[16,2560]{1,0:T(8,128)(2,1)S(1)}, u32[]{:S(2)}, u32[]{:S(2)}) collective-permute-start(bf16[16,2560]{1,0:T(8,128)(2,1)S(1)} %get-tuple-element.44), channel_id=1, source_target_pairs={{0,2},{1,3},{2,0},{3,1},{4,6},{5,7},{6,4},{7,5},{8,10},{9,11},{10,... | collective-permute-start | bytes 245768 | tf_op jit(solution)/shard_map/ppermute | solution.py:47
  26.3 4.5 %collective-permute-start.9 = (bf16[16,2560]{1,0:T(8,128)(2,1)S(1)}, bf16[16,2560]{1,0:T(8,128)(2,1)S(1)}, u32[]{:S(2)}, u32[]{:S(2)}) collective-permute-start(bf16[16,2560]{1,0:T(8,128)(2,1)S(1)} %get-tuple-element.48), channel_id=1, source_target_pairs={{0,1},{1,0},{2,3},{3,2},{4,5},{5,4},{6,7},{7,6},{8,9},{9,8},{10,11... | collective-permute-start | bytes 245768 | tf_op jit(solution)/shard_map/ppermute | solution.py:47
  30.8 8.4 %collective-permute-start.10 = (bf16[16,5120]{1,0:T(8,128)(2,1)S(1)}, bf16[16,5120]{1,0:T(8,128)(2,1)S(1)}, u32[]{:S(2)}, u32[]{:S(2)}) collective-permute-start(bf16[16,5120]{1,0:T(8,128)(2,1)S(1)} %get-tuple-element.49.gate_ref), channel_id=1, source_target_pairs={{0,4},{1,5},{2,6},{3,7},{4,0},{5,1},{6,2},{7,3},{8,12},{9,13},{10,... | collective-permute-start | bytes 491528 | tf_op jit(solution)/shard_map/ppermute | solution.py:47
  33.5 5.7 %copy-start = (bf16[64,5120]{1,0:T(8,128)(2,1)S(1)}, bf16[64,5120]{1,0:T(8,128)(2,1)}, u32[]{:S(2)}) copy-start(bf16[64,5120]{1,0:T(8,128)(2,1)} %param.19) | copy-start | bytes 1966084
  39.4 5.4 %collective-permute-start.11 = (bf16[16,5120]{1,0:T(8,128)(2,1)S(1)}, bf16[16,5120]{1,0:T(8,128)(2,1)S(1)}, u32[]{:S(2)}, u32[]{:S(2)}) collective-permute-start(bf16[16,5120]{1,0:T(8,128)(2,1)S(1)} %norm.1.refs_0_), channel_id=1, source_target_pairs={{0,2},{1,3},{2,0},{3,1},{4,6},{5,7},{6,4},{7,5},{8,10},{9,11},{10,... | collective-permute-start | bytes 491528 | tf_op jit(solution)/shard_map/ppermute | solution.py:47
  44.8 6.6 %collective-permute-start.12 = (bf16[2,16,2560]{2,1,0:T(8,128)(2,1)S(1)}, bf16[2,16,2560]{2,1,0:T(8,128)(2,1)S(1)}, u32[]{:S(2)}, u32[]{:S(2)}) collective-permute-start(bf16[2,16,2560]{2,1,0:T(8,128)(2,1)S(1)} %get-tuple-element.51), channel_id=1, source_target_pairs={{0,1},{1,0},{2,3},{3,2},{4,5},{5,4},{6,7},{7,6},{8,9},{9,8},{10,11... | collective-permute-start | bytes 491528 | tf_op jit(solution)/shard_map/ppermute | solution.py:47
  46.0 7.4 %collective-permute-start.15 = (bf16[2,16,2560]{2,1,0:T(8,128)(2,1)S(1)}, bf16[2,16,2560]{2,1,0:T(8,128)(2,1)S(1)}, u32[]{:S(2)}, u32[]{:S(2)}) collective-permute-start(bf16[2,16,2560]{2,1,0:T(8,128)(2,1)S(1)} %get-tuple-element.53), channel_id=1, source_target_pairs={{0,16},{8,24},{16,0},{24,8},{1,17},{9,25},{17,1},{25,9},{2,18},{10... | collective-permute-start | bytes 491528 | tf_op jit(solution)/shard_map/ppermute | solution.py:47
  51.4 7.1 %collective-permute-start.13 = (bf16[4,16,2560]{2,1,0:T(8,128)(2,1)S(1)}, bf16[4,16,2560]{2,1,0:T(8,128)(2,1)S(1)}, u32[]{:S(2)}, u32[]{:S(2)}) collective-permute-start(bf16[4,16,2560]{2,1,0:T(8,128)(2,1)S(1)} %constant_dynamic-update-slice_fusion.gate_ref.refs_0_), channel_id=1, source_target_pairs={{0,16},{8,24},{16,0},{24,8},{1,17},{9,25},{17,1},{25,9},{2,18},{10... | collective-permute-start | bytes 983048 | tf_op jit(solution)/shard_map/ppermute | solution.py:47
  53.5 7.1 %collective-permute-start.16 = (bf16[4,16,2560]{2,1,0:T(8,128)(2,1)S(1)}, bf16[4,16,2560]{2,1,0:T(8,128)(2,1)S(1)}, u32[]{:S(2)}, u32[]{:S(2)}) collective-permute-start(bf16[4,16,2560]{2,1,0:T(8,128)(2,1)S(1)} %pad_maximum_fusion.1), channel_id=1, source_target_pairs={{0,1},{1,0},{2,3},{3,2},{4,5},{5,4},{6,7},{7,6},{8,9},{9,8},{10,11... | collective-permute-start | bytes 983048 | tf_op jit(solution)/shard_map/ppermute | solution.py:47
  58.6 2.2 %collective-permute-start.14 = (bf16[128,2560]{1,0:T(8,128)(2,1)S(1)}, bf16[128,2560]{1,0:T(8,128)(2,1)S(1)}, u32[]{:S(2)}, u32[]{:S(2)}) collective-permute-start(bf16[128,2560]{1,0:T(8,128)(2,1)S(1)} %bitcast.5), channel_id=1, source_target_pairs={{0,8},{8,0},{16,24},{24,16},{1,9},{9,1},{17,25},{25,17},{2,10},{10... | collective-permute-start | bytes 1966088 | tf_op jit(solution)/shard_map/ppermute | solution.py:47
  60.7 4.6 %collective-permute-start.17 = (bf16[128,2560]{1,0:T(8,128)(2,1)S(1)}, bf16[128,2560]{1,0:T(8,128)(2,1)S(1)}, u32[]{:S(2)}, u32[]{:S(2)}) collective-permute-start(bf16[128,2560]{1,0:T(8,128)(2,1)S(1)} %bitcast.3), channel_id=1, source_target_pairs={{0,8},{8,0},{16,24},{24,16},{1,9},{9,1},{17,25},{25,17},{2,10},{10... | collective-permute-start | bytes 1966088 | tf_op jit(solution)/shard_map/ppermute | solution.py:47

commit v12 on v9

--- a/solution.py
+++ b/solution.py
@@ -334,6 +334,7 @@
     weight_ref,
     next_ref,
     out_ref,
+    other_ref,
     x_ref,
     peak_ref,
     sum_ref,
@@ -388,8 +389,22 @@
     lane = lax.broadcasted_iota(jnp.int32, (rows, 128), 1)
     three = jnp.where(lane // share == 0, peak, jnp.where(lane // share == 1, sums, pick))
     three = jnp.where((row - lane) % share == 0, three, 0.0)
+    mine = len(places) // 2
     for i, place in enumerate(places):
-        out_ref[place] = jnp.sum(three[i * share : (i + 1) * share], axis=0, keepdims=True)
+        near = place // (2 * tensor_size) * tensor_size + place % tensor_size
+        ref = out_ref if i < mine else other_ref
+        ref[near] = jnp.sum(three[i * share : (i + 1) * share], axis=0, keepdims=True)
+
+
+def pair_kernel(share, left_ref, right_ref, out_ref):
+    left = left_ref[...].reshape(left_ref.shape[0], 128)
+    right = right_ref[...].reshape(left_ref.shape[0], 128)
+    lane = lax.broadcasted_iota(jnp.int32, left.shape, 1) // share
+    peak = jnp.maximum(left, right)
+    shifted = pltpu.roll(peak, share, 1)
+    sums = left * jnp.exp(jnp.where(lane == 1, pltpu.roll(left, share, 1) - shifted, 0.0))
+    sums = sums + right * jnp.exp(jnp.where(lane == 1, pltpu.roll(right, share, 1) - shifted, 0.0))
+    out_ref[...] = jnp.where(lane == 0, peak, jnp.where(lane < 3, sums, 0.0)).reshape(out_ref.shape)
 
 
 def final_kernel(share, live_ref, stats_ref, out_ref):
@@ -619,11 +634,11 @@
         cost_estimate=cost(flops=work),
         name="logits_first",
     )(*map(held, (*halves[0], first_quarter, second_quarter)), stored(lm_weight))
-    stats = pl.pallas_call(
+    stats, other = pl.pallas_call(
         functools.partial(logits_kernel, vocab, spots, tensor_size),
-        out_shape=jax.ShapeDtypeStruct((group_size * tensor_size, 1, 128), F32),
+        out_shape=[jax.ShapeDtypeStruct((group_size * tensor_size // 2, 1, 128), F32)] * 2,
         in_specs=[vmem()] * 6,
-        out_specs=vmem(),
+        out_specs=[vmem()] * 2,
         scratch_shapes=[pltpu.VMEM((total_rows, half), BF16)]
         + [pltpu.VMEM((total_rows, 128), F32)] * 3
         + [pltpu.VMEM((total_rows, 1), i32)],
@@ -632,7 +647,21 @@
         name="logits",
     )(*map(held, (first, *halves[1])), wanted, held(third), held(last))
 
-    stats = lax.all_to_all(stats, ("group", "tensor"), 0, 0, tiled=True)
+    stats = pl.pallas_call(
+        functools.partial(pair_kernel, share),
+        out_shape=jax.ShapeDtypeStruct(stats.shape, F32),
+        in_specs=[vmem()] * 2,
+        out_specs=vmem(),
+        compiler_params=params(2),
+        name="pair",
+    )(held(stats), held(swap(other, "group", 1, group_size)))
+    alike = [
+        [g * tensor_size + t for g in range(core, group_size, 2) for t in range(tensor_size)]
+        for core in (0, 1)
+    ]
+    stats = lax.all_to_all(
+        stats, ("group", "tensor"), 0, 0, axis_index_groups=alike, tiled=True
+    )
     return pl.pallas_call(
         functools.partial(final_kernel, share),
         out_shape=jax.ShapeDtypeStruct((share,), F32),

time: 81.9 us -> 84.5 us (1.032)
  blocking collectives: 10.2 us -> 11.2 us
    all_to_all x1, blocking collectives: 10.2 us -> 11.2 us  [local(): lax.all_to_all(stats, ('group', 'tensor'), 0, 0, axis_index_groups=alike,...]
    ppermute x18 -> x19, waiting for transfers between devices: 19.5 us -> 20.3 us  [swap(): return lax.ppermute(x, axis, [(i, i ^ distance) for i in range(size)])]
    ppermute x18 -> x19, starting transfers between devices: 21.1 us -> 21.7 us  [swap(): return lax.ppermute(x, axis, [(i, i ^ distance) for i in range(size)])]
  transfers between devices with their start and end apart: 18 -> 19, of which waited for: 9 -> 10; matrix products, arithmetic and copies ran while one was open for 1% -> 1% of each run, Pallas kernels for 24% -> 23%
where the time goes in v12:
time: 84.5 us; the launch traced here: 84.2 us
  Pallas kernels  29.7 us (35%)
  starting transfers between devices  21.7 us (26%)
  waiting for transfers between devices  20.3 us (24%)
  blocking collectives  11.2 us (13%)
  local copies, waits for them, and re-layouts  0.92 us (1%)
    ppermute x19, starting transfers between devices, swap(): return lax.ppermute(x, axis, [(i, i ^ distance) for i in range(size)])  21.7 us
    ppermute x19, waiting for transfers between devices, swap(): return lax.ppermute(x, axis, [(i, i ^ distance) for i in range(size)])  20.3 us
    all_to_all x1, blocking collectives, local(): lax.all_to_all(stats, ('group', 'tensor'), 0, 0, axis_index_groups=alike,...  11.2 us
    pallas_call x3, Pallas kernels, fetch(): pl.pallas_call(functools.partial(fetch_kernel, start), out_shape=pltpu.VM...  10.1 us
    pallas_call x1, Pallas kernels, local(): pl.pallas_call(functools.partial(logits_kernel, vocab, spots, tensor_size...  5 us
    pallas_call x1, Pallas kernels, local(): pl.pallas_call(functools.partial(first_kernel, narrow), out_shape=[pltpu....  4.52 us
    pallas_call x1, Pallas kernels, local(): pl.pallas_call(functools.partial(own_kernel, heads, seq, share), out_shap...  3.54 us
    pallas_call x1, Pallas kernels, local(): pl.pallas_call(functools.partial(project_kernel, heads, seq, wide, group_...  3.27 us
  transfers between devices with their start and end apart: 19, of which 10 were waited for; matrix products, arithmetic and copies ran while one was open for 1% of the time, Pallas kernels for 23%

profile of v12, /device:TPU:0, one launch (start us, length us, event | category | flops | bytes accessed | tf_op | source)
XLA Modules:
  0.0 84.2 jit_solution(7270010011608788323)
XLA Ops:
  0.0 3.0 %collective-permute-start = (bf16[64,512]{1,0:T(8,128)(2,1)}, bf16[64,512]{1,0:T(8,128)(2,1)S(1)}, u32[]{:S(2)}, u32[]{:S(2)}) collective-permute-start(bf16[64,512]{1,0:T(8,128)(2,1)} %refs_0_.1), channel_id=1, source_target_pairs={{0,16},{8,24},{16,0},{24,8},{1,17},{9,25},{17,1},{25,9},{2,18},{10... | collective-permute-start | bytes 196616 | tf_op jit(solution)/shard_map/ppermute | solution.py:47
  3.0 0.9 %reshape.16.refs_1_.target_ref = s32[32,8,1]{2,1,0:T(8,128)S(1)} reshape(s32[256]{0:T(256)} %param.23) | data formatting | bytes 2048 | tf_op jit(solution)/shard_map/reshape | solution.py:446
  3.9 1.6 %collective-permute-done.refs_0_ = bf16[64,512]{1,0:T(8,128)(2,1)S(1)} collective-permute-done((bf16[64,512]{1,0:T(8,128)(2,1)}, bf16[64,512]{1,0:T(8,128)(2,1)S(1)}, u32[]{:S(2)}, u32[]{:S(2)}) %collective-permute-start) | collective-permute-done | bytes 65568 | tf_op jit(solution)/shard_map/ppermute | solution.py:47
  5.5 1.4 %load.1 = (bf16[64,512]{1,0:T(8,128)(2,1)S(1)}, bf16[64,512]{1,0:T(8,128)(2,1)S(1)}, bf16[64,512]{1,0:T(8,128)(2,1)S(1)}, bf16[512,512]{1,0:T(8,128)(2,1)S(1)}, bf16[512,512]{1,0:T(8,128)(2,1)S(1)}) custom-call(bf16[64,512]{1,0:T(8,128)(2,1)S(1)} %pass.1.gate_ref.refs_1_, bf16[64,512]{1,0:T(8,128)(2,1)} %refs_0_.1, bf16[64,512]{1,0:T(8,128)(2,1)} %refs_1_.1, ...), custom_call_target="tpu_custom_call" | custom-call | bytes 2097152 | tf_op jit(solution)/shard_map/load/pallas_call | solution.py:464
  6.9 0.9 %prefix_attention.1 = (bf16[64,640]{1,0:T(8,128)(2,1)S(1)}, bf16[64,640]{1,0:T(8,128)(2,1)S(1)}, bf16[64,640]{1,0:T(8,128)(2,1)S(1)}) custom-call(bf16[64,512]{1,0:T(8,128)(2,1)S(1)} %collective-permute-done.1.refs_0_, bf16[64,512]{1,0:T(8,128)(2,1)S(1)} %pass.1.gate_ref.refs_1_, bf16[64,512]{1,0:T(8,128)(2,1)S(1)} %collective-permute-done.2.refs_2_, ...), custom_call_target="tpu_custom_call" | custom-call | tf_op jit(solution)/shard_map/prefix_attention/pallas_call | solution.py:475
  7.8 2.2 %collective-permute-start.3 = (bf16[64,640]{1,0:T(8,128)(2,1)S(1)}, bf16[64,640]{1,0:T(8,128)(2,1)S(1)}, u32[]{:S(2)}, u32[]{:S(2)}) collective-permute-start(bf16[64,640]{1,0:T(8,128)(2,1)S(1)} %get-tuple-element.37.gate_ref), channel_id=1, source_target_pairs={{0,24},{8,16},{16,8},{24,0},{1,25},{9,17},{17,9},{25,1},{2,26},{10... | collective-permute-start | bytes 245768 | tf_op jit(solution)/shard_map/ppermute | solution.py:47
  10.1 3.5 %own_attention.1 = (f32[64,640]{1,0:T(8,128)S(1)}, f32[8,128]{1,0:T(8,128)S(1)}, bf16[512,5120]{1,0:T(8,128)(2,1)S(1)}) custom-call(s32[2]{0:T(128)} %lengths_ref.1, s32[2]{0:T(128)} %prompt_ref.3, bf16[64,512]{1,0:T(8,128)(2,1)S(1)} %get-tuple-element.32.q_ref, bf16[64,512]{1,0:T(8,128)(2,1)S(1)} %get-tuple-element.33.rk_ref, ...), custom_call_target="tpu_custom_call" | custom-call | bytes 8388608 | tf_op jit(solution)/shard_map/own_attention/pallas_call | solution.py:484
  13.7 1.0 %collective-permute-done.4.refs_1_ = bf16[64,640]{1,0:T(8,128)(2,1)S(1)} collective-permute-done((bf16[64,640]{1,0:T(8,128)(2,1)S(1)}, bf16[64,640]{1,0:T(8,128)(2,1)S(1)}, u32[]{:S(2)}, u32[]{:S(2)}) %collective-permute-start.4) | collective-permute-done | bytes 81952 | tf_op jit(solution)/shard_map/ppermute | solution.py:47
  14.7 3.3 %project.1 = (bf16[2,16,2560]{2,1,0:T(8,128)(2,1)S(1)}, f32[2,16,2560]{2,1,0:T(8,128)S(1)}, bf16[2,16,2560]{2,1,0:T(8,128)(2,1)S(1)}, f32[2,16,2560]{2,1,0:T(8,128)S(1)}) custom-call(s32[2]{0:T(128)} %prompt_ref.3, f32[64,640]{1,0:T(8,128)S(1)} %get-tuple-element.39.own_ref, bf16[64,640]{1,0:T(8,128)(2,1)S(1)} %collective-permute-done.3.refs_0_, ...), custom_call_target="tpu_custom_call" | custom-call | tf_op jit(solution)/shard_map/project/pallas_call | solution.py:527
  18.0 1.7 %collective-permute-start.6 = (bf16[2,16,2560]{2,1,0:T(8,128)(2,1)S(1)}, bf16[2,16,2560]{2,1,0:T(8,128)(2,1)S(1)}, u32[]{:S(2)}, u32[]{:S(2)}) collective-permute-start(bf16[2,16,2560]{2,1,0:T(8,128)(2,1)S(1)} %get-tuple-element.44), channel_id=1, source_target_pairs={{0,1},{1,0},{2,3},{3,2},{4,5},{5,4},{6,7},{7,6},{8,9},{9,8},{10,11... | collective-permute-start | bytes 491528 | tf_op jit(solution)/shard_map/ppermute | solution.py:47
  19.7 1.6 %collective-permute-start.8 = (bf16[2,16,2560]{2,1,0:T(8,128)(2,1)S(1)}, bf16[2,16,2560]{2,1,0:T(8,128)(2,1)S(1)}, u32[]{:S(2)}, u32[]{:S(2)}) collective-permute-start(bf16[2,16,2560]{2,1,0:T(8,128)(2,1)S(1)} %get-tuple-element.48), channel_id=1, source_target_pairs={{0,2},{1,3},{2,0},{3,1},{4,6},{5,7},{6,4},{7,5},{8,10},{9,11},{10,... | collective-permute-start | bytes 491528 | tf_op jit(solution)/shard_map/ppermute | solution.py:47
  21.3 2.5 %collective-permute-done.6.got_ref = bf16[2,16,2560]{2,1,0:T(8,128)(2,1)S(1)} collective-permute-done((bf16[2,16,2560]{2,1,0:T(8,128)(2,1)S(1)}, bf16[2,16,2560]{2,1,0:T(8,128)(2,1)S(1)}, u32[]{:S(2)}, u32[]{:S(2)}) %collective-permute-start.6) | collective-permute-done | bytes 163872 | tf_op jit(solution)/shard_map/ppermute | solution.py:47
  23.8 1.9 %collective-permute-start.7 = (bf16[16,2560]{1,0:T(8,128)(2,1)S(1)}, bf16[16,2560]{1,0:T(8,128)(2,1)S(1)}, u32[]{:S(2)}, u32[]{:S(2)}) collective-permute-start(bf16[16,2560]{1,0:T(8,128)(2,1)S(1)} %get-tuple-element.46), channel_id=1, source_target_pairs={{0,2},{1,3},{2,0},{3,1},{4,6},{5,7},{6,4},{7,5},{8,10},{9,11},{10,... | collective-permute-start | bytes 245768 | tf_op jit(solution)/shard_map/ppermute | solution.py:47
  25.7 1.6 %collective-permute-start.9 = (bf16[16,2560]{1,0:T(8,128)(2,1)S(1)}, bf16[16,2560]{1,0:T(8,128)(2,1)S(1)}, u32[]{:S(2)}, u32[]{:S(2)}) collective-permute-start(bf16[16,2560]{1,0:T(8,128)(2,1)S(1)} %get-tuple-element.50), channel_id=1, source_target_pairs={{0,1},{1,0},{2,3},{3,2},{4,5},{5,4},{6,7},{7,6},{8,9},{9,8},{10,11... | collective-permute-start | bytes 245768 | tf_op jit(solution)/shard_map/ppermute | solution.py:47
  27.3 1.0 %collective-permute-done.7.got_left_ref = bf16[16,2560]{1,0:T(8,128)(2,1)S(1)} collective-permute-done((bf16[16,2560]{1,0:T(8,128)(2,1)S(1)}, bf16[16,2560]{1,0:T(8,128)(2,1)S(1)}, u32[]{:S(2)}, u32[]{:S(2)}) %collective-permute-start.7) | collective-permute-done | bytes 81952 | tf_op jit(solution)/shard_map/ppermute | solution.py:47
  28.3 1.9 %collective-permute-done.9.got_right_ref = bf16[16,2560]{1,0:T(8,128)(2,1)S(1)} collective-permute-done((bf16[16,2560]{1,0:T(8,128)(2,1)S(1)}, bf16[16,2560]{1,0:T(8,128)(2,1)S(1)}, u32[]{:S(2)}, u32[]{:S(2)}) %collective-permute-start.9) | collective-permute-done | bytes 81952 | tf_op jit(solution)/shard_map/ppermute | solution.py:47
  30.3 2.7 %collective-permute-start.10 = (bf16[16,5120]{1,0:T(8,128)(2,1)S(1)}, bf16[16,5120]{1,0:T(8,128)(2,1)S(1)}, u32[]{:S(2)}, u32[]{:S(2)}) collective-permute-start(bf16[16,5120]{1,0:T(8,128)(2,1)S(1)} %get-tuple-element.51.gate_ref), channel_id=1, source_target_pairs={{0,4},{1,5},{2,6},{3,7},{4,0},{5,1},{6,2},{7,3},{8,12},{9,13},{10,... | collective-permute-start | bytes 491528 | tf_op jit(solution)/shard_map/ppermute | solution.py:47
  32.9 3.3 %fetch.3.first_gate_ref.weight_ref = bf16[1280,3072]{1,0:T(8,128)(2,1)S(1)} custom-call(bf16[5120,3072]{1,0:T(8,128)(2,1)} %source_ref.9, bf16[16,5120]{1,0:T(8,128)(2,1)S(1)} %get-tuple-element.51.gate_ref), custom_call_target="tpu_custom_call" | custom-call | bytes 7864320 | tf_op jit(solution)/shard_map/fetch/pallas_call | solution.py:511
  36.3 3.4 %fetch.4.second_gate_ref.next_ref = bf16[1280,3072]{1,0:T(8,128)(2,1)S(1)} custom-call(bf16[5120,3072]{1,0:T(8,128)(2,1)} %source_ref.9, bf16[16,5120]{1,0:T(8,128)(2,1)S(1)} %get-tuple-element.51.gate_ref), custom_call_target="tpu_custom_call" | custom-call | bytes 7864320 | tf_op jit(solution)/shard_map/fetch/pallas_call | solution.py:511
  39.9 1.2 %collective-permute-start.11 = (bf16[16,5120]{1,0:T(8,128)(2,1)S(1)}, bf16[16,5120]{1,0:T(8,128)(2,1)S(1)}, u32[]{:S(2)}, u32[]{:S(2)}) collective-permute-start(bf16[16,5120]{1,0:T(8,128)(2,1)S(1)} %norm.1.refs_0_), channel_id=1, source_target_pairs={{0,2},{1,3},{2,0},{3,1},{4,6},{5,7},{6,4},{7,5},{8,10},{9,11},{10,... | collective-permute-start | bytes 491528 | tf_op jit(solution)/shard_map/ppermute | solution.py:47
  41.1 4.2 %collective-permute-done.11.refs_1_ = bf16[16,5120]{1,0:T(8,128)(2,1)S(1)} collective-permute-done((bf16[16,5120]{1,0:T(8,128)(2,1)S(1)}, bf16[16,5120]{1,0:T(8,128)(2,1)S(1)}, u32[]{:S(2)}, u32[]{:S(2)}) %collective-permute-start.11) | collective-permute-done | bytes 163872 | tf_op jit(solution)/shard_map/ppermute | solution.py:47
  45.4 1.6 %collective-permute-start.12 = (bf16[2,16,2560]{2,1,0:T(8,128)(2,1)S(1)}, bf16[2,16,2560]{2,1,0:T(8,128)(2,1)S(1)}, u32[]{:S(2)}, u32[]{:S(2)}) collective-permute-start(bf16[2,16,2560]{2,1,0:T(8,128)(2,1)S(1)} %get-tuple-element.53.gate_ref.refs_0_), channel_id=1, source_target_pairs={{0,1},{1,0},{2,3},{3,2},{4,5},{5,4},{6,7},{7,6},{8,9},{9,8},{10,11... | collective-permute-start | bytes 491528 | tf_op jit(solution)/shard_map/ppermute | solution.py:47
  46.9 1.5 %collective-permute-start.15 = (bf16[2,16,2560]{2,1,0:T(8,128)(2,1)S(1)}, bf16[2,16,2560]{2,1,0:T(8,128)(2,1)S(1)}, u32[]{:S(2)}, u32[]{:S(2)}) collective-permute-start(bf16[2,16,2560]{2,1,0:T(8,128)(2,1)S(1)} %get-tuple-element.55), channel_id=1, source_target_pairs={{0,16},{8,24},{16,0},{24,8},{1,17},{9,25},{17,1},{25,9},{2,18},{10... | collective-permute-start | bytes 491528 | tf_op jit(solution)/shard_map/ppermute | solution.py:47
  48.4 3.3 %fetch.5.refs_2_.weight_ref = bf16[1280,3072]{1,0:T(8,128)(2,1)S(1)} custom-call(bf16[5120,3072]{1,0:T(8,128)(2,1)} %source_ref.9, bf16[2,16,2560]{2,1,0:T(8,128)(2,1)S(1)} %get-tuple-element.53.gate_ref.refs_0_), custom_call_target="tpu_custom_call" | custom-call | bytes 7864320 | tf_op jit(solution)/shard_map/fetch/pallas_call | solution.py:511
  52.6 1.4 %collective-permute-done.15 = bf16[2,16,2560]{2,1,0:T(8,128)(2,1)S(1)} collective-permute-done((bf16[2,16,2560]{2,1,0:T(8,128)(2,1)S(1)}, bf16[2,16,2560]{2,1,0:T(8,128)(2,1)S(1)}, u32[]{:S(2)}, u32[]{:S(2)}) %collective-permute-start.15) | collective-permute-done | bytes 163872 | tf_op jit(solution)/shard_map/ppermute | solution.py:47
  54.0 1.2 %collective-permute-start.16 = (bf16[4,16,2560]{2,1,0:T(8,128)(2,1)S(1)}, bf16[4,16,2560]{2,1,0:T(8,128)(2,1)S(1)}, u32[]{:S(2)}, u32[]{:S(2)}) collective-permute-start(bf16[4,16,2560]{2,1,0:T(8,128)(2,1)S(1)} %pad_maximum_fusion.2), channel_id=1, source_target_pairs={{0,1},{1,0},{2,3},{3,2},{4,5},{5,4},{6,7},{7,6},{8,9},{9,8},{10,11... | collective-permute-start | bytes 983048 | tf_op jit(solution)/shard_map/ppermute | solution.py:47
  55.2 3.8 %collective-permute-done.13 = bf16[4,16,2560]{2,1,0:T(8,128)(2,1)S(1)} collective-permute-done((bf16[4,16,2560]{2,1,0:T(8,128)(2,1)S(1)}, bf16[4,16,2560]{2,1,0:T(8,128)(2,1)S(1)}, u32[]{:S(2)}, u32[]{:S(2)}) %collective-permute-start.13) | collective-permute-done | bytes 327712 | tf_op jit(solution)/shard_map/ppermute | solution.py:47
  59.1 2.1 %collective-permute-done.16 = bf16[4,16,2560]{2,1,0:T(8,128)(2,1)S(1)} collective-permute-done((bf16[4,16,2560]{2,1,0:T(8,128)(2,1)S(1)}, bf16[4,16,2560]{2,1,0:T(8,128)(2,1)S(1)}, u32[]{:S(2)}, u32[]{:S(2)}) %collective-permute-start.16) | collective-permute-done | bytes 327712 | tf_op jit(solution)/shard_map/ppermute | solution.py:47
  61.4 4.5 %logits_first.1 = (f32[256,3072]{1,0:T(8,128)S(1)}, bf16[1280,3072]{1,0:T(8,128)(2,1)S(1)}) custom-call(bf16[128,2560]{1,0:T(8,128)(2,1)S(1)} %bitcast.6, bf16[128,2560]{1,0:T(8,128)(2,1)S(1)} %collective-permute-done.14.right_ref, bf16[1280,3072]{1,0:T(8,128)(2,1)S(1)} %fetch.3.first_gate_ref.weight_ref, ...), custom_call_target="tpu_custom_call" | custom-call | flops 4026531840 | tf_op jit(solution)/shard_map/logits_first/pallas_call | solution.py:624
  65.9 5.0 %logits.1 = (f32[16,1,128]{2,1,0:T(1,128)S(1)}, f32[16,1,128]{2,1,0:T(1,128)S(1)}) custom-call(f32[256,3072]{1,0:T(8,128)S(1)} %get-tuple-element.54.sum_in_ref, bf16[128,2560]{1,0:T(8,128)(2,1)S(1)} %bitcast.4, bf16[128,2560]{1,0:T(8,128)(2,1)S(1)} %collective-permute-done.17.right_ref, s32[32,8,1]{2,1,0:T(8,128)S(1)} %reshape.16.refs_1_.target_ref, ...), custom_call_target="tpu_custom_call" | custom-call | flops 4026531840 | tf_op jit(solution)/shard_map/logits/pallas_call | solution.py:637
  71.5 0.8 collective-permute-done.18.right_ref
  72.4 11.2 %all_to_all.5.stats_ref = f32[16,1,128]{2,1,0:T(1,128)S(1)} all-to-all(f32[16,1,128]{2,1,0:T(1,128)S(1)} %pair.1), channel_id=1, replica_groups={{0,1,2,3,4,5,6,7,16,17,18,19,20,21,22,23},{8,9,10,11,12,13,14,15,24,25,..., dimensions={0} | all-to-all | bytes 16384 | tf_op jit(solution)/shard_map/all_to_all | solution.py:662
  (35 shorter events, 3.0 us)
Async XLA Ops:
  0.0 5.4 %collective-permute-start = (bf16[64,512]{1,0:T(8,128)(2,1)}, bf16[64,512]{1,0:T(8,128)(2,1)S(1)}, u32[]{:S(2)}, u32[]{:S(2)}) collective-permute-start(bf16[64,512]{1,0:T(8,128)(2,1)} %refs_0_.1), channel_id=1, source_target_pairs={{0,16},{8,24},{16,0},{24,8},{1,17},{9,25},{17,1},{25,9},{2,18},{10... | collective-permute-start | bytes 196616 | tf_op jit(solution)/shard_map/ppermute | solution.py:47
  3.0 3.9 %collective-permute-start.2 = (bf16[64,512]{1,0:T(8,128)(2,1)}, bf16[64,512]{1,0:T(8,128)(2,1)S(1)}, u32[]{:S(2)}, u32[]{:S(2)}) collective-permute-start(bf16[64,512]{1,0:T(8,128)(2,1)} %refs_0_.1), channel_id=1, source_target_pairs={{0,8},{8,0},{16,24},{24,16},{1,9},{9,1},{17,25},{25,17},{2,10},{10... | collective-permute-start | bytes 196616 | tf_op jit(solution)/shard_map/ppermute | solution.py:47
  5.4 27.5 %copy-start.1 = (bf16[5120]{0:T(1024)(128)(2,1)S(1)}, bf16[5120]{0:T(1024)(128)(2,1)}, u32[]{:S(2)}) copy-start(bf16[5120]{0:T(1024)(128)(2,1)} %param.21) | copy-start | bytes 30724
  5.4 1.5 %collective-permute-start.1 = (bf16[64,512]{1,0:T(8,128)(2,1)S(1)}, bf16[64,512]{1,0:T(8,128)(2,1)S(1)}, u32[]{:S(2)}, u32[]{:S(2)}) collective-permute-start(bf16[64,512]{1,0:T(8,128)(2,1)S(1)} %pass.1.gate_ref.refs_1_), channel_id=1, source_target_pairs={{0,8},{8,0},{16,24},{24,16},{1,9},{9,1},{17,25},{25,17},{2,10},{10... | collective-permute-start | bytes 196616 | tf_op jit(solution)/shard_map/ppermute | solution.py:47
  7.8 5.9 %collective-permute-start.3 = (bf16[64,640]{1,0:T(8,128)(2,1)S(1)}, bf16[64,640]{1,0:T(8,128)(2,1)S(1)}, u32[]{:S(2)}, u32[]{:S(2)}) collective-permute-start(bf16[64,640]{1,0:T(8,128)(2,1)S(1)} %get-tuple-element.37.gate_ref), channel_id=1, source_target_pairs={{0,24},{8,16},{16,8},{24,0},{1,25},{9,17},{17,9},{25,1},{2,26},{10... | collective-permute-start | bytes 245768 | tf_op jit(solution)/shard_map/ppermute | solution.py:47
  10.0 4.7 %collective-permute-start.4 = (bf16[64,640]{1,0:T(8,128)(2,1)S(1)}, bf16[64,640]{1,0:T(8,128)(2,1)S(1)}, u32[]{:S(2)}, u32[]{:S(2)}) collective-permute-start(bf16[64,640]{1,0:T(8,128)(2,1)S(1)} %get-tuple-element.40), channel_id=1, source_target_pairs={{0,16},{8,24},{16,0},{24,8},{1,17},{9,25},{17,1},{25,9},{2,18},{10... | collective-permute-start | bytes 245768 | tf_op jit(solution)/shard_map/ppermute | solution.py:47
  10.0 4.7 %collective-permute-start.5 = (bf16[64,640]{1,0:T(8,128)(2,1)S(1)}, bf16[64,640]{1,0:T(8,128)(2,1)S(1)}, u32[]{:S(2)}, u32[]{:S(2)}) collective-permute-start(bf16[64,640]{1,0:T(8,128)(2,1)S(1)} %get-tuple-element.41), channel_id=1, source_target_pairs={{0,8},{8,0},{16,24},{24,16},{1,9},{9,1},{17,25},{25,17},{2,10},{10... | collective-permute-start | bytes 245768 | tf_op jit(solution)/shard_map/ppermute | solution.py:47
  18.0 5.8 %collective-permute-start.6 = (bf16[2,16,2560]{2,1,0:T(8,128)(2,1)S(1)}, bf16[2,16,2560]{2,1,0:T(8,128)(2,1)S(1)}, u32[]{:S(2)}, u32[]{:S(2)}) collective-permute-start(bf16[2,16,2560]{2,1,0:T(8,128)(2,1)S(1)} %get-tuple-element.44), channel_id=1, source_target_pairs={{0,1},{1,0},{2,3},{3,2},{4,5},{5,4},{6,7},{7,6},{8,9},{9,8},{10,11... | collective-permute-start | bytes 491528 | tf_op jit(solution)/shard_map/ppermute | solution.py:47
  19.7 6.0 %collective-permute-start.8 = (bf16[2,16,2560]{2,1,0:T(8,128)(2,1)S(1)}, bf16[2,16,2560]{2,1,0:T(8,128)(2,1)S(1)}, u32[]{:S(2)}, u32[]{:S(2)}) collective-permute-start(bf16[2,16,2560]{2,1,0:T(8,128)(2,1)S(1)} %get-tuple-element.48), channel_id=1, source_target_pairs={{0,2},{1,3},{2,0},{3,1},{4,6},{5,7},{6,4},{7,5},{8,10},{9,11},{10,... | collective-permute-start | bytes 491528 | tf_op jit(solution)/shard_map/ppermute | solution.py:47
  23.8 4.5 %collective-permute-start.7 = (bf16[16,2560]{1,0:T(8,128)(2,1)S(1)}, bf16[16,2560]{1,0:T(8,128)(2,1)S(1)}, u32[]{:S(2)}, u32[]{:S(2)}) collective-permute-start(bf16[16,2560]{1,0:T(8,128)(2,1)S(1)} %get-tuple-element.46), channel_id=1, source_target_pairs={{0,2},{1,3},{2,0},{3,1},{4,6},{5,7},{6,4},{7,5},{8,10},{9,11},{10,... | collective-permute-start | bytes 245768 | tf_op jit(solution)/shard_map/ppermute | solution.py:47
  25.7 4.5 %collective-permute-start.9 = (bf16[16,2560]{1,0:T(8,128)(2,1)S(1)}, bf16[16,2560]{1,0:T(8,128)(2,1)S(1)}, u32[]{:S(2)}, u32[]{:S(2)}) collective-permute-start(bf16[16,2560]{1,0:T(8,128)(2,1)S(1)} %get-tuple-element.50), channel_id=1, source_target_pairs={{0,1},{1,0},{2,3},{3,2},{4,5},{5,4},{6,7},{7,6},{8,9},{9,8},{10,11... | collective-permute-start | bytes 245768 | tf_op jit(solution)/shard_map/ppermute | solution.py:47
  30.3 9.5 %collective-permute-start.10 = (bf16[16,5120]{1,0:T(8,128)(2,1)S(1)}, bf16[16,5120]{1,0:T(8,128)(2,1)S(1)}, u32[]{:S(2)}, u32[]{:S(2)}) collective-permute-start(bf16[16,5120]{1,0:T(8,128)(2,1)S(1)} %get-tuple-element.51.gate_ref), channel_id=1, source_target_pairs={{0,4},{1,5},{2,6},{3,7},{4,0},{5,1},{6,2},{7,3},{8,12},{9,13},{10,... | collective-permute-start | bytes 491528 | tf_op jit(solution)/shard_map/ppermute | solution.py:47
  36.3 3.4 %copy-start = (bf16[64,5120]{1,0:T(8,128)(2,1)S(1)}, bf16[64,5120]{1,0:T(8,128)(2,1)}, u32[]{:S(2)}) copy-start(bf16[64,5120]{1,0:T(8,128)(2,1)} %param.19) | copy-start | bytes 1966084
  39.9 5.4 %collective-permute-start.11 = (bf16[16,5120]{1,0:T(8,128)(2,1)S(1)}, bf16[16,5120]{1,0:T(8,128)(2,1)S(1)}, u32[]{:S(2)}, u32[]{:S(2)}) collective-permute-start(bf16[16,5120]{1,0:T(8,128)(2,1)S(1)} %norm.1.refs_0_), channel_id=1, source_target_pairs={{0,2},{1,3},{2,0},{3,1},{4,6},{5,7},{6,4},{7,5},{8,10},{9,11},{10,... | collective-permute-start | bytes 491528 | tf_op jit(solution)/shard_map/ppermute | solution.py:47
  45.4 6.4 %collective-permute-start.12 = (bf16[2,16,2560]{2,1,0:T(8,128)(2,1)S(1)}, bf16[2,16,2560]{2,1,0:T(8,128)(2,1)S(1)}, u32[]{:S(2)}, u32[]{:S(2)}) collective-permute-start(bf16[2,16,2560]{2,1,0:T(8,128)(2,1)S(1)} %get-tuple-element.53.gate_ref.refs_0_), channel_id=1, source_target_pairs={{0,1},{1,0},{2,3},{3,2},{4,5},{5,4},{6,7},{7,6},{8,9},{9,8},{10,11... | collective-permute-start | bytes 491528 | tf_op jit(solution)/shard_map/ppermute | solution.py:47
  46.9 7.1 %collective-permute-start.15 = (bf16[2,16,2560]{2,1,0:T(8,128)(2,1)S(1)}, bf16[2,16,2560]{2,1,0:T(8,128)(2,1)S(1)}, u32[]{:S(2)}, u32[]{:S(2)}) collective-permute-start(bf16[2,16,2560]{2,1,0:T(8,128)(2,1)S(1)} %get-tuple-element.55), channel_id=1, source_target_pairs={{0,16},{8,24},{16,0},{24,8},{1,17},{9,25},{17,1},{25,9},{2,18},{10... | collective-permute-start | bytes 491528 | tf_op jit(solution)/shard_map/ppermute | solution.py:47
  51.8 7.1 %collective-permute-start.13 = (bf16[4,16,2560]{2,1,0:T(8,128)(2,1)S(1)}, bf16[4,16,2560]{2,1,0:T(8,128)(2,1)S(1)}, u32[]{:S(2)}, u32[]{:S(2)}) collective-permute-start(bf16[4,16,2560]{2,1,0:T(8,128)(2,1)S(1)} %join.1), channel_id=1, source_target_pairs={{0,16},{8,24},{16,0},{24,8},{1,17},{9,25},{17,1},{25,9},{2,18},{10... | collective-permute-start | bytes 983048 | tf_op jit(solution)/shard_map/ppermute | solution.py:47
  54.0 7.1 %collective-permute-start.16 = (bf16[4,16,2560]{2,1,0:T(8,128)(2,1)S(1)}, bf16[4,16,2560]{2,1,0:T(8,128)(2,1)S(1)}, u32[]{:S(2)}, u32[]{:S(2)}) collective-permute-start(bf16[4,16,2560]{2,1,0:T(8,128)(2,1)S(1)} %pad_maximum_fusion.2), channel_id=1, source_target_pairs={{0,1},{1,0},{2,3},{3,2},{4,5},{5,4},{6,7},{7,6},{8,9},{9,8},{10,11... | collective-permute-start | bytes 983048 | tf_op jit(solution)/shard_map/ppermute | solution.py:47
  59.0 2.3 %collective-permute-start.14 = (bf16[128,2560]{1,0:T(8,128)(2,1)S(1)}, bf16[128,2560]{1,0:T(8,128)(2,1)S(1)}, u32[]{:S(2)}, u32[]{:S(2)}) collective-permute-start(bf16[128,2560]{1,0:T(8,128)(2,1)S(1)} %bitcast.5), channel_id=1, source_target_pairs={{0,8},{8,0},{16,24},{24,16},{1,9},{9,1},{17,25},{25,17},{2,10},{10... | collective-permute-start | bytes 1966088 | tf_op jit(solution)/shard_map/ppermute | solution.py:47
  61.3 4.6 %collective-permute-start.17 = (bf16[128,2560]{1,0:T(8,128)(2,1)S(1)}, bf16[128,2560]{1,0:T(8,128)(2,1)S(1)}, u32[]{:S(2)}, u32[]{:S(2)}) collective-permute-start(bf16[128,2560]{1,0:T(8,128)(2,1)S(1)} %bitcast.3), channel_id=1, source_target_pairs={{0,8},{8,0},{16,24},{24,16},{1,9},{9,1},{17,25},{25,17},{2,10},{10... | collective-permute-start | bytes 1966088 | tf_op jit(solution)/shard_map/ppermute | solution.py:47
  70.9 1.4 %collective-permute-start.18 = (f32[16,1,128]{2,1,0:T(1,128)S(1)}, f32[16,1,128]{2,1,0:T(1,128)S(1)}, u32[]{:S(2)}, u32[]{:S(2)}) collective-permute-start(f32[16,1,128]{2,1,0:T(1,128)S(1)} %get-tuple-element.58), channel_id=1, source_target_pairs={{0,8},{8,0},{16,24},{24,16},{1,9},{9,1},{17,25},{25,17},{2,10},{10... | collective-permute-start | bytes 24584 | tf_op jit(solution)/shard_map/ppermute | solution.py:47

commit v13 on v9

--- a/solution.py
+++ b/solution.py
@@ -243,7 +243,8 @@
             send_right_ref[i, :, columns] = partial_ref[me ^ (i + 2)].astype(BF16)
 
 
-def fold_kernel(keep_ref, got_ref, own_ref, send_ref):
+def fold_kernel(keep_ref, got_ref, *refs):
+    own_ref, send_ref = refs[-2:]
     own_ref[...] = keep_ref[0] + got_ref[0].astype(F32)
     send_ref[...] = (keep_ref[1] + got_ref[1].astype(F32)).astype(BF16)
 
@@ -270,38 +271,44 @@
         copy.wait()
 
 
-def column_kernel(count, *refs):
-    terms, out_refs = refs[:count], refs[-2:]
-    width = out_refs[0].shape[2]
-    for i, ref in enumerate(terms):
-        for half, out_ref in enumerate(out_refs):
-            out_ref[i] = ref[:, half * width : (half + 1) * width]
-
-
-def norm_kernel(residual_ref, gain_ref, first_gate_ref, second_gate_ref, own_ref, got_ref, out_ref):
+def cut_kernel(*refs):
+    left_ref, right_ref = refs[-2:]
+    count, width = left_ref.shape[0], left_ref.shape[2]
+    for i in range(count):
+        left_ref[i] = refs[i][:, :width]
+    for i in range(right_ref.shape[0]):
+        right_ref[i] = refs[count + i][:, width:]
+
+
+def tokens_kernel(count, split, *refs):
+    blocks, out_refs = refs[:count], refs[-2:]
+    rows = blocks[0].shape[0]
+    width = out_refs[0].shape[1]
+    for half, (stacks, out_ref) in enumerate(zip((refs[count:split], refs[split:-2]), out_refs)):
+        for i, ref in enumerate(blocks):
+            out_ref[i * rows : (i + 1) * rows] = ref[:, half * width : (half + 1) * width]
+        place = count * rows
+        for ref in stacks:
+            for i in range(ref.shape[0]):
+                out_ref[place : place + rows] = ref[i]
+                place += rows
+
+
+def norm_kernel(residual_ref, gain_ref, gate_ref, own_ref, got_ref, out_ref):
     hidden = residual_ref[lax.axis_index("tensor") % 4].astype(F32)
     hidden = hidden + (own_ref[...] + got_ref[...].astype(F32))
     squares = jnp.mean(hidden * hidden, axis=-1, keepdims=True)
     out_ref[...] = (hidden * lax.rsqrt(squares + 1e-06) * gain_ref[...].astype(F32)).astype(BF16)
 
 
-def join_kernel(count, *refs):
-    out_ref = refs[-1]
-    start = 0
-    for ref in refs[:count]:
-        out_ref[start : start + ref.shape[0]] = ref[...]
-        start += ref.shape[0]
-
-
 def quarter_dots(x_ref, weight_refs, columns):
-    depth = weight_refs[0].shape[0]
-    return functools.reduce(
-        jnp.add,
-        [
-            jnp.dot(x_ref[:, i * depth : (i + 1) * depth], ref[:, columns], preferred_element_type=F32)
-            for i, ref in enumerate(weight_refs)
-        ],
-    )
+    start, total = 0, None
+    for ref in weight_refs:
+        stop = start + ref.shape[0]
+        part = jnp.dot(x_ref[:, start:stop], ref[:, columns], preferred_element_type=F32)
+        total = part if total is None else total + part
+        start = stop
+    return total
 
 
 def first_kernel(
@@ -526,25 +533,27 @@
         name="project",
     )(stored(prompt_of), *map(held, (own, *got)), held(weight))
 
-    def add(kernel, name, size, *operands):
+    def add(kernel, name, size, *operands, gates=()):
         return pl.pallas_call(
             kernel,
             out_shape=[jax.ShapeDtypeStruct(size, F32), jax.ShapeDtypeStruct(size, BF16)],
-            in_specs=[vmem()] * len(operands),
+            in_specs=[vmem()] * len(operands) + [anywhere()] * len(gates),
             out_specs=[vmem()] * 2,
             compiler_params=params(2),
             name=name,
-        )(*map(held, operands))
+        )(*map(held, operands), *gates)
+
+    early_rows = 1024 if half > 1024 else half // 2
+    first_quarter = fetch(lm_weight, 0, early_rows, send_left)
 
     got_left = swap(send_left, "tensor", 1, tensor_size)
     got_right = swap(send_right, "tensor", 2, tensor_size)
-    left, send_left = add(fold_kernel, "fold_left", (block, half), keep_left, got_left)
+    left, send_left = add(fold_kernel, "fold_left", (block, half), keep_left, got_left, gates=(first_quarter,))
     right, send_right = add(fold_kernel, "fold_right", (block, half), keep_right, got_right)
     got_left = swap(send_left, "tensor", 2, tensor_size)
     got_right = swap(send_right, "tensor", 1, tensor_size)
     total, send = add(side_kernel, "side", (block, depth), left, got_left, right, got_right)
-    first_quarter = fetch(lm_weight, 0, quarter, send)
-    second_quarter = fetch(lm_weight, quarter, quarter, send)
+    second_quarter = fetch(lm_weight, early_rows, half - early_rows, send)
     far = 4
     while 2 * far < tensor_size:
         total, send = add(
@@ -554,55 +563,54 @@
     normed = pl.pallas_call(
         norm_kernel,
         out_shape=jax.ShapeDtypeStruct((block, depth), BF16),
-        in_specs=[vmem()] * 2 + [anywhere()] * 2 + [vmem()] * 2,
+        in_specs=[vmem()] * 2 + [anywhere()] + [vmem()] * 2,
         out_specs=vmem(),
         compiler_params=params(4),
         name="norm",
     )(
         *map(held, (residual.reshape(4, block, depth), norm_gain[None])),
-        first_quarter,
         second_quarter,
         *map(held, (total, swap(send, "tensor", far, tensor_size))),
     )
 
-    order = [0, 2]
-    here = [(g, x) for g in [0] + above for x in (0, 1)]
-    column = [normed, swap(normed, "tensor", 2, tensor_size)]
-    columns = pl.pallas_call(
-        functools.partial(column_kernel, len(column)),
-        out_shape=[jax.ShapeDtypeStruct((len(column), block, half), BF16)] * 2,
-        in_specs=[vmem()] * len(column),
+    def around(x):
+        along = [swap(x, "group", d, group_size) for d in above]
+        return swap(x, "tensor", 1, tensor_size), along
+
+    sides = [around(normed)]
+    near = [normed, swap(normed, "tensor", 2, tensor_size)]
+    sides.append(around(near[1]))
+    third = fetch(lm_weight, 2 * quarter, quarter, near[1])
+
+    across = [x for x, _ in sides]
+    along = [ys[i] for i in range(len(above)) for _, ys in sides]
+    left, right = pl.pallas_call(
+        cut_kernel,
+        out_shape=[
+            jax.ShapeDtypeStruct((len(pieces), block, half), BF16) for pieces in (across, along)
+        ],
+        in_specs=[vmem()] * (len(across) + len(along)) + [anywhere()],
         out_specs=[vmem()] * 2,
         compiler_params=params(2),
-        name="column",
-    )(*map(held, column))
-
-    def join(pieces, gate):
-        blocks = sum(x.shape[0] for x in pieces)
-        return pl.pallas_call(
-            functools.partial(join_kernel, len(pieces)),
-            out_shape=jax.ShapeDtypeStruct((blocks, block, half), BF16),
-            in_specs=[vmem()] * len(pieces) + [anywhere()],
-            out_specs=vmem(),
-            compiler_params=params(2),
-            name="join",
-        )(*map(held, pieces), gate)
-
-    left, right = columns
-    got_left = swap(left, "tensor", 1, tensor_size)
-    third = fetch(lm_weight, 2 * quarter, quarter, left)
-    right = [right] + [swap(right, "group", d, group_size) for d in above]
-    left = join([left, got_left], third)
-    got_left = [swap(left, "group", d, group_size) for d in above]
-    across = swap(jnp.concatenate(right), "tensor", 1, tensor_size)
-    across = jnp.split(across, len(right))
-    right = [x for pair in zip(right, across) for x in pair]
-    halves = []
-    for tokens in (jnp.concatenate([left] + got_left), jnp.concatenate(right)):
-        tokens = tokens.reshape(-1, half)
-        halves.append((tokens, swap(tokens, "group", 1, group_size)))
+        name="cut",
+    )(*map(held, (*across, *along)), third)
+    left = [swap(left, "group", d, group_size) for d in above]
+    right = [swap(right, "tensor", 1, tensor_size)]
+    whole = near + across + along
+    count = (len(whole) + len(across) * len(above)) * block
+    halves = pl.pallas_call(
+        functools.partial(tokens_kernel, len(whole), len(whole) + len(left)),
+        out_shape=[jax.ShapeDtypeStruct((count, half), BF16)] * 2,
+        in_specs=[vmem()] * (len(whole) + len(left) + len(right)),
+        out_specs=[vmem()] * 2,
+        compiler_params=params(2),
+        name="tokens",
+    )(*map(held, (*whole, *left, *right)))
+    halves = [(tokens, swap(tokens, "group", 1, group_size)) for tokens in halves]
+    here = [(0, 0), (0, 1)] + [(g, 0) for g in above] + [(g, 1) for g in above]
+    order = [0, 2]
     spots = [(g + c, t + x) for c in (0, 1) for g, x in here for t in order]
-    total_rows = 2 * tokens.shape[0]
+    total_rows = 2 * count
     narrow = 1536 if vocab % 1536 == 0 else vocab
     limit = 10 if total_rows <= 256 else 24
     work = 2 * total_rows * (half) * vocab

time: 81.9 us -> 82.7 us (level)
  waiting for transfers between devices: 19.5 us -> 16.4 us
  blocking collectives: 10.2 us -> 12.7 us
  starting transfers between devices: 21.1 us -> 22.7 us
    ppermute x18 -> x20, waiting for transfers between devices: 19.5 us -> 16.4 us  [swap(): return lax.ppermute(x, axis, [(i, i ^ distance) for i in range(size)])]
    all_to_all x1, blocking collectives: 10.2 us -> 12.7 us  [local(): stats = lax.all_to_all(stats, ('group', 'tensor'), 0, 0, tiled=True)]
    ppermute x18 -> x20, starting transfers between devices: 21.1 us -> 22.7 us  [swap(): return lax.ppermute(x, axis, [(i, i ^ distance) for i in range(size)])]
  transfers between devices with their start and end apart: 18 -> 20, of which waited for: 9 -> 11; matrix products, arithmetic and copies ran while one was open for 1% -> 1% of each run, Pallas kernels for 24% -> 24%
where the time goes in v13:
time: 82.7 us; the launch traced here: 82.5 us
  Pallas kernels  29.6 us (36%)
  starting transfers between devices  22.7 us (27%)
  waiting for transfers between devices  16.4 us (20%)
  blocking collectives  12.7 us (15%)
  local copies, waits for them, and re-layouts  0.9 us (1%)
    ppermute x20, starting transfers between devices, swap(): return lax.ppermute(x, axis, [(i, i ^ distance) for i in range(size)])  22.7 us
    ppermute x20, waiting for transfers between devices, swap(): return lax.ppermute(x, axis, [(i, i ^ distance) for i in range(size)])  16.4 us
    all_to_all x1, blocking collectives, local(): stats = lax.all_to_all(stats, ('group', 'tensor'), 0, 0, tiled=True)  12.7 us
    pallas_call x3, Pallas kernels, fetch(): pl.pallas_call(functools.partial(fetch_kernel, start), out_shape=pltpu.VM...  10.1 us
    pallas_call x1, Pallas kernels, local(): pl.pallas_call(functools.partial(logits_kernel, vocab, spots, tensor_size...  5 us
    pallas_call x1, Pallas kernels, local(): pl.pallas_call(functools.partial(first_kernel, narrow), out_shape=[pltpu....  4.52 us
    pallas_call x1, Pallas kernels, local(): pl.pallas_call(functools.partial(own_kernel, heads, seq, share), out_shap...  3.54 us
    pallas_call x1, Pallas kernels, local(): pl.pallas_call(functools.partial(project_kernel, heads, seq, wide, group_...  3.27 us
  transfers between devices with their start and end apart: 20, of which 11 were waited for; matrix products, arithmetic and copies ran while one was open for 1% of the time, Pallas kernels for 24%

profile of v13, /device:TPU:0, one launch (start us, length us, event | category | flops | bytes accessed | tf_op | source)
XLA Modules:
  0.0 82.5 jit_solution(3137319529517386814)
XLA Ops:
  0.0 3.0 %collective-permute-start = (bf16[64,512]{1,0:T(8,128)(2,1)}, bf16[64,512]{1,0:T(8,128)(2,1)S(1)}, u32[]{:S(2)}, u32[]{:S(2)}) collective-permute-start(bf16[64,512]{1,0:T(8,128)(2,1)} %refs_0_.1), channel_id=1, source_target_pairs={{0,16},{8,24},{16,0},{24,8},{1,17},{9,25},{17,1},{25,9},{2,18},{10... | collective-permute-start | bytes 196616 | tf_op jit(solution)/shard_map/ppermute | solution.py:47
  3.0 0.9 %reshape.8.refs_1_.target_ref = s32[32,8,1]{2,1,0:T(8,128)S(1)} reshape(s32[256]{0:T(256)} %param.23) | data formatting | bytes 2048 | tf_op jit(solution)/shard_map/reshape | solution.py:438
  3.9 1.6 %collective-permute-done.refs_0_ = bf16[64,512]{1,0:T(8,128)(2,1)S(1)} collective-permute-done((bf16[64,512]{1,0:T(8,128)(2,1)}, bf16[64,512]{1,0:T(8,128)(2,1)S(1)}, u32[]{:S(2)}, u32[]{:S(2)}) %collective-permute-start) | collective-permute-done | bytes 65568 | tf_op jit(solution)/shard_map/ppermute | solution.py:47
  5.4 1.4 %load.1 = (bf16[64,512]{1,0:T(8,128)(2,1)S(1)}, bf16[64,512]{1,0:T(8,128)(2,1)S(1)}, bf16[64,512]{1,0:T(8,128)(2,1)S(1)}, bf16[512,512]{1,0:T(8,128)(2,1)S(1)}, bf16[512,512]{1,0:T(8,128)(2,1)S(1)}) custom-call(bf16[64,512]{1,0:T(8,128)(2,1)S(1)} %pass.1.gate_ref.refs_1_, bf16[64,512]{1,0:T(8,128)(2,1)} %refs_0_.1, bf16[64,512]{1,0:T(8,128)(2,1)} %refs_1_.1, ...), custom_call_target="tpu_custom_call" | custom-call | bytes 2097152 | tf_op jit(solution)/shard_map/load/pallas_call | solution.py:456
  6.8 0.9 %prefix_attention.1 = (bf16[64,640]{1,0:T(8,128)(2,1)S(1)}, bf16[64,640]{1,0:T(8,128)(2,1)S(1)}, bf16[64,640]{1,0:T(8,128)(2,1)S(1)}) custom-call(bf16[64,512]{1,0:T(8,128)(2,1)S(1)} %collective-permute-done.1.refs_0_, bf16[64,512]{1,0:T(8,128)(2,1)S(1)} %pass.1.gate_ref.refs_1_, bf16[64,512]{1,0:T(8,128)(2,1)S(1)} %collective-permute-done.2.refs_2_, ...), custom_call_target="tpu_custom_call" | custom-call | tf_op jit(solution)/shard_map/prefix_attention/pallas_call | solution.py:467
  7.7 2.1 %collective-permute-start.4 = (bf16[64,640]{1,0:T(8,128)(2,1)S(1)}, bf16[64,640]{1,0:T(8,128)(2,1)S(1)}, u32[]{:S(2)}, u32[]{:S(2)}) collective-permute-start(bf16[64,640]{1,0:T(8,128)(2,1)S(1)} %get-tuple-element.40), channel_id=1, source_target_pairs={{0,16},{8,24},{16,0},{24,8},{1,17},{9,25},{17,1},{25,9},{2,18},{10... | collective-permute-start | bytes 245768 | tf_op jit(solution)/shard_map/ppermute | solution.py:47
  10.0 3.5 %own_attention.1 = (f32[64,640]{1,0:T(8,128)S(1)}, f32[8,128]{1,0:T(8,128)S(1)}, bf16[512,5120]{1,0:T(8,128)(2,1)S(1)}) custom-call(s32[2]{0:T(128)} %lengths_ref.1, s32[2]{0:T(128)} %prompt_ref.3, bf16[64,512]{1,0:T(8,128)(2,1)S(1)} %get-tuple-element.32.q_ref, bf16[64,512]{1,0:T(8,128)(2,1)S(1)} %get-tuple-element.33.rk_ref, ...), custom_call_target="tpu_custom_call" | custom-call | bytes 8388608 | tf_op jit(solution)/shard_map/own_attention/pallas_call | solution.py:476
  13.6 0.7 collective-permute-done.3.refs_0_
  14.3 3.3 %project.1 = (bf16[2,16,2560]{2,1,0:T(8,128)(2,1)S(1)}, f32[2,16,2560]{2,1,0:T(8,128)S(1)}, bf16[2,16,2560]{2,1,0:T(8,128)(2,1)S(1)}, f32[2,16,2560]{2,1,0:T(8,128)S(1)}) custom-call(s32[2]{0:T(128)} %prompt_ref.3, f32[64,640]{1,0:T(8,128)S(1)} %get-tuple-element.39.own_ref, bf16[64,640]{1,0:T(8,128)(2,1)S(1)} %collective-permute-done.3.refs_0_, ...), custom_call_target="tpu_custom_call" | custom-call | tf_op jit(solution)/shard_map/project/pallas_call | solution.py:519
  17.6 1.9 %collective-permute-start.8 = (bf16[2,16,2560]{2,1,0:T(8,128)(2,1)S(1)}, bf16[2,16,2560]{2,1,0:T(8,128)(2,1)S(1)}, u32[]{:S(2)}, u32[]{:S(2)}) collective-permute-start(bf16[2,16,2560]{2,1,0:T(8,128)(2,1)S(1)} %get-tuple-element.48), channel_id=1, source_target_pairs={{0,2},{1,3},{2,0},{3,1},{4,6},{5,7},{6,4},{7,5},{8,10},{9,11},{10,... | collective-permute-start | bytes 491528 | tf_op jit(solution)/shard_map/ppermute | solution.py:47
  19.5 1.5 %collective-permute-start.6 = (bf16[2,16,2560]{2,1,0:T(8,128)(2,1)S(1)}, bf16[2,16,2560]{2,1,0:T(8,128)(2,1)S(1)}, u32[]{:S(2)}, u32[]{:S(2)}) collective-permute-start(bf16[2,16,2560]{2,1,0:T(8,128)(2,1)S(1)} %get-tuple-element.44.gate_ref), channel_id=1, source_target_pairs={{0,1},{1,0},{2,3},{3,2},{4,5},{5,4},{6,7},{7,6},{8,9},{9,8},{10,11... | collective-permute-start | bytes 491528 | tf_op jit(solution)/shard_map/ppermute | solution.py:47
  21.0 2.9 %fetch.3.refs_0_.weight_ref = bf16[1024,3072]{1,0:T(8,128)(2,1)S(1)} custom-call(bf16[5120,3072]{1,0:T(8,128)(2,1)} %source_ref.9, bf16[2,16,2560]{2,1,0:T(8,128)(2,1)S(1)} %get-tuple-element.44.gate_ref), custom_call_target="tpu_custom_call" | custom-call | bytes 6291456 | tf_op jit(solution)/shard_map/fetch/pallas_call | solution.py:503
  24.0 1.7 %collective-permute-start.9 = (bf16[16,2560]{1,0:T(8,128)(2,1)S(1)}, bf16[16,2560]{1,0:T(8,128)(2,1)S(1)}, u32[]{:S(2)}, u32[]{:S(2)}) collective-permute-start(bf16[16,2560]{1,0:T(8,128)(2,1)S(1)} %get-tuple-element.50), channel_id=1, source_target_pairs={{0,1},{1,0},{2,3},{3,2},{4,5},{5,4},{6,7},{7,6},{8,9},{9,8},{10,11... | collective-permute-start | bytes 245768 | tf_op jit(solution)/shard_map/ppermute | solution.py:47
  25.8 1.6 %collective-permute-start.7 = (bf16[16,2560]{1,0:T(8,128)(2,1)S(1)}, bf16[16,2560]{1,0:T(8,128)(2,1)S(1)}, u32[]{:S(2)}, u32[]{:S(2)}) collective-permute-start(bf16[16,2560]{1,0:T(8,128)(2,1)S(1)} %get-tuple-element.46), channel_id=1, source_target_pairs={{0,2},{1,3},{2,0},{3,1},{4,6},{5,7},{6,4},{7,5},{8,10},{9,11},{10,... | collective-permute-start | bytes 245768 | tf_op jit(solution)/shard_map/ppermute | solution.py:47
  27.4 1.1 %collective-permute-done.9.got_right_ref = bf16[16,2560]{1,0:T(8,128)(2,1)S(1)} collective-permute-done((bf16[16,2560]{1,0:T(8,128)(2,1)S(1)}, bf16[16,2560]{1,0:T(8,128)(2,1)S(1)}, u32[]{:S(2)}, u32[]{:S(2)}) %collective-permute-start.9) | collective-permute-done | bytes 81952 | tf_op jit(solution)/shard_map/ppermute | solution.py:47
  28.5 1.7 %collective-permute-done.7.got_left_ref = bf16[16,2560]{1,0:T(8,128)(2,1)S(1)} collective-permute-done((bf16[16,2560]{1,0:T(8,128)(2,1)S(1)}, bf16[16,2560]{1,0:T(8,128)(2,1)S(1)}, u32[]{:S(2)}, u32[]{:S(2)}) %collective-permute-start.7) | collective-permute-done | bytes 81952 | tf_op jit(solution)/shard_map/ppermute | solution.py:47
  30.3 2.7 %collective-permute-start.10 = (bf16[16,5120]{1,0:T(8,128)(2,1)S(1)}, bf16[16,5120]{1,0:T(8,128)(2,1)S(1)}, u32[]{:S(2)}, u32[]{:S(2)}) collective-permute-start(bf16[16,5120]{1,0:T(8,128)(2,1)S(1)} %get-tuple-element.51.gate_ref), channel_id=1, source_target_pairs={{0,4},{1,5},{2,6},{3,7},{4,0},{5,1},{6,2},{7,3},{8,12},{9,13},{10,... | collective-permute-start | bytes 491528 | tf_op jit(solution)/shard_map/ppermute | solution.py:47
  33.0 3.9 %fetch.4.gate_ref.next_ref = bf16[1536,3072]{1,0:T(8,128)(2,1)S(1)} custom-call(bf16[5120,3072]{1,0:T(8,128)(2,1)} %source_ref.9, bf16[16,5120]{1,0:T(8,128)(2,1)S(1)} %get-tuple-element.51.gate_ref), custom_call_target="tpu_custom_call" | custom-call | bytes 9437184 | tf_op jit(solution)/shard_map/fetch/pallas_call | solution.py:503
  36.9 2.2 %collective-permute-done.10.got_ref = bf16[16,5120]{1,0:T(8,128)(2,1)S(1)} collective-permute-done((bf16[16,5120]{1,0:T(8,128)(2,1)S(1)}, bf16[16,5120]{1,0:T(8,128)(2,1)S(1)}, u32[]{:S(2)}, u32[]{:S(2)}) %collective-permute-start.10) | collective-permute-done | bytes 163872 | tf_op jit(solution)/shard_map/ppermute | solution.py:47
  39.3 0.7 collective-permute-start.11
  40.0 1.6 %collective-permute-start.14 = (bf16[16,5120]{1,0:T(8,128)(2,1)S(1)}, bf16[16,5120]{1,0:T(8,128)(2,1)S(1)}, u32[]{:S(2)}, u32[]{:S(2)}) collective-permute-start(bf16[16,5120]{1,0:T(8,128)(2,1)S(1)} %norm.1.refs_0_), channel_id=1, source_target_pairs={{0,16},{8,24},{16,0},{24,8},{1,17},{9,25},{17,1},{25,9},{2,18},{10... | collective-permute-start | bytes 491528 | tf_op jit(solution)/shard_map/ppermute | solution.py:47
  42.2 2.5 %collective-permute-done.11.gate_ref.refs_1_ = bf16[16,5120]{1,0:T(8,128)(2,1)S(1)} collective-permute-done((bf16[16,5120]{1,0:T(8,128)(2,1)S(1)}, bf16[16,5120]{1,0:T(8,128)(2,1)S(1)}, u32[]{:S(2)}, u32[]{:S(2)}) %collective-permute-start.11) | collective-permute-done | bytes 163872 | tf_op jit(solution)/shard_map/ppermute | solution.py:47
  44.6 1.6 %collective-permute-start.15 = (bf16[16,5120]{1,0:T(8,128)(2,1)S(1)}, bf16[16,5120]{1,0:T(8,128)(2,1)S(1)}, u32[]{:S(2)}, u32[]{:S(2)}) collective-permute-start(bf16[16,5120]{1,0:T(8,128)(2,1)S(1)} %collective-permute-done.11.gate_ref.refs_1_), channel_id=1, source_target_pairs={{0,16},{8,24},{16,0},{24,8},{1,17},{9,25},{17,1},{25,9},{2,18},{10... | collective-permute-start | bytes 491528 | tf_op jit(solution)/shard_map/ppermute | solution.py:47
  46.3 1.2 %collective-permute-start.13 = (bf16[16,5120]{1,0:T(8,128)(2,1)S(1)}, bf16[16,5120]{1,0:T(8,128)(2,1)S(1)}, u32[]{:S(2)}, u32[]{:S(2)}) collective-permute-start(bf16[16,5120]{1,0:T(8,128)(2,1)S(1)} %collective-permute-done.11.gate_ref.refs_1_), channel_id=1, source_target_pairs={{0,1},{1,0},{2,3},{3,2},{4,5},{5,4},{6,7},{7,6},{8,9},{9,8},{10,11... | collective-permute-start | bytes 491528 | tf_op jit(solution)/shard_map/ppermute | solution.py:47
  47.4 3.3 %fetch.5.refs_4_.weight_ref = bf16[1280,3072]{1,0:T(8,128)(2,1)S(1)} custom-call(bf16[5120,3072]{1,0:T(8,128)(2,1)} %source_ref.9, bf16[16,5120]{1,0:T(8,128)(2,1)S(1)} %collective-permute-done.11.gate_ref.refs_1_), custom_call_target="tpu_custom_call" | custom-call | bytes 7864320 | tf_op jit(solution)/shard_map/fetch/pallas_call | solution.py:503
  50.8 0.8 collective-permute-done.13.refs_1_.refs_3_
  52.1 1.3 %collective-permute-start.17 = (bf16[2,16,2560]{2,1,0:T(8,128)(2,1)S(1)}, bf16[2,16,2560]{2,1,0:T(8,128)(2,1)S(1)}, u32[]{:S(2)}, u32[]{:S(2)}) collective-permute-start(bf16[2,16,2560]{2,1,0:T(8,128)(2,1)S(1)} %get-tuple-element.54), channel_id=1, source_target_pairs={{0,1},{1,0},{2,3},{3,2},{4,5},{5,4},{6,7},{7,6},{8,9},{9,8},{10,11... | collective-permute-start | bytes 491528 | tf_op jit(solution)/shard_map/ppermute | solution.py:47
  53.3 3.7 %collective-permute-done.16.refs_6_ = bf16[2,16,2560]{2,1,0:T(8,128)(2,1)S(1)} collective-permute-done((bf16[2,16,2560]{2,1,0:T(8,128)(2,1)S(1)}, bf16[2,16,2560]{2,1,0:T(8,128)(2,1)S(1)}, u32[]{:S(2)}, u32[]{:S(2)}) %collective-permute-start.16) | collective-permute-done | bytes 163872 | tf_op jit(solution)/shard_map/ppermute | solution.py:47
  58.1 1.6 %collective-permute-done.18.right_ref = bf16[128,2560]{1,0:T(8,128)(2,1)S(1)} collective-permute-done((bf16[128,2560]{1,0:T(8,128)(2,1)S(1)}, bf16[128,2560]{1,0:T(8,128)(2,1)S(1)}, u32[]{:S(2)}, u32[]{:S(2)}) %collective-permute-start.18) | collective-permute-done | bytes 655392 | tf_op jit(solution)/shard_map/ppermute | solution.py:47
  59.7 4.5 %logits_first.1 = (f32[256,3072]{1,0:T(8,128)S(1)}, bf16[1280,3072]{1,0:T(8,128)(2,1)S(1)}) custom-call(bf16[128,2560]{1,0:T(8,128)(2,1)S(1)} %get-tuple-element.55.left_ref, bf16[128,2560]{1,0:T(8,128)(2,1)S(1)} %collective-permute-done.18.right_ref, bf16[1024,3072]{1,0:T(8,128)(2,1)S(1)} %fetch.3.refs_0_.weight_ref, ...), custom_call_target="tpu_custom_call" | custom-call | flops 4026531840 | tf_op jit(solution)/shard_map/logits_first/pallas_call | solution.py:617
  64.2 5.0 %logits.1 = f32[32,1,128]{2,1,0:T(1,128)S(1)} custom-call(f32[256,3072]{1,0:T(8,128)S(1)} %get-tuple-element.56.sum_in_ref, bf16[128,2560]{1,0:T(8,128)(2,1)S(1)} %get-tuple-element.57.left_ref, bf16[128,2560]{1,0:T(8,128)(2,1)S(1)} %collective-permute-done.19.right_ref, s32[32,8,1]{2,1,0:T(8,128)S(1)} %reshape.8.refs_1_.target_ref, ...), custom_call_target="tpu_custom_call" | custom-call | flops 4026531840 | tf_op jit(solution)/shard_map/logits/pallas_call | solution.py:630
  69.2 12.7 %all_to_all.5.stats_ref = f32[32,1,128]{2,1,0:T(1,128)S(1)} all-to-all(f32[32,1,128]{2,1,0:T(1,128)S(1)} %logits.1), channel_id=1, replica_groups=mesh['group'=4,'tensor'=8] {'group','tensor'}, dimensions={0} | all-to-all | bytes 32768 | tf_op jit(solution)/shard_map/all_to_all | solution.py:643
  (32 shorter events, 3.5 us)
Async XLA Ops:
  0.0 5.4 %collective-permute-start = (bf16[64,512]{1,0:T(8,128)(2,1)}, bf16[64,512]{1,0:T(8,128)(2,1)S(1)}, u32[]{:S(2)}, u32[]{:S(2)}) collective-permute-start(bf16[64,512]{1,0:T(8,128)(2,1)} %refs_0_.1), channel_id=1, source_target_pairs={{0,16},{8,24},{16,0},{24,8},{1,17},{9,25},{17,1},{25,9},{2,18},{10... | collective-permute-start | bytes 196616 | tf_op jit(solution)/shard_map/ppermute | solution.py:47
  3.0 3.8 %collective-permute-start.2 = (bf16[64,512]{1,0:T(8,128)(2,1)}, bf16[64,512]{1,0:T(8,128)(2,1)S(1)}, u32[]{:S(2)}, u32[]{:S(2)}) collective-permute-start(bf16[64,512]{1,0:T(8,128)(2,1)} %refs_0_.1), channel_id=1, source_target_pairs={{0,8},{8,0},{16,24},{24,16},{1,9},{9,1},{17,25},{25,17},{2,10},{10... | collective-permute-start | bytes 196616 | tf_op jit(solution)/shard_map/ppermute | solution.py:47
  5.4 1.4 %collective-permute-start.1 = (bf16[64,512]{1,0:T(8,128)(2,1)S(1)}, bf16[64,512]{1,0:T(8,128)(2,1)S(1)}, u32[]{:S(2)}, u32[]{:S(2)}) collective-permute-start(bf16[64,512]{1,0:T(8,128)(2,1)S(1)} %pass.1.gate_ref.refs_1_), channel_id=1, source_target_pairs={{0,8},{8,0},{16,24},{24,16},{1,9},{9,1},{17,25},{25,17},{2,10},{10... | collective-permute-start | bytes 196616 | tf_op jit(solution)/shard_map/ppermute | solution.py:47
  7.7 5.9 %collective-permute-start.4 = (bf16[64,640]{1,0:T(8,128)(2,1)S(1)}, bf16[64,640]{1,0:T(8,128)(2,1)S(1)}, u32[]{:S(2)}, u32[]{:S(2)}) collective-permute-start(bf16[64,640]{1,0:T(8,128)(2,1)S(1)} %get-tuple-element.40), channel_id=1, source_target_pairs={{0,16},{8,24},{16,0},{24,8},{1,17},{9,25},{17,1},{25,9},{2,18},{10... | collective-permute-start | bytes 245768 | tf_op jit(solution)/shard_map/ppermute | solution.py:47
  9.8 3.8 %collective-permute-start.5 = (bf16[64,640]{1,0:T(8,128)(2,1)S(1)}, bf16[64,640]{1,0:T(8,128)(2,1)S(1)}, u32[]{:S(2)}, u32[]{:S(2)}) collective-permute-start(bf16[64,640]{1,0:T(8,128)(2,1)S(1)} %get-tuple-element.41), channel_id=1, source_target_pairs={{0,8},{8,0},{16,24},{24,16},{1,9},{9,1},{17,25},{25,17},{2,10},{10... | collective-permute-start | bytes 245768 | tf_op jit(solution)/shard_map/ppermute | solution.py:47
  10.0 4.3 %collective-permute-start.3 = (bf16[64,640]{1,0:T(8,128)(2,1)S(1)}, bf16[64,640]{1,0:T(8,128)(2,1)S(1)}, u32[]{:S(2)}, u32[]{:S(2)}) collective-permute-start(bf16[64,640]{1,0:T(8,128)(2,1)S(1)} %get-tuple-element.37.gate_ref), channel_id=1, source_target_pairs={{0,24},{8,16},{16,8},{24,0},{1,25},{9,17},{17,9},{25,1},{2,26},{10... | collective-permute-start | bytes 245768 | tf_op jit(solution)/shard_map/ppermute | solution.py:47
  17.6 6.4 %collective-permute-start.8 = (bf16[2,16,2560]{2,1,0:T(8,128)(2,1)S(1)}, bf16[2,16,2560]{2,1,0:T(8,128)(2,1)S(1)}, u32[]{:S(2)}, u32[]{:S(2)}) collective-permute-start(bf16[2,16,2560]{2,1,0:T(8,128)(2,1)S(1)} %get-tuple-element.48), channel_id=1, source_target_pairs={{0,2},{1,3},{2,0},{3,1},{4,6},{5,7},{6,4},{7,5},{8,10},{9,11},{10,... | collective-permute-start | bytes 491528 | tf_op jit(solution)/shard_map/ppermute | solution.py:47
  19.5 13.5 %copy-start.1 = (bf16[5120]{0:T(1024)(128)(2,1)S(1)}, bf16[5120]{0:T(1024)(128)(2,1)}, u32[]{:S(2)}) copy-start(bf16[5120]{0:T(1024)(128)(2,1)} %param.21) | copy-start | bytes 30724
  19.5 6.2 %collective-permute-start.6 = (bf16[2,16,2560]{2,1,0:T(8,128)(2,1)S(1)}, bf16[2,16,2560]{2,1,0:T(8,128)(2,1)S(1)}, u32[]{:S(2)}, u32[]{:S(2)}) collective-permute-start(bf16[2,16,2560]{2,1,0:T(8,128)(2,1)S(1)} %get-tuple-element.44.gate_ref), channel_id=1, source_target_pairs={{0,1},{1,0},{2,3},{3,2},{4,5},{5,4},{6,7},{7,6},{8,9},{9,8},{10,11... | collective-permute-start | bytes 491528 | tf_op jit(solution)/shard_map/ppermute | solution.py:47
  24.0 4.5 %collective-permute-start.9 = (bf16[16,2560]{1,0:T(8,128)(2,1)S(1)}, bf16[16,2560]{1,0:T(8,128)(2,1)S(1)}, u32[]{:S(2)}, u32[]{:S(2)}) collective-permute-start(bf16[16,2560]{1,0:T(8,128)(2,1)S(1)} %get-tuple-element.50), channel_id=1, source_target_pairs={{0,1},{1,0},{2,3},{3,2},{4,5},{5,4},{6,7},{7,6},{8,9},{9,8},{10,11... | collective-permute-start | bytes 245768 | tf_op jit(solution)/shard_map/ppermute | solution.py:47
  25.8 4.5 %collective-permute-start.7 = (bf16[16,2560]{1,0:T(8,128)(2,1)S(1)}, bf16[16,2560]{1,0:T(8,128)(2,1)S(1)}, u32[]{:S(2)}, u32[]{:S(2)}) collective-permute-start(bf16[16,2560]{1,0:T(8,128)(2,1)S(1)} %get-tuple-element.46), channel_id=1, source_target_pairs={{0,2},{1,3},{2,0},{3,1},{4,6},{5,7},{6,4},{7,5},{8,10},{9,11},{10,... | collective-permute-start | bytes 245768 | tf_op jit(solution)/shard_map/ppermute | solution.py:47
  30.3 8.7 %collective-permute-start.10 = (bf16[16,5120]{1,0:T(8,128)(2,1)S(1)}, bf16[16,5120]{1,0:T(8,128)(2,1)S(1)}, u32[]{:S(2)}, u32[]{:S(2)}) collective-permute-start(bf16[16,5120]{1,0:T(8,128)(2,1)S(1)} %get-tuple-element.51.gate_ref), channel_id=1, source_target_pairs={{0,4},{1,5},{2,6},{3,7},{4,0},{5,1},{6,2},{7,3},{8,12},{9,13},{10,... | collective-permute-start | bytes 491528 | tf_op jit(solution)/shard_map/ppermute | solution.py:47
  33.0 6.1 %copy-start = (bf16[64,5120]{1,0:T(8,128)(2,1)S(1)}, bf16[64,5120]{1,0:T(8,128)(2,1)}, u32[]{:S(2)}) copy-start(bf16[64,5120]{1,0:T(8,128)(2,1)} %param.19) | copy-start | bytes 1966084
  39.3 5.4 %collective-permute-start.11 = (bf16[16,5120]{1,0:T(8,128)(2,1)S(1)}, bf16[16,5120]{1,0:T(8,128)(2,1)S(1)}, u32[]{:S(2)}, u32[]{:S(2)}) collective-permute-start(bf16[16,5120]{1,0:T(8,128)(2,1)S(1)} %norm.1.refs_0_), channel_id=1, source_target_pairs={{0,2},{1,3},{2,0},{3,1},{4,6},{5,7},{6,4},{7,5},{8,10},{9,11},{10,... | collective-permute-start | bytes 491528 | tf_op jit(solution)/shard_map/ppermute | solution.py:47
  40.0 10.8 %collective-permute-start.14 = (bf16[16,5120]{1,0:T(8,128)(2,1)S(1)}, bf16[16,5120]{1,0:T(8,128)(2,1)S(1)}, u32[]{:S(2)}, u32[]{:S(2)}) collective-permute-start(bf16[16,5120]{1,0:T(8,128)(2,1)S(1)} %norm.1.refs_0_), channel_id=1, source_target_pairs={{0,16},{8,24},{16,0},{24,8},{1,17},{9,25},{17,1},{25,9},{2,18},{10... | collective-permute-start | bytes 491528 | tf_op jit(solution)/shard_map/ppermute | solution.py:47
  41.6 9.2 %collective-permute-start.12 = (bf16[16,5120]{1,0:T(8,128)(2,1)S(1)}, bf16[16,5120]{1,0:T(8,128)(2,1)S(1)}, u32[]{:S(2)}, u32[]{:S(2)}) collective-permute-start(bf16[16,5120]{1,0:T(8,128)(2,1)S(1)} %norm.1.refs_0_), channel_id=1, source_target_pairs={{0,1},{1,0},{2,3},{3,2},{4,5},{5,4},{6,7},{7,6},{8,9},{9,8},{10,11... | collective-permute-start | bytes 491528 | tf_op jit(solution)/shard_map/ppermute | solution.py:47
  44.6 6.2 %collective-permute-start.15 = (bf16[16,5120]{1,0:T(8,128)(2,1)S(1)}, bf16[16,5120]{1,0:T(8,128)(2,1)S(1)}, u32[]{:S(2)}, u32[]{:S(2)}) collective-permute-start(bf16[16,5120]{1,0:T(8,128)(2,1)S(1)} %collective-permute-done.11.gate_ref.refs_1_), channel_id=1, source_target_pairs={{0,16},{8,24},{16,0},{24,8},{1,17},{9,25},{17,1},{25,9},{2,18},{10... | collective-permute-start | bytes 491528 | tf_op jit(solution)/shard_map/ppermute | solution.py:47
  46.3 5.3 %collective-permute-start.13 = (bf16[16,5120]{1,0:T(8,128)(2,1)S(1)}, bf16[16,5120]{1,0:T(8,128)(2,1)S(1)}, u32[]{:S(2)}, u32[]{:S(2)}) collective-permute-start(bf16[16,5120]{1,0:T(8,128)(2,1)S(1)} %collective-permute-done.11.gate_ref.refs_1_), channel_id=1, source_target_pairs={{0,1},{1,0},{2,3},{3,2},{4,5},{5,4},{6,7},{7,6},{8,9},{9,8},{10,11... | collective-permute-start | bytes 491528 | tf_op jit(solution)/shard_map/ppermute | solution.py:47
  51.6 5.4 %collective-permute-start.16 = (bf16[2,16,2560]{2,1,0:T(8,128)(2,1)S(1)}, bf16[2,16,2560]{2,1,0:T(8,128)(2,1)S(1)}, u32[]{:S(2)}, u32[]{:S(2)}) collective-permute-start(bf16[2,16,2560]{2,1,0:T(8,128)(2,1)S(1)} %get-tuple-element.53), channel_id=1, source_target_pairs={{0,16},{8,24},{16,0},{24,8},{1,17},{9,25},{17,1},{25,9},{2,18},{10... | collective-permute-start | bytes 491528 | tf_op jit(solution)/shard_map/ppermute | solution.py:47
  52.1 5.3 %collective-permute-start.17 = (bf16[2,16,2560]{2,1,0:T(8,128)(2,1)S(1)}, bf16[2,16,2560]{2,1,0:T(8,128)(2,1)S(1)}, u32[]{:S(2)}, u32[]{:S(2)}) collective-permute-start(bf16[2,16,2560]{2,1,0:T(8,128)(2,1)S(1)} %get-tuple-element.54), channel_id=1, source_target_pairs={{0,1},{1,0},{2,3},{3,2},{4,5},{5,4},{6,7},{7,6},{8,9},{9,8},{10,11... | collective-permute-start | bytes 491528 | tf_op jit(solution)/shard_map/ppermute | solution.py:47
  57.5 2.2 %collective-permute-start.18 = (bf16[128,2560]{1,0:T(8,128)(2,1)S(1)}, bf16[128,2560]{1,0:T(8,128)(2,1)S(1)}, u32[]{:S(2)}, u32[]{:S(2)}) collective-permute-start(bf16[128,2560]{1,0:T(8,128)(2,1)S(1)} %get-tuple-element.55.left_ref), channel_id=1, source_target_pairs={{0,8},{8,0},{16,24},{24,16},{1,9},{9,1},{17,25},{25,17},{2,10},{10... | collective-permute-start | bytes 1966088 | tf_op jit(solution)/shard_map/ppermute | solution.py:47
  57.6 6.6 %collective-permute-start.19 = (bf16[128,2560]{1,0:T(8,128)(2,1)S(1)}, bf16[128,2560]{1,0:T(8,128)(2,1)S(1)}, u32[]{:S(2)}, u32[]{:S(2)}) collective-permute-start(bf16[128,2560]{1,0:T(8,128)(2,1)S(1)} %get-tuple-element.57.left_ref), channel_id=1, source_target_pairs={{0,8},{8,0},{16,24},{24,16},{1,9},{9,1},{17,25},{25,17},{2,10},{10... | collective-permute-start | bytes 1966088 | tf_op jit(solution)/shard_map/ppermute | solution.py:47

commit v14 on v13

--- a/solution.py
+++ b/solution.py
@@ -271,27 +271,12 @@
         copy.wait()
 
 
-def cut_kernel(*refs):
-    left_ref, right_ref = refs[-2:]
-    count, width = left_ref.shape[0], left_ref.shape[2]
-    for i in range(count):
-        left_ref[i] = refs[i][:, :width]
-    for i in range(right_ref.shape[0]):
-        right_ref[i] = refs[count + i][:, width:]
-
-
-def tokens_kernel(count, split, *refs):
-    blocks, out_refs = refs[:count], refs[-2:]
-    rows = blocks[0].shape[0]
-    width = out_refs[0].shape[1]
-    for half, (stacks, out_ref) in enumerate(zip((refs[count:split], refs[split:-2]), out_refs)):
-        for i, ref in enumerate(blocks):
+def tokens_kernel(count, *refs):
+    out_refs = refs[-2:]
+    rows, width = refs[0].shape[0], out_refs[0].shape[1]
+    for half, out_ref in enumerate(out_refs):
+        for i, ref in enumerate(refs[:count]):
             out_ref[i * rows : (i + 1) * rows] = ref[:, half * width : (half + 1) * width]
-        place = count * rows
-        for ref in stacks:
-            for i in range(ref.shape[0]):
-                out_ref[place : place + rows] = ref[i]
-                place += rows
 
 
 def norm_kernel(residual_ref, gain_ref, gate_ref, own_ref, got_ref, out_ref):
@@ -573,41 +558,32 @@
         *map(held, (total, swap(send, "tensor", far, tensor_size))),
     )
 
+    mesh_ids = [(g, t) for g in range(group_size) for t in range(tensor_size)]
+    here = [(g, x) for g in [0] + above for x in (0, 1)]
+    routes = {
+        (g, x): [(a * tensor_size + b, (a ^ g) * tensor_size + (b ^ x)) for a, b in mesh_ids]
+        for g, x in here
+    }
+
     def around(x):
-        along = [swap(x, "group", d, group_size) for d in above]
-        return swap(x, "tensor", 1, tensor_size), along
+        sent = [lax.ppermute(x, ("group", "tensor"), routes[place]) for place in here[:0:-1]]
+        return [x] + sent[::-1]
 
     sides = [around(normed)]
-    near = [normed, swap(normed, "tensor", 2, tensor_size)]
-    sides.append(around(near[1]))
-    third = fetch(lm_weight, 2 * quarter, quarter, near[1])
-
-    across = [x for x, _ in sides]
-    along = [ys[i] for i in range(len(above)) for _, ys in sides]
-    left, right = pl.pallas_call(
-        cut_kernel,
-        out_shape=[
-            jax.ShapeDtypeStruct((len(pieces), block, half), BF16) for pieces in (across, along)
-        ],
-        in_specs=[vmem()] * (len(across) + len(along)) + [anywhere()],
-        out_specs=[vmem()] * 2,
-        compiler_params=params(2),
-        name="cut",
-    )(*map(held, (*across, *along)), third)
-    left = [swap(left, "group", d, group_size) for d in above]
-    right = [swap(right, "tensor", 1, tensor_size)]
-    whole = near + across + along
-    count = (len(whole) + len(across) * len(above)) * block
+    near = swap(normed, "tensor", 2, tensor_size)
+    sides.append(around(near))
+    third = fetch(lm_weight, 2 * quarter, quarter, near)
+    blocks = [x for pair in zip(*sides) for x in pair]
+    count = len(blocks) * block
     halves = pl.pallas_call(
-        functools.partial(tokens_kernel, len(whole), len(whole) + len(left)),
+        functools.partial(tokens_kernel, len(blocks)),
         out_shape=[jax.ShapeDtypeStruct((count, half), BF16)] * 2,
-        in_specs=[vmem()] * (len(whole) + len(left) + len(right)),
+        in_specs=[vmem()] * len(blocks) + [anywhere()],
         out_specs=[vmem()] * 2,
         compiler_params=params(2),
         name="tokens",
-    )(*map(held, (*whole, *left, *right)))
+    )(*map(held, blocks), third)
     halves = [(tokens, swap(tokens, "group", 1, group_size)) for tokens in halves]
-    here = [(0, 0), (0, 1)] + [(g, 0) for g in above] + [(g, 1) for g in above]
     order = [0, 2]
     spots = [(g + c, t + x) for c in (0, 1) for g, x in here for t in order]
     total_rows = 2 * count

time: 82.7 us -> 80.2 us (0.970)
  blocking collectives: 12.7 us -> 11.1 us
    ppermute x20 -> x14, starting transfers between devices: 22.7 us -> 16 us  [swap(): return lax.ppermute(x, axis, [(i, i ^ distance) for i in range(size)])]
    ppermute x0 -> x6, starting transfers between devices: none -> 6.29 us  [around(): lax.ppermute(x, ('group', 'tensor'), routes[place])]
    ppermute x20 -> x14, waiting for transfers between devices: 16.4 us -> 10.2 us  [swap(): return lax.ppermute(x, axis, [(i, i ^ distance) for i in range(size)])]
    ppermute x0 -> x6, waiting for transfers between devices: none -> 5.7 us  [around(): lax.ppermute(x, ('group', 'tensor'), routes[place])]
    all_to_all x1, blocking collectives: 12.7 us -> 11.1 us  [local(): stats = lax.all_to_all(stats, ('group', 'tensor'), 0, 0, tiled=True)]
  transfers between devices with their start and end apart: 20 -> 20, of which waited for: 11 -> 13; matrix products, arithmetic and copies ran while one was open for 1% -> 1% of each run, Pallas kernels for 24% -> 24%
where the time goes in v14:
time: 80.2 us; the launch traced here: 80 us
  Pallas kernels  29.6 us (37%)
  starting transfers between devices  22.3 us (28%)
  waiting for transfers between devices  15.9 us (20%)
  blocking collectives  11.1 us (14%)
  local copies, waits for them, and re-layouts  0.9 us (1%)
    ppermute x14, starting transfers between devices, swap(): return lax.ppermute(x, axis, [(i, i ^ distance) for i in range(size)])  16 us
    all_to_all x1, blocking collectives, local(): stats = lax.all_to_all(stats, ('group', 'tensor'), 0, 0, tiled=True)  11.1 us
    ppermute x14, waiting for transfers between devices, swap(): return lax.ppermute(x, axis, [(i, i ^ distance) for i in range(size)])  10.2 us
    pallas_call x3, Pallas kernels, fetch(): pl.pallas_call(functools.partial(fetch_kernel, start), out_shape=pltpu.VM...  10.1 us
    ppermute x6, starting transfers between devices, around(): lax.ppermute(x, ('group', 'tensor'), routes[place])  6.29 us
    ppermute x6, waiting for transfers between devices, around(): lax.ppermute(x, ('group', 'tensor'), routes[place])  5.7 us
    pallas_call x1, Pallas kernels, local(): pl.pallas_call(functools.partial(logits_kernel, vocab, spots, tensor_size...  5 us
    pallas_call x1, Pallas kernels, local(): pl.pallas_call(functools.partial(first_kernel, narrow), out_shape=[pltpu....  4.52 us
  transfers between devices with their start and end apart: 20, of which 13 were waited for; matrix products, arithmetic and copies ran while one was open for 1% of the time, Pallas kernels for 24%

profile of v14, /device:TPU:0, one launch (start us, length us, event | category | flops | bytes accessed | tf_op | source)
XLA Modules:
  0.0 80.0 jit_solution(17647191661793697696)
XLA Ops:
  0.0 3.0 %collective-permute-start = (bf16[64,512]{1,0:T(8,128)(2,1)}, bf16[64,512]{1,0:T(8,128)(2,1)S(1)}, u32[]{:S(2)}, u32[]{:S(2)}) collective-permute-start(bf16[64,512]{1,0:T(8,128)(2,1)} %refs_0_.1), channel_id=1, source_target_pairs={{0,16},{8,24},{16,0},{24,8},{1,17},{9,25},{17,1},{25,9},{2,18},{10... | collective-permute-start | bytes 196616 | tf_op jit(solution)/shard_map/ppermute | solution.py:47
  3.0 0.9 %reshape.8.refs_1_.target_ref = s32[32,8,1]{2,1,0:T(8,128)S(1)} reshape(s32[256]{0:T(256)} %param.23) | data formatting | bytes 2048 | tf_op jit(solution)/shard_map/reshape | solution.py:423
  3.9 1.6 %collective-permute-done.refs_0_ = bf16[64,512]{1,0:T(8,128)(2,1)S(1)} collective-permute-done((bf16[64,512]{1,0:T(8,128)(2,1)}, bf16[64,512]{1,0:T(8,128)(2,1)S(1)}, u32[]{:S(2)}, u32[]{:S(2)}) %collective-permute-start) | collective-permute-done | bytes 65568 | tf_op jit(solution)/shard_map/ppermute | solution.py:47
  5.4 1.4 %load.1 = (bf16[64,512]{1,0:T(8,128)(2,1)S(1)}, bf16[64,512]{1,0:T(8,128)(2,1)S(1)}, bf16[64,512]{1,0:T(8,128)(2,1)S(1)}, bf16[512,512]{1,0:T(8,128)(2,1)S(1)}, bf16[512,512]{1,0:T(8,128)(2,1)S(1)}) custom-call(bf16[64,512]{1,0:T(8,128)(2,1)S(1)} %pass.1.gate_ref.refs_1_, bf16[64,512]{1,0:T(8,128)(2,1)} %refs_0_.1, bf16[64,512]{1,0:T(8,128)(2,1)} %refs_1_.1, ...), custom_call_target="tpu_custom_call" | custom-call | bytes 2097152 | tf_op jit(solution)/shard_map/load/pallas_call | solution.py:441
  6.8 0.9 %prefix_attention.1 = (bf16[64,640]{1,0:T(8,128)(2,1)S(1)}, bf16[64,640]{1,0:T(8,128)(2,1)S(1)}, bf16[64,640]{1,0:T(8,128)(2,1)S(1)}) custom-call(bf16[64,512]{1,0:T(8,128)(2,1)S(1)} %collective-permute-done.1.refs_0_, bf16[64,512]{1,0:T(8,128)(2,1)S(1)} %pass.1.gate_ref.refs_1_, bf16[64,512]{1,0:T(8,128)(2,1)S(1)} %collective-permute-done.2.refs_2_, ...), custom_call_target="tpu_custom_call" | custom-call | tf_op jit(solution)/shard_map/prefix_attention/pallas_call | solution.py:452
  7.7 2.1 %collective-permute-start.4 = (bf16[64,640]{1,0:T(8,128)(2,1)S(1)}, bf16[64,640]{1,0:T(8,128)(2,1)S(1)}, u32[]{:S(2)}, u32[]{:S(2)}) collective-permute-start(bf16[64,640]{1,0:T(8,128)(2,1)S(1)} %get-tuple-element.38), channel_id=1, source_target_pairs={{0,16},{8,24},{16,0},{24,8},{1,17},{9,25},{17,1},{25,9},{2,18},{10... | collective-permute-start | bytes 245768 | tf_op jit(solution)/shard_map/ppermute | solution.py:47
  10.0 3.5 %own_attention.1 = (f32[64,640]{1,0:T(8,128)S(1)}, f32[8,128]{1,0:T(8,128)S(1)}, bf16[512,5120]{1,0:T(8,128)(2,1)S(1)}) custom-call(s32[2]{0:T(128)} %lengths_ref.1, s32[2]{0:T(128)} %prompt_ref.3, bf16[64,512]{1,0:T(8,128)(2,1)S(1)} %get-tuple-element.30.q_ref, bf16[64,512]{1,0:T(8,128)(2,1)S(1)} %get-tuple-element.31.rk_ref, ...), custom_call_target="tpu_custom_call" | custom-call | bytes 8388608 | tf_op jit(solution)/shard_map/own_attention/pallas_call | solution.py:461
  13.6 0.7 collective-permute-done.3.refs_0_
  14.3 3.3 %project.1 = (bf16[2,16,2560]{2,1,0:T(8,128)(2,1)S(1)}, f32[2,16,2560]{2,1,0:T(8,128)S(1)}, bf16[2,16,2560]{2,1,0:T(8,128)(2,1)S(1)}, f32[2,16,2560]{2,1,0:T(8,128)S(1)}) custom-call(s32[2]{0:T(128)} %prompt_ref.3, f32[64,640]{1,0:T(8,128)S(1)} %get-tuple-element.37.own_ref, bf16[64,640]{1,0:T(8,128)(2,1)S(1)} %collective-permute-done.3.refs_0_, ...), custom_call_target="tpu_custom_call" | custom-call | tf_op jit(solution)/shard_map/project/pallas_call | solution.py:504
  17.6 1.9 %collective-permute-start.8 = (bf16[2,16,2560]{2,1,0:T(8,128)(2,1)S(1)}, bf16[2,16,2560]{2,1,0:T(8,128)(2,1)S(1)}, u32[]{:S(2)}, u32[]{:S(2)}) collective-permute-start(bf16[2,16,2560]{2,1,0:T(8,128)(2,1)S(1)} %get-tuple-element.46), channel_id=1, source_target_pairs={{0,2},{1,3},{2,0},{3,1},{4,6},{5,7},{6,4},{7,5},{8,10},{9,11},{10,... | collective-permute-start | bytes 491528 | tf_op jit(solution)/shard_map/ppermute | solution.py:47
  19.5 1.5 %collective-permute-start.6 = (bf16[2,16,2560]{2,1,0:T(8,128)(2,1)S(1)}, bf16[2,16,2560]{2,1,0:T(8,128)(2,1)S(1)}, u32[]{:S(2)}, u32[]{:S(2)}) collective-permute-start(bf16[2,16,2560]{2,1,0:T(8,128)(2,1)S(1)} %get-tuple-element.42.gate_ref), channel_id=1, source_target_pairs={{0,1},{1,0},{2,3},{3,2},{4,5},{5,4},{6,7},{7,6},{8,9},{9,8},{10,11... | collective-permute-start | bytes 491528 | tf_op jit(solution)/shard_map/ppermute | solution.py:47
  21.0 2.9 %fetch.3.refs_0_.weight_ref = bf16[1024,3072]{1,0:T(8,128)(2,1)S(1)} custom-call(bf16[5120,3072]{1,0:T(8,128)(2,1)} %source_ref.9, bf16[2,16,2560]{2,1,0:T(8,128)(2,1)S(1)} %get-tuple-element.42.gate_ref), custom_call_target="tpu_custom_call" | custom-call | bytes 6291456 | tf_op jit(solution)/shard_map/fetch/pallas_call | solution.py:488
  24.0 1.7 %collective-permute-start.9 = (bf16[16,2560]{1,0:T(8,128)(2,1)S(1)}, bf16[16,2560]{1,0:T(8,128)(2,1)S(1)}, u32[]{:S(2)}, u32[]{:S(2)}) collective-permute-start(bf16[16,2560]{1,0:T(8,128)(2,1)S(1)} %get-tuple-element.48), channel_id=1, source_target_pairs={{0,1},{1,0},{2,3},{3,2},{4,5},{5,4},{6,7},{7,6},{8,9},{9,8},{10,11... | collective-permute-start | bytes 245768 | tf_op jit(solution)/shard_map/ppermute | solution.py:47
  25.8 1.6 %collective-permute-start.7 = (bf16[16,2560]{1,0:T(8,128)(2,1)S(1)}, bf16[16,2560]{1,0:T(8,128)(2,1)S(1)}, u32[]{:S(2)}, u32[]{:S(2)}) collective-permute-start(bf16[16,2560]{1,0:T(8,128)(2,1)S(1)} %get-tuple-element.44), channel_id=1, source_target_pairs={{0,2},{1,3},{2,0},{3,1},{4,6},{5,7},{6,4},{7,5},{8,10},{9,11},{10,... | collective-permute-start | bytes 245768 | tf_op jit(solution)/shard_map/ppermute | solution.py:47
  27.4 1.1 %collective-permute-done.9.got_right_ref = bf16[16,2560]{1,0:T(8,128)(2,1)S(1)} collective-permute-done((bf16[16,2560]{1,0:T(8,128)(2,1)S(1)}, bf16[16,2560]{1,0:T(8,128)(2,1)S(1)}, u32[]{:S(2)}, u32[]{:S(2)}) %collective-permute-start.9) | collective-permute-done | bytes 81952 | tf_op jit(solution)/shard_map/ppermute | solution.py:47
  28.5 1.7 %collective-permute-done.7.got_left_ref = bf16[16,2560]{1,0:T(8,128)(2,1)S(1)} collective-permute-done((bf16[16,2560]{1,0:T(8,128)(2,1)S(1)}, bf16[16,2560]{1,0:T(8,128)(2,1)S(1)}, u32[]{:S(2)}, u32[]{:S(2)}) %collective-permute-start.7) | collective-permute-done | bytes 81952 | tf_op jit(solution)/shard_map/ppermute | solution.py:47
  30.3 2.7 %collective-permute-start.10 = (bf16[16,5120]{1,0:T(8,128)(2,1)S(1)}, bf16[16,5120]{1,0:T(8,128)(2,1)S(1)}, u32[]{:S(2)}, u32[]{:S(2)}) collective-permute-start(bf16[16,5120]{1,0:T(8,128)(2,1)S(1)} %get-tuple-element.49.gate_ref), channel_id=1, source_target_pairs={{0,4},{1,5},{2,6},{3,7},{4,0},{5,1},{6,2},{7,3},{8,12},{9,13},{10,... | collective-permute-start | bytes 491528 | tf_op jit(solution)/shard_map/ppermute | solution.py:47
  33.0 3.9 %fetch.4.gate_ref.next_ref = bf16[1536,3072]{1,0:T(8,128)(2,1)S(1)} custom-call(bf16[5120,3072]{1,0:T(8,128)(2,1)} %source_ref.9, bf16[16,5120]{1,0:T(8,128)(2,1)S(1)} %get-tuple-element.49.gate_ref), custom_call_target="tpu_custom_call" | custom-call | bytes 9437184 | tf_op jit(solution)/shard_map/fetch/pallas_call | solution.py:488
  36.9 2.2 %collective-permute-done.10.got_ref = bf16[16,5120]{1,0:T(8,128)(2,1)S(1)} collective-permute-done((bf16[16,5120]{1,0:T(8,128)(2,1)S(1)}, bf16[16,5120]{1,0:T(8,128)(2,1)S(1)}, u32[]{:S(2)}, u32[]{:S(2)}) %collective-permute-start.10) | collective-permute-done | bytes 163872 | tf_op jit(solution)/shard_map/ppermute | solution.py:47
  39.3 0.7 collective-permute-start.11
  40.0 1.6 %collective-permute-start.16 = (bf16[16,5120]{1,0:T(8,128)(2,1)S(1)}, bf16[16,5120]{1,0:T(8,128)(2,1)S(1)}, u32[]{:S(2)}, u32[]{:S(2)}) collective-permute-start(bf16[16,5120]{1,0:T(8,128)(2,1)S(1)} %norm.1.refs_0_), channel_id=1, source_target_pairs={{0,17},{1,16},{2,19},{3,18},{4,21},{5,20},{6,23},{7,22},{8,25},{9,... | collective-permute-start | bytes 491528 | tf_op jit(solution)/shard_map/ppermute | solution.py:569
  42.0 1.5 %collective-permute-start.12 = (bf16[16,5120]{1,0:T(8,128)(2,1)S(1)}, bf16[16,5120]{1,0:T(8,128)(2,1)S(1)}, u32[]{:S(2)}, u32[]{:S(2)}) collective-permute-start(bf16[16,5120]{1,0:T(8,128)(2,1)S(1)} %norm.1.refs_0_), channel_id=1, source_target_pairs={{0,1},{1,0},{2,3},{3,2},{4,5},{5,4},{6,7},{7,6},{8,9},{9,8},{10,11... | collective-permute-start | bytes 491528 | tf_op jit(solution)/shard_map/ppermute | solution.py:569
  43.5 1.2 %collective-permute-done.11.gate_ref.refs_1_ = bf16[16,5120]{1,0:T(8,128)(2,1)S(1)} collective-permute-done((bf16[16,5120]{1,0:T(8,128)(2,1)S(1)}, bf16[16,5120]{1,0:T(8,128)(2,1)S(1)}, u32[]{:S(2)}, u32[]{:S(2)}) %collective-permute-start.11) | collective-permute-done | bytes 163872 | tf_op jit(solution)/shard_map/ppermute | solution.py:47
  44.6 2.2 %collective-permute-start.17 = (bf16[16,5120]{1,0:T(8,128)(2,1)S(1)}, bf16[16,5120]{1,0:T(8,128)(2,1)S(1)}, u32[]{:S(2)}, u32[]{:S(2)}) collective-permute-start(bf16[16,5120]{1,0:T(8,128)(2,1)S(1)} %collective-permute-done.11.gate_ref.refs_1_), channel_id=1, source_target_pairs={{0,17},{1,16},{2,19},{3,18},{4,21},{5,20},{6,23},{7,22},{8,25},{9,... | collective-permute-start | bytes 491528 | tf_op jit(solution)/shard_map/ppermute | solution.py:569
  47.3 0.8 %collective-permute-done.16.refs_6_ = bf16[16,5120]{1,0:T(8,128)(2,1)S(1)} collective-permute-done((bf16[16,5120]{1,0:T(8,128)(2,1)S(1)}, bf16[16,5120]{1,0:T(8,128)(2,1)S(1)}, u32[]{:S(2)}, u32[]{:S(2)}) %collective-permute-start.16) | collective-permute-done | bytes 163872 | tf_op jit(solution)/shard_map/ppermute | solution.py:569
  48.3 3.3 %fetch.5.refs_8_.weight_ref = bf16[1280,3072]{1,0:T(8,128)(2,1)S(1)} custom-call(bf16[5120,3072]{1,0:T(8,128)(2,1)} %source_ref.9, bf16[16,5120]{1,0:T(8,128)(2,1)S(1)} %collective-permute-done.11.gate_ref.refs_1_), custom_call_target="tpu_custom_call" | custom-call | bytes 7864320 | tf_op jit(solution)/shard_map/fetch/pallas_call | solution.py:488
  52.3 2.5 %collective-permute-done.17.refs_7_ = bf16[16,5120]{1,0:T(8,128)(2,1)S(1)} collective-permute-done((bf16[16,5120]{1,0:T(8,128)(2,1)S(1)}, bf16[16,5120]{1,0:T(8,128)(2,1)S(1)}, u32[]{:S(2)}, u32[]{:S(2)}) %collective-permute-start.17) | collective-permute-done | bytes 163872 | tf_op jit(solution)/shard_map/ppermute | solution.py:569
  54.8 1.3 %collective-permute-done.15.refs_5_ = bf16[16,5120]{1,0:T(8,128)(2,1)S(1)} collective-permute-done((bf16[16,5120]{1,0:T(8,128)(2,1)S(1)}, bf16[16,5120]{1,0:T(8,128)(2,1)S(1)}, u32[]{:S(2)}, u32[]{:S(2)}) %collective-permute-start.15) | collective-permute-done | bytes 163872 | tf_op jit(solution)/shard_map/ppermute | solution.py:569
  57.2 1.6 %collective-permute-done.18.right_ref = bf16[128,2560]{1,0:T(8,128)(2,1)S(1)} collective-permute-done((bf16[128,2560]{1,0:T(8,128)(2,1)S(1)}, bf16[128,2560]{1,0:T(8,128)(2,1)S(1)}, u32[]{:S(2)}, u32[]{:S(2)}) %collective-permute-start.18) | collective-permute-done | bytes 655392 | tf_op jit(solution)/shard_map/ppermute | solution.py:47
  58.8 4.5 %logits_first.1 = (f32[256,3072]{1,0:T(8,128)S(1)}, bf16[1280,3072]{1,0:T(8,128)(2,1)S(1)}) custom-call(bf16[128,2560]{1,0:T(8,128)(2,1)S(1)} %get-tuple-element.51.left_ref, bf16[128,2560]{1,0:T(8,128)(2,1)S(1)} %collective-permute-done.18.right_ref, bf16[1024,3072]{1,0:T(8,128)(2,1)S(1)} %fetch.3.refs_0_.weight_ref, ...), custom_call_target="tpu_custom_call" | custom-call | flops 4026531840 | tf_op jit(solution)/shard_map/logits_first/pallas_call | solution.py:593
  63.3 5.0 %logits.1 = f32[32,1,128]{2,1,0:T(1,128)S(1)} custom-call(f32[256,3072]{1,0:T(8,128)S(1)} %get-tuple-element.52.sum_in_ref, bf16[128,2560]{1,0:T(8,128)(2,1)S(1)} %get-tuple-element.53.left_ref, bf16[128,2560]{1,0:T(8,128)(2,1)S(1)} %collective-permute-done.19.right_ref, s32[32,8,1]{2,1,0:T(8,128)S(1)} %reshape.8.refs_1_.target_ref, ...), custom_call_target="tpu_custom_call" | custom-call | flops 4026531840 | tf_op jit(solution)/shard_map/logits/pallas_call | solution.py:606
  68.3 11.1 %all_to_all.5.stats_ref = f32[32,1,128]{2,1,0:T(1,128)S(1)} all-to-all(f32[32,1,128]{2,1,0:T(1,128)S(1)} %logits.1), channel_id=1, replica_groups=mesh['group'=4,'tensor'=8] {'group','tensor'}, dimensions={0} | all-to-all | bytes 32768 | tf_op jit(solution)/shard_map/all_to_all | solution.py:619
  (31 shorter events, 4.1 us)
Async XLA Ops:
  0.0 5.4 %collective-permute-start = (bf16[64,512]{1,0:T(8,128)(2,1)}, bf16[64,512]{1,0:T(8,128)(2,1)S(1)}, u32[]{:S(2)}, u32[]{:S(2)}) collective-permute-start(bf16[64,512]{1,0:T(8,128)(2,1)} %refs_0_.1), channel_id=1, source_target_pairs={{0,16},{8,24},{16,0},{24,8},{1,17},{9,25},{17,1},{25,9},{2,18},{10... | collective-permute-start | bytes 196616 | tf_op jit(solution)/shard_map/ppermute | solution.py:47
  3.0 3.8 %collective-permute-start.2 = (bf16[64,512]{1,0:T(8,128)(2,1)}, bf16[64,512]{1,0:T(8,128)(2,1)S(1)}, u32[]{:S(2)}, u32[]{:S(2)}) collective-permute-start(bf16[64,512]{1,0:T(8,128)(2,1)} %refs_0_.1), channel_id=1, source_target_pairs={{0,8},{8,0},{16,24},{24,16},{1,9},{9,1},{17,25},{25,17},{2,10},{10... | collective-permute-start | bytes 196616 | tf_op jit(solution)/shard_map/ppermute | solution.py:47
  5.4 1.4 %collective-permute-start.1 = (bf16[64,512]{1,0:T(8,128)(2,1)S(1)}, bf16[64,512]{1,0:T(8,128)(2,1)S(1)}, u32[]{:S(2)}, u32[]{:S(2)}) collective-permute-start(bf16[64,512]{1,0:T(8,128)(2,1)S(1)} %pass.1.gate_ref.refs_1_), channel_id=1, source_target_pairs={{0,8},{8,0},{16,24},{24,16},{1,9},{9,1},{17,25},{25,17},{2,10},{10... | collective-permute-start | bytes 196616 | tf_op jit(solution)/shard_map/ppermute | solution.py:47
  7.7 5.9 %collective-permute-start.4 = (bf16[64,640]{1,0:T(8,128)(2,1)S(1)}, bf16[64,640]{1,0:T(8,128)(2,1)S(1)}, u32[]{:S(2)}, u32[]{:S(2)}) collective-permute-start(bf16[64,640]{1,0:T(8,128)(2,1)S(1)} %get-tuple-element.38), channel_id=1, source_target_pairs={{0,16},{8,24},{16,0},{24,8},{1,17},{9,25},{17,1},{25,9},{2,18},{10... | collective-permute-start | bytes 245768 | tf_op jit(solution)/shard_map/ppermute | solution.py:47
  9.8 3.8 %collective-permute-start.5 = (bf16[64,640]{1,0:T(8,128)(2,1)S(1)}, bf16[64,640]{1,0:T(8,128)(2,1)S(1)}, u32[]{:S(2)}, u32[]{:S(2)}) collective-permute-start(bf16[64,640]{1,0:T(8,128)(2,1)S(1)} %get-tuple-element.39), channel_id=1, source_target_pairs={{0,8},{8,0},{16,24},{24,16},{1,9},{9,1},{17,25},{25,17},{2,10},{10... | collective-permute-start | bytes 245768 | tf_op jit(solution)/shard_map/ppermute | solution.py:47
  10.0 4.3 %collective-permute-start.3 = (bf16[64,640]{1,0:T(8,128)(2,1)S(1)}, bf16[64,640]{1,0:T(8,128)(2,1)S(1)}, u32[]{:S(2)}, u32[]{:S(2)}) collective-permute-start(bf16[64,640]{1,0:T(8,128)(2,1)S(1)} %get-tuple-element.35.gate_ref), channel_id=1, source_target_pairs={{0,24},{8,16},{16,8},{24,0},{1,25},{9,17},{17,9},{25,1},{2,26},{10... | collective-permute-start | bytes 245768 | tf_op jit(solution)/shard_map/ppermute | solution.py:47
  17.6 6.4 %collective-permute-start.8 = (bf16[2,16,2560]{2,1,0:T(8,128)(2,1)S(1)}, bf16[2,16,2560]{2,1,0:T(8,128)(2,1)S(1)}, u32[]{:S(2)}, u32[]{:S(2)}) collective-permute-start(bf16[2,16,2560]{2,1,0:T(8,128)(2,1)S(1)} %get-tuple-element.46), channel_id=1, source_target_pairs={{0,2},{1,3},{2,0},{3,1},{4,6},{5,7},{6,4},{7,5},{8,10},{9,11},{10,... | collective-permute-start | bytes 491528 | tf_op jit(solution)/shard_map/ppermute | solution.py:47
  19.5 13.5 %copy-start.1 = (bf16[5120]{0:T(1024)(128)(2,1)S(1)}, bf16[5120]{0:T(1024)(128)(2,1)}, u32[]{:S(2)}) copy-start(bf16[5120]{0:T(1024)(128)(2,1)} %param.21) | copy-start | bytes 30724
  19.5 6.2 %collective-permute-start.6 = (bf16[2,16,2560]{2,1,0:T(8,128)(2,1)S(1)}, bf16[2,16,2560]{2,1,0:T(8,128)(2,1)S(1)}, u32[]{:S(2)}, u32[]{:S(2)}) collective-permute-start(bf16[2,16,2560]{2,1,0:T(8,128)(2,1)S(1)} %get-tuple-element.42.gate_ref), channel_id=1, source_target_pairs={{0,1},{1,0},{2,3},{3,2},{4,5},{5,4},{6,7},{7,6},{8,9},{9,8},{10,11... | collective-permute-start | bytes 491528 | tf_op jit(solution)/shard_map/ppermute | solution.py:47
  24.0 4.5 %collective-permute-start.9 = (bf16[16,2560]{1,0:T(8,128)(2,1)S(1)}, bf16[16,2560]{1,0:T(8,128)(2,1)S(1)}, u32[]{:S(2)}, u32[]{:S(2)}) collective-permute-start(bf16[16,2560]{1,0:T(8,128)(2,1)S(1)} %get-tuple-element.48), channel_id=1, source_target_pairs={{0,1},{1,0},{2,3},{3,2},{4,5},{5,4},{6,7},{7,6},{8,9},{9,8},{10,11... | collective-permute-start | bytes 245768 | tf_op jit(solution)/shard_map/ppermute | solution.py:47
  25.8 4.5 %collective-permute-start.7 = (bf16[16,2560]{1,0:T(8,128)(2,1)S(1)}, bf16[16,2560]{1,0:T(8,128)(2,1)S(1)}, u32[]{:S(2)}, u32[]{:S(2)}) collective-permute-start(bf16[16,2560]{1,0:T(8,128)(2,1)S(1)} %get-tuple-element.44), channel_id=1, source_target_pairs={{0,2},{1,3},{2,0},{3,1},{4,6},{5,7},{6,4},{7,5},{8,10},{9,11},{10,... | collective-permute-start | bytes 245768 | tf_op jit(solution)/shard_map/ppermute | solution.py:47
  30.3 8.7 %collective-permute-start.10 = (bf16[16,5120]{1,0:T(8,128)(2,1)S(1)}, bf16[16,5120]{1,0:T(8,128)(2,1)S(1)}, u32[]{:S(2)}, u32[]{:S(2)}) collective-permute-start(bf16[16,5120]{1,0:T(8,128)(2,1)S(1)} %get-tuple-element.49.gate_ref), channel_id=1, source_target_pairs={{0,4},{1,5},{2,6},{3,7},{4,0},{5,1},{6,2},{7,3},{8,12},{9,13},{10,... | collective-permute-start | bytes 491528 | tf_op jit(solution)/shard_map/ppermute | solution.py:47
  33.0 6.1 %copy-start = (bf16[64,5120]{1,0:T(8,128)(2,1)S(1)}, bf16[64,5120]{1,0:T(8,128)(2,1)}, u32[]{:S(2)}) copy-start(bf16[64,5120]{1,0:T(8,128)(2,1)} %param.19) | copy-start | bytes 1966084
  39.3 5.4 %collective-permute-start.11 = (bf16[16,5120]{1,0:T(8,128)(2,1)S(1)}, bf16[16,5120]{1,0:T(8,128)(2,1)S(1)}, u32[]{:S(2)}, u32[]{:S(2)}) collective-permute-start(bf16[16,5120]{1,0:T(8,128)(2,1)S(1)} %norm.1.refs_0_), channel_id=1, source_target_pairs={{0,2},{1,3},{2,0},{3,1},{4,6},{5,7},{6,4},{7,5},{8,10},{9,11},{10,... | collective-permute-start | bytes 491528 | tf_op jit(solution)/shard_map/ppermute | solution.py:47
  40.0 8.1 %collective-permute-start.16 = (bf16[16,5120]{1,0:T(8,128)(2,1)S(1)}, bf16[16,5120]{1,0:T(8,128)(2,1)S(1)}, u32[]{:S(2)}, u32[]{:S(2)}) collective-permute-start(bf16[16,5120]{1,0:T(8,128)(2,1)S(1)} %norm.1.refs_0_), channel_id=1, source_target_pairs={{0,17},{1,16},{2,19},{3,18},{4,21},{5,20},{6,23},{7,22},{8,25},{9,... | collective-permute-start | bytes 491528 | tf_op jit(solution)/shard_map/ppermute | solution.py:569
  41.6 10.7 %collective-permute-start.14 = (bf16[16,5120]{1,0:T(8,128)(2,1)S(1)}, bf16[16,5120]{1,0:T(8,128)(2,1)S(1)}, u32[]{:S(2)}, u32[]{:S(2)}) collective-permute-start(bf16[16,5120]{1,0:T(8,128)(2,1)S(1)} %norm.1.refs_0_), channel_id=1, source_target_pairs={{0,16},{1,17},{2,18},{3,19},{4,20},{5,21},{6,22},{7,23},{8,24},{9,... | collective-permute-start | bytes 491528 | tf_op jit(solution)/shard_map/ppermute | solution.py:569
  42.0 10.3 %collective-permute-start.12 = (bf16[16,5120]{1,0:T(8,128)(2,1)S(1)}, bf16[16,5120]{1,0:T(8,128)(2,1)S(1)}, u32[]{:S(2)}, u32[]{:S(2)}) collective-permute-start(bf16[16,5120]{1,0:T(8,128)(2,1)S(1)} %norm.1.refs_0_), channel_id=1, source_target_pairs={{0,1},{1,0},{2,3},{3,2},{4,5},{5,4},{6,7},{7,6},{8,9},{9,8},{10,11... | collective-permute-start | bytes 491528 | tf_op jit(solution)/shard_map/ppermute | solution.py:569
  44.6 10.2 %collective-permute-start.17 = (bf16[16,5120]{1,0:T(8,128)(2,1)S(1)}, bf16[16,5120]{1,0:T(8,128)(2,1)S(1)}, u32[]{:S(2)}, u32[]{:S(2)}) collective-permute-start(bf16[16,5120]{1,0:T(8,128)(2,1)S(1)} %collective-permute-done.11.gate_ref.refs_1_), channel_id=1, source_target_pairs={{0,17},{1,16},{2,19},{3,18},{4,21},{5,20},{6,23},{7,22},{8,25},{9,... | collective-permute-start | bytes 491528 | tf_op jit(solution)/shard_map/ppermute | solution.py:569
  46.9 9.3 %collective-permute-start.15 = (bf16[16,5120]{1,0:T(8,128)(2,1)S(1)}, bf16[16,5120]{1,0:T(8,128)(2,1)S(1)}, u32[]{:S(2)}, u32[]{:S(2)}) collective-permute-start(bf16[16,5120]{1,0:T(8,128)(2,1)S(1)} %collective-permute-done.11.gate_ref.refs_1_), channel_id=1, source_target_pairs={{0,16},{1,17},{2,18},{3,19},{4,20},{5,21},{6,22},{7,23},{8,24},{9,... | collective-permute-start | bytes 491528 | tf_op jit(solution)/shard_map/ppermute | solution.py:569
  48.1 8.4 %collective-permute-start.13 = (bf16[16,5120]{1,0:T(8,128)(2,1)S(1)}, bf16[16,5120]{1,0:T(8,128)(2,1)S(1)}, u32[]{:S(2)}, u32[]{:S(2)}) collective-permute-start(bf16[16,5120]{1,0:T(8,128)(2,1)S(1)} %collective-permute-done.11.gate_ref.refs_1_), channel_id=1, source_target_pairs={{0,1},{1,0},{2,3},{3,2},{4,5},{5,4},{6,7},{7,6},{8,9},{9,8},{10,11... | collective-permute-start | bytes 491528 | tf_op jit(solution)/shard_map/ppermute | solution.py:569
  56.6 2.2 %collective-permute-start.18 = (bf16[128,2560]{1,0:T(8,128)(2,1)S(1)}, bf16[128,2560]{1,0:T(8,128)(2,1)S(1)}, u32[]{:S(2)}, u32[]{:S(2)}) collective-permute-start(bf16[128,2560]{1,0:T(8,128)(2,1)S(1)} %get-tuple-element.51.left_ref), channel_id=1, source_target_pairs={{0,8},{8,0},{16,24},{24,16},{1,9},{9,1},{17,25},{25,17},{2,10},{10... | collective-permute-start | bytes 1966088 | tf_op jit(solution)/shard_map/ppermute | solution.py:47
  56.7 6.6 %collective-permute-start.19 = (bf16[128,2560]{1,0:T(8,128)(2,1)S(1)}, bf16[128,2560]{1,0:T(8,128)(2,1)S(1)}, u32[]{:S(2)}, u32[]{:S(2)}) collective-permute-start(bf16[128,2560]{1,0:T(8,128)(2,1)S(1)} %get-tuple-element.53.left_ref), channel_id=1, source_target_pairs={{0,8},{8,0},{16,24},{24,16},{1,9},{9,1},{17,25},{25,17},{2,10},{10... | collective-permute-start | bytes 1966088 | tf_op jit(solution)/shard_map/ppermute | solution.py:47

commit v15 on v14

--- a/solution.py
+++ b/solution.py
@@ -243,8 +243,7 @@
             send_right_ref[i, :, columns] = partial_ref[me ^ (i + 2)].astype(BF16)
 
 
-def fold_kernel(keep_ref, got_ref, *refs):
-    own_ref, send_ref = refs[-2:]
+def fold_kernel(keep_ref, got_ref, own_ref, send_ref):
     own_ref[...] = keep_ref[0] + got_ref[0].astype(F32)
     send_ref[...] = (keep_ref[1] + got_ref[1].astype(F32)).astype(BF16)
 
@@ -279,7 +278,7 @@
             out_ref[i * rows : (i + 1) * rows] = ref[:, half * width : (half + 1) * width]
 
 
-def norm_kernel(residual_ref, gain_ref, gate_ref, own_ref, got_ref, out_ref):
+def norm_kernel(residual_ref, gain_ref, first_gate_ref, second_gate_ref, own_ref, got_ref, out_ref):
     hidden = residual_ref[lax.axis_index("tensor") % 4].astype(F32)
     hidden = hidden + (own_ref[...] + got_ref[...].astype(F32))
     squares = jnp.mean(hidden * hidden, axis=-1, keepdims=True)
@@ -518,27 +517,26 @@
         name="project",
     )(stored(prompt_of), *map(held, (own, *got)), held(weight))
 
-    def add(kernel, name, size, *operands, gates=()):
+    def add(kernel, name, size, *operands):
         return pl.pallas_call(
             kernel,
             out_shape=[jax.ShapeDtypeStruct(size, F32), jax.ShapeDtypeStruct(size, BF16)],
-            in_specs=[vmem()] * len(operands) + [anywhere()] * len(gates),
+            in_specs=[vmem()] * len(operands),
             out_specs=[vmem()] * 2,
             compiler_params=params(2),
             name=name,
-        )(*map(held, operands), *gates)
-
-    early_rows = 1024 if half > 1024 else half // 2
-    first_quarter = fetch(lm_weight, 0, early_rows, send_left)
+        )(*map(held, operands))
+
 
     got_left = swap(send_left, "tensor", 1, tensor_size)
     got_right = swap(send_right, "tensor", 2, tensor_size)
-    left, send_left = add(fold_kernel, "fold_left", (block, half), keep_left, got_left, gates=(first_quarter,))
+    left, send_left = add(fold_kernel, "fold_left", (block, half), keep_left, got_left)
     right, send_right = add(fold_kernel, "fold_right", (block, half), keep_right, got_right)
     got_left = swap(send_left, "tensor", 2, tensor_size)
     got_right = swap(send_right, "tensor", 1, tensor_size)
     total, send = add(side_kernel, "side", (block, depth), left, got_left, right, got_right)
-    second_quarter = fetch(lm_weight, early_rows, half - early_rows, send)
+    first_quarter = fetch(lm_weight, 0, quarter, send)
+    second_quarter = fetch(lm_weight, quarter, quarter, send)
     far = 4
     while 2 * far < tensor_size:
         total, send = add(
@@ -548,12 +546,13 @@
     normed = pl.pallas_call(
         norm_kernel,
         out_shape=jax.ShapeDtypeStruct((block, depth), BF16),
-        in_specs=[vmem()] * 2 + [anywhere()] + [vmem()] * 2,
+        in_specs=[vmem()] * 2 + [anywhere()] * 2 + [vmem()] * 2,
         out_specs=vmem(),
         compiler_params=params(4),
         name="norm",
     )(
         *map(held, (residual.reshape(4, block, depth), norm_gain[None])),
+        first_quarter,
         second_quarter,
         *map(held, (total, swap(send, "tensor", far, tensor_size))),
     )

time: 80.2 us -> 79.8 us (level)
  starting transfers between devices: 22.3 us -> 23.7 us
  waiting for transfers between devices: 15.9 us -> 14.7 us
    ppermute x6, waiting for transfers between devices: 5.7 us -> 4.1 us  [around(): lax.ppermute(x, ('group', 'tensor'), routes[place])]
    ppermute x6, starting transfers between devices: 6.29 us -> 7.21 us  [around(): lax.ppermute(x, ('group', 'tensor'), routes[place])]
  transfers between devices with their start and end apart: 20 -> 20, of which waited for: 13 -> 11; matrix products, arithmetic and copies ran while one was open for 1% -> 1% of each run, Pallas kernels for 24% -> 25%
where the time goes in v15:
time: 79.8 us; the launch traced here: 79.6 us
  Pallas kernels  29.6 us (37%)
  starting transfers between devices  23.7 us (30%)
  waiting for transfers between devices  14.7 us (18%)
  blocking collectives  10.5 us (13%)
  local copies, waits for them, and re-layouts  0.9 us (1%)
    ppermute x14, starting transfers between devices, swap(): return lax.ppermute(x, axis, [(i, i ^ distance) for i in range(size)])  16.5 us
    ppermute x14, waiting for transfers between devices, swap(): return lax.ppermute(x, axis, [(i, i ^ distance) for i in range(size)])  10.6 us
    all_to_all x1, blocking collectives, local(): stats = lax.all_to_all(stats, ('group', 'tensor'), 0, 0, tiled=True)  10.5 us
    pallas_call x3, Pallas kernels, fetch(): pl.pallas_call(functools.partial(fetch_kernel, start), out_shape=pltpu.VM...  10.1 us
    ppermute x6, starting transfers between devices, around(): lax.ppermute(x, ('group', 'tensor'), routes[place])  7.21 us
    pallas_call x1, Pallas kernels, local(): pl.pallas_call(functools.partial(logits_kernel, vocab, spots, tensor_size...  5 us
    pallas_call x1, Pallas kernels, local(): pl.pallas_call(functools.partial(first_kernel, narrow), out_shape=[pltpu....  4.52 us
    ppermute x6, waiting for transfers between devices, around(): lax.ppermute(x, ('group', 'tensor'), routes[place])  4.1 us
  transfers between devices with their start and end apart: 20, of which 11 were waited for; matrix products, arithmetic and copies ran while one was open for 1% of the time, Pallas kernels for 25%

profile of v15, /device:TPU:0, one launch (start us, length us, event | category | flops | bytes accessed | tf_op | source)
XLA Modules:
  0.0 79.6 jit_solution(14452283521589990519)
XLA Ops:
  0.0 3.0 %collective-permute-start = (bf16[64,512]{1,0:T(8,128)(2,1)}, bf16[64,512]{1,0:T(8,128)(2,1)S(1)}, u32[]{:S(2)}, u32[]{:S(2)}) collective-permute-start(bf16[64,512]{1,0:T(8,128)(2,1)} %refs_0_.1), channel_id=1, source_target_pairs={{0,16},{8,24},{16,0},{24,8},{1,17},{9,25},{17,1},{25,9},{2,18},{10... | collective-permute-start | bytes 196616 | tf_op jit(solution)/shard_map/ppermute | solution.py:47
  3.0 0.9 %reshape.8.refs_1_.target_ref = s32[32,8,1]{2,1,0:T(8,128)S(1)} reshape(s32[256]{0:T(256)} %param.23) | data formatting | bytes 2048 | tf_op jit(solution)/shard_map/reshape | solution.py:422
  3.9 1.6 %collective-permute-done.refs_0_ = bf16[64,512]{1,0:T(8,128)(2,1)S(1)} collective-permute-done((bf16[64,512]{1,0:T(8,128)(2,1)}, bf16[64,512]{1,0:T(8,128)(2,1)S(1)}, u32[]{:S(2)}, u32[]{:S(2)}) %collective-permute-start) | collective-permute-done | bytes 65568 | tf_op jit(solution)/shard_map/ppermute | solution.py:47
  5.5 1.4 %load.1 = (bf16[64,512]{1,0:T(8,128)(2,1)S(1)}, bf16[64,512]{1,0:T(8,128)(2,1)S(1)}, bf16[64,512]{1,0:T(8,128)(2,1)S(1)}, bf16[512,512]{1,0:T(8,128)(2,1)S(1)}, bf16[512,512]{1,0:T(8,128)(2,1)S(1)}) custom-call(bf16[64,512]{1,0:T(8,128)(2,1)S(1)} %pass.1.gate_ref.refs_1_, bf16[64,512]{1,0:T(8,128)(2,1)} %refs_0_.1, bf16[64,512]{1,0:T(8,128)(2,1)} %refs_1_.1, ...), custom_call_target="tpu_custom_call" | custom-call | bytes 2097152 | tf_op jit(solution)/shard_map/load/pallas_call | solution.py:440
  6.9 0.9 %prefix_attention.1 = (bf16[64,640]{1,0:T(8,128)(2,1)S(1)}, bf16[64,640]{1,0:T(8,128)(2,1)S(1)}, bf16[64,640]{1,0:T(8,128)(2,1)S(1)}) custom-call(bf16[64,512]{1,0:T(8,128)(2,1)S(1)} %collective-permute-done.1.refs_0_, bf16[64,512]{1,0:T(8,128)(2,1)S(1)} %pass.1.gate_ref.refs_1_, bf16[64,512]{1,0:T(8,128)(2,1)S(1)} %collective-permute-done.2.refs_2_, ...), custom_call_target="tpu_custom_call" | custom-call | tf_op jit(solution)/shard_map/prefix_attention/pallas_call | solution.py:451
  7.8 2.1 %collective-permute-start.4 = (bf16[64,640]{1,0:T(8,128)(2,1)S(1)}, bf16[64,640]{1,0:T(8,128)(2,1)S(1)}, u32[]{:S(2)}, u32[]{:S(2)}) collective-permute-start(bf16[64,640]{1,0:T(8,128)(2,1)S(1)} %get-tuple-element.38), channel_id=1, source_target_pairs={{0,16},{8,24},{16,0},{24,8},{1,17},{9,25},{17,1},{25,9},{2,18},{10... | collective-permute-start | bytes 245768 | tf_op jit(solution)/shard_map/ppermute | solution.py:47
  10.1 3.5 %own_attention.1 = (f32[64,640]{1,0:T(8,128)S(1)}, f32[8,128]{1,0:T(8,128)S(1)}, bf16[512,5120]{1,0:T(8,128)(2,1)S(1)}) custom-call(s32[2]{0:T(128)} %lengths_ref.1, s32[2]{0:T(128)} %prompt_ref.3, bf16[64,512]{1,0:T(8,128)(2,1)S(1)} %get-tuple-element.30.q_ref, bf16[64,512]{1,0:T(8,128)(2,1)S(1)} %get-tuple-element.31.rk_ref, ...), custom_call_target="tpu_custom_call" | custom-call | bytes 8388608 | tf_op jit(solution)/shard_map/own_attention/pallas_call | solution.py:460
  13.7 0.7 collective-permute-done.3.refs_0_
  14.4 3.3 %project.1 = (bf16[2,16,2560]{2,1,0:T(8,128)(2,1)S(1)}, f32[2,16,2560]{2,1,0:T(8,128)S(1)}, bf16[2,16,2560]{2,1,0:T(8,128)(2,1)S(1)}, f32[2,16,2560]{2,1,0:T(8,128)S(1)}) custom-call(s32[2]{0:T(128)} %prompt_ref.3, f32[64,640]{1,0:T(8,128)S(1)} %get-tuple-element.37.own_ref, bf16[64,640]{1,0:T(8,128)(2,1)S(1)} %collective-permute-done.3.refs_0_, ...), custom_call_target="tpu_custom_call" | custom-call | tf_op jit(solution)/shard_map/project/pallas_call | solution.py:503
  17.7 1.8 %collective-permute-start.6 = (bf16[2,16,2560]{2,1,0:T(8,128)(2,1)S(1)}, bf16[2,16,2560]{2,1,0:T(8,128)(2,1)S(1)}, u32[]{:S(2)}, u32[]{:S(2)}) collective-permute-start(bf16[2,16,2560]{2,1,0:T(8,128)(2,1)S(1)} %get-tuple-element.42), channel_id=1, source_target_pairs={{0,1},{1,0},{2,3},{3,2},{4,5},{5,4},{6,7},{7,6},{8,9},{9,8},{10,11... | collective-permute-start | bytes 491528 | tf_op jit(solution)/shard_map/ppermute | solution.py:47
  19.5 1.6 %collective-permute-start.8 = (bf16[2,16,2560]{2,1,0:T(8,128)(2,1)S(1)}, bf16[2,16,2560]{2,1,0:T(8,128)(2,1)S(1)}, u32[]{:S(2)}, u32[]{:S(2)}) collective-permute-start(bf16[2,16,2560]{2,1,0:T(8,128)(2,1)S(1)} %get-tuple-element.46), channel_id=1, source_target_pairs={{0,2},{1,3},{2,0},{3,1},{4,6},{5,7},{6,4},{7,5},{8,10},{9,11},{10,... | collective-permute-start | bytes 491528 | tf_op jit(solution)/shard_map/ppermute | solution.py:47
  21.0 3.0 %collective-permute-done.6.got_ref = bf16[2,16,2560]{2,1,0:T(8,128)(2,1)S(1)} collective-permute-done((bf16[2,16,2560]{2,1,0:T(8,128)(2,1)S(1)}, bf16[2,16,2560]{2,1,0:T(8,128)(2,1)S(1)}, u32[]{:S(2)}, u32[]{:S(2)}) %collective-permute-start.6) | collective-permute-done | bytes 163872 | tf_op jit(solution)/shard_map/ppermute | solution.py:47
  24.1 1.8 %collective-permute-start.7 = (bf16[16,2560]{1,0:T(8,128)(2,1)S(1)}, bf16[16,2560]{1,0:T(8,128)(2,1)S(1)}, u32[]{:S(2)}, u32[]{:S(2)}) collective-permute-start(bf16[16,2560]{1,0:T(8,128)(2,1)S(1)} %get-tuple-element.44), channel_id=1, source_target_pairs={{0,2},{1,3},{2,0},{3,1},{4,6},{5,7},{6,4},{7,5},{8,10},{9,11},{10,... | collective-permute-start | bytes 245768 | tf_op jit(solution)/shard_map/ppermute | solution.py:47
  25.9 1.6 %collective-permute-start.9 = (bf16[16,2560]{1,0:T(8,128)(2,1)S(1)}, bf16[16,2560]{1,0:T(8,128)(2,1)S(1)}, u32[]{:S(2)}, u32[]{:S(2)}) collective-permute-start(bf16[16,2560]{1,0:T(8,128)(2,1)S(1)} %get-tuple-element.48), channel_id=1, source_target_pairs={{0,1},{1,0},{2,3},{3,2},{4,5},{5,4},{6,7},{7,6},{8,9},{9,8},{10,11... | collective-permute-start | bytes 245768 | tf_op jit(solution)/shard_map/ppermute | solution.py:47
  27.5 1.1 %collective-permute-done.7.got_left_ref = bf16[16,2560]{1,0:T(8,128)(2,1)S(1)} collective-permute-done((bf16[16,2560]{1,0:T(8,128)(2,1)S(1)}, bf16[16,2560]{1,0:T(8,128)(2,1)S(1)}, u32[]{:S(2)}, u32[]{:S(2)}) %collective-permute-start.7) | collective-permute-done | bytes 81952 | tf_op jit(solution)/shard_map/ppermute | solution.py:47
  28.6 1.8 %collective-permute-done.9.got_right_ref = bf16[16,2560]{1,0:T(8,128)(2,1)S(1)} collective-permute-done((bf16[16,2560]{1,0:T(8,128)(2,1)S(1)}, bf16[16,2560]{1,0:T(8,128)(2,1)S(1)}, u32[]{:S(2)}, u32[]{:S(2)}) %collective-permute-start.9) | collective-permute-done | bytes 81952 | tf_op jit(solution)/shard_map/ppermute | solution.py:47
  30.5 2.7 %collective-permute-start.10 = (bf16[16,5120]{1,0:T(8,128)(2,1)S(1)}, bf16[16,5120]{1,0:T(8,128)(2,1)S(1)}, u32[]{:S(2)}, u32[]{:S(2)}) collective-permute-start(bf16[16,5120]{1,0:T(8,128)(2,1)S(1)} %get-tuple-element.49.gate_ref), channel_id=1, source_target_pairs={{0,4},{1,5},{2,6},{3,7},{4,0},{5,1},{6,2},{7,3},{8,12},{9,13},{10,... | collective-permute-start | bytes 491528 | tf_op jit(solution)/shard_map/ppermute | solution.py:47
  33.1 3.3 %fetch.4.second_gate_ref.next_ref = bf16[1280,3072]{1,0:T(8,128)(2,1)S(1)} custom-call(bf16[5120,3072]{1,0:T(8,128)(2,1)} %source_ref.9, bf16[16,5120]{1,0:T(8,128)(2,1)S(1)} %get-tuple-element.49.gate_ref), custom_call_target="tpu_custom_call" | custom-call | bytes 7864320 | tf_op jit(solution)/shard_map/fetch/pallas_call | solution.py:487
  36.5 3.4 %fetch.3.first_gate_ref.weight_ref = bf16[1280,3072]{1,0:T(8,128)(2,1)S(1)} custom-call(bf16[5120,3072]{1,0:T(8,128)(2,1)} %source_ref.9, bf16[16,5120]{1,0:T(8,128)(2,1)S(1)} %get-tuple-element.49.gate_ref), custom_call_target="tpu_custom_call" | custom-call | bytes 7864320 | tf_op jit(solution)/shard_map/fetch/pallas_call | solution.py:487
  40.2 1.2 %collective-permute-start.11 = (bf16[16,5120]{1,0:T(8,128)(2,1)S(1)}, bf16[16,5120]{1,0:T(8,128)(2,1)S(1)}, u32[]{:S(2)}, u32[]{:S(2)}) collective-permute-start(bf16[16,5120]{1,0:T(8,128)(2,1)S(1)} %norm.1.refs_0_), channel_id=1, source_target_pairs={{0,2},{1,3},{2,0},{3,1},{4,6},{5,7},{6,4},{7,5},{8,10},{9,11},{10,... | collective-permute-start | bytes 491528 | tf_op jit(solution)/shard_map/ppermute | solution.py:47
  41.3 1.8 %collective-permute-start.16 = (bf16[16,5120]{1,0:T(8,128)(2,1)S(1)}, bf16[16,5120]{1,0:T(8,128)(2,1)S(1)}, u32[]{:S(2)}, u32[]{:S(2)}) collective-permute-start(bf16[16,5120]{1,0:T(8,128)(2,1)S(1)} %norm.1.refs_0_), channel_id=1, source_target_pairs={{0,17},{1,16},{2,19},{3,18},{4,21},{5,20},{6,23},{7,22},{8,25},{9,... | collective-permute-start | bytes 491528 | tf_op jit(solution)/shard_map/ppermute | solution.py:568
  43.6 1.2 %collective-permute-start.12 = (bf16[16,5120]{1,0:T(8,128)(2,1)S(1)}, bf16[16,5120]{1,0:T(8,128)(2,1)S(1)}, u32[]{:S(2)}, u32[]{:S(2)}) collective-permute-start(bf16[16,5120]{1,0:T(8,128)(2,1)S(1)} %norm.1.refs_0_), channel_id=1, source_target_pairs={{0,1},{1,0},{2,3},{3,2},{4,5},{5,4},{6,7},{7,6},{8,9},{9,8},{10,11... | collective-permute-start | bytes 491528 | tf_op jit(solution)/shard_map/ppermute | solution.py:568
  45.5 2.4 %collective-permute-start.17 = (bf16[16,5120]{1,0:T(8,128)(2,1)S(1)}, bf16[16,5120]{1,0:T(8,128)(2,1)S(1)}, u32[]{:S(2)}, u32[]{:S(2)}) collective-permute-start(bf16[16,5120]{1,0:T(8,128)(2,1)S(1)} %collective-permute-done.11.gate_ref.refs_1_), channel_id=1, source_target_pairs={{0,17},{1,16},{2,19},{3,18},{4,21},{5,20},{6,23},{7,22},{8,25},{9,... | collective-permute-start | bytes 491528 | tf_op jit(solution)/shard_map/ppermute | solution.py:568
  48.5 1.0 %collective-permute-done.16.refs_6_ = bf16[16,5120]{1,0:T(8,128)(2,1)S(1)} collective-permute-done((bf16[16,5120]{1,0:T(8,128)(2,1)S(1)}, bf16[16,5120]{1,0:T(8,128)(2,1)S(1)}, u32[]{:S(2)}, u32[]{:S(2)}) %collective-permute-start.16) | collective-permute-done | bytes 163872 | tf_op jit(solution)/shard_map/ppermute | solution.py:568
  49.5 0.8 collective-permute-start.13
  50.2 3.3 %fetch.5.refs_8_.weight_ref = bf16[1280,3072]{1,0:T(8,128)(2,1)S(1)} custom-call(bf16[5120,3072]{1,0:T(8,128)(2,1)} %source_ref.9, bf16[16,5120]{1,0:T(8,128)(2,1)S(1)} %collective-permute-done.11.gate_ref.refs_1_), custom_call_target="tpu_custom_call" | custom-call | bytes 7864320 | tf_op jit(solution)/shard_map/fetch/pallas_call | solution.py:487
  53.6 1.3 %collective-permute-done.17.refs_7_ = bf16[16,5120]{1,0:T(8,128)(2,1)S(1)} collective-permute-done((bf16[16,5120]{1,0:T(8,128)(2,1)S(1)}, bf16[16,5120]{1,0:T(8,128)(2,1)S(1)}, u32[]{:S(2)}, u32[]{:S(2)}) %collective-permute-start.17) | collective-permute-done | bytes 163872 | tf_op jit(solution)/shard_map/ppermute | solution.py:568
  54.9 1.6 %collective-permute-done.15.refs_5_ = bf16[16,5120]{1,0:T(8,128)(2,1)S(1)} collective-permute-done((bf16[16,5120]{1,0:T(8,128)(2,1)S(1)}, bf16[16,5120]{1,0:T(8,128)(2,1)S(1)}, u32[]{:S(2)}, u32[]{:S(2)}) %collective-permute-start.15) | collective-permute-done | bytes 163872 | tf_op jit(solution)/shard_map/ppermute | solution.py:568
  57.4 1.6 %collective-permute-done.18.right_ref = bf16[128,2560]{1,0:T(8,128)(2,1)S(1)} collective-permute-done((bf16[128,2560]{1,0:T(8,128)(2,1)S(1)}, bf16[128,2560]{1,0:T(8,128)(2,1)S(1)}, u32[]{:S(2)}, u32[]{:S(2)}) %collective-permute-start.18) | collective-permute-done | bytes 655392 | tf_op jit(solution)/shard_map/ppermute | solution.py:47
  59.0 4.5 %logits_first.1 = (f32[256,3072]{1,0:T(8,128)S(1)}, bf16[1280,3072]{1,0:T(8,128)(2,1)S(1)}) custom-call(bf16[128,2560]{1,0:T(8,128)(2,1)S(1)} %get-tuple-element.51.left_ref, bf16[128,2560]{1,0:T(8,128)(2,1)S(1)} %collective-permute-done.18.right_ref, bf16[1280,3072]{1,0:T(8,128)(2,1)S(1)} %fetch.3.first_gate_ref.weight_ref, ...), custom_call_target="tpu_custom_call" | custom-call | flops 4026531840 | tf_op jit(solution)/shard_map/logits_first/pallas_call | solution.py:592
  63.5 5.0 %logits.1 = f32[32,1,128]{2,1,0:T(1,128)S(1)} custom-call(f32[256,3072]{1,0:T(8,128)S(1)} %get-tuple-element.52.sum_in_ref, bf16[128,2560]{1,0:T(8,128)(2,1)S(1)} %get-tuple-element.53.left_ref, bf16[128,2560]{1,0:T(8,128)(2,1)S(1)} %collective-permute-done.19.right_ref, s32[32,8,1]{2,1,0:T(8,128)S(1)} %reshape.8.refs_1_.target_ref, ...), custom_call_target="tpu_custom_call" | custom-call | flops 4026531840 | tf_op jit(solution)/shard_map/logits/pallas_call | solution.py:605
  68.5 10.5 %all_to_all.5.stats_ref = f32[32,1,128]{2,1,0:T(1,128)S(1)} all-to-all(f32[32,1,128]{2,1,0:T(1,128)S(1)} %logits.1), channel_id=1, replica_groups=mesh['group'=4,'tensor'=8] {'group','tensor'}, dimensions={0} | all-to-all | bytes 32768 | tf_op jit(solution)/shard_map/all_to_all | solution.py:618
  (31 shorter events, 3.9 us)
Async XLA Ops:
  0.0 5.4 %collective-permute-start = (bf16[64,512]{1,0:T(8,128)(2,1)}, bf16[64,512]{1,0:T(8,128)(2,1)S(1)}, u32[]{:S(2)}, u32[]{:S(2)}) collective-permute-start(bf16[64,512]{1,0:T(8,128)(2,1)} %refs_0_.1), channel_id=1, source_target_pairs={{0,16},{8,24},{16,0},{24,8},{1,17},{9,25},{17,1},{25,9},{2,18},{10... | collective-permute-start | bytes 196616 | tf_op jit(solution)/shard_map/ppermute | solution.py:47
  3.0 3.9 %collective-permute-start.2 = (bf16[64,512]{1,0:T(8,128)(2,1)}, bf16[64,512]{1,0:T(8,128)(2,1)S(1)}, u32[]{:S(2)}, u32[]{:S(2)}) collective-permute-start(bf16[64,512]{1,0:T(8,128)(2,1)} %refs_0_.1), channel_id=1, source_target_pairs={{0,8},{8,0},{16,24},{24,16},{1,9},{9,1},{17,25},{25,17},{2,10},{10... | collective-permute-start | bytes 196616 | tf_op jit(solution)/shard_map/ppermute | solution.py:47
  5.4 27.7 %copy-start.1 = (bf16[5120]{0:T(1024)(128)(2,1)S(1)}, bf16[5120]{0:T(1024)(128)(2,1)}, u32[]{:S(2)}) copy-start(bf16[5120]{0:T(1024)(128)(2,1)} %param.21) | copy-start | bytes 30724
  5.4 1.5 %collective-permute-start.1 = (bf16[64,512]{1,0:T(8,128)(2,1)S(1)}, bf16[64,512]{1,0:T(8,128)(2,1)S(1)}, u32[]{:S(2)}, u32[]{:S(2)}) collective-permute-start(bf16[64,512]{1,0:T(8,128)(2,1)S(1)} %pass.1.gate_ref.refs_1_), channel_id=1, source_target_pairs={{0,8},{8,0},{16,24},{24,16},{1,9},{9,1},{17,25},{25,17},{2,10},{10... | collective-permute-start | bytes 196616 | tf_op jit(solution)/shard_map/ppermute | solution.py:47
  7.8 5.9 %collective-permute-start.4 = (bf16[64,640]{1,0:T(8,128)(2,1)S(1)}, bf16[64,640]{1,0:T(8,128)(2,1)S(1)}, u32[]{:S(2)}, u32[]{:S(2)}) collective-permute-start(bf16[64,640]{1,0:T(8,128)(2,1)S(1)} %get-tuple-element.38), channel_id=1, source_target_pairs={{0,16},{8,24},{16,0},{24,8},{1,17},{9,25},{17,1},{25,9},{2,18},{10... | collective-permute-start | bytes 245768 | tf_op jit(solution)/shard_map/ppermute | solution.py:47
  9.9 3.8 %collective-permute-start.5 = (bf16[64,640]{1,0:T(8,128)(2,1)S(1)}, bf16[64,640]{1,0:T(8,128)(2,1)S(1)}, u32[]{:S(2)}, u32[]{:S(2)}) collective-permute-start(bf16[64,640]{1,0:T(8,128)(2,1)S(1)} %get-tuple-element.39), channel_id=1, source_target_pairs={{0,8},{8,0},{16,24},{24,16},{1,9},{9,1},{17,25},{25,17},{2,10},{10... | collective-permute-start | bytes 245768 | tf_op jit(solution)/shard_map/ppermute | solution.py:47
  10.1 4.3 %collective-permute-start.3 = (bf16[64,640]{1,0:T(8,128)(2,1)S(1)}, bf16[64,640]{1,0:T(8,128)(2,1)S(1)}, u32[]{:S(2)}, u32[]{:S(2)}) collective-permute-start(bf16[64,640]{1,0:T(8,128)(2,1)S(1)} %get-tuple-element.35.gate_ref), channel_id=1, source_target_pairs={{0,24},{8,16},{16,8},{24,0},{1,25},{9,17},{17,9},{25,1},{2,26},{10... | collective-permute-start | bytes 245768 | tf_op jit(solution)/shard_map/ppermute | solution.py:47
  17.7 6.4 %collective-permute-start.6 = (bf16[2,16,2560]{2,1,0:T(8,128)(2,1)S(1)}, bf16[2,16,2560]{2,1,0:T(8,128)(2,1)S(1)}, u32[]{:S(2)}, u32[]{:S(2)}) collective-permute-start(bf16[2,16,2560]{2,1,0:T(8,128)(2,1)S(1)} %get-tuple-element.42), channel_id=1, source_target_pairs={{0,1},{1,0},{2,3},{3,2},{4,5},{5,4},{6,7},{7,6},{8,9},{9,8},{10,11... | collective-permute-start | bytes 491528 | tf_op jit(solution)/shard_map/ppermute | solution.py:47
  19.5 6.4 %collective-permute-start.8 = (bf16[2,16,2560]{2,1,0:T(8,128)(2,1)S(1)}, bf16[2,16,2560]{2,1,0:T(8,128)(2,1)S(1)}, u32[]{:S(2)}, u32[]{:S(2)}) collective-permute-start(bf16[2,16,2560]{2,1,0:T(8,128)(2,1)S(1)} %get-tuple-element.46), channel_id=1, source_target_pairs={{0,2},{1,3},{2,0},{3,1},{4,6},{5,7},{6,4},{7,5},{8,10},{9,11},{10,... | collective-permute-start | bytes 491528 | tf_op jit(solution)/shard_map/ppermute | solution.py:47
  24.1 4.5 %collective-permute-start.7 = (bf16[16,2560]{1,0:T(8,128)(2,1)S(1)}, bf16[16,2560]{1,0:T(8,128)(2,1)S(1)}, u32[]{:S(2)}, u32[]{:S(2)}) collective-permute-start(bf16[16,2560]{1,0:T(8,128)(2,1)S(1)} %get-tuple-element.44), channel_id=1, source_target_pairs={{0,2},{1,3},{2,0},{3,1},{4,6},{5,7},{6,4},{7,5},{8,10},{9,11},{10,... | collective-permute-start | bytes 245768 | tf_op jit(solution)/shard_map/ppermute | solution.py:47
  25.9 4.5 %collective-permute-start.9 = (bf16[16,2560]{1,0:T(8,128)(2,1)S(1)}, bf16[16,2560]{1,0:T(8,128)(2,1)S(1)}, u32[]{:S(2)}, u32[]{:S(2)}) collective-permute-start(bf16[16,2560]{1,0:T(8,128)(2,1)S(1)} %get-tuple-element.48), channel_id=1, source_target_pairs={{0,1},{1,0},{2,3},{3,2},{4,5},{5,4},{6,7},{7,6},{8,9},{9,8},{10,11... | collective-permute-start | bytes 245768 | tf_op jit(solution)/shard_map/ppermute | solution.py:47
  30.5 9.5 %collective-permute-start.10 = (bf16[16,5120]{1,0:T(8,128)(2,1)S(1)}, bf16[16,5120]{1,0:T(8,128)(2,1)S(1)}, u32[]{:S(2)}, u32[]{:S(2)}) collective-permute-start(bf16[16,5120]{1,0:T(8,128)(2,1)S(1)} %get-tuple-element.49.gate_ref), channel_id=1, source_target_pairs={{0,4},{1,5},{2,6},{3,7},{4,0},{5,1},{6,2},{7,3},{8,12},{9,13},{10,... | collective-permute-start | bytes 491528 | tf_op jit(solution)/shard_map/ppermute | solution.py:47
  36.5 3.4 %copy-start = (bf16[64,5120]{1,0:T(8,128)(2,1)S(1)}, bf16[64,5120]{1,0:T(8,128)(2,1)}, u32[]{:S(2)}) copy-start(bf16[64,5120]{1,0:T(8,128)(2,1)} %param.19) | copy-start | bytes 1966084
  40.2 5.4 %collective-permute-start.11 = (bf16[16,5120]{1,0:T(8,128)(2,1)S(1)}, bf16[16,5120]{1,0:T(8,128)(2,1)S(1)}, u32[]{:S(2)}, u32[]{:S(2)}) collective-permute-start(bf16[16,5120]{1,0:T(8,128)(2,1)S(1)} %norm.1.refs_0_), channel_id=1, source_target_pairs={{0,2},{1,3},{2,0},{3,1},{4,6},{5,7},{6,4},{7,5},{8,10},{9,11},{10,... | collective-permute-start | bytes 491528 | tf_op jit(solution)/shard_map/ppermute | solution.py:47
  41.3 8.1 %collective-permute-start.16 = (bf16[16,5120]{1,0:T(8,128)(2,1)S(1)}, bf16[16,5120]{1,0:T(8,128)(2,1)S(1)}, u32[]{:S(2)}, u32[]{:S(2)}) collective-permute-start(bf16[16,5120]{1,0:T(8,128)(2,1)S(1)} %norm.1.refs_0_), channel_id=1, source_target_pairs={{0,17},{1,16},{2,19},{3,18},{4,21},{5,20},{6,23},{7,22},{8,25},{9,... | collective-permute-start | bytes 491528 | tf_op jit(solution)/shard_map/ppermute | solution.py:568
  43.1 10.5 %collective-permute-start.14 = (bf16[16,5120]{1,0:T(8,128)(2,1)S(1)}, bf16[16,5120]{1,0:T(8,128)(2,1)S(1)}, u32[]{:S(2)}, u32[]{:S(2)}) collective-permute-start(bf16[16,5120]{1,0:T(8,128)(2,1)S(1)} %norm.1.refs_0_), channel_id=1, source_target_pairs={{0,16},{1,17},{2,18},{3,19},{4,20},{5,21},{6,22},{7,23},{8,24},{9,... | collective-permute-start | bytes 491528 | tf_op jit(solution)/shard_map/ppermute | solution.py:568
  43.6 10.0 %collective-permute-start.12 = (bf16[16,5120]{1,0:T(8,128)(2,1)S(1)}, bf16[16,5120]{1,0:T(8,128)(2,1)S(1)}, u32[]{:S(2)}, u32[]{:S(2)}) collective-permute-start(bf16[16,5120]{1,0:T(8,128)(2,1)S(1)} %norm.1.refs_0_), channel_id=1, source_target_pairs={{0,1},{1,0},{2,3},{3,2},{4,5},{5,4},{6,7},{7,6},{8,9},{9,8},{10,11... | collective-permute-start | bytes 491528 | tf_op jit(solution)/shard_map/ppermute | solution.py:568
  45.5 9.4 %collective-permute-start.17 = (bf16[16,5120]{1,0:T(8,128)(2,1)S(1)}, bf16[16,5120]{1,0:T(8,128)(2,1)S(1)}, u32[]{:S(2)}, u32[]{:S(2)}) collective-permute-start(bf16[16,5120]{1,0:T(8,128)(2,1)S(1)} %collective-permute-done.11.gate_ref.refs_1_), channel_id=1, source_target_pairs={{0,17},{1,16},{2,19},{3,18},{4,21},{5,20},{6,23},{7,22},{8,25},{9,... | collective-permute-start | bytes 491528 | tf_op jit(solution)/shard_map/ppermute | solution.py:568
  48.0 8.5 %collective-permute-start.15 = (bf16[16,5120]{1,0:T(8,128)(2,1)S(1)}, bf16[16,5120]{1,0:T(8,128)(2,1)S(1)}, u32[]{:S(2)}, u32[]{:S(2)}) collective-permute-start(bf16[16,5120]{1,0:T(8,128)(2,1)S(1)} %collective-permute-done.11.gate_ref.refs_1_), channel_id=1, source_target_pairs={{0,16},{1,17},{2,18},{3,19},{4,20},{5,21},{6,22},{7,23},{8,24},{9,... | collective-permute-start | bytes 491528 | tf_op jit(solution)/shard_map/ppermute | solution.py:568
  49.5 7.3 %collective-permute-start.13 = (bf16[16,5120]{1,0:T(8,128)(2,1)S(1)}, bf16[16,5120]{1,0:T(8,128)(2,1)S(1)}, u32[]{:S(2)}, u32[]{:S(2)}) collective-permute-start(bf16[16,5120]{1,0:T(8,128)(2,1)S(1)} %collective-permute-done.11.gate_ref.refs_1_), channel_id=1, source_target_pairs={{0,1},{1,0},{2,3},{3,2},{4,5},{5,4},{6,7},{7,6},{8,9},{9,8},{10,11... | collective-permute-start | bytes 491528 | tf_op jit(solution)/shard_map/ppermute | solution.py:568
  56.8 2.2 %collective-permute-start.18 = (bf16[128,2560]{1,0:T(8,128)(2,1)S(1)}, bf16[128,2560]{1,0:T(8,128)(2,1)S(1)}, u32[]{:S(2)}, u32[]{:S(2)}) collective-permute-start(bf16[128,2560]{1,0:T(8,128)(2,1)S(1)} %get-tuple-element.51.left_ref), channel_id=1, source_target_pairs={{0,8},{8,0},{16,24},{24,16},{1,9},{9,1},{17,25},{25,17},{2,10},{10... | collective-permute-start | bytes 1966088 | tf_op jit(solution)/shard_map/ppermute | solution.py:47
  56.9 6.6 %collective-permute-start.19 = (bf16[128,2560]{1,0:T(8,128)(2,1)S(1)}, bf16[128,2560]{1,0:T(8,128)(2,1)S(1)}, u32[]{:S(2)}, u32[]{:S(2)}) collective-permute-start(bf16[128,2560]{1,0:T(8,128)(2,1)S(1)} %get-tuple-element.53.left_ref), channel_id=1, source_target_pairs={{0,8},{8,0},{16,24},{24,16},{1,9},{9,1},{17,25},{25,17},{2,10},{10... | collective-permute-start | bytes 1966088 | tf_op jit(solution)/shard_map/ppermute | solution.py:47

commit v16 on v15

--- a/solution.py
+++ b/solution.py
@@ -420,6 +420,7 @@
     i32 = jnp.int32
 
     wanted = targets.reshape(-1, share, 1)
+    gain = norm_gain[None]
     above = list(range(2, group_size, 2))
     distances = list(range(group_size - 1, 0, -1))
     far_queries = [swap(resp_query, "group", a, group_size) for a in above]
@@ -427,11 +428,11 @@
     far_queries = pl.pallas_call(
         functools.partial(pass_kernel, len(above)),
         out_shape=[jax.ShapeDtypeStruct(x.shape, x.dtype) for x in far_queries],
-        in_specs=[vmem()] * len(above) + [anywhere()],
+        in_specs=[vmem()] * len(above) + [anywhere()] * 2,
         out_specs=[vmem()] * len(above),
         compiler_params=params(1),
         name="pass",
-    )(*map(held, far_queries), wanted)
+    )(*map(held, far_queries), wanted, gain)
     for a, x in zip(above, far_queries):
         queries[a] = x
         queries[a + 1] = swap(x, "group", 1, group_size)
@@ -551,7 +552,7 @@
         compiler_params=params(4),
         name="norm",
     )(
-        *map(held, (residual.reshape(4, block, depth), norm_gain[None])),
+        *map(held, (residual.reshape(4, block, depth), gain)),
         first_quarter,
         second_quarter,
         *map(held, (total, swap(send, "tensor", far, tensor_size))),

time: 79.8 us -> 79.8 us (level)
  waiting for transfers between devices: 14.7 us -> 13.8 us
  transfers between devices with their start and end apart: 20 -> 20, of which waited for: 11 -> 11; matrix products, arithmetic and copies ran while one was open for 1% -> 2% of each run, Pallas kernels for 25% -> 25%
where the time goes in v16:
time: 79.8 us; the launch traced here: 79.5 us
  Pallas kernels  29.6 us (37%)
  starting transfers between devices  23.7 us (30%)
  waiting for transfers between devices  13.8 us (17%)
  blocking collectives  10.5 us (13%)
  local copies, waits for them, and re-layouts  1.6 us (2%)
    ppermute x14, starting transfers between devices, swap(): return lax.ppermute(x, axis, [(i, i ^ distance) for i in range(size)])  16.4 us
    all_to_all x1, blocking collectives, local(): stats = lax.all_to_all(stats, ('group', 'tensor'), 0, 0, tiled=True)  10.5 us
    pallas_call x3, Pallas kernels, fetch(): pl.pallas_call(functools.partial(fetch_kernel, start), out_shape=pltpu.VM...  10.1 us
    ppermute x14, waiting for transfers between devices, swap(): return lax.ppermute(x, axis, [(i, i ^ distance) for i in range(size)])  9.84 us
    ppermute x6, starting transfers between devices, around(): lax.ppermute(x, ('group', 'tensor'), routes[place])  7.3 us
    pallas_call x1, Pallas kernels, local(): pl.pallas_call(functools.partial(logits_kernel, vocab, spots, tensor_size...  5 us
    pallas_call x1, Pallas kernels, local(): pl.pallas_call(functools.partial(first_kernel, narrow), out_shape=[pltpu....  4.52 us
    ppermute x6, waiting for transfers between devices, around(): lax.ppermute(x, ('group', 'tensor'), routes[place])  4 us
  transfers between devices with their start and end apart: 20, of which 11 were waited for; matrix products, arithmetic and copies ran while one was open for 2% of the time, Pallas kernels for 25%

profile of v16, /device:TPU:0, one launch (start us, length us, event | category | flops | bytes accessed | tf_op | source)
XLA Modules:
  0.0 79.5 jit_solution(12012165722322417052)
XLA Ops:
  0.0 3.0 %collective-permute-start = (bf16[64,512]{1,0:T(8,128)(2,1)}, bf16[64,512]{1,0:T(8,128)(2,1)S(1)}, u32[]{:S(2)}, u32[]{:S(2)}) collective-permute-start(bf16[64,512]{1,0:T(8,128)(2,1)} %refs_0_.1), channel_id=1, source_target_pairs={{0,16},{8,24},{16,0},{24,8},{1,17},{9,25},{17,1},{25,9},{2,18},{10... | collective-permute-start | bytes 196616 | tf_op jit(solution)/shard_map/ppermute | solution.py:47
  3.7 0.9 %reshape.8.refs_1_.target_ref = s32[32,8,1]{2,1,0:T(8,128)S(1)} reshape(s32[256]{0:T(256)} %param.23) | data formatting | bytes 2048 | tf_op jit(solution)/shard_map/reshape | solution.py:422
  4.6 0.8 %collective-permute-done.refs_0_ = bf16[64,512]{1,0:T(8,128)(2,1)S(1)} collective-permute-done((bf16[64,512]{1,0:T(8,128)(2,1)}, bf16[64,512]{1,0:T(8,128)(2,1)S(1)}, u32[]{:S(2)}, u32[]{:S(2)}) %collective-permute-start) | collective-permute-done | bytes 65568 | tf_op jit(solution)/shard_map/ppermute | solution.py:47
  5.4 1.4 %load.1 = (bf16[64,512]{1,0:T(8,128)(2,1)S(1)}, bf16[64,512]{1,0:T(8,128)(2,1)S(1)}, bf16[64,512]{1,0:T(8,128)(2,1)S(1)}, bf16[512,512]{1,0:T(8,128)(2,1)S(1)}, bf16[512,512]{1,0:T(8,128)(2,1)S(1)}) custom-call(bf16[64,512]{1,0:T(8,128)(2,1)S(1)} %pass.1.gate_ref.refs_1_, bf16[64,512]{1,0:T(8,128)(2,1)} %refs_0_.1, bf16[64,512]{1,0:T(8,128)(2,1)} %refs_1_.1, ...), custom_call_target="tpu_custom_call" | custom-call | bytes 2097152 | tf_op jit(solution)/shard_map/load/pallas_call | solution.py:441
  6.8 0.9 %prefix_attention.1 = (bf16[64,640]{1,0:T(8,128)(2,1)S(1)}, bf16[64,640]{1,0:T(8,128)(2,1)S(1)}, bf16[64,640]{1,0:T(8,128)(2,1)S(1)}) custom-call(bf16[64,512]{1,0:T(8,128)(2,1)S(1)} %collective-permute-done.1.refs_0_, bf16[64,512]{1,0:T(8,128)(2,1)S(1)} %pass.1.gate_ref.refs_1_, bf16[64,512]{1,0:T(8,128)(2,1)S(1)} %collective-permute-done.2.refs_2_, ...), custom_call_target="tpu_custom_call" | custom-call | tf_op jit(solution)/shard_map/prefix_attention/pallas_call | solution.py:452
  7.7 2.1 %collective-permute-start.4 = (bf16[64,640]{1,0:T(8,128)(2,1)S(1)}, bf16[64,640]{1,0:T(8,128)(2,1)S(1)}, u32[]{:S(2)}, u32[]{:S(2)}) collective-permute-start(bf16[64,640]{1,0:T(8,128)(2,1)S(1)} %get-tuple-element.38), channel_id=1, source_target_pairs={{0,16},{8,24},{16,0},{24,8},{1,17},{9,25},{17,1},{25,9},{2,18},{10... | collective-permute-start | bytes 245768 | tf_op jit(solution)/shard_map/ppermute | solution.py:47
  10.0 3.5 %own_attention.1 = (f32[64,640]{1,0:T(8,128)S(1)}, f32[8,128]{1,0:T(8,128)S(1)}, bf16[512,5120]{1,0:T(8,128)(2,1)S(1)}) custom-call(s32[2]{0:T(128)} %lengths_ref.1, s32[2]{0:T(128)} %prompt_ref.3, bf16[64,512]{1,0:T(8,128)(2,1)S(1)} %get-tuple-element.30.q_ref, bf16[64,512]{1,0:T(8,128)(2,1)S(1)} %get-tuple-element.31.rk_ref, ...), custom_call_target="tpu_custom_call" | custom-call | bytes 8388608 | tf_op jit(solution)/shard_map/own_attention/pallas_call | solution.py:461
  13.6 0.7 collective-permute-done.3.refs_0_
  14.3 3.3 %project.1 = (bf16[2,16,2560]{2,1,0:T(8,128)(2,1)S(1)}, f32[2,16,2560]{2,1,0:T(8,128)S(1)}, bf16[2,16,2560]{2,1,0:T(8,128)(2,1)S(1)}, f32[2,16,2560]{2,1,0:T(8,128)S(1)}) custom-call(s32[2]{0:T(128)} %prompt_ref.3, f32[64,640]{1,0:T(8,128)S(1)} %get-tuple-element.37.own_ref, bf16[64,640]{1,0:T(8,128)(2,1)S(1)} %collective-permute-done.3.refs_0_, ...), custom_call_target="tpu_custom_call" | custom-call | tf_op jit(solution)/shard_map/project/pallas_call | solution.py:504
  17.6 1.8 %collective-permute-start.6 = (bf16[2,16,2560]{2,1,0:T(8,128)(2,1)S(1)}, bf16[2,16,2560]{2,1,0:T(8,128)(2,1)S(1)}, u32[]{:S(2)}, u32[]{:S(2)}) collective-permute-start(bf16[2,16,2560]{2,1,0:T(8,128)(2,1)S(1)} %get-tuple-element.42), channel_id=1, source_target_pairs={{0,1},{1,0},{2,3},{3,2},{4,5},{5,4},{6,7},{7,6},{8,9},{9,8},{10,11... | collective-permute-start | bytes 491528 | tf_op jit(solution)/shard_map/ppermute | solution.py:47
  19.4 1.6 %collective-permute-start.8 = (bf16[2,16,2560]{2,1,0:T(8,128)(2,1)S(1)}, bf16[2,16,2560]{2,1,0:T(8,128)(2,1)S(1)}, u32[]{:S(2)}, u32[]{:S(2)}) collective-permute-start(bf16[2,16,2560]{2,1,0:T(8,128)(2,1)S(1)} %get-tuple-element.46), channel_id=1, source_target_pairs={{0,2},{1,3},{2,0},{3,1},{4,6},{5,7},{6,4},{7,5},{8,10},{9,11},{10,... | collective-permute-start | bytes 491528 | tf_op jit(solution)/shard_map/ppermute | solution.py:47
  21.0 3.0 %collective-permute-done.6.got_ref = bf16[2,16,2560]{2,1,0:T(8,128)(2,1)S(1)} collective-permute-done((bf16[2,16,2560]{2,1,0:T(8,128)(2,1)S(1)}, bf16[2,16,2560]{2,1,0:T(8,128)(2,1)S(1)}, u32[]{:S(2)}, u32[]{:S(2)}) %collective-permute-start.6) | collective-permute-done | bytes 163872 | tf_op jit(solution)/shard_map/ppermute | solution.py:47
  24.0 1.8 %collective-permute-start.7 = (bf16[16,2560]{1,0:T(8,128)(2,1)S(1)}, bf16[16,2560]{1,0:T(8,128)(2,1)S(1)}, u32[]{:S(2)}, u32[]{:S(2)}) collective-permute-start(bf16[16,2560]{1,0:T(8,128)(2,1)S(1)} %get-tuple-element.44), channel_id=1, source_target_pairs={{0,2},{1,3},{2,0},{3,1},{4,6},{5,7},{6,4},{7,5},{8,10},{9,11},{10,... | collective-permute-start | bytes 245768 | tf_op jit(solution)/shard_map/ppermute | solution.py:47
  25.9 1.6 %collective-permute-start.9 = (bf16[16,2560]{1,0:T(8,128)(2,1)S(1)}, bf16[16,2560]{1,0:T(8,128)(2,1)S(1)}, u32[]{:S(2)}, u32[]{:S(2)}) collective-permute-start(bf16[16,2560]{1,0:T(8,128)(2,1)S(1)} %get-tuple-element.48), channel_id=1, source_target_pairs={{0,1},{1,0},{2,3},{3,2},{4,5},{5,4},{6,7},{7,6},{8,9},{9,8},{10,11... | collective-permute-start | bytes 245768 | tf_op jit(solution)/shard_map/ppermute | solution.py:47
  27.4 1.1 %collective-permute-done.7.got_left_ref = bf16[16,2560]{1,0:T(8,128)(2,1)S(1)} collective-permute-done((bf16[16,2560]{1,0:T(8,128)(2,1)S(1)}, bf16[16,2560]{1,0:T(8,128)(2,1)S(1)}, u32[]{:S(2)}, u32[]{:S(2)}) %collective-permute-start.7) | collective-permute-done | bytes 81952 | tf_op jit(solution)/shard_map/ppermute | solution.py:47
  28.5 1.8 %collective-permute-done.9.got_right_ref = bf16[16,2560]{1,0:T(8,128)(2,1)S(1)} collective-permute-done((bf16[16,2560]{1,0:T(8,128)(2,1)S(1)}, bf16[16,2560]{1,0:T(8,128)(2,1)S(1)}, u32[]{:S(2)}, u32[]{:S(2)}) %collective-permute-start.9) | collective-permute-done | bytes 81952 | tf_op jit(solution)/shard_map/ppermute | solution.py:47
  30.4 2.6 %collective-permute-start.10 = (bf16[16,5120]{1,0:T(8,128)(2,1)S(1)}, bf16[16,5120]{1,0:T(8,128)(2,1)S(1)}, u32[]{:S(2)}, u32[]{:S(2)}) collective-permute-start(bf16[16,5120]{1,0:T(8,128)(2,1)S(1)} %get-tuple-element.49.gate_ref), channel_id=1, source_target_pairs={{0,4},{1,5},{2,6},{3,7},{4,0},{5,1},{6,2},{7,3},{8,12},{9,13},{10,... | collective-permute-start | bytes 491528 | tf_op jit(solution)/shard_map/ppermute | solution.py:47
  33.0 3.3 %fetch.4.second_gate_ref.next_ref = bf16[1280,3072]{1,0:T(8,128)(2,1)S(1)} custom-call(bf16[5120,3072]{1,0:T(8,128)(2,1)} %source_ref.9, bf16[16,5120]{1,0:T(8,128)(2,1)S(1)} %get-tuple-element.49.gate_ref), custom_call_target="tpu_custom_call" | custom-call | bytes 7864320 | tf_op jit(solution)/shard_map/fetch/pallas_call | solution.py:488
  36.4 3.4 %fetch.3.first_gate_ref.weight_ref = bf16[1280,3072]{1,0:T(8,128)(2,1)S(1)} custom-call(bf16[5120,3072]{1,0:T(8,128)(2,1)} %source_ref.9, bf16[16,5120]{1,0:T(8,128)(2,1)S(1)} %get-tuple-element.49.gate_ref), custom_call_target="tpu_custom_call" | custom-call | bytes 7864320 | tf_op jit(solution)/shard_map/fetch/pallas_call | solution.py:488
  40.1 1.2 %collective-permute-start.11 = (bf16[16,5120]{1,0:T(8,128)(2,1)S(1)}, bf16[16,5120]{1,0:T(8,128)(2,1)S(1)}, u32[]{:S(2)}, u32[]{:S(2)}) collective-permute-start(bf16[16,5120]{1,0:T(8,128)(2,1)S(1)} %norm.1.refs_0_), channel_id=1, source_target_pairs={{0,2},{1,3},{2,0},{3,1},{4,6},{5,7},{6,4},{7,5},{8,10},{9,11},{10,... | collective-permute-start | bytes 491528 | tf_op jit(solution)/shard_map/ppermute | solution.py:47
  41.2 1.8 %collective-permute-start.16 = (bf16[16,5120]{1,0:T(8,128)(2,1)S(1)}, bf16[16,5120]{1,0:T(8,128)(2,1)S(1)}, u32[]{:S(2)}, u32[]{:S(2)}) collective-permute-start(bf16[16,5120]{1,0:T(8,128)(2,1)S(1)} %norm.1.refs_0_), channel_id=1, source_target_pairs={{0,17},{1,16},{2,19},{3,18},{4,21},{5,20},{6,23},{7,22},{8,25},{9,... | collective-permute-start | bytes 491528 | tf_op jit(solution)/shard_map/ppermute | solution.py:569
  43.5 1.2 %collective-permute-start.12 = (bf16[16,5120]{1,0:T(8,128)(2,1)S(1)}, bf16[16,5120]{1,0:T(8,128)(2,1)S(1)}, u32[]{:S(2)}, u32[]{:S(2)}) collective-permute-start(bf16[16,5120]{1,0:T(8,128)(2,1)S(1)} %norm.1.refs_0_), channel_id=1, source_target_pairs={{0,1},{1,0},{2,3},{3,2},{4,5},{5,4},{6,7},{7,6},{8,9},{9,8},{10,11... | collective-permute-start | bytes 491528 | tf_op jit(solution)/shard_map/ppermute | solution.py:569
  45.4 2.4 %collective-permute-start.17 = (bf16[16,5120]{1,0:T(8,128)(2,1)S(1)}, bf16[16,5120]{1,0:T(8,128)(2,1)S(1)}, u32[]{:S(2)}, u32[]{:S(2)}) collective-permute-start(bf16[16,5120]{1,0:T(8,128)(2,1)S(1)} %collective-permute-done.11.gate_ref.refs_1_), channel_id=1, source_target_pairs={{0,17},{1,16},{2,19},{3,18},{4,21},{5,20},{6,23},{7,22},{8,25},{9,... | collective-permute-start | bytes 491528 | tf_op jit(solution)/shard_map/ppermute | solution.py:569
  48.4 0.9 %collective-permute-done.16.refs_6_ = bf16[16,5120]{1,0:T(8,128)(2,1)S(1)} collective-permute-done((bf16[16,5120]{1,0:T(8,128)(2,1)S(1)}, bf16[16,5120]{1,0:T(8,128)(2,1)S(1)}, u32[]{:S(2)}, u32[]{:S(2)}) %collective-permute-start.16) | collective-permute-done | bytes 163872 | tf_op jit(solution)/shard_map/ppermute | solution.py:569
  49.3 0.8 %collective-permute-start.13 = (bf16[16,5120]{1,0:T(8,128)(2,1)S(1)}, bf16[16,5120]{1,0:T(8,128)(2,1)S(1)}, u32[]{:S(2)}, u32[]{:S(2)}) collective-permute-start(bf16[16,5120]{1,0:T(8,128)(2,1)S(1)} %collective-permute-done.11.gate_ref.refs_1_), channel_id=1, source_target_pairs={{0,1},{1,0},{2,3},{3,2},{4,5},{5,4},{6,7},{7,6},{8,9},{9,8},{10,11... | collective-permute-start | bytes 491528 | tf_op jit(solution)/shard_map/ppermute | solution.py:569
  50.2 3.3 %fetch.5.refs_8_.weight_ref = bf16[1280,3072]{1,0:T(8,128)(2,1)S(1)} custom-call(bf16[5120,3072]{1,0:T(8,128)(2,1)} %source_ref.9, bf16[16,5120]{1,0:T(8,128)(2,1)S(1)} %collective-permute-done.11.gate_ref.refs_1_), custom_call_target="tpu_custom_call" | custom-call | bytes 7864320 | tf_op jit(solution)/shard_map/fetch/pallas_call | solution.py:488
  53.5 1.3 %collective-permute-done.17.refs_7_ = bf16[16,5120]{1,0:T(8,128)(2,1)S(1)} collective-permute-done((bf16[16,5120]{1,0:T(8,128)(2,1)S(1)}, bf16[16,5120]{1,0:T(8,128)(2,1)S(1)}, u32[]{:S(2)}, u32[]{:S(2)}) %collective-permute-start.17) | collective-permute-done | bytes 163872 | tf_op jit(solution)/shard_map/ppermute | solution.py:569
  54.8 1.6 %collective-permute-done.15.refs_5_ = bf16[16,5120]{1,0:T(8,128)(2,1)S(1)} collective-permute-done((bf16[16,5120]{1,0:T(8,128)(2,1)S(1)}, bf16[16,5120]{1,0:T(8,128)(2,1)S(1)}, u32[]{:S(2)}, u32[]{:S(2)}) %collective-permute-start.15) | collective-permute-done | bytes 163872 | tf_op jit(solution)/shard_map/ppermute | solution.py:569
  57.3 1.6 %collective-permute-done.18.right_ref = bf16[128,2560]{1,0:T(8,128)(2,1)S(1)} collective-permute-done((bf16[128,2560]{1,0:T(8,128)(2,1)S(1)}, bf16[128,2560]{1,0:T(8,128)(2,1)S(1)}, u32[]{:S(2)}, u32[]{:S(2)}) %collective-permute-start.18) | collective-permute-done | bytes 655392 | tf_op jit(solution)/shard_map/ppermute | solution.py:47
  58.9 4.5 %logits_first.1 = (f32[256,3072]{1,0:T(8,128)S(1)}, bf16[1280,3072]{1,0:T(8,128)(2,1)S(1)}) custom-call(bf16[128,2560]{1,0:T(8,128)(2,1)S(1)} %get-tuple-element.51.left_ref, bf16[128,2560]{1,0:T(8,128)(2,1)S(1)} %collective-permute-done.18.right_ref, bf16[1280,3072]{1,0:T(8,128)(2,1)S(1)} %fetch.3.first_gate_ref.weight_ref, ...), custom_call_target="tpu_custom_call" | custom-call | flops 4026531840 | tf_op jit(solution)/shard_map/logits_first/pallas_call | solution.py:593
  63.4 5.0 %logits.1 = f32[32,1,128]{2,1,0:T(1,128)S(1)} custom-call(f32[256,3072]{1,0:T(8,128)S(1)} %get-tuple-element.52.sum_in_ref, bf16[128,2560]{1,0:T(8,128)(2,1)S(1)} %get-tuple-element.53.left_ref, bf16[128,2560]{1,0:T(8,128)(2,1)S(1)} %collective-permute-done.19.right_ref, s32[32,8,1]{2,1,0:T(8,128)S(1)} %reshape.8.refs_1_.target_ref, ...), custom_call_target="tpu_custom_call" | custom-call | flops 4026531840 | tf_op jit(solution)/shard_map/logits/pallas_call | solution.py:606
  68.4 10.5 %all_to_all.5.stats_ref = f32[32,1,128]{2,1,0:T(1,128)S(1)} all-to-all(f32[32,1,128]{2,1,0:T(1,128)S(1)} %logits.1), channel_id=1, replica_groups=mesh['group'=4,'tensor'=8] {'group','tensor'}, dimensions={0} | all-to-all | bytes 32768 | tf_op jit(solution)/shard_map/all_to_all | solution.py:619
  (29 shorter events, 4.5 us)
Async XLA Ops:
  0.0 5.4 %collective-permute-start = (bf16[64,512]{1,0:T(8,128)(2,1)}, bf16[64,512]{1,0:T(8,128)(2,1)S(1)}, u32[]{:S(2)}, u32[]{:S(2)}) collective-permute-start(bf16[64,512]{1,0:T(8,128)(2,1)} %refs_0_.1), channel_id=1, source_target_pairs={{0,16},{8,24},{16,0},{24,8},{1,17},{9,25},{17,1},{25,9},{2,18},{10... | collective-permute-start | bytes 196616 | tf_op jit(solution)/shard_map/ppermute | solution.py:47
  3.0 3.8 %collective-permute-start.2 = (bf16[64,512]{1,0:T(8,128)(2,1)}, bf16[64,512]{1,0:T(8,128)(2,1)S(1)}, u32[]{:S(2)}, u32[]{:S(2)}) collective-permute-start(bf16[64,512]{1,0:T(8,128)(2,1)} %refs_0_.1), channel_id=1, source_target_pairs={{0,8},{8,0},{16,24},{24,16},{1,9},{9,1},{17,25},{25,17},{2,10},{10... | collective-permute-start | bytes 196616 | tf_op jit(solution)/shard_map/ppermute | solution.py:47
  5.4 1.4 %collective-permute-start.1 = (bf16[64,512]{1,0:T(8,128)(2,1)S(1)}, bf16[64,512]{1,0:T(8,128)(2,1)S(1)}, u32[]{:S(2)}, u32[]{:S(2)}) collective-permute-start(bf16[64,512]{1,0:T(8,128)(2,1)S(1)} %pass.1.gate_ref.refs_1_), channel_id=1, source_target_pairs={{0,8},{8,0},{16,24},{24,16},{1,9},{9,1},{17,25},{25,17},{2,10},{10... | collective-permute-start | bytes 196616 | tf_op jit(solution)/shard_map/ppermute | solution.py:47
  7.7 5.9 %collective-permute-start.4 = (bf16[64,640]{1,0:T(8,128)(2,1)S(1)}, bf16[64,640]{1,0:T(8,128)(2,1)S(1)}, u32[]{:S(2)}, u32[]{:S(2)}) collective-permute-start(bf16[64,640]{1,0:T(8,128)(2,1)S(1)} %get-tuple-element.38), channel_id=1, source_target_pairs={{0,16},{8,24},{16,0},{24,8},{1,17},{9,25},{17,1},{25,9},{2,18},{10... | collective-permute-start | bytes 245768 | tf_op jit(solution)/shard_map/ppermute | solution.py:47
  9.8 3.8 %collective-permute-start.5 = (bf16[64,640]{1,0:T(8,128)(2,1)S(1)}, bf16[64,640]{1,0:T(8,128)(2,1)S(1)}, u32[]{:S(2)}, u32[]{:S(2)}) collective-permute-start(bf16[64,640]{1,0:T(8,128)(2,1)S(1)} %get-tuple-element.39), channel_id=1, source_target_pairs={{0,8},{8,0},{16,24},{24,16},{1,9},{9,1},{17,25},{25,17},{2,10},{10... | collective-permute-start | bytes 245768 | tf_op jit(solution)/shard_map/ppermute | solution.py:47
  10.0 4.3 %collective-permute-start.3 = (bf16[64,640]{1,0:T(8,128)(2,1)S(1)}, bf16[64,640]{1,0:T(8,128)(2,1)S(1)}, u32[]{:S(2)}, u32[]{:S(2)}) collective-permute-start(bf16[64,640]{1,0:T(8,128)(2,1)S(1)} %get-tuple-element.35.gate_ref), channel_id=1, source_target_pairs={{0,24},{8,16},{16,8},{24,0},{1,25},{9,17},{17,9},{25,1},{2,26},{10... | collective-permute-start | bytes 245768 | tf_op jit(solution)/shard_map/ppermute | solution.py:47
  17.6 6.4 %collective-permute-start.6 = (bf16[2,16,2560]{2,1,0:T(8,128)(2,1)S(1)}, bf16[2,16,2560]{2,1,0:T(8,128)(2,1)S(1)}, u32[]{:S(2)}, u32[]{:S(2)}) collective-permute-start(bf16[2,16,2560]{2,1,0:T(8,128)(2,1)S(1)} %get-tuple-element.42), channel_id=1, source_target_pairs={{0,1},{1,0},{2,3},{3,2},{4,5},{5,4},{6,7},{7,6},{8,9},{9,8},{10,11... | collective-permute-start | bytes 491528 | tf_op jit(solution)/shard_map/ppermute | solution.py:47
  19.4 6.4 %collective-permute-start.8 = (bf16[2,16,2560]{2,1,0:T(8,128)(2,1)S(1)}, bf16[2,16,2560]{2,1,0:T(8,128)(2,1)S(1)}, u32[]{:S(2)}, u32[]{:S(2)}) collective-permute-start(bf16[2,16,2560]{2,1,0:T(8,128)(2,1)S(1)} %get-tuple-element.46), channel_id=1, source_target_pairs={{0,2},{1,3},{2,0},{3,1},{4,6},{5,7},{6,4},{7,5},{8,10},{9,11},{10,... | collective-permute-start | bytes 491528 | tf_op jit(solution)/shard_map/ppermute | solution.py:47
  24.0 4.5 %collective-permute-start.7 = (bf16[16,2560]{1,0:T(8,128)(2,1)S(1)}, bf16[16,2560]{1,0:T(8,128)(2,1)S(1)}, u32[]{:S(2)}, u32[]{:S(2)}) collective-permute-start(bf16[16,2560]{1,0:T(8,128)(2,1)S(1)} %get-tuple-element.44), channel_id=1, source_target_pairs={{0,2},{1,3},{2,0},{3,1},{4,6},{5,7},{6,4},{7,5},{8,10},{9,11},{10,... | collective-permute-start | bytes 245768 | tf_op jit(solution)/shard_map/ppermute | solution.py:47
  25.9 4.5 %collective-permute-start.9 = (bf16[16,2560]{1,0:T(8,128)(2,1)S(1)}, bf16[16,2560]{1,0:T(8,128)(2,1)S(1)}, u32[]{:S(2)}, u32[]{:S(2)}) collective-permute-start(bf16[16,2560]{1,0:T(8,128)(2,1)S(1)} %get-tuple-element.48), channel_id=1, source_target_pairs={{0,1},{1,0},{2,3},{3,2},{4,5},{5,4},{6,7},{7,6},{8,9},{9,8},{10,11... | collective-permute-start | bytes 245768 | tf_op jit(solution)/shard_map/ppermute | solution.py:47
  30.4 9.4 %collective-permute-start.10 = (bf16[16,5120]{1,0:T(8,128)(2,1)S(1)}, bf16[16,5120]{1,0:T(8,128)(2,1)S(1)}, u32[]{:S(2)}, u32[]{:S(2)}) collective-permute-start(bf16[16,5120]{1,0:T(8,128)(2,1)S(1)} %get-tuple-element.49.gate_ref), channel_id=1, source_target_pairs={{0,4},{1,5},{2,6},{3,7},{4,0},{5,1},{6,2},{7,3},{8,12},{9,13},{10,... | collective-permute-start | bytes 491528 | tf_op jit(solution)/shard_map/ppermute | solution.py:47
  36.4 3.4 %copy-start = (bf16[64,5120]{1,0:T(8,128)(2,1)S(1)}, bf16[64,5120]{1,0:T(8,128)(2,1)}, u32[]{:S(2)}) copy-start(bf16[64,5120]{1,0:T(8,128)(2,1)} %param.19) | copy-start | bytes 1966084
  40.1 5.4 %collective-permute-start.11 = (bf16[16,5120]{1,0:T(8,128)(2,1)S(1)}, bf16[16,5120]{1,0:T(8,128)(2,1)S(1)}, u32[]{:S(2)}, u32[]{:S(2)}) collective-permute-start(bf16[16,5120]{1,0:T(8,128)(2,1)S(1)} %norm.1.refs_0_), channel_id=1, source_target_pairs={{0,2},{1,3},{2,0},{3,1},{4,6},{5,7},{6,4},{7,5},{8,10},{9,11},{10,... | collective-permute-start | bytes 491528 | tf_op jit(solution)/shard_map/ppermute | solution.py:47
  41.2 8.1 %collective-permute-start.16 = (bf16[16,5120]{1,0:T(8,128)(2,1)S(1)}, bf16[16,5120]{1,0:T(8,128)(2,1)S(1)}, u32[]{:S(2)}, u32[]{:S(2)}) collective-permute-start(bf16[16,5120]{1,0:T(8,128)(2,1)S(1)} %norm.1.refs_0_), channel_id=1, source_target_pairs={{0,17},{1,16},{2,19},{3,18},{4,21},{5,20},{6,23},{7,22},{8,25},{9,... | collective-permute-start | bytes 491528 | tf_op jit(solution)/shard_map/ppermute | solution.py:569
  43.0 10.5 %collective-permute-start.14 = (bf16[16,5120]{1,0:T(8,128)(2,1)S(1)}, bf16[16,5120]{1,0:T(8,128)(2,1)S(1)}, u32[]{:S(2)}, u32[]{:S(2)}) collective-permute-start(bf16[16,5120]{1,0:T(8,128)(2,1)S(1)} %norm.1.refs_0_), channel_id=1, source_target_pairs={{0,16},{1,17},{2,18},{3,19},{4,20},{5,21},{6,22},{7,23},{8,24},{9,... | collective-permute-start | bytes 491528 | tf_op jit(solution)/shard_map/ppermute | solution.py:569
  43.5 10.0 %collective-permute-start.12 = (bf16[16,5120]{1,0:T(8,128)(2,1)S(1)}, bf16[16,5120]{1,0:T(8,128)(2,1)S(1)}, u32[]{:S(2)}, u32[]{:S(2)}) collective-permute-start(bf16[16,5120]{1,0:T(8,128)(2,1)S(1)} %norm.1.refs_0_), channel_id=1, source_target_pairs={{0,1},{1,0},{2,3},{3,2},{4,5},{5,4},{6,7},{7,6},{8,9},{9,8},{10,11... | collective-permute-start | bytes 491528 | tf_op jit(solution)/shard_map/ppermute | solution.py:569
  45.4 9.4 %collective-permute-start.17 = (bf16[16,5120]{1,0:T(8,128)(2,1)S(1)}, bf16[16,5120]{1,0:T(8,128)(2,1)S(1)}, u32[]{:S(2)}, u32[]{:S(2)}) collective-permute-start(bf16[16,5120]{1,0:T(8,128)(2,1)S(1)} %collective-permute-done.11.gate_ref.refs_1_), channel_id=1, source_target_pairs={{0,17},{1,16},{2,19},{3,18},{4,21},{5,20},{6,23},{7,22},{8,25},{9,... | collective-permute-start | bytes 491528 | tf_op jit(solution)/shard_map/ppermute | solution.py:569
  47.9 8.5 %collective-permute-start.15 = (bf16[16,5120]{1,0:T(8,128)(2,1)S(1)}, bf16[16,5120]{1,0:T(8,128)(2,1)S(1)}, u32[]{:S(2)}, u32[]{:S(2)}) collective-permute-start(bf16[16,5120]{1,0:T(8,128)(2,1)S(1)} %collective-permute-done.11.gate_ref.refs_1_), channel_id=1, source_target_pairs={{0,16},{1,17},{2,18},{3,19},{4,20},{5,21},{6,22},{7,23},{8,24},{9,... | collective-permute-start | bytes 491528 | tf_op jit(solution)/shard_map/ppermute | solution.py:569
  49.3 7.3 %collective-permute-start.13 = (bf16[16,5120]{1,0:T(8,128)(2,1)S(1)}, bf16[16,5120]{1,0:T(8,128)(2,1)S(1)}, u32[]{:S(2)}, u32[]{:S(2)}) collective-permute-start(bf16[16,5120]{1,0:T(8,128)(2,1)S(1)} %collective-permute-done.11.gate_ref.refs_1_), channel_id=1, source_target_pairs={{0,1},{1,0},{2,3},{3,2},{4,5},{5,4},{6,7},{7,6},{8,9},{9,8},{10,11... | collective-permute-start | bytes 491528 | tf_op jit(solution)/shard_map/ppermute | solution.py:569
  56.7 2.2 %collective-permute-start.18 = (bf16[128,2560]{1,0:T(8,128)(2,1)S(1)}, bf16[128,2560]{1,0:T(8,128)(2,1)S(1)}, u32[]{:S(2)}, u32[]{:S(2)}) collective-permute-start(bf16[128,2560]{1,0:T(8,128)(2,1)S(1)} %get-tuple-element.51.left_ref), channel_id=1, source_target_pairs={{0,8},{8,0},{16,24},{24,16},{1,9},{9,1},{17,25},{25,17},{2,10},{10... | collective-permute-start | bytes 1966088 | tf_op jit(solution)/shard_map/ppermute | solution.py:47
  56.8 6.6 %collective-permute-start.19 = (bf16[128,2560]{1,0:T(8,128)(2,1)S(1)}, bf16[128,2560]{1,0:T(8,128)(2,1)S(1)}, u32[]{:S(2)}, u32[]{:S(2)}) collective-permute-start(bf16[128,2560]{1,0:T(8,128)(2,1)S(1)} %get-tuple-element.53.left_ref), channel_id=1, source_target_pairs={{0,8},{8,0},{16,24},{24,16},{1,9},{9,1},{17,25},{25,17},{2,10},{10... | collective-permute-start | bytes 1966088 | tf_op jit(solution)/shard_map/ppermute | solution.py:47
